TPU v7x, 128 devices: a whole 4x4x4 slice. The times are simulated.
128 devices in a mesh: lat: 16 (over z, x_hi, core), lon: 8 (over y, x_lo).
Axes of the slice: x: 4 (x_hi: 2, x_lo: 2; x = x_hi * 2 + x_lo), y: 4, z: 4, core: 2. Of those that a mesh axis runs over, the one named last changes fastest.
Arguments:
- buffer: bfloat16 [147456, 512], P(('lat', 'lon')), may hold values from -25 to 25
- fetch_owner: int32 [16, 8, 2304, 1], P('lat', 'lon'), may hold values from 0 to 15; in each aligned block of 2304 rows (0 to 2303, 2304 to 4607, ..., all dimensions but the last counted through in order) at most 288 rows name the same one
- fetch_slot: int32 [16, 8, 2304], P('lat', 'lon'), may hold values from 0 to 1151
- norm_gain: float32 [512], replicated, may hold values from 0.1 to 1.9
- qkv_weight: bfloat16 [512, 1536], replicated, may hold values from -8 to 8
- out_weight: bfloat16 [512, 512], replicated, may hold values from -0.25 to 0.25
- out_grad: bfloat16 [192, 384, 4, 512], P('lat', 'lon'), may hold values from -6 to 6
Outputs:
- block_out: bfloat16 [192, 384, 4, 512], P('lat', 'lon')
- grad_states: bfloat16 [192, 384, 4, 512], P('lat', 'lon')
- grad_qkv: float32 [512, 1536], P(('lat', 'lon'))
- grad_outw: float32 [512, 512], P(('lat', 'lon'))
Inputs may be any that keep to these rules, and one draw needn't show every extreme that they name: `fetch_owner`: in the 2304 rows of one device at most 288 name the same owner band, and some owner band is named by exactly 288.
All inputs are finite; a program needn't handle non-finite values.
Results may differ from a plain program's by a relative error of at most 0.0091.
Values may be sent and summed in bfloat16 or wider, within the bound.
No kernel may reach another device: no remote copies, remote signals or barrier semaphores. Data moves between devices by JAX's collectives and lax.ppermute only.
A program may use at most 192 MiB of HBM per device.

v0:
```python
import jax
import jax.numpy as jnp
from jax import lax
from jax.sharding import PartitionSpec as P

HEADS = 8
WLAT = 6
WLON = 12
WLEV = 2


EPSILON = 1e-05


def from_behind(value, axis, steps):
    count = lax.axis_size(axis)
    pairs = [(source, (source + steps) % count) for source in range(count)]
    return lax.ppermute(value, axis, pairs)


def mixed_product(form, left, right):
    return jnp.einsum(form, left, right, preferred_element_type=jnp.float32)


def pair_windows(paired):
    lat_size, lon_size, lev_size, features = paired.shape[1:]
    shaped = paired.reshape(
        2, lat_size // WLAT, WLAT, lon_size // WLON, WLON, lev_size // WLEV, WLEV, features
    )
    shaped = shaped.transpose(0, 1, 3, 5, 2, 4, 6, 7)
    return shaped.reshape(
        2, lat_size // WLAT, lon_size // WLON * (lev_size // WLEV), WLAT * WLON * WLEV, features
    )


def pair_grid(windows, lat_size, lon_size, lev_size):
    features = windows.shape[-1]
    shaped = windows.reshape(
        lat_size // WLAT, 2, lon_size // WLON, lev_size // WLEV, WLAT, WLON, WLEV, features
    )
    shaped = shaped.transpose(1, 0, 4, 2, 5, 3, 6, 7)
    return shaped.reshape(2, lat_size, lon_size, lev_size, features)


def window_pass(states_win, cotan_win, group_win, norm_gain, qkv_weight, out_weight):
    win_count, win_size, features = states_win.shape
    head_size = features // HEADS
    score_scale = head_size ** (-0.5)
    inputs = states_win.astype(jnp.float32)
    centred = inputs - jnp.mean(inputs, -1, keepdims=True)
    inverse = lax.rsqrt(jnp.mean(centred * centred, -1, keepdims=True) + EPSILON)
    normed = centred * inverse
    hidden = (normed * norm_gain).astype(jnp.bfloat16)
    flat_hidden = hidden.reshape(win_count * win_size, features)
    packed = jnp.dot(flat_hidden, qkv_weight, preferred_element_type=jnp.float32).astype(
        jnp.bfloat16
    )
    packed = packed.reshape(win_count, win_size, 3, HEADS, head_size)
    queries = packed[:, :, 0]
    key_part = packed[:, :, 1]
    value_part = packed[:, :, 2]
    scores = mixed_product("nqhe,nkhe->nhqk", queries, key_part) * score_scale
    same_group = (group_win[:, :, None] == group_win[:, None, :])[:, None]
    scores = jnp.where(same_group, scores, -jnp.inf)
    shifted = jnp.exp(scores - jnp.max(scores, -1, keepdims=True))
    attention = shifted / jnp.sum(shifted, -1, keepdims=True)
    attention_low = attention.astype(jnp.bfloat16)
    attended = mixed_product("nhqk,nkhe->nqhe", attention_low, value_part).astype(jnp.bfloat16)
    attended = attended.reshape(win_count * win_size, features)
    projected = jnp.dot(attended, out_weight, preferred_element_type=jnp.float32)
    result = (inputs.reshape(win_count * win_size, features) + projected).astype(jnp.bfloat16)
    cotan_flat = cotan_win.reshape(win_count * win_size, features)
    grad_attended = jnp.dot(cotan_flat, out_weight.T, preferred_element_type=jnp.float32).astype(
        jnp.bfloat16
    )
    grad_attended = grad_attended.reshape(win_count, win_size, HEADS, head_size)
    grad_probs = mixed_product("nqhe,nkhe->nhqk", grad_attended, value_part)
    grad_values = mixed_product("nhqk,nqhe->nkhe", attention_low, grad_attended).astype(
        jnp.bfloat16
    )
    grad_scores = (
        attention * (grad_probs - jnp.sum(attention * grad_probs, -1, keepdims=True)) * score_scale
    )
    grad_scores = grad_scores.astype(jnp.bfloat16)
    grad_queries = mixed_product("nhqk,nkhe->nqhe", grad_scores, key_part).astype(jnp.bfloat16)
    grad_keys = mixed_product("nhqk,nqhe->nkhe", grad_scores, queries).astype(jnp.bfloat16)
    grad_packed = jnp.stack([grad_queries, grad_keys, grad_values], 2).reshape(
        win_count * win_size, 3 * features
    )
    grad_hidden = jnp.dot(grad_packed, qkv_weight.T, preferred_element_type=jnp.float32)
    grad_hidden = grad_hidden.reshape(win_count, win_size, features) * norm_gain
    grad_norm = inverse * (
        grad_hidden
        - jnp.mean(grad_hidden, -1, keepdims=True)
        - normed * jnp.mean(grad_hidden * normed, -1, keepdims=True)
    )
    grad_rolled = (cotan_win.astype(jnp.float32) + grad_norm).astype(jnp.bfloat16)
    both_out = jnp.stack([result.reshape(win_count, win_size, features), grad_rolled])
    return (both_out, flat_hidden, grad_packed, attended, cotan_flat)


def per_device(buffer, fetch_owner, fetch_slot, norm_gain, qkv_weight, out_weight, out_grad):
    lat_size, lon_size, lev_size, features = out_grad.shape
    tokens = lat_size * lon_size * lev_size
    owners = fetch_owner.reshape(tokens)
    slot_ids = fetch_slot.reshape(tokens)
    bands = lax.axis_size("lat")
    capacity = 2 * tokens // bands
    onehot = (owners[:, None] == jnp.arange(bands, dtype=jnp.int32)[None, :]).astype(jnp.int32)
    rank_ids = jnp.sum(jnp.cumsum(onehot, 0) * onehot, 1) - 1
    slot_index = owners * capacity + rank_ids
    requests = (
        jnp.zeros((bands * capacity,), jnp.int32)
        .at[slot_index]
        .set(slot_ids)
        .reshape(bands, capacity)
    )
    replies = lax.all_to_all(
        jnp.take(
            buffer, lax.all_to_all(requests, "lat", split_axis=0, concat_axis=0, tiled=True), axis=0
        ),
        "lat",
        split_axis=0,
        concat_axis=0,
        tiled=True,
    )
    fetched = jnp.take(replies.reshape(bands * capacity, features), slot_index, axis=0)
    states = fetched.reshape(lat_size, lon_size, lev_size, features)
    half_lat = WLAT // 2
    half_lon = WLON // 2
    paired = jnp.stack([states, out_grad])
    upper_rows = from_behind(paired[:, :half_lat], "lat", -1)
    paired = jnp.concatenate([paired[:, half_lat:], upper_rows], 1)
    side_cols = from_behind(paired[:, :, :half_lon], "lon", -1)
    paired = jnp.concatenate([paired[:, :, half_lon:], side_cols], 2)
    windows = pair_windows(paired)
    lat_blocks = lat_size // WLAT
    win_per_block = windows.shape[2]
    win_tokens = WLAT * WLON * WLEV
    block_lat = jnp.arange(lat_blocks, dtype=jnp.int32)[:, None] * WLAT
    inner_lat = jnp.arange(win_tokens, dtype=jnp.int32)[None, :] // (WLON * WLEV)
    latitude = lax.axis_index("lat") * lat_size + block_lat + inner_lat
    group_rows = (latitude >= lat_size * bands - half_lat).astype(jnp.int32)
    group_win = jnp.broadcast_to(group_rows[:, None, :], (lat_blocks, win_per_block, win_tokens))

    def window_block(pieces):
        return window_pass(pieces[0], pieces[1], pieces[2], norm_gain, qkv_weight, out_weight)

    both_out, flat_hidden, grad_packed, attended, cotan_flat = lax.map(
        window_block, (windows[0], windows[1], group_win)
    )
    flat_hidden = flat_hidden.reshape(tokens, features)
    grad_packed = grad_packed.reshape(tokens, 3 * features)
    attended = attended.reshape(tokens, features)
    cotan_flat = cotan_flat.reshape(tokens, features)
    qkv_term = jnp.dot(flat_hidden.T, grad_packed, preferred_element_type=jnp.float32)
    outw_term = jnp.dot(attended.T, cotan_flat, preferred_element_type=jnp.float32)
    grad_first, grad_second = (
        lax.psum_scatter(qkv_term, ("lat", "lon"), scatter_dimension=0, tiled=True),
        lax.psum_scatter(outw_term, ("lat", "lon"), scatter_dimension=0, tiled=True),
    )
    merged = pair_grid(both_out, lat_size, lon_size, lev_size)
    side_cols = from_behind(merged[:, :, -half_lon:], "lon", 1)
    merged = jnp.concatenate([side_cols, merged[:, :, :-half_lon]], 2)
    upper_rows = from_behind(merged[:, -half_lat:], "lat", 1)
    merged = jnp.concatenate([upper_rows, merged[:, :-half_lat]], 1)
    return (merged[0], merged[1], grad_first, grad_second)


def solution(mesh):
    return jax.shard_map(
        per_device,
        mesh=mesh,
        in_specs=(
            P(("lat", "lon"), None),
            P("lat", "lon", None, None),
            P("lat", "lon", None),
            P(),
            P(),
            P(),
            P("lat", "lon", None, None),
        ),
        out_specs=(
            P("lat", "lon", None, None),
            P("lat", "lon", None, None),
            P(("lat", "lon"), None),
            P(("lat", "lon"), None),
        ),
        check_vma=False,
    )
```

profile of v0, /device:TPU:1, one launch (start us, length us, event | category | flops | bytes accessed | tf_op | source)
XLA Modules:
  0.0 823.2 jit_solution(2105820161280674608)
XLA Ops:
  24.1 16.4 %all_to_all.20 = s32[16,1,288]{2,1,0:T(1,128)S(1)} all-to-all(s32[16,1,288]{2,1,0:T(1,128)S(1)} %all_to_all.13), channel_id=1, replica_groups=mesh['lat'=16,'lon'=8] {'lat'}, dimensions={0} | all-to-all | bytes 36864 | tf_op jit(solution)/shard_map/all_to_all | solution.py:120
  40.6 13.8 %gather_fusion = bf16[4608,512]{1,0:T(8,128)(2,1)} fusion(bf16[1152,512]{1,0:T(8,128)(2,1)S(1)} %copy-done, s32[5120]{0:T(1024)S(1)} %pad_clamp_fusion), kind=kCustom, calls=%fused_computation | custom fusion | bytes 9455616 | tf_op jit(solution)/shard_map/jit(_take)/gather | solution.py:119
  66.2 55.5 %all-to-all-done.1 = bf16[16,288,512]{2,1,0:T(8,128)(2,1)} async-done(((bf16[16,288,512]{2,1,0:T(8,128)(2,1)}), bf16[16,288,512]{2,1,0:T(8,128)(2,1)}, u32[]{:S(2)}, u32[]{:S(2)}) %all-to-all-start.1) | async-done | bytes 4718624 | tf_op jit(solution)/shard_map/all_to_all | solution.py:118
  121.7 10.0 %gather_fusion.1 = bf16[2304,512]{1,0:T(8,128)(2,1)S(1)} fusion(bf16[4608,512]{1,0:T(8,128)(2,1)} %bitcast.25, s32[3072]{0:T(1024)S(1)} %pad_clamp_fusion.1), kind=kCustom, calls=%fused_computation.1 | custom fusion | bytes 4727808 | tf_op jit(solution)/shard_map/jit(_take)/gather | solution.py:127
  143.9 12.5 %collective-permute-done = bf16[2,3,48,4,512]{4,3,2,1,0:T(4,128)(2,1)S(1)} collective-permute-done((bf16[2,3,48,4,512]{4,3,2,1,0:T(4,128)(2,1)}, bf16[2,3,48,4,512]{4,3,2,1,0:T(4,128)(2,1)S(1)}, u32[]{:S(2)}, u32[]{:S(2)}) %collective-permute-start) | collective-permute-done | bytes 1179680 | tf_op jit(solution)/shard_map/ppermute | solution.py:18
  176.3 10.5 %reshape.353 = bf16[2,2,6,4,12,2,2,512]{7,6,5,4,3,2,1,0:T(2,128)(2,1)} reshape(bf16[2,12,48,4,512]{4,3,2,1,0:T(4,128)(2,1)} %pad_maximum_fusion.2) | data formatting | bytes 9437184 | tf_op jit(solution)/shard_map/reshape | solution.py:27
  216.3 385.7 %while.18 = (s32[]{:T(128)}, bf16[2,2,8,144,512]{4,3,2,1,0:T(8,128)(2,1)}, bf16[2,1152,512]{2,1,0:T(8,128)(2,1)}, bf16[2,1152,1536]{1,2,0:T(8,128)(2,1)}, bf16[2...) while((s32[]{:T(128)}, ...), condition=%wide.region_12.13_spmd, body=%wide.region_4.12_spmd.sunk | while | flops 5917890048 | bytes 255339152 | solution.py:149
  233.4 9.5 %reshape.402 = bf16[8,144,3,8,64]{4,3,2,1,0:T(8,128)(2,1)} reshape(bf16[1152,1536]{1,0:T(8,128)(2,1)} %convolution_convert_fusion.5) | data formatting | bytes 7077888 | tf_op jit(solution)/shard_map/while/body/eval_jaxpr/reshape | solution.py:58
  304.3 17.0 %convert_bitcast_fusion.10 = bf16[8,144,1,8,64]{1,4,3,0,2:T(8,128)(2,1)} fusion(f32[8,8,144,144]{2,3,1,0:T(8,128)} %fusion.145, bf16[8,144,1,8,64]{1,4,3,0,2:T(8,128)(2,1)} %copy.118, f32[8,8,144,144]{2,3,1,0:T(8,128)} %get-tuple-element.239, f32[8,8,144]{2,1,0:T(8,128)} %copy-done.23), kind=kOutput, calls=%fused_computation.58.clone.1 | convolution fusion | flops 179758224 | bytes 13012992 | tf_op jit(solution)/shard_map/while/body/eval_jaxpr/nhqk,nkhe->nqhe/dot_general | solution.py:22
  321.4 16.9 %convert_bitcast_fusion.9 = bf16[8,144,1,8,64]{1,4,3,0,2:T(8,128)(2,1)} fusion(f32[8,8,144,144]{2,3,1,0:T(8,128)} %fusion.145, bf16[8,144,1,8,64]{1,4,3,0,2:T(8,128)(2,1)} %copy.119, f32[8,8,144,144]{2,3,1,0:T(8,128)} %get-tuple-element.239, f32[8,8,144]{2,1,0:T(8,128)} %copy-done.23), kind=kOutput, calls=%fused_computation.57.clone.1 | convolution fusion | flops 179758224 | bytes 13012992 | tf_op jit(solution)/shard_map/while/body/eval_jaxpr/nhqk,nqhe->nkhe/dot_general | solution.py:22
  348.5 11.0 %copy.121 = bf16[8,144,3,8,64]{4,3,2,1,0:T(8,128)(2,1)} copy(bf16[8,144,3,8,64]{1,4,3,0,2:T(8,128)(2,1)} %pad_maximum_fusion.7) | data formatting | bytes 7077888 | tf_op jit(solution)/shard_map/while/body/eval_jaxpr/stack | solution.py:87
  359.6 9.9 %dot_general.41 = bf16[8,144,1536]{2,1,0:T(8,128)(2,1)} reshape(bf16[8,144,3,8,64]{4,3,2,1,0:T(8,128)(2,1)} %copy.121) | data formatting | bytes 7077888 | tf_op jit(solution)/shard_map/while/body/eval_jaxpr/dot_general | solution.py:90
  382.4 9.9 %copy.123 = bf16[8,144,3,8,64]{1,0,4,3,2:T(8,128)(2,1)} copy(bf16[8,144,3,8,64]{1,4,3,0,2:T(8,128)(2,1)} %pad_maximum_fusion.7) | data formatting | bytes 7077888 | tf_op jit(solution)/shard_map/while/body/eval_jaxpr/stack | solution.py:87
  392.3 10.3 %broadcast_in_dim.113 = bf16[1,1152,1536]{1,2,0:T(8,128)(2,1)} reshape(bf16[8,144,3,8,64]{1,0,4,3,2:T(8,128)(2,1)} %copy.123) | data formatting | bytes 7077888 | tf_op jit(solution)/shard_map/while/body/jit(dynamic_update_index_in_dim)/broadcast_in_dim | solution.py:149
  487.8 17.0 %convert_bitcast_fusion.10 = bf16[8,144,1,8,64]{1,4,3,0,2:T(8,128)(2,1)} fusion(f32[8,8,144,144]{2,3,1,0:T(8,128)} %fusion.145, bf16[8,144,1,8,64]{1,4,3,0,2:T(8,128)(2,1)} %copy.118, f32[8,8,144,144]{2,3,1,0:T(8,128)} %get-tuple-element.239, f32[8,8,144]{2,1,0:T(8,128)} %copy-done.23), kind=kOutput, calls=%fused_computation.58.clone.1 | convolution fusion | flops 179758224 | bytes 13012992 | tf_op jit(solution)/shard_map/while/body/eval_jaxpr/nhqk,nkhe->nqhe/dot_general | solution.py:22
  504.9 16.9 %convert_bitcast_fusion.9 = bf16[8,144,1,8,64]{1,4,3,0,2:T(8,128)(2,1)} fusion(f32[8,8,144,144]{2,3,1,0:T(8,128)} %fusion.145, bf16[8,144,1,8,64]{1,4,3,0,2:T(8,128)(2,1)} %copy.119, f32[8,8,144,144]{2,3,1,0:T(8,128)} %get-tuple-element.239, f32[8,8,144]{2,1,0:T(8,128)} %copy-done.23), kind=kOutput, calls=%fused_computation.57.clone.1 | convolution fusion | flops 179758224 | bytes 13012992 | tf_op jit(solution)/shard_map/while/body/eval_jaxpr/nhqk,nqhe->nkhe/dot_general | solution.py:22
  532.0 11.0 %copy.121 = bf16[8,144,3,8,64]{4,3,2,1,0:T(8,128)(2,1)} copy(bf16[8,144,3,8,64]{1,4,3,0,2:T(8,128)(2,1)} %pad_maximum_fusion.7) | data formatting | bytes 7077888 | tf_op jit(solution)/shard_map/while/body/eval_jaxpr/stack | solution.py:87
  543.1 9.9 %dot_general.41 = bf16[8,144,1536]{2,1,0:T(8,128)(2,1)} reshape(bf16[8,144,3,8,64]{4,3,2,1,0:T(8,128)(2,1)} %copy.121) | data formatting | bytes 7077888 | tf_op jit(solution)/shard_map/while/body/eval_jaxpr/dot_general | solution.py:90
  566.0 9.9 %copy.123 = bf16[8,144,3,8,64]{1,0,4,3,2:T(8,128)(2,1)} copy(bf16[8,144,3,8,64]{1,4,3,0,2:T(8,128)(2,1)} %pad_maximum_fusion.7) | data formatting | bytes 7077888 | tf_op jit(solution)/shard_map/while/body/eval_jaxpr/stack | solution.py:87
  575.9 10.3 %broadcast_in_dim.113 = bf16[1,1152,1536]{1,2,0:T(8,128)(2,1)} reshape(bf16[8,144,3,8,64]{1,0,4,3,2:T(8,128)(2,1)} %copy.123) | data formatting | bytes 7077888 | tf_op jit(solution)/shard_map/while/body/jit(dynamic_update_index_in_dim)/broadcast_in_dim | solution.py:149
  610.0 9.9 %copy.108 = bf16[2,2,4,2,6,12,2,512]{7,6,3,5,2,4,0,1:T(2,128)(2,1)} copy(bf16[2,2,4,2,6,12,2,512]{7,6,5,4,3,2,1,0:T(2,128)(2,1)} %reshape.354) | data formatting | bytes 9437184 | tf_op jit(solution)/shard_map/reshape | solution.py:38
  619.9 11.4 %reshape.355 = bf16[2,12,48,4,512]{4,3,2,1,0:T(4,128)(2,1)} reshape(bf16[2,2,6,4,12,2,2,512]{7,6,5,4,3,2,1,0:T(2,128)(2,1)} %bitcast.230) | data formatting | bytes 9437184 | tf_op jit(solution)/shard_map/reshape | solution.py:42
  662.2 11.1 %collective-permute-done.3 = bf16[2,3,48,4,512]{4,3,2,1,0:T(4,128)(2,1)S(1)} collective-permute-done((bf16[2,3,48,4,512]{4,3,2,1,0:T(4,128)(2,1)S(1)}, bf16[2,3,48,4,512]{4,3,2,1,0:T(4,128)(2,1)S(1)}, u32[]{:S(2)}, u32[]{:S(2)}) %collective-permute-start.3) | collective-permute-done | bytes 1179680 | tf_op jit(solution)/shard_map/ppermute | solution.py:18
  682.4 131.0 %all-reduce.5.cloned.1.call-done = (f32[512,1536]{1,0:T(8,128)}, f32[512,512]{1,0:T(8,128)}) async-done(((f32[512,1536]{1,0:T(8,128)}, f32[512,512]{1,0:T(8,128)}), (f32[512,1536]{1,0:T(8,128)}, f32[512,512]{1,0:T(8,128)})) %all-reduce.5.cloned.1.call-update) | async-done | bytes 4194320
  (220 shorter events, 347.8 us)
Async XLA Ops:
  7.2 33.5 %copy-start = (bf16[1152,512]{1,0:T(8,128)(2,1)S(1)}, bf16[1152,512]{1,0:T(8,128)(2,1)}, u32[]{:S(2)}) copy-start(bf16[1152,512]{1,0:T(8,128)(2,1)} %param.9) | copy-start | bytes 3538948
  60.2 61.5 %all-to-all-start.1 = ((bf16[16,288,512]{2,1,0:T(8,128)(2,1)}), bf16[16,288,512]{2,1,0:T(8,128)(2,1)}, u32[]{:S(2)}, u32[]{:S(2)}) async-start(bf16[16,288,512]{2,1,0:T(8,128)(2,1)} %broadcast_select_fusion), calls=%async_computation.1 | async-start | bytes 9437184 | tf_op jit(solution)/shard_map/all_to_all | solution.py:118
  64.9 748.5 %all-reduce.5.cloned.1.call-start = ((), (), s32[]{:S(2)}) async-start(), calls=%async_computation.2 | async-start | bytes 8388608
  139.0 17.3 %collective-permute-start = (bf16[2,3,48,4,512]{4,3,2,1,0:T(4,128)(2,1)}, bf16[2,3,48,4,512]{4,3,2,1,0:T(4,128)(2,1)S(1)}, u32[]{:S(2)}, u32[]{:S(2)}) collective-permute-start(bf16[2,3,48,4,512]{4,3,2,1,0:T(4,128)(2,1)} %pad_maximum_fusion.4), channel_id=1, source_target_pairs={{0,120},{8,0},{16,8},{24,16},{32,24},{40,32},{48,40},{56,48},{64,5... | collective-permute-start | bytes 3538952 | tf_op jit(solution)/shard_map/ppermute | solution.py:18
  143.9 12.9 %copy-start.9 = (bf16[2,9,48,4,512]{4,3,2,1,0:T(4,128)(2,1)}, bf16[2,9,48,4,512]{4,3,2,1,0:T(4,128)(2,1)S(1)}, u32[]{:S(2)}) copy-start(bf16[2,9,48,4,512]{4,3,2,1,0:T(4,128)(2,1)S(1)} %fusion.69) | copy-start | bytes 10616836
  156.8 14.3 %collective-permute-start.1 = (bf16[2,12,6,4,512]{4,3,2,1,0:T(4,128)(2,1)S(1)}, bf16[2,12,6,4,512]{4,3,2,1,0:T(4,128)(2,1)S(1)}, u32[]{:S(2)}, u32[]{:S(2)}) collective-permute-start(bf16[2,12,6,4,512]{4,3,2,1,0:T(4,128)(2,1)S(1)} %pad_maximum_fusion.5), channel_id=1, source_target_pairs={{0,7},{1,0},{2,1},{3,2},{4,3},{5,4},{6,5},{7,6},{8,15},{9,8},{10,9... | collective-permute-start | bytes 1769480 | tf_op jit(solution)/shard_map/ppermute | solution.py:18
  267.0 9.7 %copy-start.23 = (f32[8,8,144]{2,1,0:T(8,128)}, f32[8,8,144]{2,1,0:T(8,128)S(1)}, u32[]{:S(2)}) copy-start(f32[8,8,144]{2,1,0:T(8,128)S(1)} %get-tuple-element.240) | copy-start | bytes 110596 | tf_op jit(solution)/shard_map/while
  338.3 6.2 copy-start.6
  338.3 6.2 copy-start.7
  369.5 5.4 copy-start.5
  369.5 5.4 copy-start.14
  369.5 5.4 copy-start.15
  450.5 9.7 %copy-start.23 = (f32[8,8,144]{2,1,0:T(8,128)}, f32[8,8,144]{2,1,0:T(8,128)S(1)}, u32[]{:S(2)}) copy-start(f32[8,8,144]{2,1,0:T(8,128)S(1)} %get-tuple-element.240) | copy-start | bytes 110596 | tf_op jit(solution)/shard_map/while
  521.8 6.2 copy-start.6
  521.8 6.2 copy-start.7
  553.0 5.4 copy-start.5
  553.0 5.4 copy-start.14
  553.0 5.4 copy-start.15
  631.3 5.9 copy-start.20
  635.0 18.4 %copy-start.8 = (bf16[2,12,42,4,512]{4,3,2,1,0:T(4,128)(2,1)}, bf16[2,12,42,4,512]{4,3,2,1,0:T(4,128)(2,1)S(1)}, u32[]{:S(2)}) copy-start(bf16[2,12,42,4,512]{4,3,2,1,0:T(4,128)(2,1)S(1)} %slice.83) | copy-start | bytes 12386308
  636.8 16.6 %collective-permute-start.2 = (bf16[2,12,6,4,512]{4,3,2,1,0:T(4,128)(2,1)S(1)}, bf16[2,12,6,4,512]{4,3,2,1,0:T(4,128)(2,1)S(1)}, u32[]{:S(2)}, u32[]{:S(2)}) collective-permute-start(bf16[2,12,6,4,512]{4,3,2,1,0:T(4,128)(2,1)S(1)} %slice.82), channel_id=1, source_target_pairs={{0,1},{1,2},{2,3},{3,4},{4,5},{5,6},{6,7},{7,0},{8,9},{9,10},{10,1... | collective-permute-start | bytes 1769480 | tf_op jit(solution)/shard_map/ppermute | solution.py:18
  645.8 12.3 %copy-start.21 = (bf16[2,1152,512]{1,2,0:T(8,128)(2,1)S(1)}, bf16[2,1152,512]{1,2,0:T(8,128)(2,1)}, u32[]{:S(2)}) copy-start(bf16[2,1152,512]{1,2,0:T(8,128)(2,1)} %get-tuple-element.73) | copy-start | bytes 7077892
  654.2 19.1 %collective-permute-start.3 = (bf16[2,3,48,4,512]{4,3,2,1,0:T(4,128)(2,1)S(1)}, bf16[2,3,48,4,512]{4,3,2,1,0:T(4,128)(2,1)S(1)}, u32[]{:S(2)}, u32[]{:S(2)}) collective-permute-start(bf16[2,3,48,4,512]{4,3,2,1,0:T(4,128)(2,1)S(1)} %pad_maximum_fusion.3), channel_id=1, source_target_pairs={{0,8},{8,16},{16,24},{24,32},{32,40},{40,48},{48,56},{56,64},{64,7... | collective-permute-start | bytes 3538952 | tf_op jit(solution)/shard_map/ppermute | solution.py:18
  678.2 138.0 %copy-start.1 = (bf16[1152,512]{1,0:T(8,128)(2,1)S(1)}, bf16[1152,512]{1,0:T(8,128)(2,1)}, u32[]{:S(2)}) copy-start(bf16[1152,512]{1,0:T(8,128)(2,1)} %param.9) | copy-start | bytes 3538948
  (23 other events, 56.8 us)
Sparse Core Ops, SparseCore 0:
  662.3 151.0 all-reduce.4
where the time goes:
time: 834 us; the launch traced here: 823 us
  local copies, waits for them, and re-layouts  316 us (38%)
  waiting for transfers between devices  225 us (27%)
  matrix products  149 us (18%)
  other arithmetic  71.2 us (9%)
  loops' own time  19 us (2%)
  blocking collectives  16.4 us (2%)
  between operations  14.5 us (2%)
  starting transfers between devices  13.1 us (2%)
    unnamed x2, waiting for transfers between devices  131 us
    dot_general x12, matrix products, mixed_product(): return jnp.einsum(form, left, right, preferred_element_type=jnp.float32)  113 us
    all_to_all x1, waiting for transfers between devices, per_device(): lax.all_to_all(jnp.take(buffer, lax.all_to_all(requests, 'lat', split_axi...  55.5 us
    another operation x4, local copies, waits for them, and re-layouts, window_pass(): jnp.stack([grad_queries, grad_keys, grad_values], 2)  41.9 us
    ppermute x4, waiting for transfers between devices, from_behind(): return lax.ppermute(value, axis, pairs)  37.9 us
    while x74, local copies, waits for them, and re-layouts  30.5 us
    broadcast_in_dim x4, local copies, waits for them, and re-layouts, per_device(): lax.map(window_block, (windows[0], windows[1], group_win))  27.8 us
    dot_general x2, local copies, waits for them, and re-layouts, window_pass(): jnp.dot(grad_packed, qkv_weight.T, preferred_element_type=jnp.float32)  19.9 us
  transfers between devices with their start and end apart: 6, of which 6 were waited for; matrix products, arithmetic and copies ran while one was open for 4% of the time, Pallas kernels for 0%

commit v1 on v0

v1 whole, which is shorter than its diff:
```python
import functools
import jax
import jax.numpy as jnp
import numpy as np
from jax import lax
from jax.experimental import pallas as pl
from jax.experimental.pallas import tpu as pltpu
from jax.sharding import PartitionSpec as P

NN = (((1,), (0,)), ((), ()))
NT = (((1,), (1,)), ((), ()))
TN = (((0,), (0,)), ((), ()))
F32 = jnp.float32
BF16 = jnp.bfloat16
I32 = jnp.int32
D = 512
BANDS, SECTORS = 16, 8
DEVICES = BANDS * SECTORS
LAT, LON, LEV = 12, 48, 4
TOKENS = LAT * LON * LEV
STRIP = LON * LEV
ROWS = 1152
CAP = 288
WIN = 144
HALF = 72
SMALL = 80
BLOCK = 2 * WIN
SCALE = 0.125
LOG2E = 1.4426950408889634
BOTH = ("lat", "lon")

UP, SIDE, CORNER = 3 * WIN + SMALL, WIN + SMALL, SMALL
INNER, EDGE = 6 * WIN, 4 * WIN + SMALL


def split_matrix(places, rows):
    matrix = np.zeros((rows, places * 4), np.float32)
    for place in range(places):
        for level in range(4):
            matrix[(level // 2) * places * 2 + place * 2 + level % 2, place * 4 + level] = 1
    return matrix


SPLIT = split_matrix(36, WIN)
SPLIT_SMALL = split_matrix(18, SMALL)


def corner_matrix():
    matrix = np.zeros((BLOCK, 4 * SMALL), np.float32)
    for r in range(2):
        for part in range(4):
            for at in range(36):
                matrix[r * WIN + part * 36 + at, part * SMALL + r * 36 + at] = 1
    return matrix


CORNER_JOIN = corner_matrix()


def corner_back():
    matrix = np.zeros((4 * SMALL, BLOCK), np.float32)
    for part in range(4):
        split = CORNER_JOIN[:, part * SMALL : part * SMALL + HALF]
        matrix[part * SMALL : part * SMALL + HALF] = SPLIT_SMALL[:HALF].T @ split.T
    return matrix


CORNER_BACK = corner_back()


def product(left, right, form=NN):
    return lax.dot_general(left, right, form, preferred_element_type=F32)


def normalise(values):
    centred = values - jnp.mean(values, -1, keepdims=True)
    inverse = lax.rsqrt(jnp.mean(centred * centred, -1, keepdims=True) + 1e-5)
    return centred * inverse, inverse


def whole(*shape):
    return pl.BlockSpec(shape, lambda *i: (0,) * len(shape))


def blocks(rows, width):
    return pl.BlockSpec((rows, width), lambda i: (i, 0))


def shapes(*dims, dtype=BF16):
    return [jax.ShapeDtypeStruct(dim, dtype) for dim in dims]


def call(kernel, name, grid, ins, outs, out_shapes, scratch, cost, vmem):
    flops, moved, exps = cost
    return pl.pallas_call(
        kernel,
        grid=grid,
        in_specs=ins,
        out_specs=outs,
        out_shape=out_shapes,
        scratch_shapes=scratch,
        compiler_params=pltpu.CompilerParams(vmem_limit_bytes=vmem * 2**20),
        cost_estimate=pl.CostEstimate(flops=flops, bytes_accessed=moved, transcendentals=exps),
        name=name,
    )


def request_kernel(owner_ref, slot_ref, lists_ref, place_ref, hits, ranks):
    owner = owner_ref[...]
    slot = slot_ref[...]
    hit = owner == lax.broadcasted_iota(I32, (BANDS, TOKENS), 0)
    hits[...] = hit.astype(F32)
    step = 256
    row = lax.broadcasted_iota(I32, (step, step), 0)
    triangle = (row <= lax.broadcasted_iota(I32, (step, step), 1)).astype(F32).astype(BF16)
    before = jnp.zeros((BANDS, 1), F32)
    for at in range(0, TOKENS, step):
        part = hits[:, at : at + step]
        count = product(part.astype(BF16), triangle) + before
        ranks[:, at : at + step] = jnp.sum(part * count, 0, keepdims=True) - 1.0
        before = before + jnp.sum(part, 1, keepdims=True)
    rank = ranks[...]
    place_ref[...] = owner * CAP + rank.astype(I32)
    high = jnp.where(hit, lax.shift_right_logical(slot, 5), 0).astype(F32).astype(BF16)
    low = jnp.where(hit, slot & 31, 0).astype(F32).astype(BF16)
    chosen = rank == lax.broadcasted_iota(I32, (CAP, TOKENS), 0).astype(F32)
    chosen = jnp.where(chosen, 1.0, 0.0).astype(BF16)
    found = product(high, chosen, NT) * 32.0 + product(low, chosen, NT)
    lists_ref[...] = found.astype(I32)


def make_requests(owners, slots):
    return call(
        request_kernel, "requests", (),
        [whole(1, TOKENS)] * 2,
        [whole(BANDS, CAP), whole(1, TOKENS)],
        shapes((BANDS, CAP), (1, TOKENS), dtype=I32),
        [pltpu.VMEM((BANDS, TOKENS), F32), pltpu.VMEM((1, TOKENS), F32)],
        (100000000, 100000, 0), 20,
    )(owners, slots)


def serve_kernel(lists_ref, buffer_ref, out_ref):
    asker = pl.program_id(0)
    lane = lax.broadcasted_iota(I32, (CAP, BANDS), 1)
    wanted = jnp.sum(jnp.where(lane == asker, lists_ref[...], 0), 1, keepdims=True)
    chosen = wanted == lax.broadcasted_iota(I32, (CAP, ROWS), 1)
    chosen = jnp.where(chosen, 1.0, 0.0).astype(BF16)
    out_ref[...] = product(chosen, buffer_ref[...]).astype(BF16)


def serve(lists, buffer):
    return call(
        serve_kernel, "serve", (BANDS,),
        [whole(CAP, BANDS), whole(ROWS, D)],
        blocks(CAP, D),
        shapes((BANDS * CAP, D))[0],
        [], (5400000000, 6000000, 0), 20,
    )(lists, buffer)


def pick_kernel(place_ref, replies_ref, out_ref):
    place = place_ref[...]
    rows = place.shape[0]
    step = 512
    total = 0.0
    for at in range(0, BANDS * CAP, step):
        chosen = (place - at) == lax.broadcasted_iota(I32, (rows, step), 1)
        chosen = jnp.where(chosen, 1.0, 0.0).astype(BF16)
        total += product(chosen, replies_ref[at : at + step, :])
    out_ref[...] = total.astype(BF16)


def pick(place, replies, rows):
    count = place.shape[0]
    return call(
        pick_kernel, "pick", (count // rows,),
        [blocks(rows, 1), whole(BANDS * CAP, D)],
        blocks(rows, D),
        shapes((count, D))[0],
        [], (count * 4718592, 6000000, 0), 30,
    )(place, replies)


def sort_kernel(grid_ref, split_ref, small_ref, up_ref, side_ref, corner_ref, inner_ref, edge_ref):
    strips = [grid_ref[i * STRIP : i * STRIP + STRIP, :].astype(F32) for i in range(LAT)]

    def put(ref, at, lats, first, cols):
        part = jnp.concatenate([strips[i][first * 4 : (first + cols) * 4] for i in lats])
        matrix = split_ref if part.shape[0] == WIN else small_ref
        ref[at : at + matrix.shape[0], :] = product(matrix[...], part.astype(BF16)).astype(BF16)

    low, mid, high = range(3), range(3, 9), range(9, 12)
    for q in range(3):
        put(up_ref, q * WIN, low, 6 + 12 * q, 12)
        put(inner_ref, q * BLOCK, range(3, 6), 6 + 12 * q, 12)
        put(inner_ref, q * BLOCK + WIN, range(6, 9), 6 + 12 * q, 12)
        put(edge_ref, WIN + q * WIN, high, 6 + 12 * q, 12)
    put(up_ref, 3 * WIN, low, 42, 6)
    put(side_ref, 0, mid, 0, 6)
    put(side_ref, WIN, high, 0, 6)
    put(corner_ref, 0, low, 0, 6)
    put(edge_ref, 0, mid, 42, 6)
    put(edge_ref, 4 * WIN, high, 42, 6)


def sort_pieces(values):
    return call(
        sort_kernel, "sort_pieces", (),
        [whole(TOKENS, D), whole(WIN, WIN), whole(SMALL, HALF)],
        [whole(n, D) for n in (UP, SIDE, CORNER, INNER, EDGE)],
        shapes(*[(n, D) for n in (UP, SIDE, CORNER, INNER, EDGE)]),
        [], (400000000, 5000000, 0), 24,
    )(values, jnp.asarray(SPLIT, BF16), jnp.asarray(SPLIT_SMALL, BF16))


def order_ids():
    ids = np.arange(TOKENS).reshape(LAT, LON, 2, 2)

    def piece(lats, first, cols):
        part = ids[lats[0] : lats[-1] + 1, first : first + cols].transpose(2, 0, 1, 3).reshape(-1)
        return np.pad(part, (0, WIN - 64 - HALF if part.size == HALF else 0))

    low, mid, high = range(3), range(3, 9), range(9, 12)
    order = [piece(low, 6 + 12 * q, 12) for q in range(3)]
    order += [piece(low, 42, 6), piece(mid, 0, 6), piece(high, 0, 6), piece(low, 0, 6)]
    for q in range(3):
        order += [piece(range(3, 6), 6 + 12 * q, 12), piece(range(6, 9), 6 + 12 * q, 12)]
    order += [piece(mid, 42, 6)]
    order += [piece(high, 6 + 12 * q, 12) for q in range(3)] + [piece(high, 42, 6)]
    return np.concatenate(order)


ORDER = order_ids()
SENT = UP + SIDE + CORNER


def join_halves(first, second):
    first, second = first.astype(F32), second.astype(F32)
    return jnp.concatenate([first[:HALF], second[:HALF], first[HALF:], second[HALF:]])


def attend(x_all, c_all, bias, w_ref, gain_ref, ow_ref, x_out, c_out, h_ref, att_ref, dp_ref, packed, slopes):
    x_out[...] = x_all.astype(BF16)
    cot = c_all.astype(BF16)
    c_out[...] = cot
    slopes[...] = product(cot, ow_ref[...], NT).astype(BF16)
    normed, _ = normalise(x_all)
    hidden = (normed * gain_ref[...]).astype(BF16)
    h_ref[...] = hidden
    for part in range(3):
        cols = slice(part * D, part * D + D)
        packed[:, cols] = product(hidden, w_ref[:, cols]).astype(BF16)
    lane = lax.broadcasted_iota(I32, (1, 128), 1)
    sides = [jnp.where(lane < 64, 1.0, 0.0).astype(BF16), jnp.where(lane < 64, 0.0, 1.0).astype(BF16)]
    for window in range(2):
        rows = slice(window * WIN, window * WIN + WIN)
        for pair in range(4):
            spot = [slice(part * D + pair * 128, part * D + pair * 128 + 128) for part in range(3)]
            q2, k2, v2 = (packed[rows, cols] for cols in spot)
            g2 = slopes[rows, spot[0]]
            att = dq = dk = dv = 0.0
            for side in sides:
                qm, km, vm, gm = q2 * side, k2 * side, v2 * side, g2 * side
                scores = product(k2, qm, NT) * (SCALE * LOG2E)
                if bias is not None:
                    scores = scores + bias[...]
                grown = jnp.exp2(scores - jnp.max(scores, 0, keepdims=True))
                probs = grown * (1.0 / jnp.sum(grown, 0, keepdims=True))
                low = probs.astype(BF16)
                weighted = probs * product(v2, gm, NT)
                slope = weighted - probs * jnp.sum(weighted, 0, keepdims=True)
                slope = (slope * SCALE).astype(BF16)
                dv += product(low, gm)
                dk += product(slope, qm)
                att += product(low, vm, TN)
                dq += product(slope, km, TN)
            att_ref[rows, spot[0]] = att.astype(BF16)
            dp_ref[rows, spot[0]] = dq.astype(BF16)
            dp_ref[rows, spot[1]] = dk.astype(BF16)
            dp_ref[rows, spot[2]] = dv.astype(BF16)


def inner_kernel(x_ref, c_ref, *refs):
    x_all = join_halves(x_ref[:WIN, :], x_ref[WIN:, :])
    c_all = join_halves(c_ref[:WIN, :], c_ref[WIN:, :])
    attend(x_all, c_all, None, *refs)


def edge_kernel(xe, xu, xs, xc, ce, cu, cs, cc, join_ref, bias_ref, *refs):
    *refs, x_all, c_all = refs
    step = pl.program_id(0)

    @pl.when(step == 0)
    def _():
        x_all[...] = join_halves(xe[:WIN, :], xs[:WIN, :])
        c_all[...] = join_halves(ce[:WIN, :], cs[:WIN, :])

    for q in range(3):

        @pl.when(step == q + 1)
        def _(q=q):
            near, far = slice(WIN + q * WIN, 2 * WIN + q * WIN), slice(q * WIN, q * WIN + WIN)
            x_all[...] = join_halves(xe[near, :], xu[far, :])
            c_all[...] = join_halves(ce[near, :], cu[far, :])

    @pl.when(step == 4)
    def _():
        near, far, along = slice(4 * WIN, EDGE), slice(3 * WIN, UP), slice(WIN, SIDE)
        parts = [xe[near, :], xs[along, :], xu[far, :], xc[...]]
        x_all[...] = product(join_ref[...], jnp.concatenate(parts))
        parts = [ce[near, :], cs[along, :], cu[far, :], cc[...]]
        c_all[...] = product(join_ref[...], jnp.concatenate(parts))

    attend(x_all[...], c_all[...], bias_ref, *refs)


def attend_specs(rows):
    outs = [blocks(BLOCK, n) for n in (D, D, D, D, 3 * D)]
    out_shapes = shapes(*[(rows, n) for n in (D, D, D, D, 3 * D)])
    scratch = [pltpu.VMEM((BLOCK, 3 * D), BF16), pltpu.VMEM((BLOCK, D), BF16)]
    cost = (rows * 6000000, rows * 10000, rows * 1200)
    return outs, out_shapes, scratch, cost


WEIGHTS = [(D, 3 * D), (1, D), (D, D)]


def attend_inner(x, cot, weights):
    outs, out_shapes, scratch, cost = attend_specs(INNER)
    return call(
        inner_kernel, "attend_inner", (3,),
        [blocks(BLOCK, D)] * 2 + [whole(*dim) for dim in WEIGHTS],
        outs, out_shapes, scratch, cost, 24,
    )(x, cot, *weights)


def attend_edge(x_parts, c_parts, bias, weights):
    rows = 5 * BLOCK
    outs, out_shapes, scratch, cost = attend_specs(rows)
    parts = [whole(n, D) for n in (EDGE, UP, SIDE, CORNER)]
    return call(
        edge_kernel, "attend_edge", (5,),
        parts * 2
        + [whole(BLOCK, 4 * SMALL), pl.BlockSpec((None, WIN, WIN), lambda i: (jnp.minimum(i, 1), 0, 0))]
        + [whole(*dim) for dim in WEIGHTS],
        outs, out_shapes, scratch + [pltpu.VMEM((BLOCK, D), F32)] * 2, cost, 32,
    )(*x_parts, *c_parts, jnp.asarray(CORNER_JOIN, BF16), bias, *weights)


def weight_kernel(hi, ai, ci, di, he, ae, ce, de, out_ref, turned):
    def chunk(c):
        if c < 3:
            cols = slice(c * D, c * D + D)
            return product(hi[...], di[:, cols], TN) + product(he[...], de[:, cols], TN)
        return product(ai[...], ci[...], TN) + product(ae[...], ce[...], TN)

    upper = lax.broadcasted_iota(I32, (64, 8, D), 1) < 4
    for pair in range(2):
        first = chunk(2 * pair).reshape(64, 8, D)
        second = chunk(2 * pair + 1).reshape(64, 8, D)
        swap = lambda v: jnp.concatenate([v[:, 4:], v[:, :4]], 1)
        even = jnp.where(upper, first, swap(second))
        odd = jnp.where(upper, swap(first), second)
        turned[:, 0, pair] = even
        turned[:, 1, pair] = odd
    out_ref[...] = turned[...].reshape(2048, D).astype(BF16)


def weight_terms(inner, edge):
    dims = [(n, w) for n in (INNER, 5 * BLOCK) for w in (D, D, D, 3 * D)]
    return call(
        weight_kernel, "weight_terms", (),
        [whole(*dim) for dim in dims],
        whole(2048, D), shapes((2048, D))[0],
        [pltpu.VMEM((64, 2, 2, 8, D), F32)],
        (TOKENS * 2 * D * 4 * D, 18000000, 0), 48,
    )(*inner, *edge)


def finished(x_ref, c_ref, att_ref, dp_ref, w_ref, gain_ref, ow_ref):
    x = x_ref[...].astype(F32)
    out = x + product(att_ref[...], ow_ref[...])
    normed, inverse = normalise(x)
    hidden = product(dp_ref[...], w_ref[...], NT) * gain_ref[...]
    hidden = (
        hidden
        - jnp.mean(hidden, -1, keepdims=True)
        - normed * jnp.mean(hidden * normed, -1, keepdims=True)
    )
    grad = c_ref[...].astype(F32) + inverse * hidden
    return out, grad


def grid_pieces(split_ref, values):
    first = jnp.concatenate([values[:HALF], values[WIN : WIN + HALF]]).astype(BF16)
    second = jnp.concatenate([values[HALF:WIN], values[WIN + HALF :]]).astype(BF16)
    return [product(split_ref[...], part, TN).astype(BF16) for part in (first, second)]


def finish_inner_kernel(split_ref, *refs):
    *refs, out_ref, grad_ref = refs
    for ref, values in zip((out_ref, grad_ref), finished(*refs)):
        first, second = grid_pieces(split_ref, values)
        ref[:WIN, :] = first
        ref[WIN:, :] = second


def finish_edge_kernel(split_ref, back_ref, *refs):
    refs, outs = refs[:7], refs[7:]
    step = pl.program_id(0)
    for (edge, up, side, corner), values in zip((outs[:4], outs[4:]), finished(*refs)):

        @pl.when(step < 4)
        def _(edge=edge, up=up, side=side, values=values):
            first, second = grid_pieces(split_ref, values)
            edge[pl.ds(pl.multiple_of(step * WIN, 16), WIN), :] = first

            @pl.when(step == 0)
            def _():
                side[:WIN, :] = second

            @pl.when(step > 0)
            def _():
                up[pl.ds(pl.multiple_of((step - 1) * WIN, 16), WIN), :] = second

        @pl.when(step == 4)
        def _(edge=edge, up=up, side=side, corner=corner, values=values):
            parts = product(back_ref[...], values.astype(BF16)).astype(BF16)
            edge[4 * WIN :, :] = parts[:SMALL]
            side[WIN:, :] = parts[SMALL : 2 * SMALL]
            up[3 * WIN :, :] = parts[2 * SMALL : 3 * SMALL]
            corner[...] = parts[3 * SMALL :]


def finish_inner(values, weights):
    return call(
        finish_inner_kernel, "finish_inner", (3,),
        [whole(WIN, WIN)] + [blocks(BLOCK, n) for n in (D, D, D, 3 * D)] + [whole(*dim) for dim in WEIGHTS],
        [blocks(BLOCK, D)] * 2, shapes((INNER, D), (INNER, D)), [],
        (INNER * 2200000, INNER * 8000, INNER), 24,
    )(jnp.asarray(SPLIT, BF16), *values, *weights)


def finish_edge(values, weights):
    dims = [(n, D) for n in (EDGE, UP, SIDE, CORNER)] * 2
    rows = 5 * BLOCK
    return call(
        finish_edge_kernel, "finish_edge", (5,),
        [whole(WIN, WIN), whole(4 * SMALL, BLOCK)]
        + [blocks(BLOCK, n) for n in (D, D, D, 3 * D)]
        + [whole(*dim) for dim in WEIGHTS],
        [whole(*dim) for dim in dims], shapes(*dims), [],
        (rows * 2200000, rows * 8000, rows), 24,
    )(jnp.asarray(SPLIT, BF16), jnp.asarray(CORNER_BACK, BF16), *values, *weights)


def join_kernel(inner, edge, up, side, corner, out_ref):
    left = [corner[...].astype(F32), side[:WIN, :].astype(F32), side[WIN:, :].astype(F32)]
    right = [up[3 * WIN :, :].astype(F32), edge[:WIN, :].astype(F32), edge[4 * WIN :, :].astype(F32)]
    run, stub = 48, 24
    for i in range(LAT):
        zone, at = (0, i) if i < 3 else (1, i - 3) if i < 9 else (2, i - 9)
        parts = [left[zone][at * stub : at * stub + stub]]
        for q in range(3):
            if zone == 0:
                start, ref = q * WIN + at * run, up
            elif zone == 1:
                start, ref = q * BLOCK + at * run, inner
            else:
                start, ref = WIN + q * WIN + at * run, edge
            parts.append(ref[start : start + run, :].astype(F32))
        parts.append(right[zone][at * stub : at * stub + stub])
        out_ref[i * STRIP : i * STRIP + STRIP, :] = jnp.concatenate(parts).astype(BF16)


def join(parts):
    return call(
        join_kernel, "join", (),
        [whole(n, D) for n in (INNER, EDGE, UP, SIDE, CORNER)],
        whole(TOKENS, D), shapes((TOKENS, D))[0], [],
        (1000000, 5000000, 0), 20,
    )(*parts)


def shift_pairs(lat_step, lon_step):
    return [
        (a * SECTORS + b, (a + lat_step) % BANDS * SECTORS + (b + lon_step) % SECTORS)
        for a in range(BANDS)
        for b in range(SECTORS)
    ]


def exchange(parts, sign):
    steps = ((sign, 0), (0, sign), (sign, sign))
    return [lax.ppermute(part, BOTH, shift_pairs(*step)) for part, step in zip(parts, steps)]


def swap_blocks(values, axis):
    return lax.all_to_all(values, axis, split_axis=0, concat_axis=0, tiled=True)


def per_device(buffer, fetch_owner, fetch_slot, norm_gain, qkv_weight, out_weight, out_grad):
    weights = (qkv_weight, norm_gain.reshape(1, D), out_weight)
    lists, place = make_requests(fetch_owner.reshape(1, TOKENS), fetch_slot.reshape(1, TOKENS))
    lists = swap_blocks(lists, "lat")
    replies = swap_blocks(serve(lists.T, buffer).reshape(BANDS, CAP, D), "lat")
    replies = replies.reshape(BANDS * CAP, D)

    c_up, c_side, c_corner, c_inner, c_edge = sort_pieces(out_grad.reshape(TOKENS, D))
    c_parts = [c_edge] + exchange([c_up, c_side, c_corner], -1)
    place = place.reshape(TOKENS)[ORDER].reshape(-1, 1)

    sent = pick(place[:SENT], replies, 272)
    arrived = exchange([sent[:UP], sent[UP : UP + SIDE], sent[UP + SIDE :]], -1)
    kept = pick(place[SENT:], replies, 304)

    last = (lax.axis_index("lat") == BANDS - 1) & (jnp.arange(2) == 1)
    group = jnp.arange(WIN) >= HALF
    apart = last[:, None, None] & (group[:, None] != group[None, :])
    bias = jnp.where(apart, -jnp.inf, 0.0).astype(F32)
    xi, ci, hi, ai, di = attend_inner(kept[:INNER], c_inner, weights)
    xe, ce, he, ae, de = attend_edge([kept[INNER:]] + arrived, c_parts, bias, weights)
    terms = swap_blocks(weight_terms((hi, ai, ci, di), (he, ae, ce, de)), BOTH)

    edges = finish_edge((xe, ce, ae, de), weights)
    returned = [exchange(edges[at + 1 : at + 4], 1) for at in (0, 4)]
    inners = finish_inner((xi, ci, ai, di), weights)
    outs = [
        join([inners[n], edges[4 * n]] + returned[n]).reshape(LAT, LON, LEV, D) for n in range(2)
    ]
    total = jnp.sum(terms.reshape(DEVICES, 4, 4, D).astype(F32), 0).transpose(1, 0, 2).reshape(4, 4 * D)
    return (outs[0], outs[1], total[:, : 3 * D], total[:, 3 * D :])


def solution(mesh):
    return jax.shard_map(
        per_device,
        mesh=mesh,
        in_specs=(
            P(BOTH, None),
            P("lat", "lon", None, None),
            P("lat", "lon", None),
            P(),
            P(),
            P(),
            P("lat", "lon", None, None),
        ),
        out_specs=(
            P("lat", "lon", None, None),
            P("lat", "lon", None, None),
            P(BOTH, None),
            P(BOTH, None),
        ),
        check_vma=False,
    )
```

time: 834 us -> 237 us (0.28); the launches traced: 823 us -> 236 us
  local copies, waits for them, and re-layouts: 316 us -> 45.7 us
  waiting for transfers between devices: 225 us -> 42.6 us
  matrix products: 149 us -> 0 us
  Pallas kernels: 0 us -> 94.1 us
  other arithmetic: 71.2 us -> 2.91 us
  starting transfers between devices: 13.1 us -> 33.2 us
  loops' own time: 19 us -> 0 us
  between operations: 14.5 us -> 1.12 us
    dot_general x22 -> x0, matrix products: 149 us -> none  [the longest x12 113 us: mixed_product(): return jnp.einsum(form, left, right, preferred_element_type=jnp.float32)]
    unnamed x2 -> x0, waiting for transfers between devices: 131 us -> none
    pallas_call x0 -> x12, Pallas kernels: none -> 94.1 us  [the longest x1 25.1 us: attend_edge(): call(edge_kernel, 'attend_edge', (5,), parts * 2 + [whole(BLOCK, 4 * SMAL...]
    reshape x13 -> x3, local copies, waits for them, and re-layouts: 93.8 us -> 8.15 us  [the longest x2 4.24 us: per_device(): join([inners[n], edges[4 * n]] + returned[n]).reshape(LAT, LON, LEV, D)]
    another operation x4 -> x0, local copies, waits for them, and re-layouts: 41.9 us -> none  [window_pass(): jnp.stack([grad_queries, grad_keys, grad_values], 2)]
    while x74 -> x0, local copies, waits for them, and re-layouts: 30.5 us -> none
    all_to_all x1 -> x2, waiting for transfers between devices: 55.5 us -> 25.9 us  [swap_blocks(): return lax.all_to_all(values, axis, split_axis=0, concat_axis=0, tiled=True)]
    broadcast_in_dim x5 -> x0, local copies, waits for them, and re-layouts: 28.4 us -> none  [the longest x4 27.8 us: per_device(): lax.map(window_block, (windows[0], windows[1], group_win))]
  transfers between devices with their start and end apart: 6 -> 14, of which waited for: 6 -> 3; matrix products, arithmetic and copies ran while one was open for 4% -> 10% of each run, Pallas kernels for 0% -> 20%
where the time goes in v1:
time: 237 us; the launch traced here: 236 us
  Pallas kernels  94.1 us (40%)
  local copies, waits for them, and re-layouts  45.7 us (19%)
  waiting for transfers between devices  42.6 us (18%)
  starting transfers between devices  33.2 us (14%)
  blocking collectives  16.4 us (7%)
  other arithmetic  2.91 us (1%)
    all_to_all x2, waiting for transfers between devices, swap_blocks(): return lax.all_to_all(values, axis, split_axis=0, concat_axis=0, tiled=True)  25.9 us
    pallas_call x1, Pallas kernels, attend_edge(): call(edge_kernel, 'attend_edge', (5,), parts * 2 + [whole(BLOCK, 4 * SMAL...  25.1 us
    ppermute x12, starting transfers between devices, exchange(): lax.ppermute(part, BOTH, shift_pairs(*step))  23.8 us
    unnamed x68, local copies, waits for them, and re-layouts  22.8 us
    pallas_call x2, Pallas kernels, pick(): call(pick_kernel, 'pick', (count // rows,), [blocks(rows, 1), whole(BANDS...  18 us
    ppermute x12, waiting for transfers between devices, exchange(): lax.ppermute(part, BOTH, shift_pairs(*step))  16.8 us
    all_to_all x1, blocking collectives, swap_blocks(): return lax.all_to_all(values, axis, split_axis=0, concat_axis=0, tiled=True)  16.4 us
    pallas_call x1, Pallas kernels, attend_inner(): call(inner_kernel, 'attend_inner', (3,), [blocks(BLOCK, D)] * 2 + [whole(...  13.3 us
  transfers between devices with their start and end apart: 14, of which 3 were waited for; matrix products, arithmetic and copies ran while one was open for 10% of the time, Pallas kernels for 20%

profile of v1, /device:TPU:1, one launch (start us, length us, event | category | flops | bytes accessed | tf_op | source)
XLA Modules:
  0.0 236.0 jit_solution(7338918724608698227)
XLA Ops:
  3.1 16.4 %all_to_all.26 = s32[16,1,288]{2,1,0:T(1,128)S(1)} all-to-all(s32[16,1,288]{2,1,0:T(1,128)S(1)} %copy.23), channel_id=1, replica_groups=mesh['lat'=16,'lon'=8] {'lat'}, dimensions={0} | all-to-all | bytes 36864 | tf_op jit(solution)/shard_map/all_to_all | solution.py:500
  20.9 10.7 %serve.1 = bf16[4608,512]{1,0:T(8,128)(2,1)S(1)} custom-call(s32[288,16]{1,0:T(8,128)S(1)} %bitcast.14, bf16[1152,512]{1,0:T(8,128)(2,1)S(1)} %copy-done.16), custom_call_target="tpu_custom_call" | custom-call | flops 5400000000 | bytes 6000000 | tf_op jit(solution)/shard_map/serve/pallas_call | solution.py:153
  31.6 2.2 copy-done
  33.7 4.7 %all-to-all-start.1 = ((bf16[16,288,512]{2,1,0:T(8,128)(2,1)}), bf16[16,288,512]{2,1,0:T(8,128)(2,1)}, u32[]{:S(2)}, u32[]{:S(2)}) async-start(bf16[16,288,512]{2,1,0:T(8,128)(2,1)} %bitcast.13), calls=%async_computation.1 | async-start | bytes 9437184 | tf_op jit(solution)/shard_map/all_to_all | solution.py:500
  38.4 3.9 %reshape.93.grid_ref = bf16[2304,512]{1,0:T(8,128)(2,1)S(1)} reshape(bf16[12,48,4,512]{3,2,1,0:T(4,128)(2,1)} %param.21) | data formatting | bytes 4718592 | tf_op jit(solution)/shard_map/reshape | solution.py:510
  45.9 2.8 %collective-permute-start.4 = (bf16[224,512]{1,0:T(8,128)(2,1)}, bf16[224,512]{1,0:T(8,128)(2,1)}, u32[]{:S(2)}, u32[]{:S(2)}) collective-permute-start(bf16[224,512]{1,0:T(8,128)(2,1)} %get-tuple-element.41), channel_id=1, source_target_pairs={{0,7},{1,0},{2,1},{3,2},{4,3},{5,4},{6,5},{7,6},{8,15},{9,8},{10,9... | collective-permute-start | bytes 688136 | tf_op jit(solution)/shard_map/ppermute | solution.py:496
  48.7 6.5 %collective-permute-start.5 = (bf16[80,512]{1,0:T(8,128)(2,1)S(1)}, bf16[80,512]{1,0:T(8,128)(2,1)S(1)}, u32[]{:S(2)}, u32[]{:S(2)}) collective-permute-start(bf16[80,512]{1,0:T(8,128)(2,1)S(1)} %get-tuple-element.42), channel_id=1, source_target_pairs={{0,127},{1,120},{2,121},{3,122},{4,123},{5,124},{6,125},{7,126},{8... | collective-permute-start | bytes 245768 | tf_op jit(solution)/shard_map/ppermute | solution.py:496
  55.3 12.7 %gather_fusion = s32[2336]{0:T(1024)S(1)} fusion(s32[2304]{0:T(1024)S(1)} %reduce.1, s32[3072]{0:T(1024)S(1)} %pad_clamp_fusion), kind=kCustom, calls=%fused_computation | custom fusion | bytes 28032 | tf_op jit(solution)/shard_map/gather | solution.py:512
  69.5 25.9 %all-to-all-done.1 = bf16[16,288,512]{2,1,0:T(8,128)(2,1)} async-done(((bf16[16,288,512]{2,1,0:T(8,128)(2,1)}), bf16[16,288,512]{2,1,0:T(8,128)(2,1)}, u32[]{:S(2)}, u32[]{:S(2)}) %all-to-all-start.1) | async-done | bytes 4718624 | tf_op jit(solution)/shard_map/all_to_all | solution.py:500
  95.3 7.1 %pick.3 = bf16[816,512]{1,0:T(8,128)(2,1)S(1)} custom-call(s32[816,1]{1,0:T(8,128)S(1)} %slice.45.place_ref, bf16[4608,512]{1,0:T(8,128)(2,1)} %bitcast.6.replies_ref), custom_call_target="tpu_custom_call" | custom-call | flops 3850371072 | bytes 6000000 | tf_op jit(solution)/shard_map/pick/pallas_call | solution.py:176
  104.0 2.8 %collective-permute-start.1 = (bf16[224,512]{1,0:T(8,128)(2,1)S(1)}, bf16[224,512]{1,0:T(8,128)(2,1)S(1)}, u32[]{:S(2)}, u32[]{:S(2)}) collective-permute-start(bf16[224,512]{1,0:T(8,128)(2,1)S(1)} %slice.53), channel_id=1, source_target_pairs={{0,7},{1,0},{2,1},{3,2},{4,3},{5,4},{6,5},{7,6},{8,15},{9,8},{10,9... | collective-permute-start | bytes 688136 | tf_op jit(solution)/shard_map/ppermute | solution.py:496
  106.7 10.9 %pick.2 = bf16[1520,512]{1,0:T(8,128)(2,1)S(1)} custom-call(s32[1520,1]{1,0:T(8,128)S(1)} %slice.44.place_ref, bf16[4608,512]{1,0:T(8,128)(2,1)} %bitcast.6.replies_ref), custom_call_target="tpu_custom_call" | custom-call | flops 7172259840 | bytes 6000000 | tf_op jit(solution)/shard_map/pick/pallas_call | solution.py:176
  119.7 13.3 %attend_inner.1 = (bf16[864,512]{1,0:T(8,128)(2,1)S(1)}, bf16[864,512]{1,0:T(8,128)(2,1)S(1)}, bf16[864,512]{1,0:T(8,128)(2,1)S(1)}, bf16[864,512]{1,0:T(8,128)(2,1)S(1)}, bf16[864,1536]{1,0:T(8,128)(2,1)S(1)}) custom-call(bf16[864,512]{1,0:T(8,128)(2,1)S(1)} %slice.49.x_ref, bf16[864,512]{1,0:T(8,128)(2,1)S(1)} %copy-done.18, ...), custom_call_target="tpu_custom_call" | custom-call | flops 5184000000 | bytes 8640000 | tf_op jit(solution)/shard_map/attend_inner/pallas_call | solution.py:331
  134.6 25.1 %attend_edge.1 = (bf16[1440,512]{1,0:T(8,128)(2,1)S(1)}, bf16[1440,512]{1,0:T(8,128)(2,1)S(1)}, bf16[1440,512]{1,0:T(8,128)(2,1)S(1)}, bf16[1440,512]{1,0:T(8,128)(2,1)S(1)}, bf16[1440,1536]{1,0:T(8,128)(2,1)S(1)}) custom-call(bf16[656,512]{1,0:T(8,128)(2,1)S(1)} %slice.50.xe, bf16[512,512]{1,0:T(8,128)(2,1)S(1)} %collective-permute-done.xu, ...), custom_call_target="tpu_custom_call" | custom-call | flops 8640000000 | bytes 14400000 | tf_op jit(solution)/shard_map/attend_edge/pallas_call | solution.py:342
  164.0 11.0 %weight_terms.1 = bf16[2048,512]{1,0:T(8,128)(2,1)} custom-call(bf16[864,512]{1,0:T(8,128)(2,1)S(1)} %get-tuple-element.56.hi, bf16[864,512]{1,0:T(8,128)(2,1)S(1)} %get-tuple-element.36.refs_2_.ai, bf16[864,512]{1,0:T(8,128)(2,1)S(1)} %get-tuple-element.35.refs_1_.ci, bf16[864,1536]{1,0:T(8,128)(2,1)} %copy-done.1, ...), custom_call_target="tpu_custom_call" | custom-call | flops 4831838208 | bytes 18000000 | tf_op jit(solution)/shard_map/weight_terms/pallas_call | solution.py:372
  175.0 4.7 %all-to-all-start.2 = ((bf16[128,16,512]{2,1,0:T(8,128)(2,1)}), bf16[128,16,512]{2,1,0:T(8,128)(2,1)}, u32[]{:S(2)}, u32[]{:S(2)}) async-start(bf16[128,16,512]{2,1,0:T(8,128)(2,1)} %bitcast.22), calls=%async_computation.2 | async-start | bytes 4194304 | tf_op jit(solution)/shard_map/all_to_all | solution.py:500
  181.7 2.3 copy-done.26
  188.1 8.6 %finish_edge.1 = (bf16[656,512]{1,0:T(8,128)(2,1)S(1)}, bf16[512,512]{1,0:T(8,128)(2,1)}, bf16[224,512]{1,0:T(8,128)(2,1)}, bf16[80,512]{1,0:T(8,128)(2,1)}, bf1...) custom-call(bf16[144,144]{1,0:T(8,128)(2,1)S(1)} %copy-done.12, ...), custom_call_target="tpu_custom_call" | custom-call | flops 3168000000 | bytes 11520000 | tf_op jit(solution)/shard_map/finish_edge/pallas_call | solution.py:448
  196.7 3.0 %collective-permute-start.9 = (bf16[512,512]{1,0:T(8,128)(2,1)S(1)}, bf16[512,512]{1,0:T(8,128)(2,1)S(1)}, u32[]{:S(2)}, u32[]{:S(2)}) collective-permute-start(bf16[512,512]{1,0:T(8,128)(2,1)S(1)} %get-tuple-element.53), channel_id=1, source_target_pairs={{0,8},{1,9},{2,10},{3,11},{4,12},{5,13},{6,14},{7,15},{8,16},{9,17... | collective-permute-start | bytes 1572872 | tf_op jit(solution)/shard_map/ppermute | solution.py:496
  199.8 2.2 collective-permute-start.11
  202.0 2.4 %collective-permute-start.7 = (bf16[224,512]{1,0:T(8,128)(2,1)}, bf16[224,512]{1,0:T(8,128)(2,1)}, u32[]{:S(2)}, u32[]{:S(2)}) collective-permute-start(bf16[224,512]{1,0:T(8,128)(2,1)} %get-tuple-element.49), channel_id=1, source_target_pairs={{0,1},{1,2},{2,3},{3,4},{4,5},{5,6},{6,7},{7,0},{8,9},{9,10},{10,1... | collective-permute-start | bytes 688136 | tf_op jit(solution)/shard_map/ppermute | solution.py:496
  204.4 3.6 %collective-permute-done.11.corner = bf16[80,512]{1,0:T(8,128)(2,1)S(1)} collective-permute-done((bf16[80,512]{1,0:T(8,128)(2,1)S(1)}, bf16[80,512]{1,0:T(8,128)(2,1)S(1)}, u32[]{:S(2)}, u32[]{:S(2)}) %collective-permute-start.11) | collective-permute-done | bytes 81952 | tf_op jit(solution)/shard_map/ppermute | solution.py:496
  208.5 3.5 %finish_inner.1 = (bf16[864,512]{1,0:T(8,128)(2,1)S(1)}, bf16[864,512]{1,0:T(8,128)(2,1)S(1)}) custom-call(bf16[144,144]{1,0:T(8,128)(2,1)S(1)} %copy-done.12, bf16[864,512]{1,0:T(8,128)(2,1)S(1)} %get-tuple-element.34.refs_0_, bf16[864,512]{1,0:T(8,128)(2,1)S(1)} %get-tuple-element.35.refs_1_.ci, bf16[864,512]{1,0:T(8,128)(2,1)S(1)} %copy-done.5, ...), custom_call_target="tpu_custom_call" | custom-call | flops 1900800000 | bytes 6912000 | tf_op jit(solution)/shard_map/finish_inner/pallas_call | solution.py:437
  213.0 13.1 %collective-permute-done.10.side = bf16[224,512]{1,0:T(8,128)(2,1)S(1)} collective-permute-done((bf16[224,512]{1,0:T(8,128)(2,1)S(1)}, bf16[224,512]{1,0:T(8,128)(2,1)S(1)}, u32[]{:S(2)}, u32[]{:S(2)}) %collective-permute-start.10) | collective-permute-done | bytes 229408 | tf_op jit(solution)/shard_map/ppermute | solution.py:496
  (110 shorter events, 35.6 us)
Async XLA Ops:
  33.7 61.6 %all-to-all-start.1 = ((bf16[16,288,512]{2,1,0:T(8,128)(2,1)}), bf16[16,288,512]{2,1,0:T(8,128)(2,1)}, u32[]{:S(2)}, u32[]{:S(2)}) async-start(bf16[16,288,512]{2,1,0:T(8,128)(2,1)} %bitcast.13), calls=%async_computation.1 | async-start | bytes 9437184 | tf_op jit(solution)/shard_map/all_to_all | solution.py:500
  45.7 88.9 %collective-permute-start.3 = (bf16[512,512]{1,0:T(8,128)(2,1)}, bf16[512,512]{1,0:T(8,128)(2,1)}, u32[]{:S(2)}, u32[]{:S(2)}) collective-permute-start(bf16[512,512]{1,0:T(8,128)(2,1)} %get-tuple-element.40), channel_id=1, source_target_pairs={{0,120},{1,121},{2,122},{3,123},{4,124},{5,125},{6,126},{7,127},{8... | collective-permute-start | bytes 1572872 | tf_op jit(solution)/shard_map/ppermute | solution.py:496
  45.9 88.6 %collective-permute-start.4 = (bf16[224,512]{1,0:T(8,128)(2,1)}, bf16[224,512]{1,0:T(8,128)(2,1)}, u32[]{:S(2)}, u32[]{:S(2)}) collective-permute-start(bf16[224,512]{1,0:T(8,128)(2,1)} %get-tuple-element.41), channel_id=1, source_target_pairs={{0,7},{1,0},{2,1},{3,2},{4,3},{5,4},{6,5},{7,6},{8,15},{9,8},{10,9... | collective-permute-start | bytes 688136 | tf_op jit(solution)/shard_map/ppermute | solution.py:496
  48.7 69.1 %collective-permute-start.5 = (bf16[80,512]{1,0:T(8,128)(2,1)S(1)}, bf16[80,512]{1,0:T(8,128)(2,1)S(1)}, u32[]{:S(2)}, u32[]{:S(2)}) collective-permute-start(bf16[80,512]{1,0:T(8,128)(2,1)S(1)} %get-tuple-element.42), channel_id=1, source_target_pairs={{0,127},{1,120},{2,121},{3,122},{4,123},{5,124},{6,125},{7,126},{8... | collective-permute-start | bytes 245768 | tf_op jit(solution)/shard_map/ppermute | solution.py:496
  102.5 17.1 %copy-start.3 = (bf16[512,1536]{1,0:T(8,128)(2,1)S(1)}, bf16[512,1536]{1,0:T(8,128)(2,1)}, u32[]{:S(2)}) copy-start(bf16[512,1536]{1,0:T(8,128)(2,1)} %refs_4_.3) | copy-start | bytes 4718596
  102.5 17.1 %copy-start.10 = (bf16[512,512]{1,0:T(8,128)(2,1)S(1)}, bf16[512,512]{1,0:T(8,128)(2,1)}, u32[]{:S(2)}) copy-start(bf16[512,512]{1,0:T(8,128)(2,1)} %refs_6_.3) | copy-start | bytes 1572868
  102.5 17.1 %copy-start.15 = (f32[512]{0:T(512)S(1)}, f32[512]{0:T(512)}, u32[]{:S(2)}) copy-start(f32[512]{0:T(512)} %param.18) | copy-start | bytes 6148
  102.5 17.1 %copy-start.18 = (bf16[864,512]{1,0:T(8,128)(2,1)S(1)}, bf16[864,512]{1,0:T(8,128)(2,1)}, u32[]{:S(2)}) copy-start(bf16[864,512]{1,0:T(8,128)(2,1)} %copy-done.17) | copy-start | bytes 2654212
  102.5 32.0 %collective-permute-start = (bf16[512,512]{1,0:T(8,128)(2,1)S(1)}, bf16[512,512]{1,0:T(8,128)(2,1)S(1)}, u32[]{:S(2)}, u32[]{:S(2)}) collective-permute-start(bf16[512,512]{1,0:T(8,128)(2,1)S(1)} %slice.52), channel_id=1, source_target_pairs={{0,120},{1,121},{2,122},{3,123},{4,124},{5,125},{6,126},{7,127},{8... | collective-permute-start | bytes 1572872 | tf_op jit(solution)/shard_map/ppermute | solution.py:496
  104.0 30.6 %collective-permute-start.1 = (bf16[224,512]{1,0:T(8,128)(2,1)S(1)}, bf16[224,512]{1,0:T(8,128)(2,1)S(1)}, u32[]{:S(2)}, u32[]{:S(2)}) collective-permute-start(bf16[224,512]{1,0:T(8,128)(2,1)S(1)} %slice.53), channel_id=1, source_target_pairs={{0,7},{1,0},{2,1},{3,2},{4,3},{5,4},{6,5},{7,6},{8,15},{9,8},{10,9... | collective-permute-start | bytes 688136 | tf_op jit(solution)/shard_map/ppermute | solution.py:496
  117.8 16.8 %collective-permute-start.2 = (bf16[80,512]{1,0:T(8,128)(2,1)S(1)}, bf16[80,512]{1,0:T(8,128)(2,1)S(1)}, u32[]{:S(2)}, u32[]{:S(2)}) collective-permute-start(bf16[80,512]{1,0:T(8,128)(2,1)S(1)} %slice.54), channel_id=1, source_target_pairs={{0,127},{1,120},{2,121},{3,122},{4,123},{5,124},{6,125},{7,126},{8... | collective-permute-start | bytes 245768 | tf_op jit(solution)/shard_map/ppermute | solution.py:496
  119.6 15.0 %copy-start.13 = (f32[2,144,144]{2,1,0:T(8,128)S(1)}, f32[2,144,144]{2,1,0:T(8,128)}, u32[]{:S(2)}) copy-start(f32[2,144,144]{2,1,0:T(8,128)} %and_select_fusion.bias_ref) | copy-start | bytes 497668
  119.6 15.0 %copy-start.20 = (bf16[656,512]{1,0:T(8,128)(2,1)S(1)}, bf16[656,512]{1,0:T(8,128)(2,1)}, u32[]{:S(2)}) copy-start(bf16[656,512]{1,0:T(8,128)(2,1)} %copy-done.19) | copy-start | bytes 2015236
  134.5 29.5 %copy-start.4 = (bf16[864,512]{1,0:T(8,128)(2,1)}, bf16[864,512]{1,0:T(8,128)(2,1)S(1)}, u32[]{:S(2)}) copy-start(bf16[864,512]{1,0:T(8,128)(2,1)S(1)} %get-tuple-element.36.refs_2_.ai) | copy-start | bytes 2654212
  175.0 57.9 %all-to-all-start.2 = ((bf16[128,16,512]{2,1,0:T(8,128)(2,1)}), bf16[128,16,512]{2,1,0:T(8,128)(2,1)}, u32[]{:S(2)}, u32[]{:S(2)}) async-start(bf16[128,16,512]{2,1,0:T(8,128)(2,1)} %bitcast.22), calls=%async_computation.2 | async-start | bytes 4194304 | tf_op jit(solution)/shard_map/all_to_all | solution.py:500
  188.1 20.4 %copy-start.2 = (bf16[864,1536]{1,0:T(8,128)(2,1)S(1)}, bf16[864,1536]{1,0:T(8,128)(2,1)}, u32[]{:S(2)}) copy-start(bf16[864,1536]{1,0:T(8,128)(2,1)} %copy-done.1) | copy-start | bytes 7962628
  188.1 20.4 %copy-start.5 = (bf16[864,512]{1,0:T(8,128)(2,1)S(1)}, bf16[864,512]{1,0:T(8,128)(2,1)}, u32[]{:S(2)}) copy-start(bf16[864,512]{1,0:T(8,128)(2,1)} %copy-done.4) | copy-start | bytes 2654212
  196.7 15.4 %copy-start.8 = (bf16[656,512]{1,0:T(8,128)(2,1)}, bf16[656,512]{1,0:T(8,128)(2,1)S(1)}, u32[]{:S(2)}) copy-start(bf16[656,512]{1,0:T(8,128)(2,1)S(1)} %get-tuple-element.47.edge) | copy-start | bytes 2015236
  196.7 29.4 %collective-permute-start.9 = (bf16[512,512]{1,0:T(8,128)(2,1)S(1)}, bf16[512,512]{1,0:T(8,128)(2,1)S(1)}, u32[]{:S(2)}, u32[]{:S(2)}) collective-permute-start(bf16[512,512]{1,0:T(8,128)(2,1)S(1)} %get-tuple-element.53), channel_id=1, source_target_pairs={{0,8},{1,9},{2,10},{3,11},{4,12},{5,13},{6,14},{7,15},{8,16},{9,17... | collective-permute-start | bytes 1572872 | tf_op jit(solution)/shard_map/ppermute | solution.py:496
  199.7 28.7 %collective-permute-start.6 = (bf16[512,512]{1,0:T(8,128)(2,1)}, bf16[512,512]{1,0:T(8,128)(2,1)}, u32[]{:S(2)}, u32[]{:S(2)}) collective-permute-start(bf16[512,512]{1,0:T(8,128)(2,1)} %get-tuple-element.48), channel_id=1, source_target_pairs={{0,8},{1,9},{2,10},{3,11},{4,12},{5,13},{6,14},{7,15},{8,16},{9,17... | collective-permute-start | bytes 1572872 | tf_op jit(solution)/shard_map/ppermute | solution.py:496
  199.8 8.2 %collective-permute-start.11 = (bf16[80,512]{1,0:T(8,128)(2,1)S(1)}, bf16[80,512]{1,0:T(8,128)(2,1)S(1)}, u32[]{:S(2)}, u32[]{:S(2)}) collective-permute-start(bf16[80,512]{1,0:T(8,128)(2,1)S(1)} %get-tuple-element.55), channel_id=1, source_target_pairs={{0,9},{1,10},{2,11},{3,12},{4,13},{5,14},{6,15},{7,8},{8,17},{9,18... | collective-permute-start | bytes 245768 | tf_op jit(solution)/shard_map/ppermute | solution.py:496
  202.0 24.0 %collective-permute-start.10 = (bf16[224,512]{1,0:T(8,128)(2,1)S(1)}, bf16[224,512]{1,0:T(8,128)(2,1)S(1)}, u32[]{:S(2)}, u32[]{:S(2)}) collective-permute-start(bf16[224,512]{1,0:T(8,128)(2,1)S(1)} %get-tuple-element.54), channel_id=1, source_target_pairs={{0,1},{1,2},{2,3},{3,4},{4,5},{5,6},{6,7},{7,0},{8,9},{9,10},{10,1... | collective-permute-start | bytes 688136 | tf_op jit(solution)/shard_map/ppermute | solution.py:496
  202.0 26.4 %collective-permute-start.7 = (bf16[224,512]{1,0:T(8,128)(2,1)}, bf16[224,512]{1,0:T(8,128)(2,1)}, u32[]{:S(2)}, u32[]{:S(2)}) collective-permute-start(bf16[224,512]{1,0:T(8,128)(2,1)} %get-tuple-element.49), channel_id=1, source_target_pairs={{0,1},{1,2},{2,3},{3,4},{4,5},{5,6},{6,7},{7,0},{8,9},{9,10},{10,1... | collective-permute-start | bytes 688136 | tf_op jit(solution)/shard_map/ppermute | solution.py:496
  208.1 20.3 %collective-permute-start.8 = (bf16[80,512]{1,0:T(8,128)(2,1)}, bf16[80,512]{1,0:T(8,128)(2,1)S(1)}, u32[]{:S(2)}, u32[]{:S(2)}) collective-permute-start(bf16[80,512]{1,0:T(8,128)(2,1)} %get-tuple-element.50), channel_id=1, source_target_pairs={{0,9},{1,10},{2,11},{3,12},{4,13},{5,14},{6,15},{7,8},{8,17},{9,18... | collective-permute-start | bytes 245768 | tf_op jit(solution)/shard_map/ppermute | solution.py:496
  (24 other events, 71.7 us)

commit v2 on v1

--- a/solution.py
+++ b/solution.py
@@ -90,7 +90,7 @@
     return [jax.ShapeDtypeStruct(dim, dtype) for dim in dims]
 
 
-def call(kernel, name, grid, ins, outs, out_shapes, scratch, cost, vmem):
+def call(kernel, name, grid, ins, outs, out_shapes, scratch, cost, vmem, aliases={}):
     flops, moved, exps = cost
     return pl.pallas_call(
         kernel,
@@ -99,28 +99,52 @@
         out_specs=outs,
         out_shape=out_shapes,
         scratch_shapes=scratch,
+        input_output_aliases=aliases,
         compiler_params=pltpu.CompilerParams(vmem_limit_bytes=vmem * 2**20),
         cost_estimate=pl.CostEstimate(flops=flops, bytes_accessed=moved, transcendentals=exps),
         name=name,
     )
 
 
-def request_kernel(owner_ref, slot_ref, lists_ref, place_ref, hits, ranks):
+ZONES = (0, 3, 9, 12)
+GROUP = 16
+COMPACT = [(b - a) * STRIP + BANDS * 2 * (GROUP - 1) for a, b in zip(ZONES, ZONES[1:])]
+
+
+def request_kernel(owner_ref, slot_ref, lists_ref, place_ref, table_ref, hits, ranks):
     owner = owner_ref[...]
     slot = slot_ref[...]
     hit = owner == lax.broadcasted_iota(I32, (BANDS, TOKENS), 0)
     hits[...] = hit.astype(F32)
-    step = 256
+    step = STRIP
     row = lax.broadcasted_iota(I32, (step, step), 0)
     triangle = (row <= lax.broadcasted_iota(I32, (step, step), 1)).astype(F32).astype(BF16)
+    row = lax.broadcasted_iota(I32, (BANDS, BANDS), 0)
+    earlier = (lax.broadcasted_iota(I32, (BANDS, BANDS), 1) < row).astype(F32).astype(BF16)
     before = jnp.zeros((BANDS, 1), F32)
-    for at in range(0, TOKENS, step):
-        part = hits[:, at : at + step]
-        count = product(part.astype(BF16), triangle) + before
-        ranks[:, at : at + step] = jnp.sum(part * count, 0, keepdims=True) - 1.0
-        before = before + jnp.sum(part, 1, keepdims=True)
+    columns = []
+    for zone in range(3):
+        first = before
+        strips = range(ZONES[zone], ZONES[zone + 1])
+        for strip in strips:
+            spot = slice(strip * step, strip * step + step)
+            part = hits[:, spot]
+            count = product(part.astype(BF16), triangle) + before
+            ranks[:, spot] = jnp.sum(part * count, 0, keepdims=True) - 1.0
+            before = before + jnp.sum(part, 1, keepdims=True)
+        start = jnp.floor(first * (1.0 / GROUP))
+        groups = jnp.floor((before + (GROUP - 1)) * (1.0 / GROUP)) - start
+        groups = jnp.where(before > first, groups, 0.0)
+        base = product(earlier, jnp.broadcast_to(groups, (BANDS, 128)).astype(BF16))[:, :1]
+        shift = (base - start) * GROUP
+        for strip in strips:
+            spot = slice(strip * step, strip * step + step)
+            moved = jnp.sum(hits[:, spot] * shift, 0, keepdims=True)
+            place_ref[:, spot] = (ranks[:, spot] + moved).astype(I32)
+        columns += [start, groups]
+    columns += [jnp.zeros((BANDS, 2), F32)]
+    table_ref[...] = jnp.concatenate(columns, 1).astype(I32)
     rank = ranks[...]
-    place_ref[...] = owner * CAP + rank.astype(I32)
     high = jnp.where(hit, lax.shift_right_logical(slot, 5), 0).astype(F32).astype(BF16)
     low = jnp.where(hit, slot & 31, 0).astype(F32).astype(BF16)
     chosen = rank == lax.broadcasted_iota(I32, (CAP, TOKENS), 0).astype(F32)
@@ -133,53 +157,84 @@
     return call(
         request_kernel, "requests", (),
         [whole(1, TOKENS)] * 2,
-        [whole(BANDS, CAP), whole(1, TOKENS)],
-        shapes((BANDS, CAP), (1, TOKENS), dtype=I32),
+        [whole(BANDS, CAP), whole(1, TOKENS), whole(BANDS, 8)],
+        shapes((BANDS, CAP), (1, TOKENS), (BANDS, 8), dtype=I32),
         [pltpu.VMEM((BANDS, TOKENS), F32), pltpu.VMEM((1, TOKENS), F32)],
         (100000000, 100000, 0), 20,
     )(owners, slots)
 
 
+ASKERS = 4
+
+
 def serve_kernel(lists_ref, buffer_ref, out_ref):
-    asker = pl.program_id(0)
     lane = lax.broadcasted_iota(I32, (CAP, BANDS), 1)
-    wanted = jnp.sum(jnp.where(lane == asker, lists_ref[...], 0), 1, keepdims=True)
-    chosen = wanted == lax.broadcasted_iota(I32, (CAP, ROWS), 1)
+    wanted = []
+    for at in range(ASKERS):
+        asker = pl.program_id(0) * ASKERS + at
+        wanted.append(jnp.sum(jnp.where(lane == asker, lists_ref[...], 0), 1, keepdims=True))
+    chosen = jnp.concatenate(wanted) == lax.broadcasted_iota(I32, (ASKERS * CAP, ROWS), 1)
     chosen = jnp.where(chosen, 1.0, 0.0).astype(BF16)
     out_ref[...] = product(chosen, buffer_ref[...]).astype(BF16)
 
 
 def serve(lists, buffer):
     return call(
-        serve_kernel, "serve", (BANDS,),
+        serve_kernel, "serve", (BANDS // ASKERS,),
         [whole(CAP, BANDS), whole(ROWS, D)],
-        blocks(CAP, D),
+        blocks(ASKERS * CAP, D),
         shapes((BANDS * CAP, D))[0],
-        [], (5400000000, 6000000, 0), 20,
+        [], (5400000000, 6000000, 0), 60,
     )(lists, buffer)
 
 
-def pick_kernel(place_ref, replies_ref, out_ref):
-    place = place_ref[...]
-    rows = place.shape[0]
-    step = 512
-    total = 0.0
-    for at in range(0, BANDS * CAP, step):
-        chosen = (place - at) == lax.broadcasted_iota(I32, (rows, step), 1)
-        chosen = jnp.where(chosen, 1.0, 0.0).astype(BF16)
-        total += product(chosen, replies_ref[at : at + step, :])
-    out_ref[...] = total.astype(BF16)
-
-
-def pick(place, replies, rows):
-    count = place.shape[0]
-    return call(
-        pick_kernel, "pick", (count // rows,),
-        [blocks(rows, 1), whole(BANDS * CAP, D)],
-        blocks(rows, D),
-        shapes((count, D))[0],
-        [], (count * 4718592, 6000000, 0), 30,
-    )(place, replies)
+def pick_kernel(table_ref, place_ref, replies_ref, up_ref, side_ref, corner_ref, inner_ref, edge_ref, compact):
+    compact[...] = jnp.zeros_like(compact)
+    firsts = (0, UP + CORNER, UP + CORNER + 2 * WIN + INNER)
+    for zone, size in enumerate(COMPACT):
+        filled = 0
+        for owner in range(BANDS):
+            start = owner * CAP + table_ref[owner, 2 * zone] * GROUP
+            groups = table_ref[owner, 2 * zone + 1]
+
+            def move(at, filled, start=start):
+                source = pl.multiple_of(start + at * GROUP, GROUP)
+                target = pl.multiple_of(filled, GROUP)
+                compact[pl.ds(target, GROUP), :] = replies_ref[pl.ds(source, GROUP), :]
+                return filled + GROUP
+
+            filled = lax.fori_loop(0, groups, move, filled)
+
+        def find(first, count, size=size):
+            place = place_ref[first : first + count, :]
+            chosen = place == lax.broadcasted_iota(I32, (count, size), 1)
+            chosen = jnp.where(chosen, 1.0, 0.0).astype(BF16)
+            return product(chosen, compact[:size, :]).astype(BF16)
+
+        first = firsts[zone]
+        if zone == 0:
+            found = find(first, UP + CORNER)
+            up_ref[...] = found[:UP]
+            corner_ref[...] = found[UP:]
+        elif zone == 1:
+            found = find(first, 2 * WIN + INNER)
+            side_ref[:WIN, :] = found[:WIN]
+            edge_ref[:WIN, :] = found[WIN : 2 * WIN]
+            inner_ref[...] = found[2 * WIN :]
+        else:
+            found = find(first, SMALL + EDGE - WIN)
+            side_ref[WIN:, :] = found[:SMALL]
+            edge_ref[WIN:, :] = found[SMALL:]
+
+
+def pick(table, place, replies):
+    return call(
+        pick_kernel, "pick", (),
+        [pl.BlockSpec(memory_space=pltpu.SMEM), whole(PLACES, 1), whole(BANDS * CAP, D)],
+        [whole(n, D) for n in (UP, SIDE, CORNER, INNER, EDGE)],
+        shapes(*[(n, D) for n in (UP, SIDE, CORNER, INNER, EDGE)]),
+        [pltpu.VMEM((max(COMPACT), D), BF16)], (3600000000, 8000000, 0), 36,
+    )(table, place, replies)
 
 
 def sort_kernel(grid_ref, split_ref, small_ref, up_ref, side_ref, corner_ref, inner_ref, edge_ref):
@@ -222,17 +277,17 @@
         return np.pad(part, (0, WIN - 64 - HALF if part.size == HALF else 0))
 
     low, mid, high = range(3), range(3, 9), range(9, 12)
-    order = [piece(low, 6 + 12 * q, 12) for q in range(3)]
-    order += [piece(low, 42, 6), piece(mid, 0, 6), piece(high, 0, 6), piece(low, 0, 6)]
+    order = [piece(low, 6 + 12 * q, 12) for q in range(3)] + [piece(low, 42, 6), piece(low, 0, 6)]
+    order += [piece(mid, 0, 6), piece(mid, 42, 6)]
     for q in range(3):
         order += [piece(range(3, 6), 6 + 12 * q, 12), piece(range(6, 9), 6 + 12 * q, 12)]
-    order += [piece(mid, 42, 6)]
+    order += [piece(high, 0, 6)]
     order += [piece(high, 6 + 12 * q, 12) for q in range(3)] + [piece(high, 42, 6)]
     return np.concatenate(order)
 
 
 ORDER = order_ids()
-SENT = UP + SIDE + CORNER
+PLACES = UP + SIDE + CORNER + INNER + EDGE
 
 
 def join_halves(first, second):
@@ -288,7 +343,7 @@
 
 
 def edge_kernel(xe, xu, xs, xc, ce, cu, cs, cc, join_ref, bias_ref, *refs):
-    *refs, x_all, c_all = refs
+    weights, (*refs, x_all, c_all) = refs[:3], refs[8:]
     step = pl.program_id(0)
 
     @pl.when(step == 0)
@@ -312,12 +367,13 @@
         parts = [ce[near, :], cs[along, :], cu[far, :], cc[...]]
         c_all[...] = product(join_ref[...], jnp.concatenate(parts))
 
-    attend(x_all[...], c_all[...], bias_ref, *refs)
-
-
-def attend_specs(rows):
-    outs = [blocks(BLOCK, n) for n in (D, D, D, D, 3 * D)]
-    out_shapes = shapes(*[(rows, n) for n in (D, D, D, D, 3 * D)])
+    attend(x_all[...], c_all[...], bias_ref, *weights, *refs)
+
+
+def attend_specs(rows, skip):
+    widths = (D, D, D, D, 3 * D)
+    outs = [pl.BlockSpec((BLOCK, n), lambda i: (i + skip, 0)) for n in widths]
+    out_shapes = shapes(*[(TOKENS, n) for n in widths])
     scratch = [pltpu.VMEM((BLOCK, 3 * D), BF16), pltpu.VMEM((BLOCK, D), BF16)]
     cost = (rows * 6000000, rows * 10000, rows * 1200)
     return outs, out_shapes, scratch, cost
@@ -327,33 +383,33 @@
 
 
 def attend_inner(x, cot, weights):
-    outs, out_shapes, scratch, cost = attend_specs(INNER)
+    outs, out_shapes, scratch, cost = attend_specs(INNER, 0)
     return call(
         inner_kernel, "attend_inner", (3,),
         [blocks(BLOCK, D)] * 2 + [whole(*dim) for dim in WEIGHTS],
-        outs, out_shapes, scratch, cost, 24,
+        outs, out_shapes, scratch, cost, 18,
     )(x, cot, *weights)
 
 
-def attend_edge(x_parts, c_parts, bias, weights):
-    rows = 5 * BLOCK
-    outs, out_shapes, scratch, cost = attend_specs(rows)
+def attend_edge(x_parts, c_parts, bias, weights, carried):
+    outs, out_shapes, scratch, cost = attend_specs(5 * BLOCK, 3)
     parts = [whole(n, D) for n in (EDGE, UP, SIDE, CORNER)]
     return call(
         edge_kernel, "attend_edge", (5,),
         parts * 2
         + [whole(BLOCK, 4 * SMALL), pl.BlockSpec((None, WIN, WIN), lambda i: (jnp.minimum(i, 1), 0, 0))]
-        + [whole(*dim) for dim in WEIGHTS],
-        outs, out_shapes, scratch + [pltpu.VMEM((BLOCK, D), F32)] * 2, cost, 32,
-    )(*x_parts, *c_parts, jnp.asarray(CORNER_JOIN, BF16), bias, *weights)
-
-
-def weight_kernel(hi, ai, ci, di, he, ae, ce, de, out_ref, turned):
+        + [whole(*dim) for dim in WEIGHTS]
+        + [pl.BlockSpec(memory_space=pl.ANY)] * 5,
+        outs, out_shapes, scratch + [pltpu.VMEM((BLOCK, D), F32)] * 2, cost, 24,
+        aliases={13 + n: n for n in range(5)},
+    )(*x_parts, *c_parts, jnp.asarray(CORNER_JOIN, BF16), bias, *weights, *carried)
+
+
+def weight_kernel(h_ref, att_ref, c_ref, dp_ref, out_ref, turned):
     def chunk(c):
         if c < 3:
-            cols = slice(c * D, c * D + D)
-            return product(hi[...], di[:, cols], TN) + product(he[...], de[:, cols], TN)
-        return product(ai[...], ci[...], TN) + product(ae[...], ce[...], TN)
+            return product(h_ref[...], dp_ref[:, c * D : c * D + D], TN)
+        return product(att_ref[...], c_ref[...], TN)
 
     upper = lax.broadcasted_iota(I32, (64, 8, D), 1) < 4
     for pair in range(2):
@@ -367,15 +423,14 @@
     out_ref[...] = turned[...].reshape(2048, D).astype(BF16)
 
 
-def weight_terms(inner, edge):
-    dims = [(n, w) for n in (INNER, 5 * BLOCK) for w in (D, D, D, 3 * D)]
+def weight_terms(hidden, att, cot, dp):
     return call(
         weight_kernel, "weight_terms", (),
-        [whole(*dim) for dim in dims],
+        [whole(TOKENS, n) for n in (D, D, D, 3 * D)],
         whole(2048, D), shapes((2048, D))[0],
         [pltpu.VMEM((64, 2, 2, 8, D), F32)],
-        (TOKENS * 2 * D * 4 * D, 18000000, 0), 48,
-    )(*inner, *edge)
+        (TOKENS * 2 * D * 4 * D, 18000000, 0), 36,
+    )(hidden, att, cot, dp)
 
 
 def finished(x_ref, c_ref, att_ref, dp_ref, w_ref, gain_ref, ow_ref):
@@ -398,33 +453,31 @@
     return [product(split_ref[...], part, TN).astype(BF16) for part in (first, second)]
 
 
-def finish_inner_kernel(split_ref, *refs):
-    *refs, out_ref, grad_ref = refs
-    for ref, values in zip((out_ref, grad_ref), finished(*refs)):
-        first, second = grid_pieces(split_ref, values)
-        ref[:WIN, :] = first
-        ref[WIN:, :] = second
-
-
-def finish_edge_kernel(split_ref, back_ref, *refs):
+def finish_kernel(split_ref, back_ref, *refs):
     refs, outs = refs[:7], refs[7:]
     step = pl.program_id(0)
-    for (edge, up, side, corner), values in zip((outs[:4], outs[4:]), finished(*refs)):
-
-        @pl.when(step < 4)
+    for (inner, edge, up, side, corner), values in zip((outs[:5], outs[5:]), finished(*refs)):
+
+        @pl.when(step < 3)
+        def _(inner=inner, values=values):
+            first, second = grid_pieces(split_ref, values)
+            inner[pl.ds(pl.multiple_of(step * BLOCK, 16), WIN), :] = first
+            inner[pl.ds(pl.multiple_of(step * BLOCK + WIN, 16), WIN), :] = second
+
+        @pl.when((step >= 3) & (step < 7))
         def _(edge=edge, up=up, side=side, values=values):
             first, second = grid_pieces(split_ref, values)
-            edge[pl.ds(pl.multiple_of(step * WIN, 16), WIN), :] = first
-
-            @pl.when(step == 0)
+            edge[pl.ds(pl.multiple_of((step - 3) * WIN, 16), WIN), :] = first
+
+            @pl.when(step == 3)
             def _():
                 side[:WIN, :] = second
 
-            @pl.when(step > 0)
+            @pl.when(step > 3)
             def _():
-                up[pl.ds(pl.multiple_of((step - 1) * WIN, 16), WIN), :] = second
-
-        @pl.when(step == 4)
+                up[pl.ds(pl.multiple_of((step - 4) * WIN, 16), WIN), :] = second
+
+        @pl.when(step == 7)
         def _(edge=edge, up=up, side=side, corner=corner, values=values):
             parts = product(back_ref[...], values.astype(BF16)).astype(BF16)
             edge[4 * WIN :, :] = parts[:SMALL]
@@ -433,25 +486,15 @@
             corner[...] = parts[3 * SMALL :]
 
 
-def finish_inner(values, weights):
-    return call(
-        finish_inner_kernel, "finish_inner", (3,),
-        [whole(WIN, WIN)] + [blocks(BLOCK, n) for n in (D, D, D, 3 * D)] + [whole(*dim) for dim in WEIGHTS],
-        [blocks(BLOCK, D)] * 2, shapes((INNER, D), (INNER, D)), [],
-        (INNER * 2200000, INNER * 8000, INNER), 24,
-    )(jnp.asarray(SPLIT, BF16), *values, *weights)
-
-
-def finish_edge(values, weights):
-    dims = [(n, D) for n in (EDGE, UP, SIDE, CORNER)] * 2
-    rows = 5 * BLOCK
-    return call(
-        finish_edge_kernel, "finish_edge", (5,),
+def finish(values, weights):
+    dims = [(n, D) for n in (INNER, EDGE, UP, SIDE, CORNER)] * 2
+    return call(
+        finish_kernel, "finish", (8,),
         [whole(WIN, WIN), whole(4 * SMALL, BLOCK)]
         + [blocks(BLOCK, n) for n in (D, D, D, 3 * D)]
         + [whole(*dim) for dim in WEIGHTS],
         [whole(*dim) for dim in dims], shapes(*dims), [],
-        (rows * 2200000, rows * 8000, rows), 24,
+        (TOKENS * 2200000, TOKENS * 8000, TOKENS), 24,
     )(jnp.asarray(SPLIT, BF16), jnp.asarray(CORNER_BACK, BF16), *values, *weights)
 
 
@@ -502,7 +545,7 @@
 
 def per_device(buffer, fetch_owner, fetch_slot, norm_gain, qkv_weight, out_weight, out_grad):
     weights = (qkv_weight, norm_gain.reshape(1, D), out_weight)
-    lists, place = make_requests(fetch_owner.reshape(1, TOKENS), fetch_slot.reshape(1, TOKENS))
+    lists, place, table = make_requests(fetch_owner.reshape(1, TOKENS), fetch_slot.reshape(1, TOKENS))
     lists = swap_blocks(lists, "lat")
     replies = swap_blocks(serve(lists.T, buffer).reshape(BANDS, CAP, D), "lat")
     replies = replies.reshape(BANDS * CAP, D)
@@ -511,24 +554,22 @@
     c_parts = [c_edge] + exchange([c_up, c_side, c_corner], -1)
     place = place.reshape(TOKENS)[ORDER].reshape(-1, 1)
 
-    sent = pick(place[:SENT], replies, 272)
-    arrived = exchange([sent[:UP], sent[UP : UP + SIDE], sent[UP + SIDE :]], -1)
-    kept = pick(place[SENT:], replies, 304)
+    x_up, x_side, x_corner, x_inner, x_edge = pick(table, place, replies)
+    x_parts = [x_edge] + exchange([x_up, x_side, x_corner], -1)
 
     last = (lax.axis_index("lat") == BANDS - 1) & (jnp.arange(2) == 1)
     group = jnp.arange(WIN) >= HALF
     apart = last[:, None, None] & (group[:, None] != group[None, :])
     bias = jnp.where(apart, -jnp.inf, 0.0).astype(F32)
-    xi, ci, hi, ai, di = attend_inner(kept[:INNER], c_inner, weights)
-    xe, ce, he, ae, de = attend_edge([kept[INNER:]] + arrived, c_parts, bias, weights)
-    terms = swap_blocks(weight_terms((hi, ai, ci, di), (he, ae, ce, de)), BOTH)
-
-    edges = finish_edge((xe, ce, ae, de), weights)
-    returned = [exchange(edges[at + 1 : at + 4], 1) for at in (0, 4)]
-    inners = finish_inner((xi, ci, ai, di), weights)
-    outs = [
-        join([inners[n], edges[4 * n]] + returned[n]).reshape(LAT, LON, LEV, D) for n in range(2)
-    ]
+    first = attend_inner(x_inner, c_inner, weights)
+    x, cot, hidden, att, dp = attend_edge(x_parts, c_parts, bias, weights, first)
+    terms = swap_blocks(weight_terms(hidden, att, cot, dp), BOTH)
+
+    done = finish((x, cot, att, dp), weights)
+    outs = []
+    for at in (0, 5):
+        returned = exchange(done[at + 2 : at + 5], 1)
+        outs.append(join(list(done[at : at + 2]) + returned).reshape(LAT, LON, LEV, D))
     total = jnp.sum(terms.reshape(DEVICES, 4, 4, D).astype(F32), 0).transpose(1, 0, 2).reshape(4, 4 * D)
     return (outs[0], outs[1], total[:, : 3 * D], total[:, 3 * D :])
 

time: 237 us -> 224 us (0.945)
  Pallas kernels: 94.1 us -> 81.5 us
  waiting for transfers between devices: 42.6 us -> 48.2 us
  local copies, waits for them, and re-layouts: 45.7 us -> 40.8 us
    pallas_call x6 -> x4, Pallas kernels: 51.8 us -> 39.1 us  [the longest x1 13.2 us: finish(): call(finish_kernel, 'finish', (8,), [whole(WIN, WIN), whole(4 * SMALL, BL...]
    unnamed x68 -> x58, local copies, waits for them, and re-layouts: 22.8 us -> 17.6 us
    all_to_all x2, waiting for transfers between devices: 25.9 us -> 28.7 us  [swap_blocks(): return lax.all_to_all(values, axis, split_axis=0, concat_axis=0, tiled=True)]
    ppermute x12, waiting for transfers between devices: 16.8 us -> 19.6 us  [exchange(): lax.ppermute(part, BOTH, shift_pairs(*step))]
  transfers between devices with their start and end apart: 14 -> 14, of which waited for: 3 -> 4; matrix products, arithmetic and copies ran while one was open for 10% -> 10% of each run, Pallas kernels for 20% -> 17%
where the time goes in v2:
time: 224 us; the launch traced here: 223 us
  Pallas kernels  81.5 us (36%)
  waiting for transfers between devices  48.2 us (22%)
  local copies, waits for them, and re-layouts  40.8 us (18%)
  starting transfers between devices  32.2 us (14%)
  blocking collectives  16.4 us (7%)
  other arithmetic  2.9 us (1%)
    all_to_all x2, waiting for transfers between devices, swap_blocks(): return lax.all_to_all(values, axis, split_axis=0, concat_axis=0, tiled=True)  28.7 us
    pallas_call x1, Pallas kernels, attend_edge(): call(edge_kernel, 'attend_edge', (5,), parts * 2 + [whole(BLOCK, 4 * SMAL...  24.9 us
    ppermute x12, starting transfers between devices, exchange(): lax.ppermute(part, BOTH, shift_pairs(*step))  21.8 us
    ppermute x12, waiting for transfers between devices, exchange(): lax.ppermute(part, BOTH, shift_pairs(*step))  19.6 us
    unnamed x58, local copies, waits for them, and re-layouts  17.6 us
    all_to_all x1, blocking collectives, swap_blocks(): return lax.all_to_all(values, axis, split_axis=0, concat_axis=0, tiled=True)  16.4 us
    pallas_call x1, Pallas kernels, attend_inner(): call(inner_kernel, 'attend_inner', (3,), [blocks(BLOCK, D)] * 2 + [whole(...  13.3 us
    pallas_call x1, Pallas kernels, finish(): call(finish_kernel, 'finish', (8,), [whole(WIN, WIN), whole(4 * SMALL, BL...  13.2 us
  transfers between devices with their start and end apart: 14, of which 4 were waited for; matrix products, arithmetic and copies ran while one was open for 10% of the time, Pallas kernels for 17%

profile of v2, /device:TPU:1, one launch (start us, length us, event | category | flops | bytes accessed | tf_op | source)
XLA Modules:
  0.0 223.0 jit_solution(17001354252090235115)
XLA Ops:
  3.4 16.4 %all_to_all.26 = s32[16,1,288]{2,1,0:T(1,128)S(1)} all-to-all(s32[16,1,288]{2,1,0:T(1,128)S(1)} %copy.26), channel_id=1, replica_groups=mesh['lat'=16,'lon'=8] {'lat'}, dimensions={0} | all-to-all | bytes 36864 | tf_op jit(solution)/shard_map/all_to_all | solution.py:543
  20.5 10.9 %serve.1 = bf16[4608,512]{1,0:T(8,128)(2,1)} custom-call(s32[288,16]{1,0:T(8,128)} %bitcast.20, bf16[1152,512]{1,0:T(8,128)(2,1)} %buffer_ref.1), custom_call_target="tpu_custom_call" | custom-call | flops 5400000000 | bytes 6000000 | tf_op jit(solution)/shard_map/serve/pallas_call | solution.py:182
  31.4 4.7 %all-to-all-start.1 = ((bf16[16,288,512]{2,1,0:T(8,128)(2,1)}), bf16[16,288,512]{2,1,0:T(8,128)(2,1)}, u32[]{:S(2)}, u32[]{:S(2)}) async-start(bf16[16,288,512]{2,1,0:T(8,128)(2,1)} %bitcast.19), calls=%async_computation.1 | async-start | bytes 9437184 | tf_op jit(solution)/shard_map/all_to_all | solution.py:543
  36.2 3.9 %reshape.94.grid_ref = bf16[2304,512]{1,0:T(8,128)(2,1)S(1)} reshape(bf16[12,48,4,512]{3,2,1,0:T(4,128)(2,1)} %param.20) | data formatting | bytes 4718592 | tf_op jit(solution)/shard_map/reshape | solution.py:553
  42.5 2.9 %collective-permute-start.5 = (bf16[80,512]{1,0:T(8,128)(2,1)S(1)}, bf16[80,512]{1,0:T(8,128)(2,1)S(1)}, u32[]{:S(2)}, u32[]{:S(2)}) collective-permute-start(bf16[80,512]{1,0:T(8,128)(2,1)S(1)} %get-tuple-element.47), channel_id=1, source_target_pairs={{0,127},{1,120},{2,121},{3,122},{4,123},{5,124},{6,125},{7,126},{8... | collective-permute-start | bytes 245768 | tf_op jit(solution)/shard_map/ppermute | solution.py:539
  46.6 3.8 %collective-permute-start.3 = (bf16[512,512]{1,0:T(8,128)(2,1)}, bf16[512,512]{1,0:T(8,128)(2,1)}, u32[]{:S(2)}, u32[]{:S(2)}) collective-permute-start(bf16[512,512]{1,0:T(8,128)(2,1)} %get-tuple-element.45), channel_id=1, source_target_pairs={{0,120},{1,121},{2,122},{3,123},{4,124},{5,125},{6,126},{7,127},{8... | collective-permute-start | bytes 1572872 | tf_op jit(solution)/shard_map/ppermute | solution.py:539
  51.1 12.7 %gather_fusion = s32[2336]{0:T(1024)S(1)} fusion(s32[2304]{0:T(1024)S(1)} %reduce.1, s32[3072]{0:T(1024)S(1)} %pad_clamp_fusion), kind=kCustom, calls=%fused_computation | custom fusion | bytes 28032 | tf_op jit(solution)/shard_map/gather | solution.py:555
  64.4 28.7 %all-to-all-done.1 = bf16[16,288,512]{2,1,0:T(8,128)(2,1)} async-done(((bf16[16,288,512]{2,1,0:T(8,128)(2,1)}), bf16[16,288,512]{2,1,0:T(8,128)(2,1)}, u32[]{:S(2)}, u32[]{:S(2)}) %all-to-all-start.1) | async-done | bytes 4718624 | tf_op jit(solution)/shard_map/all_to_all | solution.py:543
  93.0 8.5 %pick.1 = (bf16[512,512]{1,0:T(8,128)(2,1)S(1)}, bf16[224,512]{1,0:T(8,128)(2,1)S(1)}, bf16[80,512]{1,0:T(8,128)(2,1)S(1)}, bf16[864,512]{1,0:T(8,128)(2,1)S(1)}, bf16[656,512]{1,0:T(8,128)(2,1)S(1)}) custom-call(s32[16,8]{1,0:T(8,128)S(1)} %get-tuple-element.37.table_ref, s32[2336,1]{1,0:T(8,128)S(1)} %reshape.107.place_ref, ...), custom_call_target="tpu_custom_call" | custom-call | flops 3600000000 | bytes 8000000 | tf_op jit(solution)/shard_map/pick/pallas_call | solution.py:231
  104.7 3.1 %collective-permute-start.2 = (bf16[80,512]{1,0:T(8,128)(2,1)S(1)}, bf16[80,512]{1,0:T(8,128)(2,1)S(1)}, u32[]{:S(2)}, u32[]{:S(2)}) collective-permute-start(bf16[80,512]{1,0:T(8,128)(2,1)S(1)} %get-tuple-element.43), channel_id=1, source_target_pairs={{0,127},{1,120},{2,121},{3,122},{4,123},{5,124},{6,125},{7,126},{8... | collective-permute-start | bytes 245768 | tf_op jit(solution)/shard_map/ppermute | solution.py:539
  110.1 13.3 %attend_inner.1 = (bf16[2304,512]{1,0:T(8,128)(2,1)S(1)}, bf16[2304,512]{1,0:T(8,128)(2,1)S(1)}, bf16[2304,512]{1,0:T(8,128)(2,1)S(1)}, bf16[2304,512]{1,0:T(8,128)(2,1)S(1)}, bf16[2304,1536]{1,0:T(8,128)(2,1)S(1)}) custom-call(bf16[864,512]{1,0:T(8,128)(2,1)S(1)} %copy-done.26, bf16[864,512]{1,0:T(8,128)(2,1)S(1)} %copy-done.7, ...), custom_call_target="tpu_custom_call" | custom-call | flops 5184000000 | bytes 8640000 | tf_op jit(solution)/shard_map/attend_inner/pallas_call | solution.py:387
  123.5 24.9 %attend_edge.1 = (bf16[2304,512]{1,0:T(8,128)(2,1)S(1)}, bf16[2304,512]{1,0:T(8,128)(2,1)S(1)}, bf16[2304,512]{1,0:T(8,128)(2,1)S(1)}, bf16[2304,512]{1,0:T(8,128)(2,1)S(1)}, bf16[2304,1536]{1,0:T(8,128)(2,1)S(1)}) custom-call(bf16[656,512]{1,0:T(8,128)(2,1)S(1)} %copy-done.28, ...), custom_call_target="tpu_custom_call", output_to_operand_aliasing={{0}: (13, {}), {1}: (14, {}), {2}: (15, {}), {3}: (16, {}),... | custom-call | flops 8640000000 | bytes 14400000 | tf_op jit(solution)/shard_map/attend_edge/pallas_call | solution.py:397
  149.8 6.5 %weight_terms.1 = bf16[2048,512]{1,0:T(8,128)(2,1)} custom-call(bf16[2304,512]{1,0:T(8,128)(2,1)S(1)} %get-tuple-element.69.h_ref, bf16[2304,512]{1,0:T(8,128)(2,1)S(1)} %get-tuple-element.57.refs_2_.att_ref, bf16[2304,512]{1,0:T(8,128)(2,1)S(1)} %get-tuple-element.56.refs_1_.c_ref, bf16[2304,1536]{1,0:T(8,128)(2,1)S(1)} %get-tuple-element.58.refs_3_.dp_ref), custom_call_target="tpu_custom_call" | custom-call | flops 4831838208 | bytes 18000000 | tf_op jit(solution)/shard_map/weight_terms/pallas_call | solution.py:427
  156.3 5.7 %all-to-all-start.2 = ((bf16[128,16,512]{2,1,0:T(8,128)(2,1)}), bf16[128,16,512]{2,1,0:T(8,128)(2,1)}, u32[]{:S(2)}, u32[]{:S(2)}) async-start(bf16[128,16,512]{2,1,0:T(8,128)(2,1)} %bitcast.8), calls=%async_computation.2 | async-start | bytes 4194304 | tf_op jit(solution)/shard_map/all_to_all | solution.py:543
  163.0 3.0 %copy-done.18 = bf16[2304,1536]{1,0:T(8,128)(2,1)S(1)} copy-done((bf16[2304,1536]{1,0:T(8,128)(2,1)S(1)}, bf16[2304,1536]{1,0:T(8,128)(2,1)}, u32[]{:S(2)}) %copy-start.18) | copy-done | bytes 7077912
  171.0 13.2 %finish.1 = (bf16[864,512]{1,0:T(8,128)(2,1)S(1)}, bf16[656,512]{1,0:T(8,128)(2,1)S(1)}, bf16[512,512]{1,0:T(8,128)(2,1)S(1)}, bf16[224,512]{1,0:T(8,128)(2,1)S(...) custom-call(bf16[144,144]{1,0:T(8,128)(2,1)S(1)} %copy-done.2, ...), custom_call_target="tpu_custom_call" | custom-call | flops 5068800000 | bytes 18432000 | tf_op jit(solution)/shard_map/finish/pallas_call | solution.py:491
  185.1 3.1 %collective-permute-start.6 = (bf16[512,512]{1,0:T(8,128)(2,1)S(1)}, bf16[512,512]{1,0:T(8,128)(2,1)S(1)}, u32[]{:S(2)}, u32[]{:S(2)}) collective-permute-start(bf16[512,512]{1,0:T(8,128)(2,1)S(1)} %get-tuple-element.61), channel_id=1, source_target_pairs={{0,8},{1,9},{2,10},{3,11},{4,12},{5,13},{6,14},{7,15},{8,16},{9,17... | collective-permute-start | bytes 1572872 | tf_op jit(solution)/shard_map/ppermute | solution.py:539
  188.7 2.1 collective-permute-start.10
  190.7 2.8 %collective-permute-start.8 = (bf16[80,512]{1,0:T(8,128)(2,1)S(1)}, bf16[80,512]{1,0:T(8,128)(2,1)S(1)}, u32[]{:S(2)}, u32[]{:S(2)}) collective-permute-start(bf16[80,512]{1,0:T(8,128)(2,1)S(1)} %get-tuple-element.63), channel_id=1, source_target_pairs={{0,9},{1,10},{2,11},{3,12},{4,13},{5,14},{6,15},{7,8},{8,17},{9,18... | collective-permute-start | bytes 245768 | tf_op jit(solution)/shard_map/ppermute | solution.py:539
  193.5 12.2 %collective-permute-done.8.corner = bf16[80,512]{1,0:T(8,128)(2,1)S(1)} collective-permute-done((bf16[80,512]{1,0:T(8,128)(2,1)S(1)}, bf16[80,512]{1,0:T(8,128)(2,1)S(1)}, u32[]{:S(2)}, u32[]{:S(2)}) %collective-permute-start.8) | collective-permute-done | bytes 81952 | tf_op jit(solution)/shard_map/ppermute | solution.py:539
  205.8 6.4 %collective-permute-done.7.side = bf16[224,512]{1,0:T(8,128)(2,1)S(1)} collective-permute-done((bf16[224,512]{1,0:T(8,128)(2,1)S(1)}, bf16[224,512]{1,0:T(8,128)(2,1)S(1)}, u32[]{:S(2)}, u32[]{:S(2)}) %collective-permute-start.7) | collective-permute-done | bytes 229408 | tf_op jit(solution)/shard_map/ppermute | solution.py:539
  212.3 2.1 reshape.96
  217.7 2.1 reshape.97
  219.8 2.0 convert_reduce_fusion
  (90 shorter events, 26.9 us)
Async XLA Ops:
  31.4 61.6 %all-to-all-start.1 = ((bf16[16,288,512]{2,1,0:T(8,128)(2,1)}), bf16[16,288,512]{2,1,0:T(8,128)(2,1)}, u32[]{:S(2)}, u32[]{:S(2)}) async-start(bf16[16,288,512]{2,1,0:T(8,128)(2,1)} %bitcast.19), calls=%async_computation.1 | async-start | bytes 9437184 | tf_op jit(solution)/shard_map/all_to_all | solution.py:543
  42.5 21.4 %copy-start.8 = (bf16[656,512]{1,0:T(8,128)(2,1)}, bf16[656,512]{1,0:T(8,128)(2,1)S(1)}, u32[]{:S(2)}) copy-start(bf16[656,512]{1,0:T(8,128)(2,1)S(1)} %get-tuple-element.44.ce) | copy-start | bytes 2015236
  42.5 65.4 %collective-permute-start.5 = (bf16[80,512]{1,0:T(8,128)(2,1)S(1)}, bf16[80,512]{1,0:T(8,128)(2,1)S(1)}, u32[]{:S(2)}, u32[]{:S(2)}) collective-permute-start(bf16[80,512]{1,0:T(8,128)(2,1)S(1)} %get-tuple-element.47), channel_id=1, source_target_pairs={{0,127},{1,120},{2,121},{3,122},{4,123},{5,124},{6,125},{7,126},{8... | collective-permute-start | bytes 245768 | tf_op jit(solution)/shard_map/ppermute | solution.py:539
  45.4 78.0 %collective-permute-start.4 = (bf16[224,512]{1,0:T(8,128)(2,1)}, bf16[224,512]{1,0:T(8,128)(2,1)S(1)}, u32[]{:S(2)}, u32[]{:S(2)}) collective-permute-start(bf16[224,512]{1,0:T(8,128)(2,1)} %get-tuple-element.46), channel_id=1, source_target_pairs={{0,7},{1,0},{2,1},{3,2},{4,3},{5,4},{6,5},{7,6},{8,15},{9,8},{10,9... | collective-permute-start | bytes 688136 | tf_op jit(solution)/shard_map/ppermute | solution.py:539
  46.6 76.8 %collective-permute-start.3 = (bf16[512,512]{1,0:T(8,128)(2,1)}, bf16[512,512]{1,0:T(8,128)(2,1)}, u32[]{:S(2)}, u32[]{:S(2)}) collective-permute-start(bf16[512,512]{1,0:T(8,128)(2,1)} %get-tuple-element.45), channel_id=1, source_target_pairs={{0,120},{1,121},{2,122},{3,123},{4,124},{5,125},{6,126},{7,127},{8... | collective-permute-start | bytes 1572872 | tf_op jit(solution)/shard_map/ppermute | solution.py:539
  93.0 15.8 %copy-start.4 = (bf16[512,1536]{1,0:T(8,128)(2,1)S(1)}, bf16[512,1536]{1,0:T(8,128)(2,1)}, u32[]{:S(2)}) copy-start(bf16[512,1536]{1,0:T(8,128)(2,1)} %refs_4_.1) | copy-start | bytes 4718596
  93.0 15.8 %copy-start.7 = (bf16[864,512]{1,0:T(8,128)(2,1)S(1)}, bf16[864,512]{1,0:T(8,128)(2,1)}, u32[]{:S(2)}) copy-start(bf16[864,512]{1,0:T(8,128)(2,1)} %copy-done.6) | copy-start | bytes 2654212
  93.0 15.8 %copy-start.10 = (bf16[512,512]{1,0:T(8,128)(2,1)S(1)}, bf16[512,512]{1,0:T(8,128)(2,1)}, u32[]{:S(2)}) copy-start(bf16[512,512]{1,0:T(8,128)(2,1)} %refs_6_.1) | copy-start | bytes 1572868
  93.0 15.8 %copy-start.14 = (f32[512]{0:T(512)S(1)}, f32[512]{0:T(512)}, u32[]{:S(2)}) copy-start(f32[512]{0:T(512)} %param.17) | copy-start | bytes 6148
  103.3 20.2 %collective-permute-start = (bf16[512,512]{1,0:T(8,128)(2,1)S(1)}, bf16[512,512]{1,0:T(8,128)(2,1)S(1)}, u32[]{:S(2)}, u32[]{:S(2)}) collective-permute-start(bf16[512,512]{1,0:T(8,128)(2,1)S(1)} %get-tuple-element.41), channel_id=1, source_target_pairs={{0,120},{1,121},{2,122},{3,123},{4,124},{5,125},{6,126},{7,127},{8... | collective-permute-start | bytes 1572872 | tf_op jit(solution)/shard_map/ppermute | solution.py:539
  104.7 18.7 %collective-permute-start.2 = (bf16[80,512]{1,0:T(8,128)(2,1)S(1)}, bf16[80,512]{1,0:T(8,128)(2,1)S(1)}, u32[]{:S(2)}, u32[]{:S(2)}) collective-permute-start(bf16[80,512]{1,0:T(8,128)(2,1)S(1)} %get-tuple-element.43), channel_id=1, source_target_pairs={{0,127},{1,120},{2,121},{3,122},{4,123},{5,124},{6,125},{7,126},{8... | collective-permute-start | bytes 245768 | tf_op jit(solution)/shard_map/ppermute | solution.py:539
  107.9 15.6 %collective-permute-start.1 = (bf16[224,512]{1,0:T(8,128)(2,1)S(1)}, bf16[224,512]{1,0:T(8,128)(2,1)S(1)}, u32[]{:S(2)}, u32[]{:S(2)}) collective-permute-start(bf16[224,512]{1,0:T(8,128)(2,1)S(1)} %get-tuple-element.42), channel_id=1, source_target_pairs={{0,7},{1,0},{2,1},{3,2},{4,3},{5,4},{6,5},{7,6},{8,15},{9,8},{10,9... | collective-permute-start | bytes 688136 | tf_op jit(solution)/shard_map/ppermute | solution.py:539
  110.0 13.4 %copy-start.9 = (bf16[656,512]{1,0:T(8,128)(2,1)S(1)}, bf16[656,512]{1,0:T(8,128)(2,1)}, u32[]{:S(2)}) copy-start(bf16[656,512]{1,0:T(8,128)(2,1)} %copy-done.8) | copy-start | bytes 2015236
  110.0 13.4 %copy-start.16 = (bf16[288,320]{1,0:T(8,128)(2,1)S(1)}, bf16[288,320]{1,0:T(8,128)(2,1)}, u32[]{:S(2)}) copy-start(bf16[288,320]{1,0:T(8,128)(2,1)} %constant.34.clone.join_ref) | copy-start | bytes 552964
  110.1 13.4 %copy-start.28 = (bf16[656,512]{1,0:T(8,128)(2,1)S(1)}, bf16[656,512]{1,0:T(8,128)(2,1)}, u32[]{:S(2)}) copy-start(bf16[656,512]{1,0:T(8,128)(2,1)} %copy-done.27) | copy-start | bytes 2015236
  149.8 6.5 %copy-start.19 = (bf16[2304,512]{1,0:T(8,128)(2,1)}, bf16[2304,512]{1,0:T(8,128)(2,1)S(1)}, u32[]{:S(2)}) copy-start(bf16[2304,512]{1,0:T(8,128)(2,1)S(1)} %get-tuple-element.56.refs_1_.c_ref) | copy-start | bytes 7077892
  149.8 6.5 %copy-start.21 = (bf16[2304,512]{1,0:T(8,128)(2,1)}, bf16[2304,512]{1,0:T(8,128)(2,1)S(1)}, u32[]{:S(2)}) copy-start(bf16[2304,512]{1,0:T(8,128)(2,1)S(1)} %get-tuple-element.57.refs_2_.att_ref) | copy-start | bytes 7077892
  156.3 63.4 %all-to-all-start.2 = ((bf16[128,16,512]{2,1,0:T(8,128)(2,1)}), bf16[128,16,512]{2,1,0:T(8,128)(2,1)}, u32[]{:S(2)}, u32[]{:S(2)}) async-start(bf16[128,16,512]{2,1,0:T(8,128)(2,1)} %bitcast.8), calls=%async_computation.2 | async-start | bytes 4194304 | tf_op jit(solution)/shard_map/all_to_all | solution.py:543
  185.1 27.1 %collective-permute-start.6 = (bf16[512,512]{1,0:T(8,128)(2,1)S(1)}, bf16[512,512]{1,0:T(8,128)(2,1)S(1)}, u32[]{:S(2)}, u32[]{:S(2)}) collective-permute-start(bf16[512,512]{1,0:T(8,128)(2,1)S(1)} %get-tuple-element.61), channel_id=1, source_target_pairs={{0,8},{1,9},{2,10},{3,11},{4,12},{5,13},{6,14},{7,15},{8,16},{9,17... | collective-permute-start | bytes 1572872 | tf_op jit(solution)/shard_map/ppermute | solution.py:539
  188.2 27.2 %collective-permute-start.9 = (bf16[512,512]{1,0:T(8,128)(2,1)}, bf16[512,512]{1,0:T(8,128)(2,1)}, u32[]{:S(2)}, u32[]{:S(2)}) collective-permute-start(bf16[512,512]{1,0:T(8,128)(2,1)} %get-tuple-element.66), channel_id=1, source_target_pairs={{0,8},{1,9},{2,10},{3,11},{4,12},{5,13},{6,14},{7,15},{8,16},{9,17... | collective-permute-start | bytes 1572872 | tf_op jit(solution)/shard_map/ppermute | solution.py:539
  188.4 23.8 %collective-permute-start.7 = (bf16[224,512]{1,0:T(8,128)(2,1)S(1)}, bf16[224,512]{1,0:T(8,128)(2,1)S(1)}, u32[]{:S(2)}, u32[]{:S(2)}) collective-permute-start(bf16[224,512]{1,0:T(8,128)(2,1)S(1)} %get-tuple-element.62), channel_id=1, source_target_pairs={{0,1},{1,2},{2,3},{3,4},{4,5},{5,6},{6,7},{7,0},{8,9},{9,10},{10,1... | collective-permute-start | bytes 688136 | tf_op jit(solution)/shard_map/ppermute | solution.py:539
  188.7 26.7 %collective-permute-start.10 = (bf16[224,512]{1,0:T(8,128)(2,1)}, bf16[224,512]{1,0:T(8,128)(2,1)S(1)}, u32[]{:S(2)}, u32[]{:S(2)}) collective-permute-start(bf16[224,512]{1,0:T(8,128)(2,1)} %get-tuple-element.67), channel_id=1, source_target_pairs={{0,1},{1,2},{2,3},{3,4},{4,5},{5,6},{6,7},{7,0},{8,9},{9,10},{10,1... | collective-permute-start | bytes 688136 | tf_op jit(solution)/shard_map/ppermute | solution.py:539
  190.7 15.0 %collective-permute-start.8 = (bf16[80,512]{1,0:T(8,128)(2,1)S(1)}, bf16[80,512]{1,0:T(8,128)(2,1)S(1)}, u32[]{:S(2)}, u32[]{:S(2)}) collective-permute-start(bf16[80,512]{1,0:T(8,128)(2,1)S(1)} %get-tuple-element.63), channel_id=1, source_target_pairs={{0,9},{1,10},{2,11},{3,12},{4,13},{5,14},{6,15},{7,8},{8,17},{9,18... | collective-permute-start | bytes 245768 | tf_op jit(solution)/shard_map/ppermute | solution.py:539
  205.7 8.7 %collective-permute-start.11 = (bf16[80,512]{1,0:T(8,128)(2,1)}, bf16[80,512]{1,0:T(8,128)(2,1)S(1)}, u32[]{:S(2)}, u32[]{:S(2)}) collective-permute-start(bf16[80,512]{1,0:T(8,128)(2,1)} %get-tuple-element.68), channel_id=1, source_target_pairs={{0,9},{1,10},{2,11},{3,12},{4,13},{5,14},{6,15},{7,8},{8,17},{9,18... | collective-permute-start | bytes 245768 | tf_op jit(solution)/shard_map/ppermute | solution.py:539
  (19 other events, 43.3 us)

commit v3 on v2

--- a/solution.py
+++ b/solution.py
@@ -25,6 +25,7 @@
 HALF = 72
 SMALL = 80
 BLOCK = 2 * WIN
+QUAD = 256
 SCALE = 0.125
 LOG2E = 1.4426950408889634
 BOTH = ("lat", "lon")
@@ -160,7 +161,7 @@
         [whole(BANDS, CAP), whole(1, TOKENS), whole(BANDS, 8)],
         shapes((BANDS, CAP), (1, TOKENS), (BANDS, 8), dtype=I32),
         [pltpu.VMEM((BANDS, TOKENS), F32), pltpu.VMEM((1, TOKENS), F32)],
-        (100000000, 100000, 0), 20,
+        (100000000, 100000, 0), 62,
     )(owners, slots)
 
 
@@ -233,7 +234,7 @@
         [pl.BlockSpec(memory_space=pltpu.SMEM), whole(PLACES, 1), whole(BANDS * CAP, D)],
         [whole(n, D) for n in (UP, SIDE, CORNER, INNER, EDGE)],
         shapes(*[(n, D) for n in (UP, SIDE, CORNER, INNER, EDGE)]),
-        [pltpu.VMEM((max(COMPACT), D), BF16)], (3600000000, 8000000, 0), 36,
+        [pltpu.VMEM((max(COMPACT), D), BF16)], (3600000000, 8000000, 0), 60,
     )(table, place, replies)
 
 
@@ -306,34 +307,36 @@
     for part in range(3):
         cols = slice(part * D, part * D + D)
         packed[:, cols] = product(hidden, w_ref[:, cols]).astype(BF16)
-    lane = lax.broadcasted_iota(I32, (1, 128), 1)
-    sides = [jnp.where(lane < 64, 1.0, 0.0).astype(BF16), jnp.where(lane < 64, 0.0, 1.0).astype(BF16)]
+    lane = lax.broadcasted_iota(I32, (1, QUAD), 1)
+    sides = [jnp.where((lane >= 64 * n) & (lane < 64 * n + 64), 1.0, 0.0) for n in range(4)]
+    low_sides = [side.astype(BF16) for side in sides]
+
+    def spread(values):
+        return jnp.concatenate([values * side for side in low_sides])
+
+    def gather(matrix, values):
+        parts = product(matrix, values, TN)
+        return sum(parts[n * WIN : n * WIN + WIN] * side for n, side in enumerate(sides))
+
     for window in range(2):
         rows = slice(window * WIN, window * WIN + WIN)
-        for pair in range(4):
-            spot = [slice(part * D + pair * 128, part * D + pair * 128 + 128) for part in range(3)]
-            q2, k2, v2 = (packed[rows, cols] for cols in spot)
-            g2 = slopes[rows, spot[0]]
-            att = dq = dk = dv = 0.0
-            for side in sides:
-                qm, km, vm, gm = q2 * side, k2 * side, v2 * side, g2 * side
-                scores = product(k2, qm, NT) * (SCALE * LOG2E)
-                if bias is not None:
-                    scores = scores + bias[...]
-                grown = jnp.exp2(scores - jnp.max(scores, 0, keepdims=True))
-                probs = grown * (1.0 / jnp.sum(grown, 0, keepdims=True))
-                low = probs.astype(BF16)
-                weighted = probs * product(v2, gm, NT)
-                slope = weighted - probs * jnp.sum(weighted, 0, keepdims=True)
-                slope = (slope * SCALE).astype(BF16)
-                dv += product(low, gm)
-                dk += product(slope, qm)
-                att += product(low, vm, TN)
-                dq += product(slope, km, TN)
-            att_ref[rows, spot[0]] = att.astype(BF16)
-            dp_ref[rows, spot[0]] = dq.astype(BF16)
-            dp_ref[rows, spot[1]] = dk.astype(BF16)
-            dp_ref[rows, spot[2]] = dv.astype(BF16)
+        for quad in range(2):
+            spot = [slice(part * D + quad * QUAD, part * D + quad * QUAD + QUAD) for part in range(3)]
+            queries, keys, values = (packed[rows, cols] for cols in spot)
+            queries, grads = spread(queries), spread(slopes[rows, spot[0]])
+            scores = product(keys, queries, NT) * (SCALE * LOG2E)
+            if bias is not None:
+                scores = scores + bias[...]
+            grown = jnp.exp2(scores - jnp.max(scores, 0, keepdims=True))
+            probs = grown * (1.0 / jnp.sum(grown, 0, keepdims=True))
+            low = probs.astype(BF16)
+            weighted = probs * product(values, grads, NT)
+            slope = weighted - probs * jnp.sum(weighted, 0, keepdims=True)
+            slope = (slope * SCALE).astype(BF16)
+            att_ref[rows, spot[0]] = gather(low, values).astype(BF16)
+            dp_ref[rows, spot[0]] = gather(slope, keys).astype(BF16)
+            dp_ref[rows, spot[1]] = product(slope, queries).astype(BF16)
+            dp_ref[rows, spot[2]] = product(low, grads).astype(BF16)
 
 
 def inner_kernel(x_ref, c_ref, *refs):
@@ -397,7 +400,7 @@
     return call(
         edge_kernel, "attend_edge", (5,),
         parts * 2
-        + [whole(BLOCK, 4 * SMALL), pl.BlockSpec((None, WIN, WIN), lambda i: (jnp.minimum(i, 1), 0, 0))]
+        + [whole(BLOCK, 4 * SMALL), pl.BlockSpec((None, WIN, 4 * WIN), lambda i: (jnp.minimum(i, 1), 0, 0))]
         + [whole(*dim) for dim in WEIGHTS]
         + [pl.BlockSpec(memory_space=pl.ANY)] * 5,
         outs, out_shapes, scratch + [pltpu.VMEM((BLOCK, D), F32)] * 2, cost, 24,
@@ -454,76 +457,117 @@
 
 
 def finish_kernel(split_ref, back_ref, *refs):
-    refs, outs = refs[:7], refs[7:]
+    refs, (inner, edge, up, side, corner) = refs[:7], refs[7:]
     step = pl.program_id(0)
-    for (inner, edge, up, side, corner), values in zip((outs[:5], outs[5:]), finished(*refs)):
+
+    def put(ref, at, values):
+        if not isinstance(at, int):
+            at = pl.multiple_of(at, 16)
+        ref[pl.ds(at, values.shape[0]), :] = values
+
+    for n, values in enumerate(finished(*refs)):
 
         @pl.when(step < 3)
-        def _(inner=inner, values=values):
+        def _(n=n, values=values):
             first, second = grid_pieces(split_ref, values)
-            inner[pl.ds(pl.multiple_of(step * BLOCK, 16), WIN), :] = first
-            inner[pl.ds(pl.multiple_of(step * BLOCK + WIN, 16), WIN), :] = second
+            put(inner, n * INNER + step * BLOCK, first)
+            put(inner, n * INNER + step * BLOCK + WIN, second)
 
         @pl.when((step >= 3) & (step < 7))
-        def _(edge=edge, up=up, side=side, values=values):
+        def _(n=n, values=values):
             first, second = grid_pieces(split_ref, values)
-            edge[pl.ds(pl.multiple_of((step - 3) * WIN, 16), WIN), :] = first
+            put(edge, n * EDGE + (step - 3) * WIN, first)
 
             @pl.when(step == 3)
             def _():
-                side[:WIN, :] = second
+                put(side, n * SIDE, second)
 
             @pl.when(step > 3)
             def _():
-                up[pl.ds(pl.multiple_of((step - 4) * WIN, 16), WIN), :] = second
+                put(up, n * UP + (step - 4) * WIN, second)
 
         @pl.when(step == 7)
-        def _(edge=edge, up=up, side=side, corner=corner, values=values):
+        def _(n=n, values=values):
             parts = product(back_ref[...], values.astype(BF16)).astype(BF16)
-            edge[4 * WIN :, :] = parts[:SMALL]
-            side[WIN:, :] = parts[SMALL : 2 * SMALL]
-            up[3 * WIN :, :] = parts[2 * SMALL : 3 * SMALL]
-            corner[...] = parts[3 * SMALL :]
+            put(edge, n * EDGE + 4 * WIN, parts[:SMALL])
+            put(side, n * SIDE + WIN, parts[SMALL : 2 * SMALL])
+            put(up, n * UP + 3 * WIN, parts[2 * SMALL : 3 * SMALL])
+            put(corner, n * CORNER, parts[3 * SMALL :])
+
+
+PIECES = (INNER, EDGE, UP, SIDE, CORNER)
 
 
 def finish(values, weights):
-    dims = [(n, D) for n in (INNER, EDGE, UP, SIDE, CORNER)] * 2
+    dims = [(2 * n, D) for n in PIECES]
     return call(
         finish_kernel, "finish", (8,),
         [whole(WIN, WIN), whole(4 * SMALL, BLOCK)]
         + [blocks(BLOCK, n) for n in (D, D, D, 3 * D)]
         + [whole(*dim) for dim in WEIGHTS],
         [whole(*dim) for dim in dims], shapes(*dims), [],
-        (TOKENS * 2200000, TOKENS * 8000, TOKENS), 24,
+        (TOKENS * 2200000, TOKENS * 8000, TOKENS), 60,
     )(jnp.asarray(SPLIT, BF16), jnp.asarray(CORNER_BACK, BF16), *values, *weights)
 
 
-def join_kernel(inner, edge, up, side, corner, out_ref):
-    left = [corner[...].astype(F32), side[:WIN, :].astype(F32), side[WIN:, :].astype(F32)]
-    right = [up[3 * WIN :, :].astype(F32), edge[:WIN, :].astype(F32), edge[4 * WIN :, :].astype(F32)]
+def join_kernel(inner, edge, up, side, corner, *outs):
     run, stub = 48, 24
-    for i in range(LAT):
-        zone, at = (0, i) if i < 3 else (1, i - 3) if i < 9 else (2, i - 9)
-        parts = [left[zone][at * stub : at * stub + stub]]
-        for q in range(3):
-            if zone == 0:
-                start, ref = q * WIN + at * run, up
-            elif zone == 1:
-                start, ref = q * BLOCK + at * run, inner
-            else:
-                start, ref = WIN + q * WIN + at * run, edge
-            parts.append(ref[start : start + run, :].astype(F32))
-        parts.append(right[zone][at * stub : at * stub + stub])
-        out_ref[i * STRIP : i * STRIP + STRIP, :] = jnp.concatenate(parts).astype(BF16)
+
+    def load(ref, at, count):
+        return ref[at : at + count, :].astype(F32)
+
+    for zone in range(3):
+
+        @pl.when((pl.program_id(0) + 1) // 2 == zone)
+        def _(zone=zone):
+            for n, out_ref in enumerate(outs):
+                if zone == 1:
+                    half = pl.program_id(0) - 1
+                    left = load(side, n * SIDE, WIN)
+                    right = load(edge, n * EDGE, WIN)
+                    left, right = (jnp.where(half == 0, v[:HALF], v[HALF:]) for v in (left, right))
+                    full = []
+                    for q in range(3):
+                        at = pl.multiple_of(n * INNER + q * BLOCK + half * WIN, 16)
+                        full.append(inner[pl.ds(at, WIN), :].astype(F32))
+                elif zone == 0:
+                    left, right = load(corner, n * CORNER, SMALL), load(up, n * UP + 3 * WIN, SMALL)
+                    full = [load(up, n * UP + q * WIN, WIN) for q in range(3)]
+                else:
+                    left, right = load(side, n * SIDE + WIN, SMALL), load(edge, n * EDGE + 4 * WIN, SMALL)
+                    full = [load(edge, n * EDGE + WIN + q * WIN, WIN) for q in range(3)]
+                for i in range(3):
+                    parts = [left[i * stub : i * stub + stub]]
+                    parts += [part[i * run : i * run + run] for part in full]
+                    parts.append(right[i * stub : i * stub + stub])
+                    strip = jnp.concatenate(parts)
+                    out_ref[i] = strip.reshape(LON, LEV, D).astype(BF16)
 
 
 def join(parts):
-    return call(
-        join_kernel, "join", (),
-        [whole(n, D) for n in (INNER, EDGE, UP, SIDE, CORNER)],
-        whole(TOKENS, D), shapes((TOKENS, D))[0], [],
-        (1000000, 5000000, 0), 20,
+    spec = pl.BlockSpec((3, LON, LEV, D), lambda i: (i, 0, 0, 0))
+    dim = (LAT, LON, LEV, D)
+    return call(
+        join_kernel, "join", (4,),
+        [whole(2 * n, D) for n in PIECES],
+        [spec] * 2, shapes(*[dim] * 2), [],
+        (1000000, 9000000, 0), 60,
     )(*parts)
+
+
+def sum_kernel(terms_ref, qkv_ref, out_ref):
+    total = jnp.sum(terms_ref[...].astype(F32).reshape(DEVICES, 16, D), 0)
+    for c in range(3):
+        qkv_ref[:, c * D : c * D + D] = total[4 * c : 4 * c + 4]
+    out_ref[...] = total[12:]
+
+
+def sum_terms(terms):
+    return call(
+        sum_kernel, "sum_terms", (),
+        [whole(2048, D)], [whole(4, 3 * D), whole(4, D)],
+        shapes((4, 3 * D), (4, D), dtype=F32), [], (2000000, 2200000, 0), 20,
+    )(terms)
 
 
 def shift_pairs(lat_step, lon_step):
@@ -560,18 +604,15 @@
     last = (lax.axis_index("lat") == BANDS - 1) & (jnp.arange(2) == 1)
     group = jnp.arange(WIN) >= HALF
     apart = last[:, None, None] & (group[:, None] != group[None, :])
-    bias = jnp.where(apart, -jnp.inf, 0.0).astype(F32)
+    bias = jnp.tile(jnp.where(apart, -jnp.inf, 0.0).astype(F32), (1, 1, 4))
     first = attend_inner(x_inner, c_inner, weights)
     x, cot, hidden, att, dp = attend_edge(x_parts, c_parts, bias, weights, first)
     terms = swap_blocks(weight_terms(hidden, att, cot, dp), BOTH)
 
-    done = finish((x, cot, att, dp), weights)
-    outs = []
-    for at in (0, 5):
-        returned = exchange(done[at + 2 : at + 5], 1)
-        outs.append(join(list(done[at : at + 2]) + returned).reshape(LAT, LON, LEV, D))
-    total = jnp.sum(terms.reshape(DEVICES, 4, 4, D).astype(F32), 0).transpose(1, 0, 2).reshape(4, 4 * D)
-    return (outs[0], outs[1], total[:, : 3 * D], total[:, 3 * D :])
+    inner, edge, *away = finish((x, cot, att, dp), weights)
+    outs = join([inner, edge] + exchange(away, 1))
+    outs = [out.reshape(LAT, LON, LEV, D) for out in outs]
+    return (*outs, *sum_terms(terms))
 
 
 def solution(mesh):

time: 224 us -> 223 us (level)
  waiting for transfers between devices: 48.2 us -> 55.5 us
  starting transfers between devices: 32.2 us -> 28.1 us
  other arithmetic: 2.9 us -> 0.24 us
    ppermute x12 -> x9, waiting for transfers between devices: 19.6 us -> 27.6 us  [exchange(): lax.ppermute(part, BOTH, shift_pairs(*step))]
    pallas_call x1, Pallas kernels: 24.9 us -> 19.2 us  [attend_edge(): call(edge_kernel, 'attend_edge', (5,), parts * 2 + [whole(BLOCK, 4 * SMAL...]
    pallas_call x2, Pallas kernels: 1.35 us -> 6.66 us  [the longest x1 5.72 us: join(): call(join_kernel, 'join', (4,), [whole(2 * n, D) for n in PIECES], [spec]...]
    reshape x2 -> x0, local copies, waits for them, and re-layouts: 4.24 us -> none  [per_device(): join(list(done[at:at + 2]) + returned).reshape(LAT, LON, LEV, D)]
    pallas_call x1, Pallas kernels: 13.2 us -> 16.8 us  [finish(): call(finish_kernel, 'finish', (8,), [whole(WIN, WIN), whole(4 * SMALL, BL...]
    ppermute x12 -> x9, starting transfers between devices: 21.8 us -> 18.2 us  [exchange(): lax.ppermute(part, BOTH, shift_pairs(*step))]
    another operation x0 -> x2, local copies, waits for them, and re-layouts: none -> 3.22 us  [per_device(): bias = jnp.tile(jnp.where(apart, -jnp.inf, 0.0).astype(F32), (1, 1, 4))]
    pallas_call x1, Pallas kernels: 13.3 us -> 10.4 us  [attend_inner(): call(inner_kernel, 'attend_inner', (3,), [blocks(BLOCK, D)] * 2 + [whole(...]
  transfers between devices with their start and end apart: 14 -> 11, of which waited for: 4 -> 3; matrix products, arithmetic and copies ran while one was open for 10% -> 10% of each run, Pallas kernels for 17% -> 20%
where the time goes in v3:
time: 223 us
  Pallas kernels  82.8 us (37%)
  waiting for transfers between devices  55.5 us (25%)
  local copies, waits for them, and re-layouts  38.7 us (17%)
  starting transfers between devices  28.1 us (13%)
  blocking collectives  16.4 us (7%)
    all_to_all x2, waiting for transfers between devices, swap_blocks(): return lax.all_to_all(values, axis, split_axis=0, concat_axis=0, tiled=True)  27.9 us
    ppermute x9, waiting for transfers between devices, exchange(): lax.ppermute(part, BOTH, shift_pairs(*step))  27.6 us
    pallas_call x1, Pallas kernels, attend_edge(): call(edge_kernel, 'attend_edge', (5,), parts * 2 + [whole(BLOCK, 4 * SMAL...  19.2 us
    ppermute x9, starting transfers between devices, exchange(): lax.ppermute(part, BOTH, shift_pairs(*step))  18.2 us
    pallas_call x1, Pallas kernels, finish(): call(finish_kernel, 'finish', (8,), [whole(WIN, WIN), whole(4 * SMALL, BL...  16.8 us
    all_to_all x1, blocking collectives, swap_blocks(): return lax.all_to_all(values, axis, split_axis=0, concat_axis=0, tiled=True)  16.4 us
    unnamed x50, local copies, waits for them, and re-layouts  15.4 us
    gather x1, local copies, waits for them, and re-layouts, per_device(): place = place.reshape(TOKENS)[ORDER].reshape(-1, 1)  12.7 us
  transfers between devices with their start and end apart: 11, of which 3 were waited for; matrix products, arithmetic and copies ran while one was open for 10% of the time, Pallas kernels for 20%

profile of v3, /device:TPU:1, one launch (start us, length us, event | category | flops | bytes accessed | tf_op | source)
XLA Modules:
  0.0 222.5 jit_solution(7505395300420632286)
XLA Ops:
  0.6 2.6 %requests.1 = (s32[16,288]{1,0:T(8,128)}, s32[1,2304]{1,0:T(1,128)}, s32[16,8]{1,0:T(8,128)}) custom-call(s32[1,2304]{1,0:T(1,128)} %bitcast.19, s32[1,2304]{1,0:T(1,128)} %bitcast.20), custom_call_target="tpu_custom_call" | custom-call | flops 100000000 | bytes 100000 | tf_op jit(solution)/shard_map/requests/pallas_call | solution.py:158
  4.0 16.4 %all_to_all.28 = s32[16,1,288]{2,1,0:T(1,128)S(1)} all-to-all(s32[16,1,288]{2,1,0:T(1,128)S(1)} %copy.26), channel_id=1, replica_groups=mesh['lat'=16,'lon'=8] {'lat'}, dimensions={0} | all-to-all | bytes 36864 | tf_op jit(solution)/shard_map/all_to_all | solution.py:587
  21.2 10.9 %serve.1 = bf16[4608,512]{1,0:T(8,128)(2,1)} custom-call(s32[288,16]{1,0:T(8,128)} %bitcast.17, bf16[1152,512]{1,0:T(8,128)(2,1)} %buffer_ref.1), custom_call_target="tpu_custom_call" | custom-call | flops 5400000000 | bytes 6000000 | tf_op jit(solution)/shard_map/serve/pallas_call | solution.py:183
  32.1 4.7 %all-to-all-start.1 = ((bf16[16,288,512]{2,1,0:T(8,128)(2,1)}), bf16[16,288,512]{2,1,0:T(8,128)(2,1)}, u32[]{:S(2)}, u32[]{:S(2)}) async-start(bf16[16,288,512]{2,1,0:T(8,128)(2,1)} %bitcast.16), calls=%async_computation.1 | async-start | bytes 9437184 | tf_op jit(solution)/shard_map/all_to_all | solution.py:587
  36.8 3.9 %reshape.87.grid_ref = bf16[2304,512]{1,0:T(8,128)(2,1)S(1)} reshape(bf16[12,48,4,512]{3,2,1,0:T(4,128)(2,1)} %param.20) | data formatting | bytes 4718592 | tf_op jit(solution)/shard_map/reshape | solution.py:597
  43.1 2.9 %collective-permute-start.5 = (bf16[80,512]{1,0:T(8,128)(2,1)S(1)}, bf16[80,512]{1,0:T(8,128)(2,1)S(1)}, u32[]{:S(2)}, u32[]{:S(2)}) collective-permute-start(bf16[80,512]{1,0:T(8,128)(2,1)S(1)} %get-tuple-element.46), channel_id=1, source_target_pairs={{0,127},{1,120},{2,121},{3,122},{4,123},{5,124},{6,125},{7,126},{8... | collective-permute-start | bytes 245768 | tf_op jit(solution)/shard_map/ppermute | solution.py:583
  47.2 3.8 %collective-permute-start.3 = (bf16[512,512]{1,0:T(8,128)(2,1)}, bf16[512,512]{1,0:T(8,128)(2,1)}, u32[]{:S(2)}, u32[]{:S(2)}) collective-permute-start(bf16[512,512]{1,0:T(8,128)(2,1)} %get-tuple-element.44), channel_id=1, source_target_pairs={{0,120},{1,121},{2,122},{3,123},{4,124},{5,125},{6,126},{7,127},{8... | collective-permute-start | bytes 1572872 | tf_op jit(solution)/shard_map/ppermute | solution.py:583
  51.1 12.7 %gather_fusion = s32[2336]{0:T(1024)S(1)} fusion(s32[2304]{0:T(1024)S(1)} %reduce, s32[3072]{0:T(1024)S(1)} %pad_clamp_fusion), kind=kCustom, calls=%fused_computation | custom fusion | bytes 28032 | tf_op jit(solution)/shard_map/gather | solution.py:599
  63.8 1.9 reshape.97.place_ref
  65.8 27.9 %all-to-all-done.1 = bf16[16,288,512]{2,1,0:T(8,128)(2,1)} async-done(((bf16[16,288,512]{2,1,0:T(8,128)(2,1)}), bf16[16,288,512]{2,1,0:T(8,128)(2,1)}, u32[]{:S(2)}, u32[]{:S(2)}) %all-to-all-start.1) | async-done | bytes 4718624 | tf_op jit(solution)/shard_map/all_to_all | solution.py:587
  93.7 9.6 %pick.1 = (bf16[512,512]{1,0:T(8,128)(2,1)}, bf16[224,512]{1,0:T(8,128)(2,1)}, bf16[80,512]{1,0:T(8,128)(2,1)}, bf16[864,512]{1,0:T(8,128)(2,1)}, bf16[656,512]{1,0:T(8,128)(2,1)}) custom-call(s32[16,8]{1,0:T(8,128)} %get-tuple-element.36.table_ref, s32[2336,1]{1,0:T(8,128)} %reshape.97.place_ref, bf16[4608,512]{1,0:T(8,128)(2,1)} %bitcast.6.replies_ref), custom_call_target="tpu_custom_call" | custom-call | flops 3600000000 | bytes 8000000 | tf_op jit(solution)/shard_map/pick/pallas_call | solution.py:232
  106.0 2.0 tile.10.bias_ref
  108.0 3.2 %collective-permute-start.2 = (bf16[80,512]{1,0:T(8,128)(2,1)S(1)}, bf16[80,512]{1,0:T(8,128)(2,1)S(1)}, u32[]{:S(2)}, u32[]{:S(2)}) collective-permute-start(bf16[80,512]{1,0:T(8,128)(2,1)S(1)} %copy-done.24), channel_id=1, source_target_pairs={{0,127},{1,120},{2,121},{3,122},{4,123},{5,124},{6,125},{7,126},{8... | collective-permute-start | bytes 245768 | tf_op jit(solution)/shard_map/ppermute | solution.py:583
  114.4 10.4 %attend_inner.1 = (bf16[2304,512]{1,0:T(8,128)(2,1)S(1)}, bf16[2304,512]{1,0:T(8,128)(2,1)S(1)}, bf16[2304,512]{1,0:T(8,128)(2,1)S(1)}, bf16[2304,512]{1,0:T(8,128)(2,1)S(1)}, bf16[2304,1536]{1,0:T(8,128)(2,1)S(1)}) custom-call(bf16[864,512]{1,0:T(8,128)(2,1)S(1)} %copy-done.17, bf16[864,512]{1,0:T(8,128)(2,1)S(1)} %get-tuple-element.48.c_ref, ...), custom_call_target="tpu_custom_call" | custom-call | flops 5184000000 | bytes 8640000 | tf_op jit(solution)/shard_map/attend_inner/pallas_call | solution.py:390
  124.9 19.2 %attend_edge.1 = (bf16[2304,512]{1,0:T(8,128)(2,1)S(1)}, bf16[2304,512]{1,0:T(8,128)(2,1)S(1)}, bf16[2304,512]{1,0:T(8,128)(2,1)S(1)}, bf16[2304,512]{1,0:T(8,128)(2,1)S(1)}, bf16[2304,1536]{1,0:T(8,128)(2,1)S(1)}) custom-call(bf16[656,512]{1,0:T(8,128)(2,1)S(1)} %copy-done.18, ...), custom_call_target="tpu_custom_call", output_to_operand_aliasing={{0}: (13, {}), {1}: (14, {}), {2}: (15, {}), {3}: (16, {}),... | custom-call | flops 8640000000 | bytes 14400000 | tf_op jit(solution)/shard_map/attend_edge/pallas_call | solution.py:400
  148.3 3.4 %copy-done.13 = bf16[2304,512]{1,0:T(8,128)(2,1)S(1)} copy-done((bf16[2304,512]{1,0:T(8,128)(2,1)S(1)}, bf16[2304,512]{1,0:T(8,128)(2,1)}, u32[]{:S(2)}) %copy-start.13) | copy-done | bytes 2359320
  151.7 2.2 copy-done.15
  153.9 5.1 %weight_terms.1 = bf16[2048,512]{1,0:T(8,128)(2,1)S(1)} custom-call(bf16[2304,512]{1,0:T(8,128)(2,1)S(1)} %copy-done.13, bf16[2304,512]{1,0:T(8,128)(2,1)S(1)} %copy-done.15, bf16[2304,512]{1,0:T(8,128)(2,1)S(1)} %get-tuple-element.55.refs_1_.c_ref, bf16[2304,1536]{1,0:T(8,128)(2,1)S(1)} %get-tuple-element.57.refs_3_.dp_ref), custom_call_target="tpu_custom_call" | custom-call | flops 4831838208 | bytes 18000000 | tf_op jit(solution)/shard_map/weight_terms/pallas_call | solution.py:430
  160.4 5.2 %all-to-all-start.2 = ((bf16[128,16,512]{2,1,0:T(8,128)(2,1)}), bf16[128,16,512]{2,1,0:T(8,128)(2,1)S(1)}, u32[]{:S(2)}, u32[]{:S(2)}) async-start(bf16[128,16,512]{2,1,0:T(8,128)(2,1)} %bitcast.12), calls=%async_computation.2 | async-start | bytes 4194304 | tf_op jit(solution)/shard_map/all_to_all | solution.py:587
  165.6 16.8 %finish.1 = (bf16[1728,512]{1,0:T(8,128)(2,1)}, bf16[1312,512]{1,0:T(8,128)(2,1)}, bf16[1024,512]{1,0:T(8,128)(2,1)}, bf16[448,512]{1,0:T(8,128)(2,1)}, bf16[160,512]{1,0:T(8,128)(2,1)}) custom-call(bf16[144,144]{1,0:T(8,128)(2,1)} %constant.30.clone.split_ref, bf16[320,288]{1,0:T(8,128)(2,1)} %constant.35.clone.back_ref, bf16[2304,512]{1,0:T(8,128)(2,1)} %copy-done.16, ...), custom_call_target="tpu_custom_call" | custom-call | flops 5068800000 | bytes 18432000 | tf_op jit(solution)/shard_map/finish/pallas_call | solution.py:503
  182.4 3.1 %collective-permute-start.6 = (bf16[1024,512]{1,0:T(8,128)(2,1)}, bf16[1024,512]{1,0:T(8,128)(2,1)S(1)}, u32[]{:S(2)}, u32[]{:S(2)}) collective-permute-start(bf16[1024,512]{1,0:T(8,128)(2,1)} %get-tuple-element.60), channel_id=1, source_target_pairs={{0,8},{1,9},{2,10},{3,11},{4,12},{5,13},{6,14},{7,15},{8,16},{9,17... | collective-permute-start | bytes 3145736 | tf_op jit(solution)/shard_map/ppermute | solution.py:583
  187.2 18.9 %collective-permute-done.8.corner = bf16[160,512]{1,0:T(8,128)(2,1)S(1)} collective-permute-done((bf16[160,512]{1,0:T(8,128)(2,1)}, bf16[160,512]{1,0:T(8,128)(2,1)S(1)}, u32[]{:S(2)}, u32[]{:S(2)}) %collective-permute-start.8) | collective-permute-done | bytes 163872 | tf_op jit(solution)/shard_map/ppermute | solution.py:583
  206.0 8.7 %collective-permute-done.7.side = bf16[448,512]{1,0:T(8,128)(2,1)S(1)} collective-permute-done((bf16[448,512]{1,0:T(8,128)(2,1)}, bf16[448,512]{1,0:T(8,128)(2,1)S(1)}, u32[]{:S(2)}, u32[]{:S(2)}) %collective-permute-start.7) | collective-permute-done | bytes 458784 | tf_op jit(solution)/shard_map/ppermute | solution.py:583
  215.9 5.7 %join.1 = (bf16[12,48,4,512]{3,2,1,0:T(4,128)(2,1)}, bf16[12,48,4,512]{3,2,1,0:T(4,128)(2,1)}) custom-call(bf16[1728,512]{1,0:T(8,128)(2,1)} %get-tuple-element.58.inner, bf16[1312,512]{1,0:T(8,128)(2,1)} %get-tuple-element.59.edge, bf16[1024,512]{1,0:T(8,128)(2,1)} %copy-done.19, bf16[448,512]{1,0:T(8,128)(2,1)} %copy-done.20, bf16[160,512]{1,0:T(8,128)(2,1)} %copy-done.21), custom_call_target="tpu_custom_call" | custom-call | flops 1000000 | bytes 9000000 | tf_op jit(solution)/shard_map/join/pallas_call | solution.py:550
  (72 shorter events, 20.4 us)
Async XLA Ops:
  32.1 61.6 %all-to-all-start.1 = ((bf16[16,288,512]{2,1,0:T(8,128)(2,1)}), bf16[16,288,512]{2,1,0:T(8,128)(2,1)}, u32[]{:S(2)}, u32[]{:S(2)}) async-start(bf16[16,288,512]{2,1,0:T(8,128)(2,1)} %bitcast.16), calls=%async_computation.1 | async-start | bytes 9437184 | tf_op jit(solution)/shard_map/all_to_all | solution.py:587
  36.8 3.9 %copy-start.2 = (bf16[80,72]{1,0:T(8,128)(2,1)S(1)}, bf16[80,72]{1,0:T(8,128)(2,1)}, u32[]{:S(2)}) copy-start(bf16[80,72]{1,0:T(8,128)(2,1)} %constant.31.clone.small_ref) | copy-start | bytes 34564
  40.8 10.3 %copy-start.23 = (s32[1,2304]{1,0:T(1,128)S(1)}, s32[1,2304]{1,0:T(1,128)}, u32[]{:S(2)}) copy-start(s32[1,2304]{1,0:T(1,128)} %get-tuple-element.37) | copy-start | bytes 27652
  40.8 10.3 %copy-start.22 = (s32[2336]{0:T(1024)S(1)}, s32[2336]{0:T(1024)}, u32[]{:S(2)}) copy-start(s32[2336]{0:T(1024)} %constant.40) | copy-start | bytes 28036
  43.1 68.0 %collective-permute-start.5 = (bf16[80,512]{1,0:T(8,128)(2,1)S(1)}, bf16[80,512]{1,0:T(8,128)(2,1)S(1)}, u32[]{:S(2)}, u32[]{:S(2)}) collective-permute-start(bf16[80,512]{1,0:T(8,128)(2,1)S(1)} %get-tuple-element.46), channel_id=1, source_target_pairs={{0,127},{1,120},{2,121},{3,122},{4,123},{5,124},{6,125},{7,126},{8... | collective-permute-start | bytes 245768 | tf_op jit(solution)/shard_map/ppermute | solution.py:583
  46.1 78.7 %collective-permute-start.4 = (bf16[224,512]{1,0:T(8,128)(2,1)}, bf16[224,512]{1,0:T(8,128)(2,1)}, u32[]{:S(2)}, u32[]{:S(2)}) collective-permute-start(bf16[224,512]{1,0:T(8,128)(2,1)} %get-tuple-element.45), channel_id=1, source_target_pairs={{0,7},{1,0},{2,1},{3,2},{4,3},{5,4},{6,5},{7,6},{8,15},{9,8},{10,9... | collective-permute-start | bytes 688136 | tf_op jit(solution)/shard_map/ppermute | solution.py:583
  47.2 77.6 %collective-permute-start.3 = (bf16[512,512]{1,0:T(8,128)(2,1)}, bf16[512,512]{1,0:T(8,128)(2,1)}, u32[]{:S(2)}, u32[]{:S(2)}) collective-permute-start(bf16[512,512]{1,0:T(8,128)(2,1)} %get-tuple-element.44), channel_id=1, source_target_pairs={{0,120},{1,121},{2,122},{3,123},{4,124},{5,125},{6,126},{7,127},{8... | collective-permute-start | bytes 1572872 | tf_op jit(solution)/shard_map/ppermute | solution.py:583
  103.3 4.7 %copy-start.24 = (bf16[80,512]{1,0:T(8,128)(2,1)S(1)}, bf16[80,512]{1,0:T(8,128)(2,1)}, u32[]{:S(2)}) copy-start(bf16[80,512]{1,0:T(8,128)(2,1)} %get-tuple-element.42) | copy-start | bytes 245764
  103.3 8.9 %copy-start.3 = (bf16[512,1536]{1,0:T(8,128)(2,1)S(1)}, bf16[512,1536]{1,0:T(8,128)(2,1)}, u32[]{:S(2)}) copy-start(bf16[512,1536]{1,0:T(8,128)(2,1)} %refs_4_.1) | copy-start | bytes 4718596
  103.3 8.9 %copy-start.8 = (f32[512]{0:T(512)S(1)}, f32[512]{0:T(512)}, u32[]{:S(2)}) copy-start(f32[512]{0:T(512)} %param.17) | copy-start | bytes 6148
  103.3 21.6 %collective-permute-start = (bf16[512,512]{1,0:T(8,128)(2,1)}, bf16[512,512]{1,0:T(8,128)(2,1)}, u32[]{:S(2)}, u32[]{:S(2)}) collective-permute-start(bf16[512,512]{1,0:T(8,128)(2,1)} %get-tuple-element.40), channel_id=1, source_target_pairs={{0,120},{1,121},{2,122},{3,123},{4,124},{5,125},{6,126},{7,127},{8... | collective-permute-start | bytes 1572872 | tf_op jit(solution)/shard_map/ppermute | solution.py:583
  108.0 16.8 %collective-permute-start.2 = (bf16[80,512]{1,0:T(8,128)(2,1)S(1)}, bf16[80,512]{1,0:T(8,128)(2,1)S(1)}, u32[]{:S(2)}, u32[]{:S(2)}) collective-permute-start(bf16[80,512]{1,0:T(8,128)(2,1)S(1)} %copy-done.24), channel_id=1, source_target_pairs={{0,127},{1,120},{2,121},{3,122},{4,123},{5,124},{6,125},{7,126},{8... | collective-permute-start | bytes 245768 | tf_op jit(solution)/shard_map/ppermute | solution.py:583
  111.2 13.7 %collective-permute-start.1 = (bf16[224,512]{1,0:T(8,128)(2,1)}, bf16[224,512]{1,0:T(8,128)(2,1)S(1)}, u32[]{:S(2)}, u32[]{:S(2)}) collective-permute-start(bf16[224,512]{1,0:T(8,128)(2,1)} %get-tuple-element.41), channel_id=1, source_target_pairs={{0,7},{1,0},{2,1},{3,2},{4,3},{5,4},{6,5},{7,6},{8,15},{9,8},{10,9... | collective-permute-start | bytes 688136 | tf_op jit(solution)/shard_map/ppermute | solution.py:583
  114.4 10.4 %copy-start.5 = (bf16[656,512]{1,0:T(8,128)(2,1)S(1)}, bf16[656,512]{1,0:T(8,128)(2,1)}, u32[]{:S(2)}) copy-start(bf16[656,512]{1,0:T(8,128)(2,1)} %copy-done.4) | copy-start | bytes 2015236
  114.4 10.4 %copy-start.7 = (bf16[512,512]{1,0:T(8,128)(2,1)S(1)}, bf16[512,512]{1,0:T(8,128)(2,1)}, u32[]{:S(2)}) copy-start(bf16[512,512]{1,0:T(8,128)(2,1)} %refs_6_.1) | copy-start | bytes 1572868
  114.4 10.4 %copy-start.9 = (bf16[288,320]{1,0:T(8,128)(2,1)S(1)}, bf16[288,320]{1,0:T(8,128)(2,1)}, u32[]{:S(2)}) copy-start(bf16[288,320]{1,0:T(8,128)(2,1)} %constant.34.clone.join_ref) | copy-start | bytes 552964
  114.4 10.5 %copy-start.18 = (bf16[656,512]{1,0:T(8,128)(2,1)S(1)}, bf16[656,512]{1,0:T(8,128)(2,1)}, u32[]{:S(2)}) copy-start(bf16[656,512]{1,0:T(8,128)(2,1)} %get-tuple-element.39.xe) | copy-start | bytes 2015236
  148.3 10.8 %copy-start.10 = (bf16[2304,1536]{1,0:T(8,128)(2,1)}, bf16[2304,1536]{1,0:T(8,128)(2,1)S(1)}, u32[]{:S(2)}) copy-start(bf16[2304,1536]{1,0:T(8,128)(2,1)S(1)} %get-tuple-element.57.refs_3_.dp_ref) | copy-start | bytes 21233668
  148.3 10.8 %copy-start.11 = (bf16[2304,512]{1,0:T(8,128)(2,1)}, bf16[2304,512]{1,0:T(8,128)(2,1)S(1)}, u32[]{:S(2)}) copy-start(bf16[2304,512]{1,0:T(8,128)(2,1)S(1)} %get-tuple-element.55.refs_1_.c_ref) | copy-start | bytes 7077892
  160.4 61.2 %all-to-all-start.2 = ((bf16[128,16,512]{2,1,0:T(8,128)(2,1)}), bf16[128,16,512]{2,1,0:T(8,128)(2,1)S(1)}, u32[]{:S(2)}, u32[]{:S(2)}) async-start(bf16[128,16,512]{2,1,0:T(8,128)(2,1)} %bitcast.12), calls=%async_computation.2 | async-start | bytes 4194304 | tf_op jit(solution)/shard_map/all_to_all | solution.py:587
  182.4 32.3 %collective-permute-start.6 = (bf16[1024,512]{1,0:T(8,128)(2,1)}, bf16[1024,512]{1,0:T(8,128)(2,1)S(1)}, u32[]{:S(2)}, u32[]{:S(2)}) collective-permute-start(bf16[1024,512]{1,0:T(8,128)(2,1)} %get-tuple-element.60), channel_id=1, source_target_pairs={{0,8},{1,9},{2,10},{3,11},{4,12},{5,13},{6,14},{7,15},{8,16},{9,17... | collective-permute-start | bytes 3145736 | tf_op jit(solution)/shard_map/ppermute | solution.py:583
  185.5 29.2 %collective-permute-start.7 = (bf16[448,512]{1,0:T(8,128)(2,1)}, bf16[448,512]{1,0:T(8,128)(2,1)S(1)}, u32[]{:S(2)}, u32[]{:S(2)}) collective-permute-start(bf16[448,512]{1,0:T(8,128)(2,1)} %get-tuple-element.61), channel_id=1, source_target_pairs={{0,1},{1,2},{2,3},{3,4},{4,5},{5,6},{6,7},{7,0},{8,9},{9,10},{10,1... | collective-permute-start | bytes 1376264 | tf_op jit(solution)/shard_map/ppermute | solution.py:583
  185.8 20.2 %collective-permute-start.8 = (bf16[160,512]{1,0:T(8,128)(2,1)}, bf16[160,512]{1,0:T(8,128)(2,1)S(1)}, u32[]{:S(2)}, u32[]{:S(2)}) collective-permute-start(bf16[160,512]{1,0:T(8,128)(2,1)} %get-tuple-element.62), channel_id=1, source_target_pairs={{0,9},{1,10},{2,11},{3,12},{4,13},{5,14},{6,15},{7,8},{8,17},{9,18... | collective-permute-start | bytes 491528 | tf_op jit(solution)/shard_map/ppermute | solution.py:583
  206.0 8.7 %copy-start.21 = (bf16[160,512]{1,0:T(8,128)(2,1)}, bf16[160,512]{1,0:T(8,128)(2,1)S(1)}, u32[]{:S(2)}) copy-start(bf16[160,512]{1,0:T(8,128)(2,1)S(1)} %collective-permute-done.8.corner) | copy-start | bytes 491524
  (12 other events, 20.1 us)

commit v4 on v3

--- a/solution.py
+++ b/solution.py
@@ -28,6 +28,7 @@
 QUAD = 256
 SCALE = 0.125
 LOG2E = 1.4426950408889634
+FAR = -1e30
 BOTH = ("lat", "lon")
 
 UP, SIDE, CORNER = 3 * WIN + SMALL, WIN + SMALL, SMALL
@@ -291,19 +292,29 @@
 PLACES = UP + SIDE + CORNER + INNER + EDGE
 
 
+EDGE_BLOCKS = (
+    (WIN, lambda i: i),
+    (WIN, lambda i: jnp.maximum(i - 1, 0)),
+    (WIN, lambda i: i // 4),
+    (SMALL, lambda i: 0),
+)
+EDGE_SPECS = [pl.BlockSpec((n, D), lambda i, at=at: (at(i), 0)) for n, at in EDGE_BLOCKS]
+EDGE_PAIRS = [pl.BlockSpec((2, n, D), lambda i, at=at: (0, at(i), 0)) for n, at in EDGE_BLOCKS]
+
+
 def join_halves(first, second):
     first, second = first.astype(F32), second.astype(F32)
     return jnp.concatenate([first[:HALF], second[:HALF], first[HALF:], second[HALF:]])
 
 
-def attend(x_all, c_all, bias, w_ref, gain_ref, ow_ref, x_out, c_out, h_ref, att_ref, dp_ref, packed, slopes):
+def attend(x_all, c_all, bias, w_ref, gain_ref, ow_ref, x_out, ha_ref, dp_ref, packed, slopes):
     x_out[...] = x_all.astype(BF16)
     cot = c_all.astype(BF16)
-    c_out[...] = cot
+    dp_ref[:, 3 * D :] = cot
     slopes[...] = product(cot, ow_ref[...], NT).astype(BF16)
     normed, _ = normalise(x_all)
     hidden = (normed * gain_ref[...]).astype(BF16)
-    h_ref[...] = hidden
+    ha_ref[:, :D] = hidden
     for part in range(3):
         cols = slice(part * D, part * D + D)
         packed[:, cols] = product(hidden, w_ref[:, cols]).astype(BF16)
@@ -326,14 +337,14 @@
             queries, grads = spread(queries), spread(slopes[rows, spot[0]])
             scores = product(keys, queries, NT) * (SCALE * LOG2E)
             if bias is not None:
-                scores = scores + bias[...]
+                scores = scores + bias()
             grown = jnp.exp2(scores - jnp.max(scores, 0, keepdims=True))
             probs = grown * (1.0 / jnp.sum(grown, 0, keepdims=True))
             low = probs.astype(BF16)
             weighted = probs * product(values, grads, NT)
             slope = weighted - probs * jnp.sum(weighted, 0, keepdims=True)
             slope = (slope * SCALE).astype(BF16)
-            att_ref[rows, spot[0]] = gather(low, values).astype(BF16)
+            ha_ref[rows, slice(D + quad * QUAD, D + quad * QUAD + QUAD)] = gather(low, values).astype(BF16)
             dp_ref[rows, spot[0]] = gather(slope, keys).astype(BF16)
             dp_ref[rows, spot[1]] = product(slope, queries).astype(BF16)
             dp_ref[rows, spot[2]] = product(low, grads).astype(BF16)
@@ -345,36 +356,33 @@
     attend(x_all, c_all, None, *refs)
 
 
-def edge_kernel(xe, xu, xs, xc, ce, cu, cs, cc, join_ref, bias_ref, *refs):
-    weights, (*refs, x_all, c_all) = refs[:3], refs[8:]
+def edge_kernel(flag_ref, xe, xu, xs, xc, ce, cu, cs, cc, join_ref, apart_ref, *refs):
+    weights, (*refs, x_all, c_all) = refs[:3], refs[6:]
     step = pl.program_id(0)
 
     @pl.when(step == 0)
     def _():
-        x_all[...] = join_halves(xe[:WIN, :], xs[:WIN, :])
-        c_all[...] = join_halves(ce[:WIN, :], cs[:WIN, :])
-
-    for q in range(3):
-
-        @pl.when(step == q + 1)
-        def _(q=q):
-            near, far = slice(WIN + q * WIN, 2 * WIN + q * WIN), slice(q * WIN, q * WIN + WIN)
-            x_all[...] = join_halves(xe[near, :], xu[far, :])
-            c_all[...] = join_halves(ce[near, :], cu[far, :])
+        x_all[...] = join_halves(xe[...], xs[...])
+        c_all[...] = join_halves(ce[...], cs[...])
+
+    @pl.when((step > 0) & (step < 4))
+    def _():
+        x_all[...] = join_halves(xe[...], xu[...])
+        c_all[...] = join_halves(ce[...], cu[...])
 
     @pl.when(step == 4)
     def _():
-        near, far, along = slice(4 * WIN, EDGE), slice(3 * WIN, UP), slice(WIN, SIDE)
-        parts = [xe[near, :], xs[along, :], xu[far, :], xc[...]]
+        parts = [xe[:SMALL, :], xs[:SMALL, :], xu[:SMALL, :], xc[...]]
         x_all[...] = product(join_ref[...], jnp.concatenate(parts))
-        parts = [ce[near, :], cs[along, :], cu[far, :], cc[...]]
+        parts = [ce[:SMALL, :], cs[:SMALL, :], cu[:SMALL, :], cc[...]]
         c_all[...] = product(join_ref[...], jnp.concatenate(parts))
 
-    attend(x_all[...], c_all[...], bias_ref, *weights, *refs)
+    seam = jnp.where(step > 0, flag_ref[0], 0).astype(F32)
+    attend(x_all[...], c_all[...], lambda: apart_ref[...] * seam, *weights, *refs)
 
 
 def attend_specs(rows, skip):
-    widths = (D, D, D, D, 3 * D)
+    widths = (D, 2 * D, 4 * D)
     outs = [pl.BlockSpec((BLOCK, n), lambda i: (i + skip, 0)) for n in widths]
     out_shapes = shapes(*[(TOKENS, n) for n in widths])
     scratch = [pltpu.VMEM((BLOCK, 3 * D), BF16), pltpu.VMEM((BLOCK, D), BF16)]
@@ -390,63 +398,87 @@
     return call(
         inner_kernel, "attend_inner", (3,),
         [blocks(BLOCK, D)] * 2 + [whole(*dim) for dim in WEIGHTS],
-        outs, out_shapes, scratch, cost, 18,
+        outs, out_shapes, scratch, cost, 60,
     )(x, cot, *weights)
 
 
-def attend_edge(x_parts, c_parts, bias, weights, carried):
+def apart_matrix():
+    late = np.arange(WIN) >= HALF
+    return np.tile(np.where(late[:, None] != late[None, :], FAR, 0.0).astype(np.float32), (1, 4))
+
+
+def attend_edge(x_parts, c_parts, flag, weights, carried):
     outs, out_shapes, scratch, cost = attend_specs(5 * BLOCK, 3)
-    parts = [whole(n, D) for n in (EDGE, UP, SIDE, CORNER)]
     return call(
         edge_kernel, "attend_edge", (5,),
-        parts * 2
-        + [whole(BLOCK, 4 * SMALL), pl.BlockSpec((None, WIN, 4 * WIN), lambda i: (jnp.minimum(i, 1), 0, 0))]
+        [pl.BlockSpec(memory_space=pltpu.SMEM)]
+        + EDGE_SPECS * 2
+        + [whole(BLOCK, 4 * SMALL), whole(WIN, 4 * WIN)]
         + [whole(*dim) for dim in WEIGHTS]
-        + [pl.BlockSpec(memory_space=pl.ANY)] * 5,
-        outs, out_shapes, scratch + [pltpu.VMEM((BLOCK, D), F32)] * 2, cost, 24,
-        aliases={13 + n: n for n in range(5)},
-    )(*x_parts, *c_parts, jnp.asarray(CORNER_JOIN, BF16), bias, *weights, *carried)
-
-
-def weight_kernel(h_ref, att_ref, c_ref, dp_ref, out_ref, turned):
-    def chunk(c):
-        if c < 3:
-            return product(h_ref[...], dp_ref[:, c * D : c * D + D], TN)
-        return product(att_ref[...], c_ref[...], TN)
-
-    upper = lax.broadcasted_iota(I32, (64, 8, D), 1) < 4
-    for pair in range(2):
-        first = chunk(2 * pair).reshape(64, 8, D)
-        second = chunk(2 * pair + 1).reshape(64, 8, D)
-        swap = lambda v: jnp.concatenate([v[:, 4:], v[:, :4]], 1)
-        even = jnp.where(upper, first, swap(second))
-        odd = jnp.where(upper, swap(first), second)
-        turned[:, 0, pair] = even
-        turned[:, 1, pair] = odd
-    out_ref[...] = turned[...].reshape(2048, D).astype(BF16)
-
-
-def weight_terms(hidden, att, cot, dp):
-    return call(
-        weight_kernel, "weight_terms", (),
-        [whole(TOKENS, n) for n in (D, D, D, 3 * D)],
-        whole(2048, D), shapes((2048, D))[0],
+        + [pl.BlockSpec(memory_space=pl.ANY)] * 3,
+        outs, out_shapes, scratch + [pltpu.VMEM((BLOCK, D), F32)] * 2, cost, 60,
+        aliases={14 + n: n for n in range(3)},
+    )(flag, *x_parts, *c_parts, jnp.asarray(CORNER_JOIN, BF16), jnp.asarray(apart_matrix()), *weights, *carried)
+
+
+def weight_kernel(core_ref, left_ref, right_ref, own_ref, away_ref, turned):
+    step = pl.program_id(0)
+    chunk = product(left_ref[...], right_ref[...], TN).reshape(64, 8, D)
+    for c in range(4):
+
+        @pl.when(step == c)
+        def _(c=c):
+            half = c % 2 * 4
+            turned[:, 0, c // 2, half : half + 4] = chunk[:, :4]
+            turned[:, 1, c // 2, half : half + 4] = chunk[:, 4:]
+
+    @pl.when(step == 3)
+    def _():
+        core = core_ref[0]
+        for at in range(BANDS // 2):
+            for ref, which in ((own_ref, core), (away_ref, 1 - core)):
+                part = turned[pl.ds(at * 8 + which * 4, 4)].reshape(128, D)
+                ref[at * 128 : at * 128 + 128, :] = part.astype(ref.dtype)
+
+
+def weight_terms(core, left, right):
+    return call(
+        weight_kernel, "weight_terms", (4,),
+        [
+            pl.BlockSpec(memory_space=pltpu.SMEM),
+            pl.BlockSpec((TOKENS, D), lambda c: (0, c // 3)),
+            pl.BlockSpec((TOKENS, D), lambda c: (0, c)),
+        ],
+        [whole(1024, D)] * 2,
+        [jax.ShapeDtypeStruct((1024, D), F32), jax.ShapeDtypeStruct((1024, D), BF16)],
         [pltpu.VMEM((64, 2, 2, 8, D), F32)],
-        (TOKENS * 2 * D * 4 * D, 18000000, 0), 36,
-    )(hidden, att, cot, dp)
-
-
-def finished(x_ref, c_ref, att_ref, dp_ref, w_ref, gain_ref, ow_ref):
+        (TOKENS * 2 * D * 4 * D, 18000000, 0), 60,
+    )(core, left, right)
+
+
+def add_kernel(own_ref, got_ref, out_ref):
+    out_ref[...] = (own_ref[...] + got_ref[...].astype(F32)).astype(BF16)
+
+
+def add_halves(own, got):
+    return call(
+        add_kernel, "add_halves", (4,),
+        [blocks(256, D)] * 2, blocks(256, D), shapes((1024, D))[0], [],
+        (1000000, 4000000, 0), 60,
+    )(own, got)
+
+
+def finished(x_ref, att_ref, dp_ref, w_ref, gain_ref, ow_ref):
     x = x_ref[...].astype(F32)
     out = x + product(att_ref[...], ow_ref[...])
     normed, inverse = normalise(x)
-    hidden = product(dp_ref[...], w_ref[...], NT) * gain_ref[...]
+    hidden = product(dp_ref[:, : 3 * D], w_ref[...], NT) * gain_ref[...]
     hidden = (
         hidden
         - jnp.mean(hidden, -1, keepdims=True)
         - normed * jnp.mean(hidden * normed, -1, keepdims=True)
     )
-    grad = c_ref[...].astype(F32) + inverse * hidden
+    grad = dp_ref[:, 3 * D :].astype(F32) + inverse * hidden
     return out, grad
 
 
@@ -456,65 +488,76 @@
     return [product(split_ref[...], part, TN).astype(BF16) for part in (first, second)]
 
 
-def finish_kernel(split_ref, back_ref, *refs):
-    refs, (inner, edge, up, side, corner) = refs[:7], refs[7:]
+def finish_inner_kernel(split_ref, *refs):
+    *refs, inner = refs
+    for n, values in enumerate(finished(*refs)):
+        first, second = grid_pieces(split_ref, values)
+        inner[n, :WIN, :] = first
+        inner[n, WIN:, :] = second
+
+
+def finish_edge_kernel(split_ref, back_ref, *refs):
+    refs, (edge, up, side, corner) = refs[:6], refs[6:]
     step = pl.program_id(0)
-
-    def put(ref, at, values):
-        if not isinstance(at, int):
-            at = pl.multiple_of(at, 16)
-        ref[pl.ds(at, values.shape[0]), :] = values
-
     for n, values in enumerate(finished(*refs)):
 
-        @pl.when(step < 3)
+        @pl.when(step < 4)
         def _(n=n, values=values):
             first, second = grid_pieces(split_ref, values)
-            put(inner, n * INNER + step * BLOCK, first)
-            put(inner, n * INNER + step * BLOCK + WIN, second)
-
-        @pl.when((step >= 3) & (step < 7))
-        def _(n=n, values=values):
-            first, second = grid_pieces(split_ref, values)
-            put(edge, n * EDGE + (step - 3) * WIN, first)
-
-            @pl.when(step == 3)
+            edge[n] = first
+
+            @pl.when(step == 0)
             def _():
-                put(side, n * SIDE, second)
-
-            @pl.when(step > 3)
+                side[n] = second
+
+            @pl.when(step > 0)
             def _():
-                put(up, n * UP + (step - 4) * WIN, second)
-
-        @pl.when(step == 7)
+                up[n] = second
+
+        @pl.when(step == 4)
         def _(n=n, values=values):
             parts = product(back_ref[...], values.astype(BF16)).astype(BF16)
-            put(edge, n * EDGE + 4 * WIN, parts[:SMALL])
-            put(side, n * SIDE + WIN, parts[SMALL : 2 * SMALL])
-            put(up, n * UP + 3 * WIN, parts[2 * SMALL : 3 * SMALL])
-            put(corner, n * CORNER, parts[3 * SMALL :])
+            edge[n, :SMALL, :] = parts[:SMALL]
+            side[n, :SMALL, :] = parts[SMALL : 2 * SMALL]
+            up[n, :SMALL, :] = parts[2 * SMALL : 3 * SMALL]
+            corner[n] = parts[3 * SMALL :]
 
 
 PIECES = (INNER, EDGE, UP, SIDE, CORNER)
 
 
-def finish(values, weights):
-    dims = [(2 * n, D) for n in PIECES]
-    return call(
-        finish_kernel, "finish", (8,),
-        [whole(WIN, WIN), whole(4 * SMALL, BLOCK)]
-        + [blocks(BLOCK, n) for n in (D, D, D, 3 * D)]
-        + [whole(*dim) for dim in WEIGHTS],
-        [whole(*dim) for dim in dims], shapes(*dims), [],
-        (TOKENS * 2200000, TOKENS * 8000, TOKENS), 60,
+def finish_specs(skip):
+    row = lambda width, col: pl.BlockSpec((BLOCK, width), lambda i: (i + skip, col))
+    return [row(D, 0), row(D, 1), row(4 * D, 0)] + [whole(*dim) for dim in WEIGHTS]
+
+
+def finish_cost(rows):
+    return rows * 2200000, rows * 9000, rows
+
+
+def finish_inner(values, weights):
+    return call(
+        finish_inner_kernel, "finish_inner", (3,),
+        [whole(WIN, WIN)] + finish_specs(0),
+        pl.BlockSpec((2, BLOCK, D), lambda i: (0, i, 0)), shapes((2, INNER, D))[0], [],
+        finish_cost(INNER), 60,
+    )(jnp.asarray(SPLIT, BF16), *values, *weights)
+
+
+def finish_edge(values, weights):
+    return call(
+        finish_edge_kernel, "finish_edge", (5,),
+        [whole(WIN, WIN), whole(4 * SMALL, BLOCK)] + finish_specs(3),
+        EDGE_PAIRS, shapes(*[(2, n, D) for n in PIECES[1:]]), [],
+        finish_cost(5 * BLOCK), 60,
     )(jnp.asarray(SPLIT, BF16), jnp.asarray(CORNER_BACK, BF16), *values, *weights)
 
 
 def join_kernel(inner, edge, up, side, corner, *outs):
     run, stub = 48, 24
 
-    def load(ref, at, count):
-        return ref[at : at + count, :].astype(F32)
+    def load(ref, n, at, count):
+        return ref[n, at : at + count, :].astype(F32)
 
     for zone in range(3):
 
@@ -523,19 +566,19 @@
             for n, out_ref in enumerate(outs):
                 if zone == 1:
                     half = pl.program_id(0) - 1
-                    left = load(side, n * SIDE, WIN)
-                    right = load(edge, n * EDGE, WIN)
+                    left = load(side, n, 0, WIN)
+                    right = load(edge, n, 0, WIN)
                     left, right = (jnp.where(half == 0, v[:HALF], v[HALF:]) for v in (left, right))
                     full = []
                     for q in range(3):
-                        at = pl.multiple_of(n * INNER + q * BLOCK + half * WIN, 16)
-                        full.append(inner[pl.ds(at, WIN), :].astype(F32))
+                        at = pl.multiple_of(q * BLOCK + half * WIN, 16)
+                        full.append(inner[n, pl.ds(at, WIN), :].astype(F32))
                 elif zone == 0:
-                    left, right = load(corner, n * CORNER, SMALL), load(up, n * UP + 3 * WIN, SMALL)
-                    full = [load(up, n * UP + q * WIN, WIN) for q in range(3)]
+                    left, right = load(corner, n, 0, SMALL), load(up, n, 3 * WIN, SMALL)
+                    full = [load(up, n, q * WIN, WIN) for q in range(3)]
                 else:
-                    left, right = load(side, n * SIDE + WIN, SMALL), load(edge, n * EDGE + 4 * WIN, SMALL)
-                    full = [load(edge, n * EDGE + WIN + q * WIN, WIN) for q in range(3)]
+                    left, right = load(side, n, WIN, SMALL), load(edge, n, 4 * WIN, SMALL)
+                    full = [load(edge, n, WIN + q * WIN, WIN) for q in range(3)]
                 for i in range(3):
                     parts = [left[i * stub : i * stub + stub]]
                     parts += [part[i * run : i * run + run] for part in full]
@@ -549,14 +592,14 @@
     dim = (LAT, LON, LEV, D)
     return call(
         join_kernel, "join", (4,),
-        [whole(2 * n, D) for n in PIECES],
+        [whole(2, n, D) for n in PIECES],
         [spec] * 2, shapes(*[dim] * 2), [],
         (1000000, 9000000, 0), 60,
     )(*parts)
 
 
 def sum_kernel(terms_ref, qkv_ref, out_ref):
-    total = jnp.sum(terms_ref[...].astype(F32).reshape(DEVICES, 16, D), 0)
+    total = jnp.sum(terms_ref[...].astype(F32).reshape(DEVICES // 2, 16, D), 0)
     for c in range(3):
         qkv_ref[:, c * D : c * D + D] = total[4 * c : 4 * c + 4]
     out_ref[...] = total[12:]
@@ -565,7 +608,7 @@
 def sum_terms(terms):
     return call(
         sum_kernel, "sum_terms", (),
-        [whole(2048, D)], [whole(4, 3 * D), whole(4, D)],
+        [whole(1024, D)], [whole(4, 3 * D), whole(4, D)],
         shapes((4, 3 * D), (4, D), dtype=F32), [], (2000000, 2200000, 0), 20,
     )(terms)
 
@@ -583,8 +626,16 @@
     return [lax.ppermute(part, BOTH, shift_pairs(*step)) for part, step in zip(parts, steps)]
 
 
-def swap_blocks(values, axis):
-    return lax.all_to_all(values, axis, split_axis=0, concat_axis=0, tiled=True)
+def swap_blocks(values, axis, groups=None):
+    return lax.all_to_all(
+        values, axis, split_axis=0, concat_axis=0, axis_index_groups=groups, tiled=True
+    )
+
+
+SAME_CORE = [
+    [a * SECTORS + b for a in range(core, BANDS, 2) for b in range(SECTORS)] for core in range(2)
+]
+OTHER_CORE = [(d, d ^ SECTORS) for d in range(DEVICES)]
 
 
 def per_device(buffer, fetch_owner, fetch_slot, norm_gain, qkv_weight, out_weight, out_grad):
@@ -601,17 +652,21 @@
     x_up, x_side, x_corner, x_inner, x_edge = pick(table, place, replies)
     x_parts = [x_edge] + exchange([x_up, x_side, x_corner], -1)
 
-    last = (lax.axis_index("lat") == BANDS - 1) & (jnp.arange(2) == 1)
-    group = jnp.arange(WIN) >= HALF
-    apart = last[:, None, None] & (group[:, None] != group[None, :])
-    bias = jnp.tile(jnp.where(apart, -jnp.inf, 0.0).astype(F32), (1, 1, 4))
+    band = lax.axis_index("lat")
+    flag = (band == BANDS - 1).astype(I32).reshape(1)
+    core = (band % 2).astype(I32).reshape(1)
     first = attend_inner(x_inner, c_inner, weights)
-    x, cot, hidden, att, dp = attend_edge(x_parts, c_parts, bias, weights, first)
-    terms = swap_blocks(weight_terms(hidden, att, cot, dp), BOTH)
-
-    inner, edge, *away = finish((x, cot, att, dp), weights)
-    outs = join([inner, edge] + exchange(away, 1))
-    outs = [out.reshape(LAT, LON, LEV, D) for out in outs]
+    x, left, right = attend_edge(x_parts, c_parts, flag, weights, first)
+    own, away = weight_terms(core, left, right)
+    got = lax.ppermute(away, BOTH, OTHER_CORE)
+    edge, *away = finish_edge((x, left, right), weights)
+    returned = exchange(away, 1)
+    got, edge = lax.optimization_barrier((got, edge))
+    half = add_halves(own, got)
+    terms = swap_blocks(half, BOTH, SAME_CORE)
+    half, x = lax.optimization_barrier((half, x))
+    inner = finish_inner((x, left, right), weights)
+    outs = join([inner, edge] + returned)
     return (*outs, *sum_terms(terms))
 
 

time: 223 us -> 220 us (0.987)
  Pallas kernels: 82.8 us -> 98.9 us
  local copies, waits for them, and re-layouts: 38.7 us -> 25.6 us
  waiting for transfers between devices: 55.5 us -> 46 us
  starting transfers between devices: 28.1 us -> 31.8 us
    pallas_call x5 -> x7, Pallas kernels: 47.8 us -> 61.8 us  [the longest x1 21.8 us: attend_edge(): call(edge_kernel, 'attend_edge', (5,), [pl.BlockSpec(memory_space=pltpu.S...]
    unnamed x50 -> x36, local copies, waits for them, and re-layouts: 15.4 us -> 5.57 us
    ppermute x9, waiting for transfers between devices: 27.6 us -> 18 us  [exchange(): lax.ppermute(part, BOTH, shift_pairs(*step))]
    all_to_all x2, starting transfers between devices: 9.85 us -> 13.6 us  [swap_blocks(): lax.all_to_all(values, axis, split_axis=0, concat_axis=0, axis_index_grou...]
    another operation x2 -> x0, local copies, waits for them, and re-layouts: 3.22 us -> none  [per_device(): bias = jnp.tile(jnp.where(apart, -jnp.inf, 0.0).astype(F32), (1, 1, 4))]
    pallas_call x1, Pallas kernels: 10.4 us -> 13.2 us  [attend_inner(): call(inner_kernel, 'attend_inner', (3,), [blocks(BLOCK, D)] * 2 + [whole(...]
  transfers between devices with their start and end apart: 11 -> 12, of which waited for: 3 -> 3; matrix products, arithmetic and copies ran while one was open for 10% -> 8% of each run, Pallas kernels for 20% -> 23%
where the time goes in v4:
time: 220 us
  Pallas kernels  98.9 us (45%)
  waiting for transfers between devices  46 us (21%)
  starting transfers between devices  31.8 us (14%)
  local copies, waits for them, and re-layouts  25.6 us (12%)
  blocking collectives  16.4 us (7%)
    all_to_all x2, waiting for transfers between devices, swap_blocks(): lax.all_to_all(values, axis, split_axis=0, concat_axis=0, axis_index_grou...  28 us
    pallas_call x1, Pallas kernels, attend_edge(): call(edge_kernel, 'attend_edge', (5,), [pl.BlockSpec(memory_space=pltpu.S...  21.8 us
    ppermute x9, waiting for transfers between devices, exchange(): lax.ppermute(part, BOTH, shift_pairs(*step))  18 us
    ppermute x9, starting transfers between devices, exchange(): lax.ppermute(part, BOTH, shift_pairs(*step))  17.6 us
    all_to_all x1, blocking collectives, swap_blocks(): lax.all_to_all(values, axis, split_axis=0, concat_axis=0, axis_index_grou...  16.4 us
    all_to_all x2, starting transfers between devices, swap_blocks(): lax.all_to_all(values, axis, split_axis=0, concat_axis=0, axis_index_grou...  13.6 us
    pallas_call x1, Pallas kernels, attend_inner(): call(inner_kernel, 'attend_inner', (3,), [blocks(BLOCK, D)] * 2 + [whole(...  13.2 us
    gather x1, local copies, waits for them, and re-layouts, per_device(): place = place.reshape(TOKENS)[ORDER].reshape(-1, 1)  12.7 us
  transfers between devices with their start and end apart: 12, of which 3 were waited for; matrix products, arithmetic and copies ran while one was open for 8% of the time, Pallas kernels for 23%

profile of v4, /device:TPU:1, one launch (start us, length us, event | category | flops | bytes accessed | tf_op | source)
XLA Modules:
  0.0 219.7 jit_solution(12294256307506962486)
XLA Ops:
  0.6 2.6 %requests.1 = (s32[16,288]{1,0:T(8,128)}, s32[1,2304]{1,0:T(1,128)}, s32[16,8]{1,0:T(8,128)}) custom-call(s32[1,2304]{1,0:T(1,128)} %bitcast.22, s32[1,2304]{1,0:T(1,128)} %bitcast.23), custom_call_target="tpu_custom_call" | custom-call | flops 100000000 | bytes 100000 | tf_op jit(solution)/shard_map/requests/pallas_call | solution.py:159
  4.0 16.4 %all_to_all.28 = s32[16,1,288]{2,1,0:T(1,128)S(1)} all-to-all(s32[16,1,288]{2,1,0:T(1,128)S(1)} %copy.26), channel_id=1, replica_groups=mesh['lat'=16,'lon'=8] {'lat'}, dimensions={0} | all-to-all | bytes 36864 | tf_op jit(solution)/shard_map/all_to_all | solution.py:630
  21.2 11.0 %serve.1 = bf16[4608,512]{1,0:T(8,128)(2,1)} custom-call(s32[288,16]{1,0:T(8,128)} %bitcast.16, bf16[1152,512]{1,0:T(8,128)(2,1)} %buffer_ref.1), custom_call_target="tpu_custom_call" | custom-call | flops 5400000000 | bytes 6000000 | tf_op jit(solution)/shard_map/serve/pallas_call | solution.py:184
  32.2 4.7 %all-to-all-start.1 = ((bf16[16,288,512]{2,1,0:T(8,128)(2,1)}), bf16[16,288,512]{2,1,0:T(8,128)(2,1)}, u32[]{:S(2)}, u32[]{:S(2)}) async-start(bf16[16,288,512]{2,1,0:T(8,128)(2,1)} %bitcast.14), calls=%async_computation.1 | async-start | bytes 9437184 | tf_op jit(solution)/shard_map/all_to_all | solution.py:630
  36.9 3.9 %reshape.53.grid_ref = bf16[2304,512]{1,0:T(8,128)(2,1)S(1)} reshape(bf16[12,48,4,512]{3,2,1,0:T(4,128)(2,1)} %param.22) | data formatting | bytes 4718592 | tf_op jit(solution)/shard_map/reshape | solution.py:648
  43.4 2.9 %collective-permute-start.5 = (bf16[80,512]{1,0:T(8,128)(2,1)S(1)}, bf16[80,512]{1,0:T(8,128)(2,1)S(1)}, u32[]{:S(2)}, u32[]{:S(2)}) collective-permute-start(bf16[80,512]{1,0:T(8,128)(2,1)S(1)} %get-tuple-element.46), channel_id=1, source_target_pairs={{0,127},{1,120},{2,121},{3,122},{4,123},{5,124},{6,125},{7,126},{8... | collective-permute-start | bytes 245768 | tf_op jit(solution)/shard_map/ppermute | solution.py:626
  46.3 4.7 %collective-permute-start.3 = (bf16[512,512]{1,0:T(8,128)(2,1)S(1)}, bf16[512,512]{1,0:T(8,128)(2,1)S(1)}, u32[]{:S(2)}, u32[]{:S(2)}) collective-permute-start(bf16[512,512]{1,0:T(8,128)(2,1)S(1)} %get-tuple-element.44), channel_id=1, source_target_pairs={{0,120},{1,121},{2,122},{3,123},{4,124},{5,125},{6,126},{7,127},{8... | collective-permute-start | bytes 1572872 | tf_op jit(solution)/shard_map/ppermute | solution.py:626
  51.1 12.7 %gather_fusion = s32[2336]{0:T(1024)S(1)} fusion(s32[2304]{0:T(1024)S(1)} %reduce, s32[3072]{0:T(1024)S(1)} %pad_clamp_fusion), kind=kCustom, calls=%fused_computation | custom fusion | bytes 28032 | tf_op jit(solution)/shard_map/gather | solution.py:650
  63.8 1.9 reshape.65.place_ref
  65.7 28.0 %all-to-all-done.1 = bf16[16,288,512]{2,1,0:T(8,128)(2,1)} async-done(((bf16[16,288,512]{2,1,0:T(8,128)(2,1)}), bf16[16,288,512]{2,1,0:T(8,128)(2,1)}, u32[]{:S(2)}, u32[]{:S(2)}) %all-to-all-start.1) | async-done | bytes 4718624 | tf_op jit(solution)/shard_map/all_to_all | solution.py:630
  93.8 9.5 %pick.1 = (bf16[512,512]{1,0:T(8,128)(2,1)}, bf16[224,512]{1,0:T(8,128)(2,1)}, bf16[80,512]{1,0:T(8,128)(2,1)}, bf16[864,512]{1,0:T(8,128)(2,1)}, bf16[656,512]{1,0:T(8,128)(2,1)}) custom-call(s32[16,8]{1,0:T(8,128)} %get-tuple-element.36.table_ref, s32[2336,1]{1,0:T(8,128)} %reshape.65.place_ref, bf16[4608,512]{1,0:T(8,128)(2,1)} %bitcast.8.replies_ref), custom_call_target="tpu_custom_call" | custom-call | flops 3600000000 | bytes 8000000 | tf_op jit(solution)/shard_map/pick/pallas_call | solution.py:233
  103.3 1.4 collective-permute-start
  104.7 2.8 %collective-permute-start.4 = (bf16[224,512]{1,0:T(8,128)(2,1)S(1)}, bf16[224,512]{1,0:T(8,128)(2,1)S(1)}, u32[]{:S(2)}, u32[]{:S(2)}) collective-permute-start(bf16[224,512]{1,0:T(8,128)(2,1)S(1)} %get-tuple-element.45), channel_id=1, source_target_pairs={{0,7},{1,0},{2,1},{3,2},{4,3},{5,4},{6,5},{7,6},{8,15},{9,8},{10,9... | collective-permute-start | bytes 688136 | tf_op jit(solution)/shard_map/ppermute | solution.py:626
  107.4 1.6 collective-permute-start.2
  109.7 13.2 %attend_inner.1 = (bf16[2304,512]{1,0:T(8,128)(2,1)}, bf16[2304,1024]{1,0:T(8,128)(2,1)}, bf16[2304,2048]{1,0:T(8,128)(2,1)}) custom-call(bf16[864,512]{1,0:T(8,128)(2,1)} %get-tuple-element.47.x_ref, bf16[864,512]{1,0:T(8,128)(2,1)} %copy-done.2, bf16[512,1536]{1,0:T(8,128)(2,1)} %refs_3_.3, f32[1,512]{1,0:T(1,128)} %bitcast.18, bf16[512,512]{1,0:T(8,128)(2,1)} %refs_5_.3), custom_call_target="tpu_custom_call" | custom-call | flops 5184000000 | bytes 8640000 | tf_op jit(solution)/shard_map/attend_inner/pallas_call | solution.py:398
  124.0 21.8 %attend_edge.1 = (bf16[2304,512]{1,0:T(8,128)(2,1)}, bf16[2304,1024]{1,0:T(8,128)(2,1)}, bf16[2304,2048]{1,0:T(8,128)(2,1)}) custom-call(s32[1]{0:T(128)} %bitcast.1.flag_ref, bf16[656,512]{1,0:T(8,128)(2,1)} %get-tuple-element.39.xe, bf16[512,512]{1,0:T(8,128)(2,1)} %copy-done.11, ...), custom_call_target="tpu_custom_call", output_to_operand_aliasing={{0}: (14, {}), {1}: (15, {}), {2}: (16, {})} | custom-call | flops 8640000000 | bytes 14400000 | tf_op jit(solution)/shard_map/attend_edge/pallas_call | solution.py:412
  145.8 11.5 %weight_terms.1 = (f32[1024,512]{1,0:T(8,128)}, bf16[1024,512]{1,0:T(8,128)(2,1)}) custom-call(s32[1]{0:T(128)} %bitcast.core_ref, bf16[2304,1024]{1,0:T(8,128)(2,1)} %get-tuple-element.52.left_ref.refs_1_, bf16[2304,2048]{1,0:T(8,128)(2,1)} %get-tuple-element.53.right_ref.refs_2_), custom_call_target="tpu_custom_call" | custom-call | flops 4831838208 | bytes 18000000 | tf_op jit(solution)/shard_map/weight_terms/pallas_call | solution.py:445
  157.9 11.2 %finish_edge.1 = (bf16[2,656,512]{2,1,0:T(8,128)(2,1)}, bf16[2,512,512]{2,1,0:T(8,128)(2,1)}, bf16[2,224,512]{2,1,0:T(8,128)(2,1)}, bf16[2,80,512]{2,1,0:T(8,128)(2,1)}) custom-call(bf16[144,144]{1,0:T(8,128)(2,1)} %constant.37.clone.split_ref, bf16[320,288]{1,0:T(8,128)(2,1)} %constant.43.clone.back_ref, bf16[2304,512]{1,0:T(8,128)(2,1)} %get-tuple-element.59.refs_0_, ...), custom_call_target="tpu_custom_call" | custom-call | flops 3168000000 | bytes 12960000 | tf_op jit(solution)/shard_map/finish_edge/pallas_call | solution.py:548
  169.1 2.1 collective-permute-start.7
  172.2 3.8 %add_halves.1 = bf16[1024,512]{1,0:T(8,128)(2,1)} custom-call(f32[1024,512]{1,0:T(8,128)} %get-tuple-element.54.own_ref, bf16[1024,512]{1,0:T(8,128)(2,1)} %copy-done.5), custom_call_target="tpu_custom_call" | custom-call | flops 1000000 | bytes 4000000 | tf_op jit(solution)/shard_map/add_halves/pallas_call | solution.py:464
  176.0 8.9 %all-to-all-start.2 = ((bf16[64,16,512]{2,1,0:T(8,128)(2,1)}), bf16[64,16,512]{2,1,0:T(8,128)(2,1)S(1)}, u32[]{:S(2)}, u32[]{:S(2)}) async-start(bf16[64,16,512]{2,1,0:T(8,128)(2,1)} %bitcast.15), calls=%async_computation.2 | async-start | bytes 2097152 | tf_op jit(solution)/shard_map/all_to_all | solution.py:630
  186.5 7.0 %finish_inner.1.inner = bf16[2,864,512]{2,1,0:T(8,128)(2,1)} custom-call(bf16[144,144]{1,0:T(8,128)(2,1)} %constant.37.clone.split_ref, bf16[2304,512]{1,0:T(8,128)(2,1)} %get-tuple-element.59.refs_0_, bf16[2304,1024]{1,0:T(8,128)(2,1)} %get-tuple-element.52.left_ref.refs_1_, bf16[2304,2048]{1,0:T(8,128)(2,1)} %get-tuple-element.53.right_ref.refs_2_, ...), custom_call_target="tpu_custom_call" | custom-call | flops 1900800000 | bytes 7776000 | tf_op jit(solution)/shard_map/finish_inner/pallas_call | solution.py:539
  193.5 17.5 %collective-permute-done.9.corner = bf16[2,80,512]{2,1,0:T(8,128)(2,1)S(1)} collective-permute-done((bf16[2,80,512]{2,1,0:T(8,128)(2,1)S(1)}, bf16[2,80,512]{2,1,0:T(8,128)(2,1)S(1)}, u32[]{:S(2)}, u32[]{:S(2)}) %collective-permute-start.9) | collective-permute-done | bytes 163872 | tf_op jit(solution)/shard_map/ppermute | solution.py:626
  213.2 5.7 %join.1 = (bf16[12,48,4,512]{3,2,1,0:T(4,128)(2,1)}, bf16[12,48,4,512]{3,2,1,0:T(4,128)(2,1)}) custom-call(bf16[2,864,512]{2,1,0:T(8,128)(2,1)} %finish_inner.1.inner, bf16[2,656,512]{2,1,0:T(8,128)(2,1)} %get-tuple-element.60.edge, bf16[2,512,512]{2,1,0:T(8,128)(2,1)} %copy-done.4, bf16[2,224,512]{2,1,0:T(8,128)(2,1)} %copy-done.6, ...), custom_call_target="tpu_custom_call" | custom-call | flops 1000000 | bytes 9000000 | tf_op jit(solution)/shard_map/join/pallas_call | solution.py:593
  (56 shorter events, 12.1 us)
Async XLA Ops:
  32.2 61.6 %all-to-all-start.1 = ((bf16[16,288,512]{2,1,0:T(8,128)(2,1)}), bf16[16,288,512]{2,1,0:T(8,128)(2,1)}, u32[]{:S(2)}, u32[]{:S(2)}) async-start(bf16[16,288,512]{2,1,0:T(8,128)(2,1)} %bitcast.14), calls=%async_computation.1 | async-start | bytes 9437184 | tf_op jit(solution)/shard_map/all_to_all | solution.py:630
  36.9 3.9 %copy-start = (bf16[144,144]{1,0:T(8,128)(2,1)S(1)}, bf16[144,144]{1,0:T(8,128)(2,1)}, u32[]{:S(2)}) copy-start(bf16[144,144]{1,0:T(8,128)(2,1)} %constant.37.clone.split_ref) | copy-start | bytes 124420
  36.9 3.9 %copy-start.1 = (bf16[80,72]{1,0:T(8,128)(2,1)S(1)}, bf16[80,72]{1,0:T(8,128)(2,1)}, u32[]{:S(2)}) copy-start(bf16[80,72]{1,0:T(8,128)(2,1)} %constant.38.clone.small_ref) | copy-start | bytes 34564
  40.8 10.2 %copy-start.9 = (s32[1,2304]{1,0:T(1,128)S(1)}, s32[1,2304]{1,0:T(1,128)}, u32[]{:S(2)}) copy-start(s32[1,2304]{1,0:T(1,128)} %get-tuple-element.37) | copy-start | bytes 27652
  40.8 10.3 %copy-start.8 = (s32[2336]{0:T(1024)S(1)}, s32[2336]{0:T(1024)}, u32[]{:S(2)}) copy-start(s32[2336]{0:T(1024)} %constant.48) | copy-start | bytes 28036
  41.6 0.9 copy-start.2
  43.4 65.6 %collective-permute-start.5 = (bf16[80,512]{1,0:T(8,128)(2,1)S(1)}, bf16[80,512]{1,0:T(8,128)(2,1)S(1)}, u32[]{:S(2)}, u32[]{:S(2)}) collective-permute-start(bf16[80,512]{1,0:T(8,128)(2,1)S(1)} %get-tuple-element.46), channel_id=1, source_target_pairs={{0,127},{1,120},{2,121},{3,122},{4,123},{5,124},{6,125},{7,126},{8... | collective-permute-start | bytes 245768 | tf_op jit(solution)/shard_map/ppermute | solution.py:626
  46.3 76.6 %collective-permute-start.3 = (bf16[512,512]{1,0:T(8,128)(2,1)S(1)}, bf16[512,512]{1,0:T(8,128)(2,1)S(1)}, u32[]{:S(2)}, u32[]{:S(2)}) collective-permute-start(bf16[512,512]{1,0:T(8,128)(2,1)S(1)} %get-tuple-element.44), channel_id=1, source_target_pairs={{0,120},{1,121},{2,122},{3,123},{4,124},{5,125},{6,126},{7,127},{8... | collective-permute-start | bytes 1572872 | tf_op jit(solution)/shard_map/ppermute | solution.py:626
  103.3 19.6 %collective-permute-start = (bf16[512,512]{1,0:T(8,128)(2,1)}, bf16[512,512]{1,0:T(8,128)(2,1)S(1)}, u32[]{:S(2)}, u32[]{:S(2)}) collective-permute-start(bf16[512,512]{1,0:T(8,128)(2,1)} %get-tuple-element.40), channel_id=1, source_target_pairs={{0,120},{1,121},{2,122},{3,123},{4,124},{5,125},{6,126},{7,127},{8... | collective-permute-start | bytes 1572872 | tf_op jit(solution)/shard_map/ppermute | solution.py:626
  104.7 18.2 %collective-permute-start.4 = (bf16[224,512]{1,0:T(8,128)(2,1)S(1)}, bf16[224,512]{1,0:T(8,128)(2,1)S(1)}, u32[]{:S(2)}, u32[]{:S(2)}) collective-permute-start(bf16[224,512]{1,0:T(8,128)(2,1)S(1)} %get-tuple-element.45), channel_id=1, source_target_pairs={{0,7},{1,0},{2,1},{3,2},{4,3},{5,4},{6,5},{7,6},{8,15},{9,8},{10,9... | collective-permute-start | bytes 688136 | tf_op jit(solution)/shard_map/ppermute | solution.py:626
  107.4 15.5 %collective-permute-start.2 = (bf16[80,512]{1,0:T(8,128)(2,1)}, bf16[80,512]{1,0:T(8,128)(2,1)S(1)}, u32[]{:S(2)}, u32[]{:S(2)}) collective-permute-start(bf16[80,512]{1,0:T(8,128)(2,1)} %get-tuple-element.42), channel_id=1, source_target_pairs={{0,127},{1,120},{2,121},{3,122},{4,123},{5,124},{6,125},{7,126},{8... | collective-permute-start | bytes 245768 | tf_op jit(solution)/shard_map/ppermute | solution.py:626
  109.0 13.9 %copy-start.16 = (bf16[80,512]{1,0:T(8,128)(2,1)}, bf16[80,512]{1,0:T(8,128)(2,1)S(1)}, u32[]{:S(2)}) copy-start(bf16[80,512]{1,0:T(8,128)(2,1)S(1)} %collective-permute-done.5.cc) | copy-start | bytes 245764
  109.0 13.9 %collective-permute-start.1 = (bf16[224,512]{1,0:T(8,128)(2,1)}, bf16[224,512]{1,0:T(8,128)(2,1)S(1)}, u32[]{:S(2)}, u32[]{:S(2)}) collective-permute-start(bf16[224,512]{1,0:T(8,128)(2,1)} %get-tuple-element.41), channel_id=1, source_target_pairs={{0,7},{1,0},{2,1},{3,2},{4,3},{5,4},{6,5},{7,6},{8,15},{9,8},{10,9... | collective-permute-start | bytes 688136 | tf_op jit(solution)/shard_map/ppermute | solution.py:626
  122.9 1.0 copy-start.14
  122.9 1.1 copy-start.11
  157.3 13.9 %collective-permute-start.6 = (bf16[1024,512]{1,0:T(8,128)(2,1)}, bf16[1024,512]{1,0:T(8,128)(2,1)S(1)}, u32[]{:S(2)}, u32[]{:S(2)}) collective-permute-start(bf16[1024,512]{1,0:T(8,128)(2,1)} %get-tuple-element.55), channel_id=1, source_target_pairs={{0,8},{1,9},{2,10},{3,11},{4,12},{5,13},{6,14},{7,15},{8,0},{9,1},... | collective-permute-start | bytes 3145736 | tf_op jit(solution)/shard_map/ppermute | solution.py:661
  169.1 42.4 %collective-permute-start.7 = (bf16[2,512,512]{2,1,0:T(8,128)(2,1)}, bf16[2,512,512]{2,1,0:T(8,128)(2,1)S(1)}, u32[]{:S(2)}, u32[]{:S(2)}) collective-permute-start(bf16[2,512,512]{2,1,0:T(8,128)(2,1)} %get-tuple-element.61), channel_id=1, source_target_pairs={{0,8},{1,9},{2,10},{3,11},{4,12},{5,13},{6,14},{7,15},{8,16},{9,17... | collective-permute-start | bytes 3145736 | tf_op jit(solution)/shard_map/ppermute | solution.py:626
  171.1 1.0 copy-start.5
  172.1 12.8 %copy-start.12 = (bf16[2,224,512]{2,1,0:T(8,128)(2,1)S(1)}, bf16[2,224,512]{2,1,0:T(8,128)(2,1)}, u32[]{:S(2)}) copy-start(bf16[2,224,512]{2,1,0:T(8,128)(2,1)} %get-tuple-element.62) | copy-start | bytes 1376260
  172.1 13.9 %copy-start.15 = (bf16[2,80,512]{2,1,0:T(8,128)(2,1)S(1)}, bf16[2,80,512]{2,1,0:T(8,128)(2,1)}, u32[]{:S(2)}) copy-start(bf16[2,80,512]{2,1,0:T(8,128)(2,1)} %get-tuple-element.63) | copy-start | bytes 491524
  176.0 42.9 %all-to-all-start.2 = ((bf16[64,16,512]{2,1,0:T(8,128)(2,1)}), bf16[64,16,512]{2,1,0:T(8,128)(2,1)S(1)}, u32[]{:S(2)}, u32[]{:S(2)}) async-start(bf16[64,16,512]{2,1,0:T(8,128)(2,1)} %bitcast.15), calls=%async_computation.2 | async-start | bytes 2097152 | tf_op jit(solution)/shard_map/all_to_all | solution.py:630
  184.9 26.5 %collective-permute-start.8 = (bf16[2,224,512]{2,1,0:T(8,128)(2,1)S(1)}, bf16[2,224,512]{2,1,0:T(8,128)(2,1)S(1)}, u32[]{:S(2)}, u32[]{:S(2)}) collective-permute-start(bf16[2,224,512]{2,1,0:T(8,128)(2,1)S(1)} %copy-done.12), channel_id=1, source_target_pairs={{0,1},{1,2},{2,3},{3,4},{4,5},{5,6},{6,7},{7,0},{8,9},{9,10},{10,1... | collective-permute-start | bytes 1376264 | tf_op jit(solution)/shard_map/ppermute | solution.py:626
  186.0 24.9 %collective-permute-start.9 = (bf16[2,80,512]{2,1,0:T(8,128)(2,1)S(1)}, bf16[2,80,512]{2,1,0:T(8,128)(2,1)S(1)}, u32[]{:S(2)}, u32[]{:S(2)}) collective-permute-start(bf16[2,80,512]{2,1,0:T(8,128)(2,1)S(1)} %copy-done.15), channel_id=1, source_target_pairs={{0,9},{1,10},{2,11},{3,12},{4,13},{5,14},{6,15},{7,8},{8,17},{9,18... | collective-permute-start | bytes 491528 | tf_op jit(solution)/shard_map/ppermute | solution.py:626
  212.2 1.0 copy-start.4
  (6 other events, 4.7 us)

commit v5 on v4

--- a/solution.py
+++ b/solution.py
@@ -398,7 +398,7 @@
     return call(
         inner_kernel, "attend_inner", (3,),
         [blocks(BLOCK, D)] * 2 + [whole(*dim) for dim in WEIGHTS],
-        outs, out_shapes, scratch, cost, 60,
+        outs, out_shapes, scratch, cost, 18,
     )(x, cot, *weights)
 
 
@@ -416,7 +416,7 @@
         + [whole(BLOCK, 4 * SMALL), whole(WIN, 4 * WIN)]
         + [whole(*dim) for dim in WEIGHTS]
         + [pl.BlockSpec(memory_space=pl.ANY)] * 3,
-        outs, out_shapes, scratch + [pltpu.VMEM((BLOCK, D), F32)] * 2, cost, 60,
+        outs, out_shapes, scratch + [pltpu.VMEM((BLOCK, D), F32)] * 2, cost, 24,
         aliases={14 + n: n for n in range(3)},
     )(flag, *x_parts, *c_parts, jnp.asarray(CORNER_JOIN, BF16), jnp.asarray(apart_matrix()), *weights, *carried)
 
@@ -452,7 +452,7 @@
         [whole(1024, D)] * 2,
         [jax.ShapeDtypeStruct((1024, D), F32), jax.ShapeDtypeStruct((1024, D), BF16)],
         [pltpu.VMEM((64, 2, 2, 8, D), F32)],
-        (TOKENS * 2 * D * 4 * D, 18000000, 0), 60,
+        (TOKENS * 2 * D * 4 * D, 18000000, 0), 24,
     )(core, left, right)
 
 
@@ -464,7 +464,7 @@
     return call(
         add_kernel, "add_halves", (4,),
         [blocks(256, D)] * 2, blocks(256, D), shapes((1024, D))[0], [],
-        (1000000, 4000000, 0), 60,
+        (1000000, 4000000, 0), 10,
     )(own, got)
 
 
@@ -540,7 +540,7 @@
         finish_inner_kernel, "finish_inner", (3,),
         [whole(WIN, WIN)] + finish_specs(0),
         pl.BlockSpec((2, BLOCK, D), lambda i: (0, i, 0)), shapes((2, INNER, D))[0], [],
-        finish_cost(INNER), 60,
+        finish_cost(INNER), 20,
     )(jnp.asarray(SPLIT, BF16), *values, *weights)
 
 
@@ -549,7 +549,7 @@
         finish_edge_kernel, "finish_edge", (5,),
         [whole(WIN, WIN), whole(4 * SMALL, BLOCK)] + finish_specs(3),
         EDGE_PAIRS, shapes(*[(2, n, D) for n in PIECES[1:]]), [],
-        finish_cost(5 * BLOCK), 60,
+        finish_cost(5 * BLOCK), 24,
     )(jnp.asarray(SPLIT, BF16), jnp.asarray(CORNER_BACK, BF16), *values, *weights)
 
 
@@ -594,7 +594,7 @@
         join_kernel, "join", (4,),
         [whole(2, n, D) for n in PIECES],
         [spec] * 2, shapes(*[dim] * 2), [],
-        (1000000, 9000000, 0), 60,
+        (1000000, 9000000, 0), 26,
     )(*parts)
 
 
@@ -657,15 +657,14 @@
     core = (band % 2).astype(I32).reshape(1)
     first = attend_inner(x_inner, c_inner, weights)
     x, left, right = attend_edge(x_parts, c_parts, flag, weights, first)
+    edge, *away = finish_edge((x, left, right), weights)
+    returned = exchange(away, 1)
+    left, right, edge = lax.optimization_barrier((left, right, edge))
     own, away = weight_terms(core, left, right)
     got = lax.ppermute(away, BOTH, OTHER_CORE)
-    edge, *away = finish_edge((x, left, right), weights)
-    returned = exchange(away, 1)
-    got, edge = lax.optimization_barrier((got, edge))
-    half = add_halves(own, got)
-    terms = swap_blocks(half, BOTH, SAME_CORE)
-    half, x = lax.optimization_barrier((half, x))
     inner = finish_inner((x, left, right), weights)
+    got, inner, returned = lax.optimization_barrier((got, inner, returned))
+    terms = swap_blocks(add_halves(own, got), BOTH, SAME_CORE)
     outs = join([inner, edge] + returned)
     return (*outs, *sum_terms(terms))
 

time: 220 us -> 209 us (0.950)
  Pallas kernels: 98.9 us -> 78.6 us
  waiting for transfers between devices: 46 us -> 50.3 us
  local copies, waits for them, and re-layouts: 25.6 us -> 28.2 us
    all_to_all x2, waiting for transfers between devices: 28 us -> 37.9 us  [swap_blocks(): lax.all_to_all(values, axis, split_axis=0, concat_axis=0, axis_index_grou...]
    ppermute x9, waiting for transfers between devices: 18 us -> 12.4 us  [exchange(): lax.ppermute(part, BOTH, shift_pairs(*step))]
    pallas_call x1, Pallas kernels: 11.5 us -> 7.67 us  [weight_terms(): call(weight_kernel, 'weight_terms', (4,), [pl.BlockSpec(memory_space=pltp...]
    ppermute x9, starting transfers between devices: 17.6 us -> 21.3 us  [exchange(): lax.ppermute(part, BOTH, shift_pairs(*step))]
    pallas_call x1, Pallas kernels: 3.83 us -> 0.25 us  [add_halves(): call(add_kernel, 'add_halves', (4,), [blocks(256, D)] * 2, blocks(256, D)...]
    pallas_call x1, Pallas kernels: 6.99 us -> 3.7 us  [finish_inner(): call(finish_inner_kernel, 'finish_inner', (3,), [whole(WIN, WIN)] + finis...]
    pallas_call x1, Pallas kernels: 13.2 us -> 10.4 us  [attend_inner(): call(inner_kernel, 'attend_inner', (3,), [blocks(BLOCK, D)] * 2 + [whole(...]
    pallas_call x1, Pallas kernels: 11.2 us -> 8.51 us  [finish_edge(): call(finish_edge_kernel, 'finish_edge', (5,), [whole(WIN, WIN), whole(4 *...]
  transfers between devices with their start and end apart: 12 -> 12, of which waited for: 3 -> 4; matrix products, arithmetic and copies ran while one was open for 8% -> 9% of each run, Pallas kernels for 23% -> 17%
where the time goes in v5:
time: 209 us; the launch traced here: 208 us
  Pallas kernels  78.6 us (38%)
  waiting for transfers between devices  50.3 us (24%)
  starting transfers between devices  33.8 us (16%)
  local copies, waits for them, and re-layouts  28.2 us (13%)
  blocking collectives  16.4 us (8%)
    all_to_all x2, waiting for transfers between devices, swap_blocks(): lax.all_to_all(values, axis, split_axis=0, concat_axis=0, axis_index_grou...  37.9 us
    ppermute x9, starting transfers between devices, exchange(): lax.ppermute(part, BOTH, shift_pairs(*step))  21.3 us
    pallas_call x1, Pallas kernels, attend_edge(): call(edge_kernel, 'attend_edge', (5,), [pl.BlockSpec(memory_space=pltpu.S...  19.3 us
    all_to_all x1, blocking collectives, swap_blocks(): lax.all_to_all(values, axis, split_axis=0, concat_axis=0, axis_index_grou...  16.4 us
    gather x1, local copies, waits for them, and re-layouts, per_device(): place = place.reshape(TOKENS)[ORDER].reshape(-1, 1)  12.7 us
    ppermute x9, waiting for transfers between devices, exchange(): lax.ppermute(part, BOTH, shift_pairs(*step))  12.4 us
    all_to_all x2, starting transfers between devices, swap_blocks(): lax.all_to_all(values, axis, split_axis=0, concat_axis=0, axis_index_grou...  12.4 us
    pallas_call x1, Pallas kernels, serve(): call(serve_kernel, 'serve', (BANDS // ASKERS,), [whole(CAP, BANDS), whole...  10.9 us
  transfers between devices with their start and end apart: 12, of which 4 were waited for; matrix products, arithmetic and copies ran while one was open for 9% of the time, Pallas kernels for 17%

profile of v5, /device:TPU:1, one launch (start us, length us, event | category | flops | bytes accessed | tf_op | source)
XLA Modules:
  0.0 208.3 jit_solution(11720753775424349989)
XLA Ops:
  0.6 2.6 %requests.1 = (s32[16,288]{1,0:T(8,128)}, s32[1,2304]{1,0:T(1,128)}, s32[16,8]{1,0:T(8,128)}) custom-call(s32[1,2304]{1,0:T(1,128)} %bitcast.22, s32[1,2304]{1,0:T(1,128)} %bitcast.23), custom_call_target="tpu_custom_call" | custom-call | flops 100000000 | bytes 100000 | tf_op jit(solution)/shard_map/requests/pallas_call | solution.py:159
  4.0 16.4 %all_to_all.28 = s32[16,1,288]{2,1,0:T(1,128)S(1)} all-to-all(s32[16,1,288]{2,1,0:T(1,128)S(1)} %copy.26), channel_id=1, replica_groups=mesh['lat'=16,'lon'=8] {'lat'}, dimensions={0} | all-to-all | bytes 36864 | tf_op jit(solution)/shard_map/all_to_all | solution.py:630
  21.2 10.9 %serve.1 = bf16[4608,512]{1,0:T(8,128)(2,1)} custom-call(s32[288,16]{1,0:T(8,128)} %bitcast.20, bf16[1152,512]{1,0:T(8,128)(2,1)} %buffer_ref.1), custom_call_target="tpu_custom_call" | custom-call | flops 5400000000 | bytes 6000000 | tf_op jit(solution)/shard_map/serve/pallas_call | solution.py:184
  32.1 4.7 %all-to-all-start.1 = ((bf16[16,288,512]{2,1,0:T(8,128)(2,1)}), bf16[16,288,512]{2,1,0:T(8,128)(2,1)}, u32[]{:S(2)}, u32[]{:S(2)}) async-start(bf16[16,288,512]{2,1,0:T(8,128)(2,1)} %bitcast.19), calls=%async_computation.1 | async-start | bytes 9437184 | tf_op jit(solution)/shard_map/all_to_all | solution.py:630
  36.8 3.9 %reshape.53.grid_ref = bf16[2304,512]{1,0:T(8,128)(2,1)S(1)} reshape(bf16[12,48,4,512]{3,2,1,0:T(4,128)(2,1)} %param.22) | data formatting | bytes 4718592 | tf_op jit(solution)/shard_map/reshape | solution.py:648
  43.8 2.9 %collective-permute-start.5 = (bf16[80,512]{1,0:T(8,128)(2,1)S(1)}, bf16[80,512]{1,0:T(8,128)(2,1)S(1)}, u32[]{:S(2)}, u32[]{:S(2)}) collective-permute-start(bf16[80,512]{1,0:T(8,128)(2,1)S(1)} %get-tuple-element.51), channel_id=1, source_target_pairs={{0,127},{1,120},{2,121},{3,122},{4,123},{5,124},{6,125},{7,126},{8... | collective-permute-start | bytes 245768 | tf_op jit(solution)/shard_map/ppermute | solution.py:626
  46.8 4.7 %collective-permute-start.3 = (bf16[512,512]{1,0:T(8,128)(2,1)}, bf16[512,512]{1,0:T(8,128)(2,1)}, u32[]{:S(2)}, u32[]{:S(2)}) collective-permute-start(bf16[512,512]{1,0:T(8,128)(2,1)} %get-tuple-element.49), channel_id=1, source_target_pairs={{0,120},{1,121},{2,122},{3,123},{4,124},{5,125},{6,126},{7,127},{8... | collective-permute-start | bytes 1572872 | tf_op jit(solution)/shard_map/ppermute | solution.py:626
  51.6 12.7 %gather_fusion = s32[2336]{0:T(1024)S(1)} fusion(s32[2304]{0:T(1024)S(1)} %reduce, s32[3072]{0:T(1024)S(1)} %pad_clamp_fusion), kind=kCustom, calls=%fused_computation | custom fusion | bytes 28032 | tf_op jit(solution)/shard_map/gather | solution.py:650
  64.3 1.9 reshape.65.place_ref
  66.2 27.5 %all-to-all-done.1 = bf16[16,288,512]{2,1,0:T(8,128)(2,1)} async-done(((bf16[16,288,512]{2,1,0:T(8,128)(2,1)}), bf16[16,288,512]{2,1,0:T(8,128)(2,1)}, u32[]{:S(2)}, u32[]{:S(2)}) %all-to-all-start.1) | async-done | bytes 4718624 | tf_op jit(solution)/shard_map/all_to_all | solution.py:630
  93.7 9.7 %pick.1 = (bf16[512,512]{1,0:T(8,128)(2,1)}, bf16[224,512]{1,0:T(8,128)(2,1)}, bf16[80,512]{1,0:T(8,128)(2,1)}, bf16[864,512]{1,0:T(8,128)(2,1)}, bf16[656,512]{1,0:T(8,128)(2,1)}) custom-call(s32[16,8]{1,0:T(8,128)} %get-tuple-element.41.table_ref, s32[2336,1]{1,0:T(8,128)} %reshape.65.place_ref, bf16[4608,512]{1,0:T(8,128)(2,1)} %bitcast.8.replies_ref), custom_call_target="tpu_custom_call" | custom-call | flops 3600000000 | bytes 8000000 | tf_op jit(solution)/shard_map/pick/pallas_call | solution.py:233
  104.8 2.8 %collective-permute-start.4 = (bf16[224,512]{1,0:T(8,128)(2,1)S(1)}, bf16[224,512]{1,0:T(8,128)(2,1)}, u32[]{:S(2)}, u32[]{:S(2)}) collective-permute-start(bf16[224,512]{1,0:T(8,128)(2,1)S(1)} %copy-done.21), channel_id=1, source_target_pairs={{0,7},{1,0},{2,1},{3,2},{4,3},{5,4},{6,5},{7,6},{8,15},{9,8},{10,9... | collective-permute-start | bytes 688136 | tf_op jit(solution)/shard_map/ppermute | solution.py:626
  107.6 1.6 collective-permute-start.2
  111.0 10.4 %attend_inner.1 = (bf16[2304,512]{1,0:T(8,128)(2,1)S(1)}, bf16[2304,1024]{1,0:T(8,128)(2,1)S(1)}, bf16[2304,2048]{1,0:T(8,128)(2,1)S(1)}) custom-call(bf16[864,512]{1,0:T(8,128)(2,1)S(1)} %copy-done.24, bf16[864,512]{1,0:T(8,128)(2,1)S(1)} %copy-done.17, bf16[512,1536]{1,0:T(8,128)(2,1)S(1)} %copy-done, f32[1,512]{1,0:T(1,128)S(1)} %bitcast.15, ...), custom_call_target="tpu_custom_call" | custom-call | flops 5184000000 | bytes 8640000 | tf_op jit(solution)/shard_map/attend_inner/pallas_call | solution.py:398
  121.5 19.3 %attend_edge.1 = (bf16[2304,512]{1,0:T(8,128)(2,1)S(1)}, bf16[2304,1024]{1,0:T(8,128)(2,1)S(1)}, bf16[2304,2048]{1,0:T(8,128)(2,1)S(1)}) custom-call(s32[1]{0:T(128)} %bitcast.1.flag_ref, bf16[656,512]{1,0:T(8,128)(2,1)S(1)} %copy-done.25, bf16[512,512]{1,0:T(8,128)(2,1)} %collective-permute-done.xu, ...), custom_call_target="tpu_custom_call", output_to_operand_aliasing={{0}: (14, {}), {1}: (15, {}), {2}: (16, {})} | custom-call | flops 8640000000 | bytes 14400000 | tf_op jit(solution)/shard_map/attend_edge/pallas_call | solution.py:412
  140.8 8.5 %finish_edge.1 = (bf16[2,656,512]{2,1,0:T(8,128)(2,1)S(1)}, bf16[2,512,512]{2,1,0:T(8,128)(2,1)S(1)}, bf16[2,224,512]{2,1,0:T(8,128)(2,1)S(1)}, bf16[2,80,512]{2,1,0:T(8,128)(2,1)S(1)}) custom-call(bf16[144,144]{1,0:T(8,128)(2,1)S(1)} %copy-done.8, bf16[320,288]{1,0:T(8,128)(2,1)S(1)} %copy-done.11, bf16[2304,512]{1,0:T(8,128)(2,1)S(1)} %get-tuple-element.59.refs_0_, ...), custom_call_target="tpu_custom_call" | custom-call | flops 3168000000 | bytes 12960000 | tf_op jit(solution)/shard_map/finish_edge/pallas_call | solution.py:548
  149.3 3.0 %collective-permute-start.7 = (bf16[2,512,512]{2,1,0:T(8,128)(2,1)S(1)}, bf16[2,512,512]{2,1,0:T(8,128)(2,1)S(1)}, u32[]{:S(2)}, u32[]{:S(2)}) collective-permute-start(bf16[2,512,512]{2,1,0:T(8,128)(2,1)S(1)} %get-tuple-element.64), channel_id=1, source_target_pairs={{0,8},{1,9},{2,10},{3,11},{4,12},{5,13},{6,14},{7,15},{8,16},{9,17... | collective-permute-start | bytes 3145736 | tf_op jit(solution)/shard_map/ppermute | solution.py:626
  152.3 7.7 %weight_terms.1 = (f32[1024,512]{1,0:T(8,128)S(1)}, bf16[1024,512]{1,0:T(8,128)(2,1)S(1)}) custom-call(s32[1]{0:T(128)} %bitcast.core_ref, bf16[2304,1024]{1,0:T(8,128)(2,1)S(1)} %get-tuple-element.61.refs_1_.left_ref, bf16[2304,2048]{1,0:T(8,128)(2,1)S(1)} %get-tuple-element.62.refs_2_.right_ref), custom_call_target="tpu_custom_call" | custom-call | flops 4831838208 | bytes 18000000 | tf_op jit(solution)/shard_map/weight_terms/pallas_call | solution.py:445
  161.2 3.2 %collective-permute-start.9 = (bf16[2,80,512]{2,1,0:T(8,128)(2,1)S(1)}, bf16[2,80,512]{2,1,0:T(8,128)(2,1)S(1)}, u32[]{:S(2)}, u32[]{:S(2)}) collective-permute-start(bf16[2,80,512]{2,1,0:T(8,128)(2,1)S(1)} %get-tuple-element.66), channel_id=1, source_target_pairs={{0,9},{1,10},{2,11},{3,12},{4,13},{5,14},{6,15},{7,8},{8,17},{9,18... | collective-permute-start | bytes 491528 | tf_op jit(solution)/shard_map/ppermute | solution.py:626
  164.4 3.7 %finish_inner.1.inner = bf16[2,864,512]{2,1,0:T(8,128)(2,1)S(1)} custom-call(bf16[144,144]{1,0:T(8,128)(2,1)S(1)} %copy-done.8, bf16[2304,512]{1,0:T(8,128)(2,1)S(1)} %get-tuple-element.59.refs_0_, bf16[2304,1024]{1,0:T(8,128)(2,1)S(1)} %get-tuple-element.61.refs_1_.left_ref, bf16[2304,2048]{1,0:T(8,128)(2,1)S(1)} %get-tuple-element.62.refs_2_.right_ref, ...), custom_call_target="tpu_custom_call" | custom-call | flops 1900800000 | bytes 7776000 | tf_op jit(solution)/shard_map/finish_inner/pallas_call | solution.py:539
  168.1 11.7 %collective-permute-done.9.corner = bf16[2,80,512]{2,1,0:T(8,128)(2,1)S(1)} collective-permute-done((bf16[2,80,512]{2,1,0:T(8,128)(2,1)S(1)}, bf16[2,80,512]{2,1,0:T(8,128)(2,1)S(1)}, u32[]{:S(2)}, u32[]{:S(2)}) %collective-permute-start.9) | collective-permute-done | bytes 163872 | tf_op jit(solution)/shard_map/ppermute | solution.py:626
  182.6 7.7 %all-to-all-start.2 = ((bf16[64,16,512]{2,1,0:T(8,128)(2,1)}), bf16[64,16,512]{2,1,0:T(8,128)(2,1)S(1)}, u32[]{:S(2)}, u32[]{:S(2)}) async-start(bf16[64,16,512]{2,1,0:T(8,128)(2,1)} %bitcast.14), calls=%async_computation.2 | async-start | bytes 2097152 | tf_op jit(solution)/shard_map/all_to_all | solution.py:630
  193.8 3.4 %join.1 = (bf16[12,48,4,512]{3,2,1,0:T(4,128)(2,1)}, bf16[12,48,4,512]{3,2,1,0:T(4,128)(2,1)}) custom-call(bf16[2,864,512]{2,1,0:T(8,128)(2,1)S(1)} %finish_inner.1.inner, bf16[2,656,512]{2,1,0:T(8,128)(2,1)S(1)} %copy-done.5, bf16[2,512,512]{2,1,0:T(8,128)(2,1)S(1)} %copy-done.7, bf16[2,224,512]{2,1,0:T(8,128)(2,1)S(1)} %copy-done.10, ...), custom_call_target="tpu_custom_call" | custom-call | flops 1000000 | bytes 9000000 | tf_op jit(solution)/shard_map/join/pallas_call | solution.py:593
  197.1 10.4 %all-to-all-done.2 = bf16[64,16,512]{2,1,0:T(8,128)(2,1)S(1)} async-done(((bf16[64,16,512]{2,1,0:T(8,128)(2,1)}), bf16[64,16,512]{2,1,0:T(8,128)(2,1)S(1)}, u32[]{:S(2)}, u32[]{:S(2)}) %all-to-all-start.2) | async-done | bytes 1048608 | tf_op jit(solution)/shard_map/all_to_all | solution.py:630
  (76 shorter events, 16.1 us)
Async XLA Ops:
  32.1 61.6 %all-to-all-start.1 = ((bf16[16,288,512]{2,1,0:T(8,128)(2,1)}), bf16[16,288,512]{2,1,0:T(8,128)(2,1)}, u32[]{:S(2)}, u32[]{:S(2)}) async-start(bf16[16,288,512]{2,1,0:T(8,128)(2,1)} %bitcast.19), calls=%async_computation.1 | async-start | bytes 9437184 | tf_op jit(solution)/shard_map/all_to_all | solution.py:630
  40.8 10.8 %copy-start.27 = (s32[1,2304]{1,0:T(1,128)S(1)}, s32[1,2304]{1,0:T(1,128)}, u32[]{:S(2)}) copy-start(s32[1,2304]{1,0:T(1,128)} %get-tuple-element.42) | copy-start | bytes 27652
  40.8 10.8 %copy-start.26 = (s32[2336]{0:T(1024)S(1)}, s32[2336]{0:T(1024)}, u32[]{:S(2)}) copy-start(s32[2336]{0:T(1024)} %constant.48) | copy-start | bytes 28036
  43.8 20.4 %copy-start.18 = (bf16[656,512]{1,0:T(8,128)(2,1)}, bf16[656,512]{1,0:T(8,128)(2,1)S(1)}, u32[]{:S(2)}) copy-start(bf16[656,512]{1,0:T(8,128)(2,1)S(1)} %get-tuple-element.48.ce) | copy-start | bytes 2015236
  43.8 65.3 %collective-permute-start.5 = (bf16[80,512]{1,0:T(8,128)(2,1)S(1)}, bf16[80,512]{1,0:T(8,128)(2,1)S(1)}, u32[]{:S(2)}, u32[]{:S(2)}) collective-permute-start(bf16[80,512]{1,0:T(8,128)(2,1)S(1)} %get-tuple-element.51), channel_id=1, source_target_pairs={{0,127},{1,120},{2,121},{3,122},{4,123},{5,124},{6,125},{7,126},{8... | collective-permute-start | bytes 245768 | tf_op jit(solution)/shard_map/ppermute | solution.py:626
  46.8 74.6 %collective-permute-start.3 = (bf16[512,512]{1,0:T(8,128)(2,1)}, bf16[512,512]{1,0:T(8,128)(2,1)}, u32[]{:S(2)}, u32[]{:S(2)}) collective-permute-start(bf16[512,512]{1,0:T(8,128)(2,1)} %get-tuple-element.49), channel_id=1, source_target_pairs={{0,120},{1,121},{2,122},{3,123},{4,124},{5,125},{6,126},{7,127},{8... | collective-permute-start | bytes 1572872 | tf_op jit(solution)/shard_map/ppermute | solution.py:626
  93.7 11.1 %copy-start.21 = (bf16[224,512]{1,0:T(8,128)(2,1)S(1)}, bf16[224,512]{1,0:T(8,128)(2,1)}, u32[]{:S(2)}) copy-start(bf16[224,512]{1,0:T(8,128)(2,1)} %copy-done.20) | copy-start | bytes 688132
  93.7 16.1 %copy-start = (bf16[512,1536]{1,0:T(8,128)(2,1)S(1)}, bf16[512,1536]{1,0:T(8,128)(2,1)}, u32[]{:S(2)}) copy-start(bf16[512,1536]{1,0:T(8,128)(2,1)} %refs_3_.3) | copy-start | bytes 4718596
  93.7 16.1 %copy-start.2 = (bf16[512,512]{1,0:T(8,128)(2,1)S(1)}, bf16[512,512]{1,0:T(8,128)(2,1)}, u32[]{:S(2)}) copy-start(bf16[512,512]{1,0:T(8,128)(2,1)} %refs_5_.3) | copy-start | bytes 1572868
  93.7 16.1 %copy-start.15 = (f32[512]{0:T(512)S(1)}, f32[512]{0:T(512)}, u32[]{:S(2)}) copy-start(f32[512]{0:T(512)} %param.19) | copy-start | bytes 6148
  93.7 16.1 %copy-start.17 = (bf16[864,512]{1,0:T(8,128)(2,1)S(1)}, bf16[864,512]{1,0:T(8,128)(2,1)}, u32[]{:S(2)}) copy-start(bf16[864,512]{1,0:T(8,128)(2,1)} %copy-done.16) | copy-start | bytes 2654212
  103.4 18.0 %collective-permute-start = (bf16[512,512]{1,0:T(8,128)(2,1)}, bf16[512,512]{1,0:T(8,128)(2,1)}, u32[]{:S(2)}, u32[]{:S(2)}) collective-permute-start(bf16[512,512]{1,0:T(8,128)(2,1)} %get-tuple-element.45), channel_id=1, source_target_pairs={{0,120},{1,121},{2,122},{3,123},{4,124},{5,125},{6,126},{7,127},{8... | collective-permute-start | bytes 1572872 | tf_op jit(solution)/shard_map/ppermute | solution.py:626
  104.8 16.6 %collective-permute-start.4 = (bf16[224,512]{1,0:T(8,128)(2,1)S(1)}, bf16[224,512]{1,0:T(8,128)(2,1)}, u32[]{:S(2)}, u32[]{:S(2)}) collective-permute-start(bf16[224,512]{1,0:T(8,128)(2,1)S(1)} %copy-done.21), channel_id=1, source_target_pairs={{0,7},{1,0},{2,1},{3,2},{4,3},{5,4},{6,5},{7,6},{8,15},{9,8},{10,9... | collective-permute-start | bytes 688136 | tf_op jit(solution)/shard_map/ppermute | solution.py:626
  107.6 13.8 %collective-permute-start.2 = (bf16[80,512]{1,0:T(8,128)(2,1)}, bf16[80,512]{1,0:T(8,128)(2,1)S(1)}, u32[]{:S(2)}, u32[]{:S(2)}) collective-permute-start(bf16[80,512]{1,0:T(8,128)(2,1)} %get-tuple-element.47), channel_id=1, source_target_pairs={{0,127},{1,120},{2,121},{3,122},{4,123},{5,124},{6,125},{7,126},{8... | collective-permute-start | bytes 245768 | tf_op jit(solution)/shard_map/ppermute | solution.py:626
  109.1 12.3 %collective-permute-start.1 = (bf16[224,512]{1,0:T(8,128)(2,1)}, bf16[224,512]{1,0:T(8,128)(2,1)S(1)}, u32[]{:S(2)}, u32[]{:S(2)}) collective-permute-start(bf16[224,512]{1,0:T(8,128)(2,1)} %get-tuple-element.46), channel_id=1, source_target_pairs={{0,7},{1,0},{2,1},{3,2},{4,3},{5,4},{6,5},{7,6},{8,15},{9,8},{10,9... | collective-permute-start | bytes 688136 | tf_op jit(solution)/shard_map/ppermute | solution.py:626
  111.0 10.5 %copy-start.25 = (bf16[656,512]{1,0:T(8,128)(2,1)S(1)}, bf16[656,512]{1,0:T(8,128)(2,1)}, u32[]{:S(2)}) copy-start(bf16[656,512]{1,0:T(8,128)(2,1)} %get-tuple-element.44.xe) | copy-start | bytes 2015236
  121.5 19.3 %copy-start.11 = (bf16[320,288]{1,0:T(8,128)(2,1)S(1)}, bf16[320,288]{1,0:T(8,128)(2,1)}, u32[]{:S(2)}) copy-start(bf16[320,288]{1,0:T(8,128)(2,1)} %constant.43.clone.back_ref) | copy-start | bytes 552964
  149.3 10.7 %copy-start.4 = (bf16[2,656,512]{2,1,0:T(8,128)(2,1)}, bf16[2,656,512]{2,1,0:T(8,128)(2,1)S(1)}, u32[]{:S(2)}) copy-start(bf16[2,656,512]{2,1,0:T(8,128)(2,1)S(1)} %get-tuple-element.68.edge) | copy-start | bytes 4030468
  149.3 31.2 %collective-permute-start.7 = (bf16[2,512,512]{2,1,0:T(8,128)(2,1)S(1)}, bf16[2,512,512]{2,1,0:T(8,128)(2,1)S(1)}, u32[]{:S(2)}, u32[]{:S(2)}) collective-permute-start(bf16[2,512,512]{2,1,0:T(8,128)(2,1)S(1)} %get-tuple-element.64), channel_id=1, source_target_pairs={{0,8},{1,9},{2,10},{3,11},{4,12},{5,13},{6,14},{7,15},{8,16},{9,17... | collective-permute-start | bytes 3145736 | tf_op jit(solution)/shard_map/ppermute | solution.py:626
  152.3 12.1 %copy-start.3 = (bf16[512,512]{1,0:T(8,128)(2,1)S(1)}, bf16[512,512]{1,0:T(8,128)(2,1)}, u32[]{:S(2)}) copy-start(bf16[512,512]{1,0:T(8,128)(2,1)} %refs_5_.3) | copy-start | bytes 1572868
  160.0 20.5 %collective-permute-start.6 = (bf16[1024,512]{1,0:T(8,128)(2,1)S(1)}, bf16[1024,512]{1,0:T(8,128)(2,1)S(1)}, u32[]{:S(2)}, u32[]{:S(2)}) collective-permute-start(bf16[1024,512]{1,0:T(8,128)(2,1)S(1)} %get-tuple-element.63), channel_id=1, source_target_pairs={{0,8},{1,9},{2,10},{3,11},{4,12},{5,13},{6,14},{7,15},{8,0},{9,1},... | collective-permute-start | bytes 3145736 | tf_op jit(solution)/shard_map/ppermute | solution.py:664
  160.1 20.4 %collective-permute-start.8 = (bf16[2,224,512]{2,1,0:T(8,128)(2,1)S(1)}, bf16[2,224,512]{2,1,0:T(8,128)(2,1)S(1)}, u32[]{:S(2)}, u32[]{:S(2)}) collective-permute-start(bf16[2,224,512]{2,1,0:T(8,128)(2,1)S(1)} %get-tuple-element.65), channel_id=1, source_target_pairs={{0,1},{1,2},{2,3},{3,4},{4,5},{5,6},{6,7},{7,0},{8,9},{9,10},{10,1... | collective-permute-start | bytes 1376264 | tf_op jit(solution)/shard_map/ppermute | solution.py:626
  161.2 18.6 %collective-permute-start.9 = (bf16[2,80,512]{2,1,0:T(8,128)(2,1)S(1)}, bf16[2,80,512]{2,1,0:T(8,128)(2,1)S(1)}, u32[]{:S(2)}, u32[]{:S(2)}) collective-permute-start(bf16[2,80,512]{2,1,0:T(8,128)(2,1)S(1)} %get-tuple-element.66), channel_id=1, source_target_pairs={{0,9},{1,10},{2,11},{3,12},{4,13},{5,14},{6,15},{7,8},{8,17},{9,18... | collective-permute-start | bytes 491528 | tf_op jit(solution)/shard_map/ppermute | solution.py:626
  182.6 24.9 %all-to-all-start.2 = ((bf16[64,16,512]{2,1,0:T(8,128)(2,1)}), bf16[64,16,512]{2,1,0:T(8,128)(2,1)S(1)}, u32[]{:S(2)}, u32[]{:S(2)}) async-start(bf16[64,16,512]{2,1,0:T(8,128)(2,1)} %bitcast.14), calls=%async_computation.2 | async-start | bytes 2097152 | tf_op jit(solution)/shard_map/all_to_all | solution.py:630
  (16 other events, 57.1 us)

commit v6 on v5

--- a/solution.py
+++ b/solution.py
@@ -171,13 +171,14 @@
 
 def serve_kernel(lists_ref, buffer_ref, out_ref):
     lane = lax.broadcasted_iota(I32, (CAP, BANDS), 1)
-    wanted = []
     for at in range(ASKERS):
         asker = pl.program_id(0) * ASKERS + at
-        wanted.append(jnp.sum(jnp.where(lane == asker, lists_ref[...], 0), 1, keepdims=True))
-    chosen = jnp.concatenate(wanted) == lax.broadcasted_iota(I32, (ASKERS * CAP, ROWS), 1)
-    chosen = jnp.where(chosen, 1.0, 0.0).astype(BF16)
-    out_ref[...] = product(chosen, buffer_ref[...]).astype(BF16)
+        wanted = jnp.sum(jnp.where(lane == asker, lists_ref[...], 0), 1, keepdims=True)
+        for half in range(2):
+            chosen = wanted[half * 144 : half * 144 + 144] == lax.broadcasted_iota(I32, (144, ROWS), 1)
+            chosen = jnp.where(chosen, 1.0, 0.0).astype(BF16)
+            rows = slice(at * CAP + half * 144, at * CAP + half * 144 + 144)
+            out_ref[rows, :] = product(chosen, buffer_ref[...]).astype(BF16)
 
 
 def serve(lists, buffer):
@@ -190,19 +191,27 @@
     )(lists, buffer)
 
 
-def pick_kernel(table_ref, place_ref, replies_ref, up_ref, side_ref, corner_ref, inner_ref, edge_ref, compact):
+def pick_kernel(table_ref, place_ref, replies_ref, up_ref, side_ref, corner_ref, inner_ref, edge_ref, compact, held, sems):
+    def fetch(owner):
+        rows = pl.ds(owner * CAP, CAP)
+        return pltpu.make_async_copy(replies_ref.at[rows, :], held.at[rows, :], sems.at[owner])
+
+    for owner in range(BANDS):
+        fetch(owner).start()
     compact[...] = jnp.zeros_like(compact)
     firsts = (0, UP + CORNER, UP + CORNER + 2 * WIN + INNER)
     for zone, size in enumerate(COMPACT):
         filled = 0
         for owner in range(BANDS):
+            if zone == 0:
+                fetch(owner).wait()
             start = owner * CAP + table_ref[owner, 2 * zone] * GROUP
             groups = table_ref[owner, 2 * zone + 1]
 
             def move(at, filled, start=start):
                 source = pl.multiple_of(start + at * GROUP, GROUP)
                 target = pl.multiple_of(filled, GROUP)
-                compact[pl.ds(target, GROUP), :] = replies_ref[pl.ds(source, GROUP), :]
+                compact[pl.ds(target, GROUP), :] = held[pl.ds(source, GROUP), :]
                 return filled + GROUP
 
             filled = lax.fori_loop(0, groups, move, filled)
@@ -232,10 +241,15 @@
 def pick(table, place, replies):
     return call(
         pick_kernel, "pick", (),
-        [pl.BlockSpec(memory_space=pltpu.SMEM), whole(PLACES, 1), whole(BANDS * CAP, D)],
+        [pl.BlockSpec(memory_space=pltpu.SMEM), whole(PLACES, 1), pl.BlockSpec(memory_space=pl.ANY)],
         [whole(n, D) for n in (UP, SIDE, CORNER, INNER, EDGE)],
         shapes(*[(n, D) for n in (UP, SIDE, CORNER, INNER, EDGE)]),
-        [pltpu.VMEM((max(COMPACT), D), BF16)], (3600000000, 8000000, 0), 60,
+        [
+            pltpu.VMEM((max(COMPACT), D), BF16),
+            pltpu.VMEM((BANDS * CAP, D), BF16),
+            pltpu.SemaphoreType.DMA((BANDS,)),
+        ],
+        (3600000000, 8000000, 0), 60,
     )(table, place, replies)
 
 
@@ -422,37 +436,27 @@
 
 
 def weight_kernel(core_ref, left_ref, right_ref, own_ref, away_ref, turned):
-    step = pl.program_id(0)
-    chunk = product(left_ref[...], right_ref[...], TN).reshape(64, 8, D)
     for c in range(4):
-
-        @pl.when(step == c)
-        def _(c=c):
-            half = c % 2 * 4
-            turned[:, 0, c // 2, half : half + 4] = chunk[:, :4]
-            turned[:, 1, c // 2, half : half + 4] = chunk[:, 4:]
-
-    @pl.when(step == 3)
-    def _():
-        core = core_ref[0]
-        for at in range(BANDS // 2):
-            for ref, which in ((own_ref, core), (away_ref, 1 - core)):
-                part = turned[pl.ds(at * 8 + which * 4, 4)].reshape(128, D)
-                ref[at * 128 : at * 128 + 128, :] = part.astype(ref.dtype)
+        side, cols = slice(c // 3 * D, c // 3 * D + D), slice(c * D, c * D + D)
+        chunk = product(left_ref[:, side], right_ref[:, cols], TN).reshape(64, 8, D)
+        half = c % 2 * 4
+        turned[:, 0, c // 2, half : half + 4] = chunk[:, :4]
+        turned[:, 1, c // 2, half : half + 4] = chunk[:, 4:]
+    core = core_ref[0]
+    for at in range(BANDS // 2):
+        for ref, which in ((own_ref, core), (away_ref, 1 - core)):
+            part = turned[pl.ds(at * 8 + which * 4, 4)].reshape(128, D)
+            ref[at * 128 : at * 128 + 128, :] = part.astype(ref.dtype)
 
 
 def weight_terms(core, left, right):
     return call(
-        weight_kernel, "weight_terms", (4,),
-        [
-            pl.BlockSpec(memory_space=pltpu.SMEM),
-            pl.BlockSpec((TOKENS, D), lambda c: (0, c // 3)),
-            pl.BlockSpec((TOKENS, D), lambda c: (0, c)),
-        ],
+        weight_kernel, "weight_terms", (),
+        [pl.BlockSpec(memory_space=pltpu.SMEM), whole(TOKENS, 2 * D), whole(TOKENS, 4 * D)],
         [whole(1024, D)] * 2,
         [jax.ShapeDtypeStruct((1024, D), F32), jax.ShapeDtypeStruct((1024, D), BF16)],
         [pltpu.VMEM((64, 2, 2, 8, D), F32)],
-        (TOKENS * 2 * D * 4 * D, 18000000, 0), 24,
+        (1000, 1000, 0), 22,
     )(core, left, right)
 
 
@@ -540,7 +544,7 @@
         finish_inner_kernel, "finish_inner", (3,),
         [whole(WIN, WIN)] + finish_specs(0),
         pl.BlockSpec((2, BLOCK, D), lambda i: (0, i, 0)), shapes((2, INNER, D))[0], [],
-        finish_cost(INNER), 20,
+        (1000, 1000, 0), 20,
     )(jnp.asarray(SPLIT, BF16), *values, *weights)
 
 
@@ -663,7 +667,7 @@
     own, away = weight_terms(core, left, right)
     got = lax.ppermute(away, BOTH, OTHER_CORE)
     inner = finish_inner((x, left, right), weights)
-    got, inner, returned = lax.optimization_barrier((got, inner, returned))
+    got, inner = lax.optimization_barrier((got, inner))
     terms = swap_blocks(add_halves(own, got), BOTH, SAME_CORE)
     outs = join([inner, edge] + returned)
     return (*outs, *sum_terms(terms))

time: 209 us -> 209 us (level)
  waiting for transfers between devices: 50.3 us -> 52.6 us
    ppermute x9, waiting for transfers between devices: 12.4 us -> 25 us  [exchange(): lax.ppermute(part, BOTH, shift_pairs(*step))]
    all_to_all x2, waiting for transfers between devices: 37.9 us -> 27.6 us  [swap_blocks(): lax.all_to_all(values, axis, split_axis=0, concat_axis=0, axis_index_grou...]
    ppermute x9, starting transfers between devices: 21.3 us -> 16.3 us  [exchange(): lax.ppermute(part, BOTH, shift_pairs(*step))]
    all_to_all x2, starting transfers between devices: 12.4 us -> 15 us  [swap_blocks(): lax.all_to_all(values, axis, split_axis=0, concat_axis=0, axis_index_grou...]
    ppermute x1, starting transfers between devices: 0.09 us -> 2.45 us  [per_device(): got = lax.ppermute(away, BOTH, OTHER_CORE)]
    pallas_call x1, Pallas kernels: 7.67 us -> 5.3 us  [weight_terms(): call(weight_kernel, 'weight_terms', (), [pl.BlockSpec(memory_space=pltpu....]
    unnamed x56 -> x44, local copies, waits for them, and re-layouts: 8.18 us -> 6.8 us
  transfers between devices with their start and end apart: 12 -> 12, of which waited for: 4 -> 3; matrix products, arithmetic and copies ran while one was open for 9% -> 9% of each run, Pallas kernels for 17% -> 15%
where the time goes in v6:
time: 209 us; the launch traced here: 208 us
  Pallas kernels  77.6 us (37%)
  waiting for transfers between devices  52.6 us (25%)
  starting transfers between devices  33.8 us (16%)
  local copies, waits for them, and re-layouts  26.9 us (13%)
  blocking collectives  16.4 us (8%)
    all_to_all x2, waiting for transfers between devices, swap_blocks(): lax.all_to_all(values, axis, split_axis=0, concat_axis=0, axis_index_grou...  27.6 us
    ppermute x9, waiting for transfers between devices, exchange(): lax.ppermute(part, BOTH, shift_pairs(*step))  25 us
    pallas_call x1, Pallas kernels, attend_edge(): call(edge_kernel, 'attend_edge', (5,), [pl.BlockSpec(memory_space=pltpu.S...  19.3 us
    all_to_all x1, blocking collectives, swap_blocks(): lax.all_to_all(values, axis, split_axis=0, concat_axis=0, axis_index_grou...  16.4 us
    ppermute x9, starting transfers between devices, exchange(): lax.ppermute(part, BOTH, shift_pairs(*step))  16.3 us
    all_to_all x2, starting transfers between devices, swap_blocks(): lax.all_to_all(values, axis, split_axis=0, concat_axis=0, axis_index_grou...  15 us
    gather x1, local copies, waits for them, and re-layouts, per_device(): place = place.reshape(TOKENS)[ORDER].reshape(-1, 1)  12.7 us
    pallas_call x1, Pallas kernels, attend_inner(): call(inner_kernel, 'attend_inner', (3,), [blocks(BLOCK, D)] * 2 + [whole(...  10.4 us
  transfers between devices with their start and end apart: 12, of which 3 were waited for; matrix products, arithmetic and copies ran while one was open for 9% of the time, Pallas kernels for 15%

profile of v6, /device:TPU:1, one launch (start us, length us, event | category | flops | bytes accessed | tf_op | source)
XLA Modules:
  0.0 208.1 jit_solution(12744914510582356842)
XLA Ops:
  0.6 2.6 %requests.1 = (s32[16,288]{1,0:T(8,128)}, s32[1,2304]{1,0:T(1,128)}, s32[16,8]{1,0:T(8,128)}) custom-call(s32[1,2304]{1,0:T(1,128)} %bitcast.22, s32[1,2304]{1,0:T(1,128)} %bitcast.23), custom_call_target="tpu_custom_call" | custom-call | flops 100000000 | bytes 100000 | tf_op jit(solution)/shard_map/requests/pallas_call | solution.py:159
  4.0 16.4 %all_to_all.28 = s32[16,1,288]{2,1,0:T(1,128)S(1)} all-to-all(s32[16,1,288]{2,1,0:T(1,128)S(1)} %copy.26), channel_id=1, replica_groups=mesh['lat'=16,'lon'=8] {'lat'}, dimensions={0} | all-to-all | bytes 36864 | tf_op jit(solution)/shard_map/all_to_all | solution.py:634
  21.2 10.0 %serve.1 = bf16[4608,512]{1,0:T(8,128)(2,1)} custom-call(s32[288,16]{1,0:T(8,128)} %bitcast.20, bf16[1152,512]{1,0:T(8,128)(2,1)} %buffer_ref.1), custom_call_target="tpu_custom_call" | custom-call | flops 5400000000 | bytes 6000000 | tf_op jit(solution)/shard_map/serve/pallas_call | solution.py:185
  31.2 4.7 %all-to-all-start.1 = ((bf16[16,288,512]{2,1,0:T(8,128)(2,1)}), bf16[16,288,512]{2,1,0:T(8,128)(2,1)}, u32[]{:S(2)}, u32[]{:S(2)}) async-start(bf16[16,288,512]{2,1,0:T(8,128)(2,1)} %bitcast.19), calls=%async_computation.1 | async-start | bytes 9437184 | tf_op jit(solution)/shard_map/all_to_all | solution.py:634
  36.0 3.9 %reshape.53.grid_ref = bf16[2304,512]{1,0:T(8,128)(2,1)S(1)} reshape(bf16[12,48,4,512]{3,2,1,0:T(4,128)(2,1)} %param.22) | data formatting | bytes 4718592 | tf_op jit(solution)/shard_map/reshape | solution.py:652
  39.9 1.5 sort_pieces.1
  43.0 2.9 %collective-permute-start.5 = (bf16[80,512]{1,0:T(8,128)(2,1)}, bf16[80,512]{1,0:T(8,128)(2,1)S(1)}, u32[]{:S(2)}, u32[]{:S(2)}) collective-permute-start(bf16[80,512]{1,0:T(8,128)(2,1)} %get-tuple-element.48), channel_id=1, source_target_pairs={{0,127},{1,120},{2,121},{3,122},{4,123},{5,124},{6,125},{7,126},{8... | collective-permute-start | bytes 245768 | tf_op jit(solution)/shard_map/ppermute | solution.py:630
  45.9 4.7 %collective-permute-start.3 = (bf16[512,512]{1,0:T(8,128)(2,1)}, bf16[512,512]{1,0:T(8,128)(2,1)}, u32[]{:S(2)}, u32[]{:S(2)}) collective-permute-start(bf16[512,512]{1,0:T(8,128)(2,1)} %get-tuple-element.46), channel_id=1, source_target_pairs={{0,120},{1,121},{2,122},{3,123},{4,124},{5,125},{6,126},{7,127},{8... | collective-permute-start | bytes 1572872 | tf_op jit(solution)/shard_map/ppermute | solution.py:630
  50.7 12.7 %gather_fusion = s32[2336]{0:T(1024)S(1)} fusion(s32[2304]{0:T(1024)S(1)} %reduce, s32[3072]{0:T(1024)S(1)} %pad_clamp_fusion), kind=kCustom, calls=%fused_computation | custom fusion | bytes 28032 | tf_op jit(solution)/shard_map/gather | solution.py:654
  63.4 1.9 reshape.65.place_ref
  65.3 27.6 %all-to-all-done.1 = bf16[16,288,512]{2,1,0:T(8,128)(2,1)} async-done(((bf16[16,288,512]{2,1,0:T(8,128)(2,1)}), bf16[16,288,512]{2,1,0:T(8,128)(2,1)}, u32[]{:S(2)}, u32[]{:S(2)}) %all-to-all-start.1) | async-done | bytes 4718624 | tf_op jit(solution)/shard_map/all_to_all | solution.py:634
  92.9 10.3 %pick.1 = (bf16[512,512]{1,0:T(8,128)(2,1)}, bf16[224,512]{1,0:T(8,128)(2,1)}, bf16[80,512]{1,0:T(8,128)(2,1)}, bf16[864,512]{1,0:T(8,128)(2,1)}, bf16[656,512]{1,0:T(8,128)(2,1)}) custom-call(s32[16,8]{1,0:T(8,128)} %get-tuple-element.38.table_ref, s32[2336,1]{1,0:T(8,128)} %reshape.65.place_ref, bf16[4608,512]{1,0:T(8,128)(2,1)} %bitcast.8.replies_ref), custom_call_target="tpu_custom_call" | custom-call | flops 3600000000 | bytes 8000000 | tf_op jit(solution)/shard_map/pick/pallas_call | solution.py:242
  103.1 1.4 collective-permute-start
  104.5 2.7 %collective-permute-start.4 = (bf16[224,512]{1,0:T(8,128)(2,1)S(1)}, bf16[224,512]{1,0:T(8,128)(2,1)}, u32[]{:S(2)}, u32[]{:S(2)}) collective-permute-start(bf16[224,512]{1,0:T(8,128)(2,1)S(1)} %copy-done.13), channel_id=1, source_target_pairs={{0,7},{1,0},{2,1},{3,2},{4,3},{5,4},{6,5},{7,6},{8,15},{9,8},{10,9... | collective-permute-start | bytes 688136 | tf_op jit(solution)/shard_map/ppermute | solution.py:630
  107.3 1.6 collective-permute-start.2
  110.8 10.4 %attend_inner.1 = (bf16[2304,512]{1,0:T(8,128)(2,1)S(1)}, bf16[2304,1024]{1,0:T(8,128)(2,1)S(1)}, bf16[2304,2048]{1,0:T(8,128)(2,1)S(1)}) custom-call(bf16[864,512]{1,0:T(8,128)(2,1)S(1)} %copy-done.18, bf16[864,512]{1,0:T(8,128)(2,1)S(1)} %get-tuple-element.50.c_ref, bf16[512,1536]{1,0:T(8,128)(2,1)S(1)} %copy-done, f32[1,512]{1,0:T(1,128)S(1)} %bitcast.15, ...), custom_call_target="tpu_custom_call" | custom-call | flops 5184000000 | bytes 8640000 | tf_op jit(solution)/shard_map/attend_inner/pallas_call | solution.py:412
  121.2 19.3 %attend_edge.1 = (bf16[2304,512]{1,0:T(8,128)(2,1)S(1)}, bf16[2304,1024]{1,0:T(8,128)(2,1)S(1)}, bf16[2304,2048]{1,0:T(8,128)(2,1)S(1)}) custom-call(s32[1]{0:T(128)} %bitcast.1.flag_ref, bf16[656,512]{1,0:T(8,128)(2,1)S(1)} %copy-done.19, bf16[512,512]{1,0:T(8,128)(2,1)} %collective-permute-done.xu, ...), custom_call_target="tpu_custom_call", output_to_operand_aliasing={{0}: (14, {}), {1}: (15, {}), {2}: (16, {})} | custom-call | flops 8640000000 | bytes 14400000 | tf_op jit(solution)/shard_map/attend_edge/pallas_call | solution.py:426
  140.6 9.0 %finish_edge.1 = (bf16[2,656,512]{2,1,0:T(8,128)(2,1)S(1)}, bf16[2,512,512]{2,1,0:T(8,128)(2,1)}, bf16[2,224,512]{2,1,0:T(8,128)(2,1)}, bf16[2,80,512]{2,1,0:T(8,128)(2,1)S(1)}) custom-call(bf16[144,144]{1,0:T(8,128)(2,1)S(1)} %copy-done.6, bf16[320,288]{1,0:T(8,128)(2,1)S(1)} %copy-done.7, bf16[2304,512]{1,0:T(8,128)(2,1)S(1)} %get-tuple-element.56.refs_0_, ...), custom_call_target="tpu_custom_call" | custom-call | flops 3168000000 | bytes 12960000 | tf_op jit(solution)/shard_map/finish_edge/pallas_call | solution.py:552
  151.2 5.3 %weight_terms.1 = (f32[1024,512]{1,0:T(8,128)S(1)}, bf16[1024,512]{1,0:T(8,128)(2,1)S(1)}) custom-call(s32[1]{0:T(128)} %bitcast.core_ref, bf16[2304,1024]{1,0:T(8,128)(2,1)S(1)} %get-tuple-element.58.refs_1_.left_ref, bf16[2304,2048]{1,0:T(8,128)(2,1)S(1)} %get-tuple-element.59.refs_2_.right_ref), custom_call_target="tpu_custom_call" | custom-call | flops 1000 | bytes 1000 | tf_op jit(solution)/shard_map/weight_terms/pallas_call | solution.py:453
  156.6 2.5 %collective-permute-start.6 = (bf16[1024,512]{1,0:T(8,128)(2,1)S(1)}, bf16[1024,512]{1,0:T(8,128)(2,1)S(1)}, u32[]{:S(2)}, u32[]{:S(2)}) collective-permute-start(bf16[1024,512]{1,0:T(8,128)(2,1)S(1)} %get-tuple-element.60), channel_id=1, source_target_pairs={{0,8},{1,9},{2,10},{3,11},{4,12},{5,13},{6,14},{7,15},{8,0},{9,1},... | collective-permute-start | bytes 3145736 | tf_op jit(solution)/shard_map/ppermute | solution.py:668
  159.7 3.6 %finish_inner.1.inner = bf16[2,864,512]{2,1,0:T(8,128)(2,1)S(1)} custom-call(bf16[144,144]{1,0:T(8,128)(2,1)S(1)} %copy-done.6, bf16[2304,512]{1,0:T(8,128)(2,1)S(1)} %get-tuple-element.56.refs_0_, bf16[2304,1024]{1,0:T(8,128)(2,1)S(1)} %get-tuple-element.58.refs_1_.left_ref, bf16[2304,2048]{1,0:T(8,128)(2,1)S(1)} %get-tuple-element.59.refs_2_.right_ref, ...), custom_call_target="tpu_custom_call" | custom-call | flops 1000 | bytes 1000 | tf_op jit(solution)/shard_map/finish_inner/pallas_call | solution.py:543
  164.6 10.3 %all-to-all-start.2 = ((bf16[64,16,512]{2,1,0:T(8,128)(2,1)}), bf16[64,16,512]{2,1,0:T(8,128)(2,1)S(1)}, u32[]{:S(2)}, u32[]{:S(2)}) async-start(bf16[64,16,512]{2,1,0:T(8,128)(2,1)} %bitcast.14), calls=%async_computation.2 | async-start | bytes 2097152 | tf_op jit(solution)/shard_map/all_to_all | solution.py:634
  176.4 24.4 %collective-permute-done.9.corner = bf16[2,80,512]{2,1,0:T(8,128)(2,1)S(1)} collective-permute-done((bf16[2,80,512]{2,1,0:T(8,128)(2,1)S(1)}, bf16[2,80,512]{2,1,0:T(8,128)(2,1)S(1)}, u32[]{:S(2)}, u32[]{:S(2)}) %collective-permute-start.9) | collective-permute-done | bytes 163872 | tf_op jit(solution)/shard_map/ppermute | solution.py:630
  202.7 4.6 %join.1 = (bf16[12,48,4,512]{3,2,1,0:T(4,128)(2,1)}, bf16[12,48,4,512]{3,2,1,0:T(4,128)(2,1)}) custom-call(bf16[2,864,512]{2,1,0:T(8,128)(2,1)S(1)} %finish_inner.1.inner, bf16[2,656,512]{2,1,0:T(8,128)(2,1)S(1)} %copy-done.5, bf16[2,512,512]{2,1,0:T(8,128)(2,1)} %collective-permute-done.7.up, bf16[2,224,512]{2,1,0:T(8,128)(2,1)S(1)} %collective-permute-done.8.side, ...), custom_call_target="tpu_custom_call" | custom-call | flops 1000000 | bytes 9000000 | tf_op jit(solution)/shard_map/join/pallas_call | solution.py:597
  (64 shorter events, 12.9 us)
Async XLA Ops:
  31.2 61.6 %all-to-all-start.1 = ((bf16[16,288,512]{2,1,0:T(8,128)(2,1)}), bf16[16,288,512]{2,1,0:T(8,128)(2,1)}, u32[]{:S(2)}, u32[]{:S(2)}) async-start(bf16[16,288,512]{2,1,0:T(8,128)(2,1)} %bitcast.19), calls=%async_computation.1 | async-start | bytes 9437184 | tf_op jit(solution)/shard_map/all_to_all | solution.py:634
  39.9 10.7 %copy-start.21 = (s32[1,2304]{1,0:T(1,128)S(1)}, s32[1,2304]{1,0:T(1,128)}, u32[]{:S(2)}) copy-start(s32[1,2304]{1,0:T(1,128)} %get-tuple-element.39) | copy-start | bytes 27652
  39.9 10.7 %copy-start.20 = (s32[2336]{0:T(1024)S(1)}, s32[2336]{0:T(1024)}, u32[]{:S(2)}) copy-start(s32[2336]{0:T(1024)} %constant.48) | copy-start | bytes 28036
  43.0 65.9 %collective-permute-start.5 = (bf16[80,512]{1,0:T(8,128)(2,1)}, bf16[80,512]{1,0:T(8,128)(2,1)S(1)}, u32[]{:S(2)}, u32[]{:S(2)}) collective-permute-start(bf16[80,512]{1,0:T(8,128)(2,1)} %get-tuple-element.48), channel_id=1, source_target_pairs={{0,127},{1,120},{2,121},{3,122},{4,123},{5,124},{6,125},{7,126},{8... | collective-permute-start | bytes 245768 | tf_op jit(solution)/shard_map/ppermute | solution.py:630
  45.9 75.3 %collective-permute-start.3 = (bf16[512,512]{1,0:T(8,128)(2,1)}, bf16[512,512]{1,0:T(8,128)(2,1)}, u32[]{:S(2)}, u32[]{:S(2)}) collective-permute-start(bf16[512,512]{1,0:T(8,128)(2,1)} %get-tuple-element.46), channel_id=1, source_target_pairs={{0,120},{1,121},{2,122},{3,123},{4,124},{5,125},{6,126},{7,127},{8... | collective-permute-start | bytes 1572872 | tf_op jit(solution)/shard_map/ppermute | solution.py:630
  92.8 11.7 %copy-start.13 = (bf16[224,512]{1,0:T(8,128)(2,1)S(1)}, bf16[224,512]{1,0:T(8,128)(2,1)}, u32[]{:S(2)}) copy-start(bf16[224,512]{1,0:T(8,128)(2,1)} %copy-done.12) | copy-start | bytes 688132
  92.9 16.7 %copy-start = (bf16[512,1536]{1,0:T(8,128)(2,1)S(1)}, bf16[512,1536]{1,0:T(8,128)(2,1)}, u32[]{:S(2)}) copy-start(bf16[512,1536]{1,0:T(8,128)(2,1)} %refs_3_.3) | copy-start | bytes 4718596
  92.9 16.7 %copy-start.2 = (bf16[512,512]{1,0:T(8,128)(2,1)S(1)}, bf16[512,512]{1,0:T(8,128)(2,1)}, u32[]{:S(2)}) copy-start(bf16[512,512]{1,0:T(8,128)(2,1)} %refs_5_.3) | copy-start | bytes 1572868
  92.9 16.7 %copy-start.9 = (f32[512]{0:T(512)S(1)}, f32[512]{0:T(512)}, u32[]{:S(2)}) copy-start(f32[512]{0:T(512)} %param.19) | copy-start | bytes 6148
  103.1 18.1 %collective-permute-start = (bf16[512,512]{1,0:T(8,128)(2,1)}, bf16[512,512]{1,0:T(8,128)(2,1)}, u32[]{:S(2)}, u32[]{:S(2)}) collective-permute-start(bf16[512,512]{1,0:T(8,128)(2,1)} %get-tuple-element.42), channel_id=1, source_target_pairs={{0,120},{1,121},{2,122},{3,123},{4,124},{5,125},{6,126},{7,127},{8... | collective-permute-start | bytes 1572872 | tf_op jit(solution)/shard_map/ppermute | solution.py:630
  104.5 16.6 %collective-permute-start.4 = (bf16[224,512]{1,0:T(8,128)(2,1)S(1)}, bf16[224,512]{1,0:T(8,128)(2,1)}, u32[]{:S(2)}, u32[]{:S(2)}) collective-permute-start(bf16[224,512]{1,0:T(8,128)(2,1)S(1)} %copy-done.13), channel_id=1, source_target_pairs={{0,7},{1,0},{2,1},{3,2},{4,3},{5,4},{6,5},{7,6},{8,15},{9,8},{10,9... | collective-permute-start | bytes 688136 | tf_op jit(solution)/shard_map/ppermute | solution.py:630
  107.3 13.9 %collective-permute-start.2 = (bf16[80,512]{1,0:T(8,128)(2,1)}, bf16[80,512]{1,0:T(8,128)(2,1)S(1)}, u32[]{:S(2)}, u32[]{:S(2)}) collective-permute-start(bf16[80,512]{1,0:T(8,128)(2,1)} %get-tuple-element.44), channel_id=1, source_target_pairs={{0,127},{1,120},{2,121},{3,122},{4,123},{5,124},{6,125},{7,126},{8... | collective-permute-start | bytes 245768 | tf_op jit(solution)/shard_map/ppermute | solution.py:630
  108.9 12.3 %collective-permute-start.1 = (bf16[224,512]{1,0:T(8,128)(2,1)}, bf16[224,512]{1,0:T(8,128)(2,1)S(1)}, u32[]{:S(2)}, u32[]{:S(2)}) collective-permute-start(bf16[224,512]{1,0:T(8,128)(2,1)} %get-tuple-element.43), channel_id=1, source_target_pairs={{0,7},{1,0},{2,1},{3,2},{4,3},{5,4},{6,5},{7,6},{8,15},{9,8},{10,9... | collective-permute-start | bytes 688136 | tf_op jit(solution)/shard_map/ppermute | solution.py:630
  110.7 10.5 %copy-start.11 = (bf16[656,512]{1,0:T(8,128)(2,1)S(1)}, bf16[656,512]{1,0:T(8,128)(2,1)}, u32[]{:S(2)}) copy-start(bf16[656,512]{1,0:T(8,128)(2,1)} %copy-done.10) | copy-start | bytes 2015236
  110.7 10.5 %copy-start.16 = (f32[144,576]{1,0:T(8,128)S(1)}, f32[144,576]{1,0:T(8,128)}, u32[]{:S(2)}) copy-start(f32[144,576]{1,0:T(8,128)} %constant.42.clone.apart_ref) | copy-start | bytes 995332
  110.7 10.5 %copy-start.17 = (bf16[288,320]{1,0:T(8,128)(2,1)S(1)}, bf16[288,320]{1,0:T(8,128)(2,1)}, u32[]{:S(2)}) copy-start(bf16[288,320]{1,0:T(8,128)(2,1)} %constant.41.clone.join_ref) | copy-start | bytes 552964
  110.7 10.5 %copy-start.19 = (bf16[656,512]{1,0:T(8,128)(2,1)S(1)}, bf16[656,512]{1,0:T(8,128)(2,1)}, u32[]{:S(2)}) copy-start(bf16[656,512]{1,0:T(8,128)(2,1)} %get-tuple-element.41.xe) | copy-start | bytes 2015236
  121.2 19.3 %copy-start.7 = (bf16[320,288]{1,0:T(8,128)(2,1)S(1)}, bf16[320,288]{1,0:T(8,128)(2,1)}, u32[]{:S(2)}) copy-start(bf16[320,288]{1,0:T(8,128)(2,1)} %constant.43.clone.back_ref) | copy-start | bytes 552964
  156.6 6.8 %collective-permute-start.6 = (bf16[1024,512]{1,0:T(8,128)(2,1)S(1)}, bf16[1024,512]{1,0:T(8,128)(2,1)S(1)}, u32[]{:S(2)}, u32[]{:S(2)}) collective-permute-start(bf16[1024,512]{1,0:T(8,128)(2,1)S(1)} %get-tuple-element.60), channel_id=1, source_target_pairs={{0,8},{1,9},{2,10},{3,11},{4,12},{5,13},{6,14},{7,15},{8,0},{9,1},... | collective-permute-start | bytes 3145736 | tf_op jit(solution)/shard_map/ppermute | solution.py:668
  159.0 42.4 %collective-permute-start.7 = (bf16[2,512,512]{2,1,0:T(8,128)(2,1)}, bf16[2,512,512]{2,1,0:T(8,128)(2,1)}, u32[]{:S(2)}, u32[]{:S(2)}) collective-permute-start(bf16[2,512,512]{2,1,0:T(8,128)(2,1)} %get-tuple-element.63), channel_id=1, source_target_pairs={{0,8},{1,9},{2,10},{3,11},{4,12},{5,13},{6,14},{7,15},{8,16},{9,17... | collective-permute-start | bytes 3145736 | tf_op jit(solution)/shard_map/ppermute | solution.py:630
  163.3 12.6 %copy-start.15 = (bf16[2,80,512]{2,1,0:T(8,128)(2,1)S(1)}, bf16[2,80,512]{2,1,0:T(8,128)(2,1)}, u32[]{:S(2)}) copy-start(bf16[2,80,512]{2,1,0:T(8,128)(2,1)} %copy-done.14) | copy-start | bytes 491524
  164.6 42.7 %all-to-all-start.2 = ((bf16[64,16,512]{2,1,0:T(8,128)(2,1)}), bf16[64,16,512]{2,1,0:T(8,128)(2,1)S(1)}, u32[]{:S(2)}, u32[]{:S(2)}) async-start(bf16[64,16,512]{2,1,0:T(8,128)(2,1)} %bitcast.14), calls=%async_computation.2 | async-start | bytes 2097152 | tf_op jit(solution)/shard_map/all_to_all | solution.py:634
  174.9 26.5 %collective-permute-start.8 = (bf16[2,224,512]{2,1,0:T(8,128)(2,1)}, bf16[2,224,512]{2,1,0:T(8,128)(2,1)S(1)}, u32[]{:S(2)}, u32[]{:S(2)}) collective-permute-start(bf16[2,224,512]{2,1,0:T(8,128)(2,1)} %get-tuple-element.64), channel_id=1, source_target_pairs={{0,1},{1,2},{2,3},{3,4},{4,5},{5,6},{6,7},{7,0},{8,9},{9,10},{10,1... | collective-permute-start | bytes 1376264 | tf_op jit(solution)/shard_map/ppermute | solution.py:630
  176.0 24.9 %collective-permute-start.9 = (bf16[2,80,512]{2,1,0:T(8,128)(2,1)S(1)}, bf16[2,80,512]{2,1,0:T(8,128)(2,1)S(1)}, u32[]{:S(2)}, u32[]{:S(2)}) collective-permute-start(bf16[2,80,512]{2,1,0:T(8,128)(2,1)S(1)} %copy-done.15), channel_id=1, source_target_pairs={{0,9},{1,10},{2,11},{3,12},{4,13},{5,14},{6,15},{7,8},{8,17},{9,18... | collective-permute-start | bytes 491528 | tf_op jit(solution)/shard_map/ppermute | solution.py:630
  (10 other events, 23.1 us)

commit v7 on v6

--- a/solution.py
+++ b/solution.py
@@ -152,15 +152,15 @@
     chosen = rank == lax.broadcasted_iota(I32, (CAP, TOKENS), 0).astype(F32)
     chosen = jnp.where(chosen, 1.0, 0.0).astype(BF16)
     found = product(high, chosen, NT) * 32.0 + product(low, chosen, NT)
-    lists_ref[...] = found.astype(I32)
+    lists_ref[...] = found.astype(I32).reshape(BANDS, 1, CAP)
 
 
 def make_requests(owners, slots):
     return call(
         request_kernel, "requests", (),
         [whole(1, TOKENS)] * 2,
-        [whole(BANDS, CAP), whole(1, TOKENS), whole(BANDS, 8)],
-        shapes((BANDS, CAP), (1, TOKENS), (BANDS, 8), dtype=I32),
+        [whole(BANDS, 1, CAP), whole(1, TOKENS), whole(BANDS, 8)],
+        shapes((BANDS, 1, CAP), (1, TOKENS), (BANDS, 8), dtype=I32),
         [pltpu.VMEM((BANDS, TOKENS), F32), pltpu.VMEM((1, TOKENS), F32)],
         (100000000, 100000, 0), 62,
     )(owners, slots)
@@ -170,10 +170,9 @@
 
 
 def serve_kernel(lists_ref, buffer_ref, out_ref):
-    lane = lax.broadcasted_iota(I32, (CAP, BANDS), 1)
     for at in range(ASKERS):
-        asker = pl.program_id(0) * ASKERS + at
-        wanted = jnp.sum(jnp.where(lane == asker, lists_ref[...], 0), 1, keepdims=True)
+        row = jnp.broadcast_to(lists_ref[at].astype(F32), (8, CAP))
+        wanted = row.T[:, :1].astype(I32)
         for half in range(2):
             chosen = wanted[half * 144 : half * 144 + 144] == lax.broadcasted_iota(I32, (144, ROWS), 1)
             chosen = jnp.where(chosen, 1.0, 0.0).astype(BF16)
@@ -184,34 +183,26 @@
 def serve(lists, buffer):
     return call(
         serve_kernel, "serve", (BANDS // ASKERS,),
-        [whole(CAP, BANDS), whole(ROWS, D)],
+        [pl.BlockSpec((ASKERS, 1, CAP), lambda i: (i, 0, 0)), whole(ROWS, D)],
         blocks(ASKERS * CAP, D),
         shapes((BANDS * CAP, D))[0],
         [], (5400000000, 6000000, 0), 60,
     )(lists, buffer)
 
 
-def pick_kernel(table_ref, place_ref, replies_ref, up_ref, side_ref, corner_ref, inner_ref, edge_ref, compact, held, sems):
-    def fetch(owner):
-        rows = pl.ds(owner * CAP, CAP)
-        return pltpu.make_async_copy(replies_ref.at[rows, :], held.at[rows, :], sems.at[owner])
-
-    for owner in range(BANDS):
-        fetch(owner).start()
+def pick_kernel(table_ref, place_ref, replies_ref, up_ref, side_ref, corner_ref, inner_ref, edge_ref, compact):
     compact[...] = jnp.zeros_like(compact)
     firsts = (0, UP + CORNER, UP + CORNER + 2 * WIN + INNER)
     for zone, size in enumerate(COMPACT):
         filled = 0
         for owner in range(BANDS):
-            if zone == 0:
-                fetch(owner).wait()
             start = owner * CAP + table_ref[owner, 2 * zone] * GROUP
             groups = table_ref[owner, 2 * zone + 1]
 
             def move(at, filled, start=start):
                 source = pl.multiple_of(start + at * GROUP, GROUP)
                 target = pl.multiple_of(filled, GROUP)
-                compact[pl.ds(target, GROUP), :] = held[pl.ds(source, GROUP), :]
+                compact[pl.ds(target, GROUP), :] = replies_ref[pl.ds(source, GROUP), :]
                 return filled + GROUP
 
             filled = lax.fori_loop(0, groups, move, filled)
@@ -241,15 +232,10 @@
 def pick(table, place, replies):
     return call(
         pick_kernel, "pick", (),
-        [pl.BlockSpec(memory_space=pltpu.SMEM), whole(PLACES, 1), pl.BlockSpec(memory_space=pl.ANY)],
+        [pl.BlockSpec(memory_space=pltpu.SMEM), whole(PLACES, 1), whole(BANDS * CAP, D)],
         [whole(n, D) for n in (UP, SIDE, CORNER, INNER, EDGE)],
         shapes(*[(n, D) for n in (UP, SIDE, CORNER, INNER, EDGE)]),
-        [
-            pltpu.VMEM((max(COMPACT), D), BF16),
-            pltpu.VMEM((BANDS * CAP, D), BF16),
-            pltpu.SemaphoreType.DMA((BANDS,)),
-        ],
-        (3600000000, 8000000, 0), 60,
+        [pltpu.VMEM((max(COMPACT), D), BF16)], (3600000000, 8000000, 0), 60,
     )(table, place, replies)
 
 
@@ -646,7 +632,7 @@
     weights = (qkv_weight, norm_gain.reshape(1, D), out_weight)
     lists, place, table = make_requests(fetch_owner.reshape(1, TOKENS), fetch_slot.reshape(1, TOKENS))
     lists = swap_blocks(lists, "lat")
-    replies = swap_blocks(serve(lists.T, buffer).reshape(BANDS, CAP, D), "lat")
+    replies = swap_blocks(serve(lists, buffer).reshape(BANDS, CAP, D), "lat")
     replies = replies.reshape(BANDS * CAP, D)
 
     c_up, c_side, c_corner, c_inner, c_edge = sort_pieces(out_grad.reshape(TOKENS, D))
@@ -661,14 +647,15 @@
     core = (band % 2).astype(I32).reshape(1)
     first = attend_inner(x_inner, c_inner, weights)
     x, left, right = attend_edge(x_parts, c_parts, flag, weights, first)
-    edge, *away = finish_edge((x, left, right), weights)
-    returned = exchange(away, 1)
-    left, right, edge = lax.optimization_barrier((left, right, edge))
     own, away = weight_terms(core, left, right)
     got = lax.ppermute(away, BOTH, OTHER_CORE)
+    edge, *away = finish_edge((x, left, right), weights)
+    up, side, corner = exchange(away, 1)
     inner = finish_inner((x, left, right), weights)
-    got, inner = lax.optimization_barrier((got, inner))
-    terms = swap_blocks(add_halves(own, got), BOTH, SAME_CORE)
+    half = add_halves(own, got)
+    half, inner, side, corner = lax.optimization_barrier((half, inner, side, corner))
+    terms = swap_blocks(half, BOTH, SAME_CORE)
+    returned = [up, side, corner]
     outs = join([inner, edge] + returned)
     return (*outs, *sum_terms(terms))
 

time: 209 us -> 203 us (0.971)
  starting transfers between devices: 33.8 us -> 30.6 us
    ppermute x9, waiting for transfers between devices: 25 us -> 13.4 us  [exchange(): lax.ppermute(part, BOTH, shift_pairs(*step))]
    all_to_all x2, waiting for transfers between devices: 27.6 us -> 38.4 us  [swap_blocks(): lax.all_to_all(values, axis, split_axis=0, concat_axis=0, axis_index_grou...]
    all_to_all x2, starting transfers between devices: 15 us -> 10.8 us  [swap_blocks(): lax.all_to_all(values, axis, split_axis=0, concat_axis=0, axis_index_grou...]
    unnamed x44 -> x52, local copies, waits for them, and re-layouts: 6.8 us -> 6.55 us
  transfers between devices with their start and end apart: 12 -> 12, of which waited for: 3 -> 3; matrix products, arithmetic and copies ran while one was open for 9% -> 9% of each run, Pallas kernels for 15% -> 19%
where the time goes in v7:
time: 203 us; the launch traced here: 202 us
  Pallas kernels  77.3 us (38%)
  waiting for transfers between devices  51.8 us (26%)
  starting transfers between devices  30.6 us (15%)
  local copies, waits for them, and re-layouts  25.1 us (12%)
  blocking collectives  16.7 us (8%)
    all_to_all x2, waiting for transfers between devices, swap_blocks(): lax.all_to_all(values, axis, split_axis=0, concat_axis=0, axis_index_grou...  38.4 us
    pallas_call x1, Pallas kernels, attend_edge(): call(edge_kernel, 'attend_edge', (5,), [pl.BlockSpec(memory_space=pltpu.S...  19.2 us
    ppermute x9, starting transfers between devices, exchange(): lax.ppermute(part, BOTH, shift_pairs(*step))  17 us
    all_to_all x1, blocking collectives, swap_blocks(): lax.all_to_all(values, axis, split_axis=0, concat_axis=0, axis_index_grou...  16.7 us
    ppermute x9, waiting for transfers between devices, exchange(): lax.ppermute(part, BOTH, shift_pairs(*step))  13.4 us
    gather x1, local copies, waits for them, and re-layouts, per_device(): place = place.reshape(TOKENS)[ORDER].reshape(-1, 1)  12.7 us
    all_to_all x2, starting transfers between devices, swap_blocks(): lax.all_to_all(values, axis, split_axis=0, concat_axis=0, axis_index_grou...  10.8 us
    pallas_call x1, Pallas kernels, attend_inner(): call(inner_kernel, 'attend_inner', (3,), [blocks(BLOCK, D)] * 2 + [whole(...  10.4 us
  transfers between devices with their start and end apart: 12, of which 3 were waited for; matrix products, arithmetic and copies ran while one was open for 9% of the time, Pallas kernels for 19%

profile of v7, /device:TPU:1, one launch (start us, length us, event | category | flops | bytes accessed | tf_op | source)
XLA Modules:
  0.0 202.4 jit_solution(18091766117728088352)
XLA Ops:
  0.6 2.7 %requests.1 = (s32[16,1,288]{2,1,0:T(1,128)}, s32[1,2304]{1,0:T(1,128)}, s32[16,8]{1,0:T(8,128)}) custom-call(s32[1,2304]{1,0:T(1,128)} %bitcast.16, s32[1,2304]{1,0:T(1,128)} %bitcast.17), custom_call_target="tpu_custom_call" | custom-call | flops 100000000 | bytes 100000 | tf_op jit(solution)/shard_map/requests/pallas_call | solution.py:159
  3.3 16.7 %all_to_all.21.lists_ref = s32[16,1,288]{2,1,0:T(1,128)} all-to-all(s32[16,1,288]{2,1,0:T(1,128)} %get-tuple-element.39), channel_id=1, replica_groups=mesh['lat'=16,'lon'=8] {'lat'}, dimensions={0} | all-to-all | bytes 36864 | tf_op jit(solution)/shard_map/all_to_all | solution.py:620
  20.0 10.3 %serve.1 = bf16[4608,512]{1,0:T(8,128)(2,1)} custom-call(s32[16,1,288]{2,1,0:T(1,128)} %all_to_all.21.lists_ref, bf16[1152,512]{1,0:T(8,128)(2,1)} %buffer_ref.1), custom_call_target="tpu_custom_call" | custom-call | flops 5400000000 | bytes 6000000 | tf_op jit(solution)/shard_map/serve/pallas_call | solution.py:184
  30.3 4.7 %all-to-all-start.1 = ((bf16[16,288,512]{2,1,0:T(8,128)(2,1)}), bf16[16,288,512]{2,1,0:T(8,128)(2,1)}, u32[]{:S(2)}, u32[]{:S(2)}) async-start(bf16[16,288,512]{2,1,0:T(8,128)(2,1)} %bitcast.15), calls=%async_computation.1 | async-start | bytes 9437184 | tf_op jit(solution)/shard_map/all_to_all | solution.py:620
  35.0 3.9 %reshape.51.grid_ref = bf16[2304,512]{1,0:T(8,128)(2,1)S(1)} reshape(bf16[12,48,4,512]{3,2,1,0:T(4,128)(2,1)} %param.22) | data formatting | bytes 4718592 | tf_op jit(solution)/shard_map/reshape | solution.py:638
  42.0 2.9 %collective-permute-start.5 = (bf16[80,512]{1,0:T(8,128)(2,1)S(1)}, bf16[80,512]{1,0:T(8,128)(2,1)S(1)}, u32[]{:S(2)}, u32[]{:S(2)}) collective-permute-start(bf16[80,512]{1,0:T(8,128)(2,1)S(1)} %get-tuple-element.47), channel_id=1, source_target_pairs={{0,127},{1,120},{2,121},{3,122},{4,123},{5,124},{6,125},{7,126},{8... | collective-permute-start | bytes 245768 | tf_op jit(solution)/shard_map/ppermute | solution.py:616
  44.9 4.7 %collective-permute-start.3 = (bf16[512,512]{1,0:T(8,128)(2,1)}, bf16[512,512]{1,0:T(8,128)(2,1)}, u32[]{:S(2)}, u32[]{:S(2)}) collective-permute-start(bf16[512,512]{1,0:T(8,128)(2,1)} %get-tuple-element.45), channel_id=1, source_target_pairs={{0,120},{1,121},{2,122},{3,123},{4,124},{5,125},{6,126},{7,127},{8... | collective-permute-start | bytes 1572872 | tf_op jit(solution)/shard_map/ppermute | solution.py:616
  49.7 12.7 %gather_fusion = s32[2336]{0:T(1024)S(1)} fusion(s32[2304]{0:T(1024)S(1)} %reduce, s32[3072]{0:T(1024)S(1)} %pad_clamp_fusion), kind=kCustom, calls=%fused_computation | custom fusion | bytes 28032 | tf_op jit(solution)/shard_map/gather | solution.py:640
  62.5 1.9 reshape.63.place_ref
  64.4 27.5 %all-to-all-done.1 = bf16[16,288,512]{2,1,0:T(8,128)(2,1)} async-done(((bf16[16,288,512]{2,1,0:T(8,128)(2,1)}), bf16[16,288,512]{2,1,0:T(8,128)(2,1)}, u32[]{:S(2)}, u32[]{:S(2)}) %all-to-all-start.1) | async-done | bytes 4718624 | tf_op jit(solution)/shard_map/all_to_all | solution.py:620
  91.9 9.7 %pick.1 = (bf16[512,512]{1,0:T(8,128)(2,1)}, bf16[224,512]{1,0:T(8,128)(2,1)}, bf16[80,512]{1,0:T(8,128)(2,1)}, bf16[864,512]{1,0:T(8,128)(2,1)}, bf16[656,512]{1,0:T(8,128)(2,1)}) custom-call(s32[16,8]{1,0:T(8,128)} %get-tuple-element.37.table_ref, s32[2336,1]{1,0:T(8,128)} %reshape.63.place_ref, bf16[4608,512]{1,0:T(8,128)(2,1)} %bitcast.5.replies_ref), custom_call_target="tpu_custom_call" | custom-call | flops 3600000000 | bytes 8000000 | tf_op jit(solution)/shard_map/pick/pallas_call | solution.py:233
  102.9 2.8 %collective-permute-start.4 = (bf16[224,512]{1,0:T(8,128)(2,1)S(1)}, bf16[224,512]{1,0:T(8,128)(2,1)}, u32[]{:S(2)}, u32[]{:S(2)}) collective-permute-start(bf16[224,512]{1,0:T(8,128)(2,1)S(1)} %copy-done.19), channel_id=1, source_target_pairs={{0,7},{1,0},{2,1},{3,2},{4,3},{5,4},{6,5},{7,6},{8,15},{9,8},{10,9... | collective-permute-start | bytes 688136 | tf_op jit(solution)/shard_map/ppermute | solution.py:616
  105.7 1.6 collective-permute-start.2
  109.2 10.4 %attend_inner.1 = (bf16[2304,512]{1,0:T(8,128)(2,1)S(1)}, bf16[2304,1024]{1,0:T(8,128)(2,1)S(1)}, bf16[2304,2048]{1,0:T(8,128)(2,1)S(1)}) custom-call(bf16[864,512]{1,0:T(8,128)(2,1)S(1)} %copy-done.22, bf16[864,512]{1,0:T(8,128)(2,1)S(1)} %copy-done.15, bf16[512,1536]{1,0:T(8,128)(2,1)S(1)} %copy-done, f32[1,512]{1,0:T(1,128)S(1)} %bitcast.11, ...), custom_call_target="tpu_custom_call" | custom-call | flops 5184000000 | bytes 8640000 | tf_op jit(solution)/shard_map/attend_inner/pallas_call | solution.py:398
  119.7 19.2 %attend_edge.1 = (bf16[2304,512]{1,0:T(8,128)(2,1)S(1)}, bf16[2304,1024]{1,0:T(8,128)(2,1)S(1)}, bf16[2304,2048]{1,0:T(8,128)(2,1)S(1)}) custom-call(s32[1]{0:T(128)} %bitcast.1.flag_ref, bf16[656,512]{1,0:T(8,128)(2,1)S(1)} %copy-done.23, bf16[512,512]{1,0:T(8,128)(2,1)} %collective-permute-done.xu, ...), custom_call_target="tpu_custom_call", output_to_operand_aliasing={{0}: (14, {}), {1}: (15, {}), {2}: (16, {})} | custom-call | flops 8640000000 | bytes 14400000 | tf_op jit(solution)/shard_map/attend_edge/pallas_call | solution.py:412
  138.9 5.3 %weight_terms.1 = (f32[1024,512]{1,0:T(8,128)S(1)}, bf16[1024,512]{1,0:T(8,128)(2,1)S(1)}) custom-call(s32[1]{0:T(128)} %bitcast.core_ref, bf16[2304,1024]{1,0:T(8,128)(2,1)S(1)} %get-tuple-element.53.left_ref.refs_1_, bf16[2304,2048]{1,0:T(8,128)(2,1)S(1)} %get-tuple-element.54.right_ref.refs_2_), custom_call_target="tpu_custom_call" | custom-call | flops 1000 | bytes 1000 | tf_op jit(solution)/shard_map/weight_terms/pallas_call | solution.py:439
  144.2 2.8 %collective-permute-start.6 = (bf16[1024,512]{1,0:T(8,128)(2,1)S(1)}, bf16[1024,512]{1,0:T(8,128)(2,1)S(1)}, u32[]{:S(2)}, u32[]{:S(2)}) collective-permute-start(bf16[1024,512]{1,0:T(8,128)(2,1)S(1)} %get-tuple-element.56), channel_id=1, source_target_pairs={{0,8},{1,9},{2,10},{3,11},{4,12},{5,13},{6,14},{7,15},{8,0},{9,1},... | collective-permute-start | bytes 3145736 | tf_op jit(solution)/shard_map/ppermute | solution.py:651
  146.9 8.9 %finish_edge.1 = (bf16[2,656,512]{2,1,0:T(8,128)(2,1)S(1)}, bf16[2,512,512]{2,1,0:T(8,128)(2,1)}, bf16[2,224,512]{2,1,0:T(8,128)(2,1)S(1)}, bf16[2,80,512]{2,1,0:T(8,128)(2,1)S(1)}) custom-call(bf16[144,144]{1,0:T(8,128)(2,1)S(1)} %copy-done.6, bf16[320,288]{1,0:T(8,128)(2,1)S(1)} %copy-done.9, bf16[2304,512]{1,0:T(8,128)(2,1)S(1)} %get-tuple-element.57.refs_0_, ...), custom_call_target="tpu_custom_call" | custom-call | flops 3168000000 | bytes 12960000 | tf_op jit(solution)/shard_map/finish_edge/pallas_call | solution.py:538
  155.9 1.6 collective-permute-start.7
  158.9 3.7 %finish_inner.1.inner = bf16[2,864,512]{2,1,0:T(8,128)(2,1)S(1)} custom-call(bf16[144,144]{1,0:T(8,128)(2,1)S(1)} %copy-done.6, bf16[2304,512]{1,0:T(8,128)(2,1)S(1)} %get-tuple-element.57.refs_0_, bf16[2304,1024]{1,0:T(8,128)(2,1)S(1)} %get-tuple-element.53.left_ref.refs_1_, bf16[2304,2048]{1,0:T(8,128)(2,1)S(1)} %get-tuple-element.54.right_ref.refs_2_, ...), custom_call_target="tpu_custom_call" | custom-call | flops 1000 | bytes 1000 | tf_op jit(solution)/shard_map/finish_inner/pallas_call | solution.py:529
  162.9 13.4 %collective-permute-done.8.corner = bf16[2,80,512]{2,1,0:T(8,128)(2,1)S(1)} collective-permute-done((bf16[2,80,512]{2,1,0:T(8,128)(2,1)S(1)}, bf16[2,80,512]{2,1,0:T(8,128)(2,1)S(1)}, u32[]{:S(2)}, u32[]{:S(2)}) %collective-permute-start.8) | collective-permute-done | bytes 163872 | tf_op jit(solution)/shard_map/ppermute | solution.py:616
  177.8 6.1 %all-to-all-start.2 = ((bf16[64,16,512]{2,1,0:T(8,128)(2,1)}), bf16[64,16,512]{2,1,0:T(8,128)(2,1)S(1)}, u32[]{:S(2)}, u32[]{:S(2)}) async-start(bf16[64,16,512]{2,1,0:T(8,128)(2,1)} %bitcast.10), calls=%async_computation.2 | async-start | bytes 2097152 | tf_op jit(solution)/shard_map/all_to_all | solution.py:620
  186.2 4.6 %join.1 = (bf16[12,48,4,512]{3,2,1,0:T(4,128)(2,1)}, bf16[12,48,4,512]{3,2,1,0:T(4,128)(2,1)}) custom-call(bf16[2,864,512]{2,1,0:T(8,128)(2,1)S(1)} %finish_inner.1.inner, bf16[2,656,512]{2,1,0:T(8,128)(2,1)S(1)} %copy-done.5, bf16[2,512,512]{2,1,0:T(8,128)(2,1)} %collective-permute-done.9.up, bf16[2,224,512]{2,1,0:T(8,128)(2,1)S(1)} %copy-done.8, ...), custom_call_target="tpu_custom_call" | custom-call | flops 1000000 | bytes 9000000 | tf_op jit(solution)/shard_map/join/pallas_call | solution.py:583
  190.8 10.9 %all-to-all-done.2 = bf16[64,16,512]{2,1,0:T(8,128)(2,1)S(1)} async-done(((bf16[64,16,512]{2,1,0:T(8,128)(2,1)}), bf16[64,16,512]{2,1,0:T(8,128)(2,1)S(1)}, u32[]{:S(2)}, u32[]{:S(2)}) %all-to-all-start.2) | async-done | bytes 1048608 | tf_op jit(solution)/shard_map/all_to_all | solution.py:620
  (70 shorter events, 12.6 us)
Async XLA Ops:
  30.3 61.6 %all-to-all-start.1 = ((bf16[16,288,512]{2,1,0:T(8,128)(2,1)}), bf16[16,288,512]{2,1,0:T(8,128)(2,1)}, u32[]{:S(2)}, u32[]{:S(2)}) async-start(bf16[16,288,512]{2,1,0:T(8,128)(2,1)} %bitcast.15), calls=%async_computation.1 | async-start | bytes 9437184 | tf_op jit(solution)/shard_map/all_to_all | solution.py:620
  38.9 10.7 %copy-start.25 = (s32[1,2304]{1,0:T(1,128)S(1)}, s32[1,2304]{1,0:T(1,128)}, u32[]{:S(2)}) copy-start(s32[1,2304]{1,0:T(1,128)} %get-tuple-element.38) | copy-start | bytes 27652
  38.9 10.8 %copy-start.24 = (s32[2336]{0:T(1024)S(1)}, s32[2336]{0:T(1024)}, u32[]{:S(2)}) copy-start(s32[2336]{0:T(1024)} %constant.48) | copy-start | bytes 28036
  42.0 20.5 %copy-start.16 = (bf16[656,512]{1,0:T(8,128)(2,1)}, bf16[656,512]{1,0:T(8,128)(2,1)S(1)}, u32[]{:S(2)}) copy-start(bf16[656,512]{1,0:T(8,128)(2,1)S(1)} %get-tuple-element.44.ce) | copy-start | bytes 2015236
  42.0 65.3 %collective-permute-start.5 = (bf16[80,512]{1,0:T(8,128)(2,1)S(1)}, bf16[80,512]{1,0:T(8,128)(2,1)S(1)}, u32[]{:S(2)}, u32[]{:S(2)}) collective-permute-start(bf16[80,512]{1,0:T(8,128)(2,1)S(1)} %get-tuple-element.47), channel_id=1, source_target_pairs={{0,127},{1,120},{2,121},{3,122},{4,123},{5,124},{6,125},{7,126},{8... | collective-permute-start | bytes 245768 | tf_op jit(solution)/shard_map/ppermute | solution.py:616
  44.9 74.6 %collective-permute-start.3 = (bf16[512,512]{1,0:T(8,128)(2,1)}, bf16[512,512]{1,0:T(8,128)(2,1)}, u32[]{:S(2)}, u32[]{:S(2)}) collective-permute-start(bf16[512,512]{1,0:T(8,128)(2,1)} %get-tuple-element.45), channel_id=1, source_target_pairs={{0,120},{1,121},{2,122},{3,123},{4,124},{5,125},{6,126},{7,127},{8... | collective-permute-start | bytes 1572872 | tf_op jit(solution)/shard_map/ppermute | solution.py:616
  91.9 11.1 %copy-start.19 = (bf16[224,512]{1,0:T(8,128)(2,1)S(1)}, bf16[224,512]{1,0:T(8,128)(2,1)}, u32[]{:S(2)}) copy-start(bf16[224,512]{1,0:T(8,128)(2,1)} %copy-done.18) | copy-start | bytes 688132
  91.9 16.1 %copy-start = (bf16[512,1536]{1,0:T(8,128)(2,1)S(1)}, bf16[512,1536]{1,0:T(8,128)(2,1)}, u32[]{:S(2)}) copy-start(bf16[512,1536]{1,0:T(8,128)(2,1)} %refs_3_.3) | copy-start | bytes 4718596
  91.9 16.1 %copy-start.2 = (bf16[512,512]{1,0:T(8,128)(2,1)S(1)}, bf16[512,512]{1,0:T(8,128)(2,1)}, u32[]{:S(2)}) copy-start(bf16[512,512]{1,0:T(8,128)(2,1)} %refs_5_.3) | copy-start | bytes 1572868
  91.9 16.1 %copy-start.13 = (f32[512]{0:T(512)S(1)}, f32[512]{0:T(512)}, u32[]{:S(2)}) copy-start(f32[512]{0:T(512)} %param.19) | copy-start | bytes 6148
  91.9 16.1 %copy-start.15 = (bf16[864,512]{1,0:T(8,128)(2,1)S(1)}, bf16[864,512]{1,0:T(8,128)(2,1)}, u32[]{:S(2)}) copy-start(bf16[864,512]{1,0:T(8,128)(2,1)} %copy-done.14) | copy-start | bytes 2654212
  101.6 18.0 %collective-permute-start = (bf16[512,512]{1,0:T(8,128)(2,1)}, bf16[512,512]{1,0:T(8,128)(2,1)}, u32[]{:S(2)}, u32[]{:S(2)}) collective-permute-start(bf16[512,512]{1,0:T(8,128)(2,1)} %get-tuple-element.41), channel_id=1, source_target_pairs={{0,120},{1,121},{2,122},{3,123},{4,124},{5,125},{6,126},{7,127},{8... | collective-permute-start | bytes 1572872 | tf_op jit(solution)/shard_map/ppermute | solution.py:616
  102.9 16.6 %collective-permute-start.4 = (bf16[224,512]{1,0:T(8,128)(2,1)S(1)}, bf16[224,512]{1,0:T(8,128)(2,1)}, u32[]{:S(2)}, u32[]{:S(2)}) collective-permute-start(bf16[224,512]{1,0:T(8,128)(2,1)S(1)} %copy-done.19), channel_id=1, source_target_pairs={{0,7},{1,0},{2,1},{3,2},{4,3},{5,4},{6,5},{7,6},{8,15},{9,8},{10,9... | collective-permute-start | bytes 688136 | tf_op jit(solution)/shard_map/ppermute | solution.py:616
  105.7 13.9 %collective-permute-start.2 = (bf16[80,512]{1,0:T(8,128)(2,1)}, bf16[80,512]{1,0:T(8,128)(2,1)S(1)}, u32[]{:S(2)}, u32[]{:S(2)}) collective-permute-start(bf16[80,512]{1,0:T(8,128)(2,1)} %get-tuple-element.43), channel_id=1, source_target_pairs={{0,127},{1,120},{2,121},{3,122},{4,123},{5,124},{6,125},{7,126},{8... | collective-permute-start | bytes 245768 | tf_op jit(solution)/shard_map/ppermute | solution.py:616
  107.3 12.3 %collective-permute-start.1 = (bf16[224,512]{1,0:T(8,128)(2,1)}, bf16[224,512]{1,0:T(8,128)(2,1)S(1)}, u32[]{:S(2)}, u32[]{:S(2)}) collective-permute-start(bf16[224,512]{1,0:T(8,128)(2,1)} %get-tuple-element.42), channel_id=1, source_target_pairs={{0,7},{1,0},{2,1},{3,2},{4,3},{5,4},{6,5},{7,6},{8,15},{9,8},{10,9... | collective-permute-start | bytes 688136 | tf_op jit(solution)/shard_map/ppermute | solution.py:616
  109.2 10.5 %copy-start.21 = (bf16[288,320]{1,0:T(8,128)(2,1)S(1)}, bf16[288,320]{1,0:T(8,128)(2,1)}, u32[]{:S(2)}) copy-start(bf16[288,320]{1,0:T(8,128)(2,1)} %constant.41.clone.join_ref) | copy-start | bytes 552964
  109.2 10.5 %copy-start.23 = (bf16[656,512]{1,0:T(8,128)(2,1)S(1)}, bf16[656,512]{1,0:T(8,128)(2,1)}, u32[]{:S(2)}) copy-start(bf16[656,512]{1,0:T(8,128)(2,1)} %get-tuple-element.40.xe) | copy-start | bytes 2015236
  144.2 18.4 %collective-permute-start.6 = (bf16[1024,512]{1,0:T(8,128)(2,1)S(1)}, bf16[1024,512]{1,0:T(8,128)(2,1)S(1)}, u32[]{:S(2)}, u32[]{:S(2)}) collective-permute-start(bf16[1024,512]{1,0:T(8,128)(2,1)S(1)} %get-tuple-element.56), channel_id=1, source_target_pairs={{0,8},{1,9},{2,10},{3,11},{4,12},{5,13},{6,14},{7,15},{8,0},{9,1},... | collective-permute-start | bytes 3145736 | tf_op jit(solution)/shard_map/ppermute | solution.py:651
  146.9 11.9 %copy-start.3 = (bf16[512,512]{1,0:T(8,128)(2,1)S(1)}, bf16[512,512]{1,0:T(8,128)(2,1)}, u32[]{:S(2)}) copy-start(bf16[512,512]{1,0:T(8,128)(2,1)} %refs_5_.3) | copy-start | bytes 1572868
  155.9 21.1 %collective-permute-start.7 = (bf16[2,224,512]{2,1,0:T(8,128)(2,1)S(1)}, bf16[2,224,512]{2,1,0:T(8,128)(2,1)S(1)}, u32[]{:S(2)}, u32[]{:S(2)}) collective-permute-start(bf16[2,224,512]{2,1,0:T(8,128)(2,1)S(1)} %get-tuple-element.58), channel_id=1, source_target_pairs={{0,1},{1,2},{2,3},{3,4},{4,5},{5,6},{6,7},{7,0},{8,9},{9,10},{10,1... | collective-permute-start | bytes 1376264 | tf_op jit(solution)/shard_map/ppermute | solution.py:616
  157.4 18.9 %collective-permute-start.8 = (bf16[2,80,512]{2,1,0:T(8,128)(2,1)S(1)}, bf16[2,80,512]{2,1,0:T(8,128)(2,1)S(1)}, u32[]{:S(2)}, u32[]{:S(2)}) collective-permute-start(bf16[2,80,512]{2,1,0:T(8,128)(2,1)S(1)} %get-tuple-element.59), channel_id=1, source_target_pairs={{0,9},{1,10},{2,11},{3,12},{4,13},{5,14},{6,15},{7,8},{8,17},{9,18... | collective-permute-start | bytes 491528 | tf_op jit(solution)/shard_map/ppermute | solution.py:616
  157.6 26.3 %collective-permute-start.9 = (bf16[2,512,512]{2,1,0:T(8,128)(2,1)}, bf16[2,512,512]{2,1,0:T(8,128)(2,1)}, u32[]{:S(2)}, u32[]{:S(2)}) collective-permute-start(bf16[2,512,512]{2,1,0:T(8,128)(2,1)} %get-tuple-element.62), channel_id=1, source_target_pairs={{0,8},{1,9},{2,10},{3,11},{4,12},{5,13},{6,14},{7,15},{8,16},{9,17... | collective-permute-start | bytes 3145736 | tf_op jit(solution)/shard_map/ppermute | solution.py:616
  162.9 14.1 %copy-start.1 = (bf16[1024,512]{1,0:T(8,128)(2,1)}, bf16[1024,512]{1,0:T(8,128)(2,1)S(1)}, u32[]{:S(2)}) copy-start(bf16[1024,512]{1,0:T(8,128)(2,1)S(1)} %add_halves.1) | copy-start | bytes 3145732
  177.8 23.9 %all-to-all-start.2 = ((bf16[64,16,512]{2,1,0:T(8,128)(2,1)}), bf16[64,16,512]{2,1,0:T(8,128)(2,1)S(1)}, u32[]{:S(2)}, u32[]{:S(2)}) async-start(bf16[64,16,512]{2,1,0:T(8,128)(2,1)} %bitcast.10), calls=%async_computation.2 | async-start | bytes 2097152 | tf_op jit(solution)/shard_map/all_to_all | solution.py:620
  (14 other events, 56.2 us)

commit v8 on v7

--- a/solution.py
+++ b/solution.py
@@ -68,6 +68,22 @@
 
 
 CORNER_BACK = corner_back()
+
+
+def back_matrices():
+    back = np.zeros((2, WIN + 3 * SMALL, BLOCK), np.float32)
+    rows = np.arange(WIN)
+    first = rows + np.where(rows < HALF, 0, HALF)
+    for part in range(2):
+        back[0, part * WIN : part * WIN + WIN, first + part * HALF] = SPLIT
+    edge, side, up, corner = CORNER_BACK.reshape(4, SMALL, BLOCK)
+    back[1, :SMALL] = edge
+    for at, part in enumerate((up, side, corner)):
+        back[1, WIN + at * SMALL : WIN + at * SMALL + SMALL] = part
+    return back
+
+
+BACK = back_matrices()
 
 
 def product(left, right, form=NN):
@@ -282,7 +298,8 @@
     order = [piece(low, 6 + 12 * q, 12) for q in range(3)] + [piece(low, 42, 6), piece(low, 0, 6)]
     order += [piece(mid, 0, 6), piece(mid, 42, 6)]
     for q in range(3):
-        order += [piece(range(3, 6), 6 + 12 * q, 12), piece(range(6, 9), 6 + 12 * q, 12)]
+        first, second = piece(range(3, 6), 6 + 12 * q, 12), piece(range(6, 9), 6 + 12 * q, 12)
+        order += [first[:HALF], second[:HALF], first[HALF:], second[HALF:]]
     order += [piece(high, 0, 6)]
     order += [piece(high, 6 + 12 * q, 12) for q in range(3)] + [piece(high, 42, 6)]
     return np.concatenate(order)
@@ -307,11 +324,8 @@
     return jnp.concatenate([first[:HALF], second[:HALF], first[HALF:], second[HALF:]])
 
 
-def attend(x_all, c_all, bias, w_ref, gain_ref, ow_ref, x_out, ha_ref, dp_ref, packed, slopes):
+def attend(x_all, bias, ga_ref, w_ref, gain_ref, x_out, ha_ref, dp_ref, packed):
     x_out[...] = x_all.astype(BF16)
-    cot = c_all.astype(BF16)
-    dp_ref[:, 3 * D :] = cot
-    slopes[...] = product(cot, ow_ref[...], NT).astype(BF16)
     normed, _ = normalise(x_all)
     hidden = (normed * gain_ref[...]).astype(BF16)
     ha_ref[:, :D] = hidden
@@ -334,7 +348,7 @@
         for quad in range(2):
             spot = [slice(part * D + quad * QUAD, part * D + quad * QUAD + QUAD) for part in range(3)]
             queries, keys, values = (packed[rows, cols] for cols in spot)
-            queries, grads = spread(queries), spread(slopes[rows, spot[0]])
+            queries, grads = spread(queries), spread(ga_ref[rows, spot[0]])
             scores = product(keys, queries, NT) * (SCALE * LOG2E)
             if bias is not None:
                 scores = scores + bias()
@@ -350,56 +364,103 @@
             dp_ref[rows, spot[2]] = product(low, grads).astype(BF16)
 
 
-def inner_kernel(x_ref, c_ref, *refs):
-    x_all = join_halves(x_ref[:WIN, :], x_ref[WIN:, :])
-    c_all = join_halves(c_ref[:WIN, :], c_ref[WIN:, :])
-    attend(x_all, c_all, None, *refs)
-
-
-def edge_kernel(flag_ref, xe, xu, xs, xc, ce, cu, cs, cc, join_ref, apart_ref, *refs):
-    weights, (*refs, x_all, c_all) = refs[:3], refs[6:]
+def join_corner(join_ref, edge, side, up, corner):
+    parts = [edge[:SMALL, :], side[:SMALL, :], up[:SMALL, :], corner[...]]
+    return product(join_ref[...], jnp.concatenate(parts))
+
+
+def slopes(c_all, ow_ref, cot_ref, ga_ref):
+    cot = c_all.astype(BF16)
+    cot_ref[...] = cot
+    ga_ref[...] = product(cot, ow_ref[...], NT).astype(BF16)
+
+
+def prepare_inner_kernel(inner, ow_ref, cot_ref, ga_ref):
+    slopes(join_halves(inner[:WIN, :], inner[WIN:, :]), ow_ref, cot_ref, ga_ref)
+
+
+def prepare_edge_kernel(edge, up, side, corner, join_ref, ow_ref, _, cot_ref, ga_ref, c_all):
+    step = pl.program_id(0)
+
+    @pl.when(step == 0)
+    def _():
+        c_all[...] = join_halves(edge[...], side[...])
+
+    @pl.when((step > 0) & (step < 4))
+    def _():
+        c_all[...] = join_halves(edge[...], up[...])
+
+    @pl.when(step == 4)
+    def _():
+        c_all[...] = join_corner(join_ref, edge, side, up, corner)
+
+    slopes(c_all[...], ow_ref, cot_ref, ga_ref)
+
+
+def prepare_inner(inner, ow):
+    return call(
+        prepare_inner_kernel, "prepare_inner", (3,),
+        [blocks(BLOCK, D), whole(D, D)],
+        [blocks(BLOCK, D)] * 2, shapes((TOKENS, D), (INNER, D)),
+        [], (500000000, 3000000, 0), 20,
+    )(inner, ow)
+
+
+def prepare_edge(parts, ow, cot):
+    return call(
+        prepare_edge_kernel, "prepare_edge", (5,),
+        EDGE_SPECS + [whole(BLOCK, 4 * SMALL), whole(D, D), pl.BlockSpec(memory_space=pl.ANY)],
+        [pl.BlockSpec((BLOCK, D), lambda i: (i + 3, 0)), blocks(BLOCK, D)],
+        shapes((TOKENS, D), (5 * BLOCK, D)),
+        [pltpu.VMEM((BLOCK, D), F32)], (800000000, 5000000, 0), 20,
+        aliases={6: 0},
+    )(*parts, jnp.asarray(CORNER_JOIN, BF16), ow, cot)
+
+
+def inner_kernel(x_ref, *refs):
+    attend(x_ref[...].astype(F32), None, *refs)
+
+
+def edge_kernel(flag_ref, xe, xu, xs, xc, join_ref, apart_ref, *refs):
+    sources, (*refs, x_all) = refs[:3], refs[6:]
     step = pl.program_id(0)
 
     @pl.when(step == 0)
     def _():
         x_all[...] = join_halves(xe[...], xs[...])
-        c_all[...] = join_halves(ce[...], cs[...])
 
     @pl.when((step > 0) & (step < 4))
     def _():
         x_all[...] = join_halves(xe[...], xu[...])
-        c_all[...] = join_halves(ce[...], cu[...])
 
     @pl.when(step == 4)
     def _():
-        parts = [xe[:SMALL, :], xs[:SMALL, :], xu[:SMALL, :], xc[...]]
-        x_all[...] = product(join_ref[...], jnp.concatenate(parts))
-        parts = [ce[:SMALL, :], cs[:SMALL, :], cu[:SMALL, :], cc[...]]
-        c_all[...] = product(join_ref[...], jnp.concatenate(parts))
+        x_all[...] = join_corner(join_ref, xe, xs, xu, xc)
 
     seam = jnp.where(step > 0, flag_ref[0], 0).astype(F32)
-    attend(x_all[...], c_all[...], lambda: apart_ref[...] * seam, *weights, *refs)
+    attend(x_all[...], lambda: apart_ref[...] * seam, *sources, *refs)
 
 
 def attend_specs(rows, skip):
-    widths = (D, 2 * D, 4 * D)
-    outs = [pl.BlockSpec((BLOCK, n), lambda i: (i + skip, 0)) for n in widths]
+    widths = (D, 2 * D, 3 * D)
+    row = lambda n: pl.BlockSpec((BLOCK, n), lambda i: (i + skip, 0))
+    sources = [blocks(BLOCK, D), whole(D, 3 * D), whole(1, D)]
     out_shapes = shapes(*[(TOKENS, n) for n in widths])
-    scratch = [pltpu.VMEM((BLOCK, 3 * D), BF16), pltpu.VMEM((BLOCK, D), BF16)]
+    scratch = [pltpu.VMEM((BLOCK, 3 * D), BF16)]
     cost = (rows * 6000000, rows * 10000, rows * 1200)
-    return outs, out_shapes, scratch, cost
+    return sources, [row(n) for n in widths], out_shapes, scratch, cost
 
 
 WEIGHTS = [(D, 3 * D), (1, D), (D, D)]
 
 
-def attend_inner(x, cot, weights):
-    outs, out_shapes, scratch, cost = attend_specs(INNER, 0)
+def attend_inner(x, ga, weights):
+    sources, outs, out_shapes, scratch, cost = attend_specs(INNER, 0)
     return call(
         inner_kernel, "attend_inner", (3,),
-        [blocks(BLOCK, D)] * 2 + [whole(*dim) for dim in WEIGHTS],
+        [blocks(BLOCK, D)] + sources,
         outs, out_shapes, scratch, cost, 18,
-    )(x, cot, *weights)
+    )(x, ga, *weights[:2])
 
 
 def apart_matrix():
@@ -407,24 +468,24 @@
     return np.tile(np.where(late[:, None] != late[None, :], FAR, 0.0).astype(np.float32), (1, 4))
 
 
-def attend_edge(x_parts, c_parts, flag, weights, carried):
-    outs, out_shapes, scratch, cost = attend_specs(5 * BLOCK, 3)
+def attend_edge(parts, ga, flag, weights, carried):
+    sources, outs, out_shapes, scratch, cost = attend_specs(5 * BLOCK, 3)
     return call(
         edge_kernel, "attend_edge", (5,),
         [pl.BlockSpec(memory_space=pltpu.SMEM)]
-        + EDGE_SPECS * 2
+        + EDGE_SPECS
         + [whole(BLOCK, 4 * SMALL), whole(WIN, 4 * WIN)]
-        + [whole(*dim) for dim in WEIGHTS]
+        + sources
         + [pl.BlockSpec(memory_space=pl.ANY)] * 3,
-        outs, out_shapes, scratch + [pltpu.VMEM((BLOCK, D), F32)] * 2, cost, 24,
-        aliases={14 + n: n for n in range(3)},
-    )(flag, *x_parts, *c_parts, jnp.asarray(CORNER_JOIN, BF16), jnp.asarray(apart_matrix()), *weights, *carried)
-
-
-def weight_kernel(core_ref, left_ref, right_ref, own_ref, away_ref, turned):
+        outs, out_shapes, scratch + [pltpu.VMEM((BLOCK, D), F32)], cost, 24,
+        aliases={10 + n: n for n in range(3)},
+    )(flag, *parts, jnp.asarray(CORNER_JOIN, BF16), jnp.asarray(apart_matrix()), ga, *weights[:2], *carried)
+
+
+def weight_kernel(core_ref, left_ref, dp_ref, cot_ref, own_ref, away_ref, turned):
     for c in range(4):
-        side, cols = slice(c // 3 * D, c // 3 * D + D), slice(c * D, c * D + D)
-        chunk = product(left_ref[:, side], right_ref[:, cols], TN).reshape(64, 8, D)
+        right = dp_ref[:, c * D : c * D + D] if c < 3 else cot_ref[...]
+        chunk = product(left_ref[:, c // 3 * D : c // 3 * D + D], right, TN).reshape(64, 8, D)
         half = c % 2 * 4
         turned[:, 0, c // 2, half : half + 4] = chunk[:, :4]
         turned[:, 1, c // 2, half : half + 4] = chunk[:, 4:]
@@ -435,15 +496,15 @@
             ref[at * 128 : at * 128 + 128, :] = part.astype(ref.dtype)
 
 
-def weight_terms(core, left, right):
+def weight_terms(core, left, dp, cot):
     return call(
         weight_kernel, "weight_terms", (),
-        [pl.BlockSpec(memory_space=pltpu.SMEM), whole(TOKENS, 2 * D), whole(TOKENS, 4 * D)],
+        [pl.BlockSpec(memory_space=pltpu.SMEM), whole(TOKENS, 2 * D), whole(TOKENS, 3 * D), whole(TOKENS, D)],
         [whole(1024, D)] * 2,
         [jax.ShapeDtypeStruct((1024, D), F32), jax.ShapeDtypeStruct((1024, D), BF16)],
         [pltpu.VMEM((64, 2, 2, 8, D), F32)],
         (1000, 1000, 0), 22,
-    )(core, left, right)
+    )(core, left, dp, cot)
 
 
 def add_kernel(own_ref, got_ref, out_ref):
@@ -458,17 +519,17 @@
     )(own, got)
 
 
-def finished(x_ref, att_ref, dp_ref, w_ref, gain_ref, ow_ref):
+def finished(x_ref, att_ref, dp_ref, c_ref, w_ref, gain_ref, ow_ref):
     x = x_ref[...].astype(F32)
     out = x + product(att_ref[...], ow_ref[...])
     normed, inverse = normalise(x)
-    hidden = product(dp_ref[:, : 3 * D], w_ref[...], NT) * gain_ref[...]
+    hidden = product(dp_ref[...], w_ref[...], NT) * gain_ref[...]
     hidden = (
         hidden
         - jnp.mean(hidden, -1, keepdims=True)
         - normed * jnp.mean(hidden * normed, -1, keepdims=True)
     )
-    grad = dp_ref[:, 3 * D :].astype(F32) + inverse * hidden
+    grad = c_ref[...].astype(F32) + inverse * hidden
     return out, grad
 
 
@@ -486,31 +547,22 @@
         inner[n, WIN:, :] = second
 
 
-def finish_edge_kernel(split_ref, back_ref, *refs):
-    refs, (edge, up, side, corner) = refs[:6], refs[6:]
+def finish_edge_kernel(back_ref, *refs):
+    refs, (edge, up, side, corner) = refs[:7], refs[7:]
     step = pl.program_id(0)
     for n, values in enumerate(finished(*refs)):
-
-        @pl.when(step < 4)
-        def _(n=n, values=values):
-            first, second = grid_pieces(split_ref, values)
-            edge[n] = first
-
-            @pl.when(step == 0)
-            def _():
-                side[n] = second
-
-            @pl.when(step > 0)
-            def _():
-                up[n] = second
+        parts = product(back_ref[...], values.astype(BF16)).astype(BF16)
+        edge[n] = parts[:WIN]
+        up[n] = parts[WIN:BLOCK]
+
+        @pl.when(step == 0)
+        def _(n=n, parts=parts):
+            side[n] = parts[WIN:BLOCK]
 
         @pl.when(step == 4)
-        def _(n=n, values=values):
-            parts = product(back_ref[...], values.astype(BF16)).astype(BF16)
-            edge[n, :SMALL, :] = parts[:SMALL]
-            side[n, :SMALL, :] = parts[SMALL : 2 * SMALL]
-            up[n, :SMALL, :] = parts[2 * SMALL : 3 * SMALL]
-            corner[n] = parts[3 * SMALL :]
+        def _(n=n, parts=parts):
+            side[n, :SMALL, :] = parts[WIN + SMALL : WIN + 2 * SMALL]
+            corner[n] = parts[WIN + 2 * SMALL :]
 
 
 PIECES = (INNER, EDGE, UP, SIDE, CORNER)
@@ -518,7 +570,7 @@
 
 def finish_specs(skip):
     row = lambda width, col: pl.BlockSpec((BLOCK, width), lambda i: (i + skip, col))
-    return [row(D, 0), row(D, 1), row(4 * D, 0)] + [whole(*dim) for dim in WEIGHTS]
+    return [row(D, 0), row(D, 1), row(3 * D, 0), row(D, 0)] + [whole(*dim) for dim in WEIGHTS]
 
 
 def finish_cost(rows):
@@ -537,10 +589,10 @@
 def finish_edge(values, weights):
     return call(
         finish_edge_kernel, "finish_edge", (5,),
-        [whole(WIN, WIN), whole(4 * SMALL, BLOCK)] + finish_specs(3),
+        [pl.BlockSpec((None,) + BACK.shape[1:], lambda i: (i // 4, 0, 0))] + finish_specs(3),
         EDGE_PAIRS, shapes(*[(2, n, D) for n in PIECES[1:]]), [],
         finish_cost(5 * BLOCK), 24,
-    )(jnp.asarray(SPLIT, BF16), jnp.asarray(CORNER_BACK, BF16), *values, *weights)
+    )(jnp.asarray(BACK, BF16), *values, *weights)
 
 
 def join_kernel(inner, edge, up, side, corner, *outs):
@@ -584,7 +636,7 @@
         join_kernel, "join", (4,),
         [whole(2, n, D) for n in PIECES],
         [spec] * 2, shapes(*[dim] * 2), [],
-        (1000000, 9000000, 0), 26,
+        (60000000000, 9000000, 0), 26,
     )(*parts)
 
 
@@ -637,24 +689,27 @@
 
     c_up, c_side, c_corner, c_inner, c_edge = sort_pieces(out_grad.reshape(TOKENS, D))
     c_parts = [c_edge] + exchange([c_up, c_side, c_corner], -1)
+    cot, ga_inner = prepare_inner(c_inner, out_weight)
+    cot, ga_edge = prepare_edge(c_parts, out_weight, cot)
     place = place.reshape(TOKENS)[ORDER].reshape(-1, 1)
 
+    replies, ga_inner = lax.optimization_barrier((replies, ga_inner))
     x_up, x_side, x_corner, x_inner, x_edge = pick(table, place, replies)
     x_parts = [x_edge] + exchange([x_up, x_side, x_corner], -1)
 
     band = lax.axis_index("lat")
     flag = (band == BANDS - 1).astype(I32).reshape(1)
     core = (band % 2).astype(I32).reshape(1)
-    first = attend_inner(x_inner, c_inner, weights)
-    x, left, right = attend_edge(x_parts, c_parts, flag, weights, first)
-    own, away = weight_terms(core, left, right)
+    first = attend_inner(x_inner, ga_inner, weights)
+    x, left, dp = attend_edge(x_parts, ga_edge, flag, weights, first)
+    edge, *away = finish_edge((x, left, dp, cot), weights)
+    up, side, corner = exchange(away, 1)
+    left, dp, edge = lax.optimization_barrier((left, dp, edge))
+    own, away = weight_terms(core, left, dp, cot)
     got = lax.ppermute(away, BOTH, OTHER_CORE)
-    edge, *away = finish_edge((x, left, right), weights)
-    up, side, corner = exchange(away, 1)
-    inner = finish_inner((x, left, right), weights)
-    half = add_halves(own, got)
-    half, inner, side, corner = lax.optimization_barrier((half, inner, side, corner))
-    terms = swap_blocks(half, BOTH, SAME_CORE)
+    inner = finish_inner((x, left, dp, cot), weights)
+    got, inner = lax.optimization_barrier((got, inner))
+    terms = swap_blocks(add_halves(own, got), BOTH, SAME_CORE)
     returned = [up, side, corner]
     outs = join([inner, edge] + returned)
     return (*outs, *sum_terms(terms))

time: 203 us -> 195 us (0.961)
  waiting for transfers between devices: 51.8 us -> 40.5 us
  Pallas kernels: 77.3 us -> 82.3 us
    all_to_all x2, waiting for transfers between devices: 38.4 us -> 24.3 us  [swap_blocks(): lax.all_to_all(values, axis, split_axis=0, concat_axis=0, axis_index_grou...]
    pallas_call x2 -> x4, Pallas kernels: 19.3 us -> 24.3 us  [the longest x1 10.3 us: attend_inner(): call(inner_kernel, 'attend_inner', (3,), [blocks(BLOCK, D)] + sources, ou...]
    ppermute x9, waiting for transfers between devices: 13.4 us -> 16.1 us  [exchange(): lax.ppermute(part, BOTH, shift_pairs(*step))]
    ppermute x1, starting transfers between devices: 2.76 us -> 0.31 us  [per_device(): got = lax.ppermute(away, BOTH, OTHER_CORE)]
    all_to_all x2, starting transfers between devices: 10.8 us -> 12.9 us  [swap_blocks(): lax.all_to_all(values, axis, split_axis=0, concat_axis=0, axis_index_grou...]
    unnamed x52 -> x46, local copies, waits for them, and re-layouts: 6.55 us -> 4.58 us
  transfers between devices with their start and end apart: 12 -> 12, of which waited for: 3 -> 4; matrix products, arithmetic and copies ran while one was open for 9% -> 10% of each run, Pallas kernels for 19% -> 19%
where the time goes in v8:
time: 195 us
  Pallas kernels  82.3 us (42%)
  waiting for transfers between devices  40.5 us (21%)
  starting transfers between devices  30.9 us (16%)
  local copies, waits for them, and re-layouts  23.1 us (12%)
  blocking collectives  16.7 us (9%)
    all_to_all x2, waiting for transfers between devices, swap_blocks(): lax.all_to_all(values, axis, split_axis=0, concat_axis=0, axis_index_grou...  24.3 us
    ppermute x9, starting transfers between devices, exchange(): lax.ppermute(part, BOTH, shift_pairs(*step))  17.7 us
    pallas_call x1, Pallas kernels, attend_edge(): call(edge_kernel, 'attend_edge', (5,), [pl.BlockSpec(memory_space=pltpu.S...  17.7 us
    all_to_all x1, blocking collectives, swap_blocks(): lax.all_to_all(values, axis, split_axis=0, concat_axis=0, axis_index_grou...  16.7 us
    ppermute x9, waiting for transfers between devices, exchange(): lax.ppermute(part, BOTH, shift_pairs(*step))  16.1 us
    all_to_all x2, starting transfers between devices, swap_blocks(): lax.all_to_all(values, axis, split_axis=0, concat_axis=0, axis_index_grou...  12.9 us
    gather x1, local copies, waits for them, and re-layouts, per_device(): place = place.reshape(TOKENS)[ORDER].reshape(-1, 1)  12.7 us
    pallas_call x1, Pallas kernels, attend_inner(): call(inner_kernel, 'attend_inner', (3,), [blocks(BLOCK, D)] + sources, ou...  10.3 us
  transfers between devices with their start and end apart: 12, of which 4 were waited for; matrix products, arithmetic and copies ran while one was open for 10% of the time, Pallas kernels for 19%

profile of v8, /device:TPU:1, one launch (start us, length us, event | category | flops | bytes accessed | tf_op | source)
XLA Modules:
  0.0 194.5 jit_solution(3235600157674886058)
XLA Ops:
  0.6 2.7 %requests.1 = (s32[16,1,288]{2,1,0:T(1,128)}, s32[1,2304]{1,0:T(1,128)}, s32[16,8]{1,0:T(8,128)}) custom-call(s32[1,2304]{1,0:T(1,128)} %bitcast.15, s32[1,2304]{1,0:T(1,128)} %bitcast.16), custom_call_target="tpu_custom_call" | custom-call | flops 100000000 | bytes 100000 | tf_op jit(solution)/shard_map/requests/pallas_call | solution.py:175
  3.3 16.7 %all_to_all.21.lists_ref = s32[16,1,288]{2,1,0:T(1,128)} all-to-all(s32[16,1,288]{2,1,0:T(1,128)} %get-tuple-element.46), channel_id=1, replica_groups=mesh['lat'=16,'lon'=8] {'lat'}, dimensions={0} | all-to-all | bytes 36864 | tf_op jit(solution)/shard_map/all_to_all | solution.py:672
  20.0 10.3 %serve.1 = bf16[4608,512]{1,0:T(8,128)(2,1)} custom-call(s32[16,1,288]{2,1,0:T(1,128)} %all_to_all.21.lists_ref, bf16[1152,512]{1,0:T(8,128)(2,1)} %buffer_ref.1), custom_call_target="tpu_custom_call" | custom-call | flops 5400000000 | bytes 6000000 | tf_op jit(solution)/shard_map/serve/pallas_call | solution.py:200
  30.3 4.7 %all-to-all-start.1 = ((bf16[16,288,512]{2,1,0:T(8,128)(2,1)}), bf16[16,288,512]{2,1,0:T(8,128)(2,1)}, u32[]{:S(2)}, u32[]{:S(2)}) async-start(bf16[16,288,512]{2,1,0:T(8,128)(2,1)} %bitcast.14), calls=%async_computation.1 | async-start | bytes 9437184 | tf_op jit(solution)/shard_map/all_to_all | solution.py:672
  35.0 3.9 %reshape.51.grid_ref = bf16[2304,512]{1,0:T(8,128)(2,1)S(1)} reshape(bf16[12,48,4,512]{3,2,1,0:T(4,128)(2,1)} %param.22) | data formatting | bytes 4718592 | tf_op jit(solution)/shard_map/reshape | solution.py:690
  39.0 1.5 sort_pieces.1
  41.7 7.9 %collective-permute-start.5 = (bf16[80,512]{1,0:T(8,128)(2,1)}, bf16[80,512]{1,0:T(8,128)(2,1)}, u32[]{:S(2)}, u32[]{:S(2)}) collective-permute-start(bf16[80,512]{1,0:T(8,128)(2,1)} %get-tuple-element.57), channel_id=1, source_target_pairs={{0,127},{1,120},{2,121},{3,122},{4,123},{5,124},{6,125},{7,126},{8... | collective-permute-start | bytes 245768 | tf_op jit(solution)/shard_map/ppermute | solution.py:668
  50.8 12.7 %gather_fusion = s32[2336]{0:T(1024)S(1)} fusion(s32[2304]{0:T(1024)S(1)} %reduce, s32[3072]{0:T(1024)S(1)} %pad_clamp_fusion), kind=kCustom, calls=%fused_computation | custom fusion | bytes 28032 | tf_op jit(solution)/shard_map/gather | solution.py:694
  63.5 1.9 reshape.63.place_ref
  68.6 23.3 %all-to-all-done.1 = bf16[16,288,512]{2,1,0:T(8,128)(2,1)} async-done(((bf16[16,288,512]{2,1,0:T(8,128)(2,1)}), bf16[16,288,512]{2,1,0:T(8,128)(2,1)}, u32[]{:S(2)}, u32[]{:S(2)}) %all-to-all-start.1) | async-done | bytes 4718624 | tf_op jit(solution)/shard_map/all_to_all | solution.py:672
  91.9 9.6 %pick.1 = (bf16[512,512]{1,0:T(8,128)(2,1)}, bf16[224,512]{1,0:T(8,128)(2,1)}, bf16[80,512]{1,0:T(8,128)(2,1)}, bf16[864,512]{1,0:T(8,128)(2,1)}, bf16[656,512]{1,0:T(8,128)(2,1)}) custom-call(s32[16,8]{1,0:T(8,128)} %get-tuple-element.44.table_ref, s32[2336,1]{1,0:T(8,128)} %reshape.63.place_ref, bf16[4608,512]{1,0:T(8,128)(2,1)} %bitcast.5.replies_ref), custom_call_target="tpu_custom_call" | custom-call | flops 3600000000 | bytes 8000000 | tf_op jit(solution)/shard_map/pick/pallas_call | solution.py:249
  103.0 4.5 %prepare_edge.1 = (bf16[2304,512]{1,0:T(8,128)(2,1)S(1)}, bf16[1440,512]{1,0:T(8,128)(2,1)S(1)}) custom-call(bf16[656,512]{1,0:T(8,128)(2,1)S(1)} %get-tuple-element.54.edge, bf16[512,512]{1,0:T(8,128)(2,1)} %collective-permute-done.3.up, bf16[224,512]{1,0:T(8,128)(2,1)} %collective-permute-done.4.side, ...), custom_call_target="tpu_custom_call", output_to_operand_aliasing={{0}: (6, {})} | custom-call | flops 800000000 | bytes 5000000 | tf_op jit(solution)/shard_map/prepare_edge/pallas_call | solution.py:410
  107.5 3.5 %collective-permute-start.2 = (bf16[80,512]{1,0:T(8,128)(2,1)S(1)}, bf16[80,512]{1,0:T(8,128)(2,1)S(1)}, u32[]{:S(2)}, u32[]{:S(2)}) collective-permute-start(bf16[80,512]{1,0:T(8,128)(2,1)S(1)} %copy-done.22), channel_id=1, source_target_pairs={{0,127},{1,120},{2,121},{3,122},{4,123},{5,124},{6,125},{7,126},{8... | collective-permute-start | bytes 245768 | tf_op jit(solution)/shard_map/ppermute | solution.py:668
  112.0 10.3 %attend_inner.1 = (bf16[2304,512]{1,0:T(8,128)(2,1)S(1)}, bf16[2304,1024]{1,0:T(8,128)(2,1)S(1)}, bf16[2304,1536]{1,0:T(8,128)(2,1)S(1)}) custom-call(bf16[864,512]{1,0:T(8,128)(2,1)S(1)} %copy-done.17, bf16[864,512]{1,0:T(8,128)(2,1)S(1)} %copy-done.16, bf16[512,1536]{1,0:T(8,128)(2,1)S(1)} %copy-done, f32[1,512]{1,0:T(1,128)S(1)} %bitcast.10), custom_call_target="tpu_custom_call" | custom-call | flops 5184000000 | bytes 8640000 | tf_op jit(solution)/shard_map/attend_inner/pallas_call | solution.py:459
  122.3 17.7 %attend_edge.1 = (bf16[2304,512]{1,0:T(8,128)(2,1)S(1)}, bf16[2304,1024]{1,0:T(8,128)(2,1)S(1)}, bf16[2304,1536]{1,0:T(8,128)(2,1)S(1)}) custom-call(s32[1]{0:T(128)} %bitcast.1.flag_ref, bf16[656,512]{1,0:T(8,128)(2,1)S(1)} %copy-done.18, ...), custom_call_target="tpu_custom_call", output_to_operand_aliasing={{0}: (10, {}), {1}: (11, {}), {2}: (12, {})} | custom-call | flops 8640000000 | bytes 14400000 | tf_op jit(solution)/shard_map/attend_edge/pallas_call | solution.py:473
  140.0 8.5 %finish_edge.1 = (bf16[2,656,512]{2,1,0:T(8,128)(2,1)S(1)}, bf16[2,512,512]{2,1,0:T(8,128)(2,1)}, bf16[2,224,512]{2,1,0:T(8,128)(2,1)S(1)}, bf16[2,80,512]{2,1,0:T(8,128)(2,1)S(1)}) custom-call(bf16[2,384,288]{2,1,0:T(8,128)(2,1)S(1)} %copy-done.4, bf16[2304,512]{1,0:T(8,128)(2,1)S(1)} %get-tuple-element.67.refs_0_, ...), custom_call_target="tpu_custom_call" | custom-call | flops 3168000000 | bytes 12960000 | tf_op jit(solution)/shard_map/finish_edge/pallas_call | solution.py:590
  148.5 5.3 %weight_terms.1 = (f32[1024,512]{1,0:T(8,128)S(1)}, bf16[1024,512]{1,0:T(8,128)(2,1)S(1)}) custom-call(s32[1]{0:T(128)} %bitcast.core_ref, bf16[2304,1024]{1,0:T(8,128)(2,1)S(1)} %get-tuple-element.70.refs_1_.left_ref, bf16[2304,1536]{1,0:T(8,128)(2,1)S(1)} %get-tuple-element.71.refs_2_.dp_ref, bf16[2304,512]{1,0:T(8,128)(2,1)S(1)} %get-tuple-element.68.refs_3_.cot_ref), custom_call_target="tpu_custom_call" | custom-call | flops 1000 | bytes 1000 | tf_op jit(solution)/shard_map/weight_terms/pallas_call | solution.py:500
  154.2 2.6 %collective-permute-start.7 = (bf16[2,512,512]{2,1,0:T(8,128)(2,1)}, bf16[2,512,512]{2,1,0:T(8,128)(2,1)}, u32[]{:S(2)}, u32[]{:S(2)}) collective-permute-start(bf16[2,512,512]{2,1,0:T(8,128)(2,1)} %get-tuple-element.75), channel_id=1, source_target_pairs={{0,8},{1,9},{2,10},{3,11},{4,12},{5,13},{6,14},{7,15},{8,16},{9,17... | collective-permute-start | bytes 3145736 | tf_op jit(solution)/shard_map/ppermute | solution.py:668
  156.8 3.7 %finish_inner.1.inner = bf16[2,864,512]{2,1,0:T(8,128)(2,1)S(1)} custom-call(bf16[144,144]{1,0:T(8,128)(2,1)S(1)} %copy-done.6, bf16[2304,512]{1,0:T(8,128)(2,1)S(1)} %get-tuple-element.67.refs_0_, bf16[2304,1024]{1,0:T(8,128)(2,1)S(1)} %get-tuple-element.70.refs_1_.left_ref, bf16[2304,1536]{1,0:T(8,128)(2,1)S(1)} %get-tuple-element.71.refs_2_.dp_ref, ...), custom_call_target="tpu_custom_call" | custom-call | flops 1000 | bytes 1000 | tf_op jit(solution)/shard_map/finish_inner/pallas_call | solution.py:581
  160.5 1.6 add_halves.1
  162.2 8.2 %all-to-all-start.2 = ((bf16[64,16,512]{2,1,0:T(8,128)(2,1)}), bf16[64,16,512]{2,1,0:T(8,128)(2,1)S(1)}, u32[]{:S(2)}, u32[]{:S(2)}) async-start(bf16[64,16,512]{2,1,0:T(8,128)(2,1)} %bitcast.7), calls=%async_computation.2 | async-start | bytes 2097152 | tf_op jit(solution)/shard_map/all_to_all | solution.py:672
  170.3 3.2 %collective-permute-done.9.corner = bf16[2,80,512]{2,1,0:T(8,128)(2,1)} collective-permute-done((bf16[2,80,512]{2,1,0:T(8,128)(2,1)S(1)}, bf16[2,80,512]{2,1,0:T(8,128)(2,1)}, u32[]{:S(2)}, u32[]{:S(2)}) %collective-permute-start.9) | collective-permute-done | bytes 163872 | tf_op jit(solution)/shard_map/ppermute | solution.py:668
  173.6 12.9 %collective-permute-done.8.side = bf16[2,224,512]{2,1,0:T(8,128)(2,1)} collective-permute-done((bf16[2,224,512]{2,1,0:T(8,128)(2,1)S(1)}, bf16[2,224,512]{2,1,0:T(8,128)(2,1)}, u32[]{:S(2)}, u32[]{:S(2)}) %collective-permute-start.8) | collective-permute-done | bytes 458784 | tf_op jit(solution)/shard_map/ppermute | solution.py:668
  187.9 4.7 %join.1 = (bf16[12,48,4,512]{3,2,1,0:T(4,128)(2,1)}, bf16[12,48,4,512]{3,2,1,0:T(4,128)(2,1)}) custom-call(bf16[2,864,512]{2,1,0:T(8,128)(2,1)S(1)} %copy-done.3, bf16[2,656,512]{2,1,0:T(8,128)(2,1)S(1)} %copy-done.11, bf16[2,512,512]{2,1,0:T(8,128)(2,1)} %collective-permute-done.7.up, bf16[2,224,512]{2,1,0:T(8,128)(2,1)} %collective-permute-done.8.side, ...), custom_call_target="tpu_custom_call" | custom-call | flops 60000002048 | bytes 9000000 | tf_op jit(solution)/shard_map/join/pallas_call | solution.py:635
  (66 shorter events, 11.6 us)
Async XLA Ops:
  30.3 61.6 %all-to-all-start.1 = ((bf16[16,288,512]{2,1,0:T(8,128)(2,1)}), bf16[16,288,512]{2,1,0:T(8,128)(2,1)}, u32[]{:S(2)}, u32[]{:S(2)}) async-start(bf16[16,288,512]{2,1,0:T(8,128)(2,1)} %bitcast.14), calls=%async_computation.1 | async-start | bytes 9437184 | tf_op jit(solution)/shard_map/all_to_all | solution.py:672
  38.9 11.8 %copy-start.20 = (s32[1,2304]{1,0:T(1,128)S(1)}, s32[1,2304]{1,0:T(1,128)}, u32[]{:S(2)}) copy-start(s32[1,2304]{1,0:T(1,128)} %get-tuple-element.45) | copy-start | bytes 27652
  38.9 11.8 %copy-start.19 = (s32[2336]{0:T(1024)S(1)}, s32[2336]{0:T(1024)}, u32[]{:S(2)}) copy-start(s32[2336]{0:T(1024)} %constant.48) | copy-start | bytes 28036
  41.4 61.5 %collective-permute-start.3 = (bf16[512,512]{1,0:T(8,128)(2,1)}, bf16[512,512]{1,0:T(8,128)(2,1)}, u32[]{:S(2)}, u32[]{:S(2)}) collective-permute-start(bf16[512,512]{1,0:T(8,128)(2,1)} %get-tuple-element.55), channel_id=1, source_target_pairs={{0,120},{1,121},{2,122},{3,123},{4,124},{5,125},{6,126},{7,127},{8... | collective-permute-start | bytes 1572872 | tf_op jit(solution)/shard_map/ppermute | solution.py:668
  41.7 61.3 %collective-permute-start.5 = (bf16[80,512]{1,0:T(8,128)(2,1)}, bf16[80,512]{1,0:T(8,128)(2,1)}, u32[]{:S(2)}, u32[]{:S(2)}) collective-permute-start(bf16[80,512]{1,0:T(8,128)(2,1)} %get-tuple-element.57), channel_id=1, source_target_pairs={{0,127},{1,120},{2,121},{3,122},{4,123},{5,124},{6,125},{7,126},{8... | collective-permute-start | bytes 245768 | tf_op jit(solution)/shard_map/ppermute | solution.py:668
  49.5 53.4 %collective-permute-start.4 = (bf16[224,512]{1,0:T(8,128)(2,1)}, bf16[224,512]{1,0:T(8,128)(2,1)}, u32[]{:S(2)}, u32[]{:S(2)}) collective-permute-start(bf16[224,512]{1,0:T(8,128)(2,1)} %get-tuple-element.56), channel_id=1, source_target_pairs={{0,7},{1,0},{2,1},{3,2},{4,3},{5,4},{6,5},{7,6},{8,15},{9,8},{10,9... | collective-permute-start | bytes 688136 | tf_op jit(solution)/shard_map/ppermute | solution.py:668
  50.8 14.6 %copy-start.1 = (bf16[512,512]{1,0:T(8,128)(2,1)S(1)}, bf16[512,512]{1,0:T(8,128)(2,1)}, u32[]{:S(2)}) copy-start(bf16[512,512]{1,0:T(8,128)(2,1)} %refs_6_.3) | copy-start | bytes 1572868
  91.9 11.1 %copy-start.7 = (bf16[288,320]{1,0:T(8,128)(2,1)S(1)}, bf16[288,320]{1,0:T(8,128)(2,1)}, u32[]{:S(2)}) copy-start(bf16[288,320]{1,0:T(8,128)(2,1)} %constant.39.clone.join_ref) | copy-start | bytes 552964
  101.5 10.4 %copy-start = (bf16[512,1536]{1,0:T(8,128)(2,1)S(1)}, bf16[512,1536]{1,0:T(8,128)(2,1)}, u32[]{:S(2)}) copy-start(bf16[512,1536]{1,0:T(8,128)(2,1)} %refs_4_.3) | copy-start | bytes 4718596
  101.5 10.4 %copy-start.9 = (f32[512]{0:T(512)S(1)}, f32[512]{0:T(512)}, u32[]{:S(2)}) copy-start(f32[512]{0:T(512)} %param.19) | copy-start | bytes 6148
  101.5 10.4 %copy-start.16 = (bf16[864,512]{1,0:T(8,128)(2,1)S(1)}, bf16[864,512]{1,0:T(8,128)(2,1)}, u32[]{:S(2)}) copy-start(bf16[864,512]{1,0:T(8,128)(2,1)} %copy-done.15) | copy-start | bytes 2654212
  101.5 10.4 %copy-start.17 = (bf16[864,512]{1,0:T(8,128)(2,1)S(1)}, bf16[864,512]{1,0:T(8,128)(2,1)}, u32[]{:S(2)}) copy-start(bf16[864,512]{1,0:T(8,128)(2,1)} %get-tuple-element.60.x_ref) | copy-start | bytes 2654212
  101.5 20.8 %collective-permute-start = (bf16[512,512]{1,0:T(8,128)(2,1)}, bf16[512,512]{1,0:T(8,128)(2,1)S(1)}, u32[]{:S(2)}, u32[]{:S(2)}) collective-permute-start(bf16[512,512]{1,0:T(8,128)(2,1)} %get-tuple-element.51), channel_id=1, source_target_pairs={{0,120},{1,121},{2,122},{3,123},{4,124},{5,125},{6,126},{7,127},{8... | collective-permute-start | bytes 1572872 | tf_op jit(solution)/shard_map/ppermute | solution.py:668
  107.5 14.8 %collective-permute-start.2 = (bf16[80,512]{1,0:T(8,128)(2,1)S(1)}, bf16[80,512]{1,0:T(8,128)(2,1)S(1)}, u32[]{:S(2)}, u32[]{:S(2)}) collective-permute-start(bf16[80,512]{1,0:T(8,128)(2,1)S(1)} %copy-done.22), channel_id=1, source_target_pairs={{0,127},{1,120},{2,121},{3,122},{4,123},{5,124},{6,125},{7,126},{8... | collective-permute-start | bytes 245768 | tf_op jit(solution)/shard_map/ppermute | solution.py:668
  111.0 11.3 %collective-permute-start.1 = (bf16[224,512]{1,0:T(8,128)(2,1)S(1)}, bf16[224,512]{1,0:T(8,128)(2,1)S(1)}, u32[]{:S(2)}, u32[]{:S(2)}) collective-permute-start(bf16[224,512]{1,0:T(8,128)(2,1)S(1)} %copy-done.21), channel_id=1, source_target_pairs={{0,7},{1,0},{2,1},{3,2},{4,3},{5,4},{6,5},{7,6},{8,15},{9,8},{10,9... | collective-permute-start | bytes 688136 | tf_op jit(solution)/shard_map/ppermute | solution.py:668
  111.9 10.4 %copy-start.14 = (f32[144,576]{1,0:T(8,128)S(1)}, f32[144,576]{1,0:T(8,128)}, u32[]{:S(2)}) copy-start(f32[144,576]{1,0:T(8,128)} %constant.42.clone.apart_ref) | copy-start | bytes 995332
  112.0 10.4 %copy-start.18 = (bf16[656,512]{1,0:T(8,128)(2,1)S(1)}, bf16[656,512]{1,0:T(8,128)(2,1)}, u32[]{:S(2)}) copy-start(bf16[656,512]{1,0:T(8,128)(2,1)} %get-tuple-element.50.xe) | copy-start | bytes 2015236
  122.3 17.7 %copy-start.4 = (bf16[2,384,288]{2,1,0:T(8,128)(2,1)S(1)}, bf16[2,384,288]{2,1,0:T(8,128)(2,1)}, u32[]{:S(2)}) copy-start(bf16[2,384,288]{2,1,0:T(8,128)(2,1)} %constant.43.clone.back_ref) | copy-start | bytes 1327108
  153.9 6.6 %collective-permute-start.6 = (bf16[1024,512]{1,0:T(8,128)(2,1)S(1)}, bf16[1024,512]{1,0:T(8,128)(2,1)S(1)}, u32[]{:S(2)}, u32[]{:S(2)}) collective-permute-start(bf16[1024,512]{1,0:T(8,128)(2,1)S(1)} %get-tuple-element.72), channel_id=1, source_target_pairs={{0,8},{1,9},{2,10},{3,11},{4,12},{5,13},{6,14},{7,15},{8,0},{9,1},... | collective-permute-start | bytes 3145736 | tf_op jit(solution)/shard_map/ppermute | solution.py:709
  154.2 32.3 %collective-permute-start.7 = (bf16[2,512,512]{2,1,0:T(8,128)(2,1)}, bf16[2,512,512]{2,1,0:T(8,128)(2,1)}, u32[]{:S(2)}, u32[]{:S(2)}) collective-permute-start(bf16[2,512,512]{2,1,0:T(8,128)(2,1)} %get-tuple-element.75), channel_id=1, source_target_pairs={{0,8},{1,9},{2,10},{3,11},{4,12},{5,13},{6,14},{7,15},{8,16},{9,17... | collective-permute-start | bytes 3145736 | tf_op jit(solution)/shard_map/ppermute | solution.py:668
  156.8 29.7 %collective-permute-start.8 = (bf16[2,224,512]{2,1,0:T(8,128)(2,1)S(1)}, bf16[2,224,512]{2,1,0:T(8,128)(2,1)}, u32[]{:S(2)}, u32[]{:S(2)}) collective-permute-start(bf16[2,224,512]{2,1,0:T(8,128)(2,1)S(1)} %get-tuple-element.76), channel_id=1, source_target_pairs={{0,1},{1,2},{2,3},{3,4},{4,5},{5,6},{6,7},{7,0},{8,9},{9,10},{10,1... | collective-permute-start | bytes 1376264 | tf_op jit(solution)/shard_map/ppermute | solution.py:668
  156.8 16.8 %collective-permute-start.9 = (bf16[2,80,512]{2,1,0:T(8,128)(2,1)S(1)}, bf16[2,80,512]{2,1,0:T(8,128)(2,1)}, u32[]{:S(2)}, u32[]{:S(2)}) collective-permute-start(bf16[2,80,512]{2,1,0:T(8,128)(2,1)S(1)} %get-tuple-element.77), channel_id=1, source_target_pairs={{0,9},{1,10},{2,11},{3,12},{4,13},{5,14},{6,15},{7,8},{8,17},{9,18... | collective-permute-start | bytes 491528 | tf_op jit(solution)/shard_map/ppermute | solution.py:668
  160.5 25.9 %copy-start.11 = (bf16[2,656,512]{2,1,0:T(8,128)(2,1)S(1)}, bf16[2,656,512]{2,1,0:T(8,128)(2,1)}, u32[]{:S(2)}) copy-start(bf16[2,656,512]{2,1,0:T(8,128)(2,1)} %copy-done.10) | copy-start | bytes 4030468
  162.2 31.6 %all-to-all-start.2 = ((bf16[64,16,512]{2,1,0:T(8,128)(2,1)}), bf16[64,16,512]{2,1,0:T(8,128)(2,1)S(1)}, u32[]{:S(2)}, u32[]{:S(2)}) async-start(bf16[64,16,512]{2,1,0:T(8,128)(2,1)} %bitcast.7), calls=%async_computation.2 | async-start | bytes 2097152 | tf_op jit(solution)/shard_map/all_to_all | solution.py:672
  (11 other events, 43.2 us)

commit v9 on v8

--- a/solution.py
+++ b/solution.py
@@ -357,10 +357,10 @@
             low = probs.astype(BF16)
             weighted = probs * product(values, grads, NT)
             slope = weighted - probs * jnp.sum(weighted, 0, keepdims=True)
-            slope = (slope * SCALE).astype(BF16)
+            slope = slope.astype(BF16)
             ha_ref[rows, slice(D + quad * QUAD, D + quad * QUAD + QUAD)] = gather(low, values).astype(BF16)
-            dp_ref[rows, spot[0]] = gather(slope, keys).astype(BF16)
-            dp_ref[rows, spot[1]] = product(slope, queries).astype(BF16)
+            dp_ref[rows, spot[0]] = (gather(slope, keys) * SCALE).astype(BF16)
+            dp_ref[rows, spot[1]] = (product(slope, queries) * SCALE).astype(BF16)
             dp_ref[rows, spot[2]] = product(low, grads).astype(BF16)
 
 
@@ -402,7 +402,7 @@
         prepare_inner_kernel, "prepare_inner", (3,),
         [blocks(BLOCK, D), whole(D, D)],
         [blocks(BLOCK, D)] * 2, shapes((TOKENS, D), (INNER, D)),
-        [], (500000000, 3000000, 0), 20,
+        [], (500000000, 3000000, 0), 10,
     )(inner, ow)
 
 
@@ -412,7 +412,7 @@
         EDGE_SPECS + [whole(BLOCK, 4 * SMALL), whole(D, D), pl.BlockSpec(memory_space=pl.ANY)],
         [pl.BlockSpec((BLOCK, D), lambda i: (i + 3, 0)), blocks(BLOCK, D)],
         shapes((TOKENS, D), (5 * BLOCK, D)),
-        [pltpu.VMEM((BLOCK, D), F32)], (800000000, 5000000, 0), 20,
+        [pltpu.VMEM((BLOCK, D), F32)], (800000000, 5000000, 0), 12,
         aliases={6: 0},
     )(*parts, jnp.asarray(CORNER_JOIN, BF16), ow, cot)
 
@@ -459,7 +459,7 @@
     return call(
         inner_kernel, "attend_inner", (3,),
         [blocks(BLOCK, D)] + sources,
-        outs, out_shapes, scratch, cost, 18,
+        outs, out_shapes, scratch, cost, 14,
     )(x, ga, *weights[:2])
 
 
@@ -477,7 +477,7 @@
         + [whole(BLOCK, 4 * SMALL), whole(WIN, 4 * WIN)]
         + sources
         + [pl.BlockSpec(memory_space=pl.ANY)] * 3,
-        outs, out_shapes, scratch + [pltpu.VMEM((BLOCK, D), F32)], cost, 24,
+        outs, out_shapes, scratch + [pltpu.VMEM((BLOCK, D), F32)], cost, 16,
         aliases={10 + n: n for n in range(3)},
     )(flag, *parts, jnp.asarray(CORNER_JOIN, BF16), jnp.asarray(apart_matrix()), ga, *weights[:2], *carried)
 
@@ -503,7 +503,7 @@
         [whole(1024, D)] * 2,
         [jax.ShapeDtypeStruct((1024, D), F32), jax.ShapeDtypeStruct((1024, D), BF16)],
         [pltpu.VMEM((64, 2, 2, 8, D), F32)],
-        (1000, 1000, 0), 22,
+        (1000, 1000, 0), 14,
     )(core, left, dp, cot)
 
 
@@ -515,7 +515,7 @@
     return call(
         add_kernel, "add_halves", (4,),
         [blocks(256, D)] * 2, blocks(256, D), shapes((1024, D))[0], [],
-        (1000000, 4000000, 0), 10,
+        (1000000, 4000000, 0), 6,
     )(own, got)
 
 
@@ -582,7 +582,7 @@
         finish_inner_kernel, "finish_inner", (3,),
         [whole(WIN, WIN)] + finish_specs(0),
         pl.BlockSpec((2, BLOCK, D), lambda i: (0, i, 0)), shapes((2, INNER, D))[0], [],
-        (1000, 1000, 0), 20,
+        (1000, 1000, 0), 14,
     )(jnp.asarray(SPLIT, BF16), *values, *weights)
 
 
@@ -591,7 +591,7 @@
         finish_edge_kernel, "finish_edge", (5,),
         [pl.BlockSpec((None,) + BACK.shape[1:], lambda i: (i // 4, 0, 0))] + finish_specs(3),
         EDGE_PAIRS, shapes(*[(2, n, D) for n in PIECES[1:]]), [],
-        finish_cost(5 * BLOCK), 24,
+        finish_cost(5 * BLOCK), 16,
     )(jnp.asarray(BACK, BF16), *values, *weights)
 
 
@@ -636,7 +636,7 @@
         join_kernel, "join", (4,),
         [whole(2, n, D) for n in PIECES],
         [spec] * 2, shapes(*[dim] * 2), [],
-        (60000000000, 9000000, 0), 26,
+        (60000000000, 9000000, 0), 16,
     )(*parts)
 
 

time: 195 us -> 195 us (level)
  no operation moved by 1% of the time
where the time goes in v9:
time: 195 us; the launch traced here: 194 us
  Pallas kernels  82.2 us (42%)
  waiting for transfers between devices  40.5 us (21%)
  starting transfers between devices  30.9 us (16%)
  local copies, waits for them, and re-layouts  23.1 us (12%)
  blocking collectives  16.7 us (9%)
    all_to_all x2, waiting for transfers between devices, swap_blocks(): lax.all_to_all(values, axis, split_axis=0, concat_axis=0, axis_index_grou...  24.4 us
    ppermute x9, starting transfers between devices, exchange(): lax.ppermute(part, BOTH, shift_pairs(*step))  17.7 us
    pallas_call x1, Pallas kernels, attend_edge(): call(edge_kernel, 'attend_edge', (5,), [pl.BlockSpec(memory_space=pltpu.S...  17.6 us
    all_to_all x1, blocking collectives, swap_blocks(): lax.all_to_all(values, axis, split_axis=0, concat_axis=0, axis_index_grou...  16.7 us
    ppermute x9, waiting for transfers between devices, exchange(): lax.ppermute(part, BOTH, shift_pairs(*step))  16.1 us
    all_to_all x2, starting transfers between devices, swap_blocks(): lax.all_to_all(values, axis, split_axis=0, concat_axis=0, axis_index_grou...  12.9 us
    gather x1, local copies, waits for them, and re-layouts, per_device(): place = place.reshape(TOKENS)[ORDER].reshape(-1, 1)  12.7 us
    pallas_call x1, Pallas kernels, serve(): call(serve_kernel, 'serve', (BANDS // ASKERS,), [pl.BlockSpec((ASKERS, 1,...  10.3 us
  transfers between devices with their start and end apart: 12, of which 4 were waited for; matrix products, arithmetic and copies ran while one was open for 10% of the time, Pallas kernels for 19%

profile of v9, /device:TPU:1, one launch (start us, length us, event | category | flops | bytes accessed | tf_op | source)
XLA Modules:
  0.0 194.4 jit_solution(16494800593384617117)
XLA Ops:
  0.6 2.7 %requests.1 = (s32[16,1,288]{2,1,0:T(1,128)}, s32[1,2304]{1,0:T(1,128)}, s32[16,8]{1,0:T(8,128)}) custom-call(s32[1,2304]{1,0:T(1,128)} %bitcast.15, s32[1,2304]{1,0:T(1,128)} %bitcast.16), custom_call_target="tpu_custom_call" | custom-call | flops 100000000 | bytes 100000 | tf_op jit(solution)/shard_map/requests/pallas_call | solution.py:175
  3.3 16.7 %all_to_all.21.lists_ref = s32[16,1,288]{2,1,0:T(1,128)} all-to-all(s32[16,1,288]{2,1,0:T(1,128)} %get-tuple-element.46), channel_id=1, replica_groups=mesh['lat'=16,'lon'=8] {'lat'}, dimensions={0} | all-to-all | bytes 36864 | tf_op jit(solution)/shard_map/all_to_all | solution.py:672
  20.0 10.3 %serve.1 = bf16[4608,512]{1,0:T(8,128)(2,1)} custom-call(s32[16,1,288]{2,1,0:T(1,128)} %all_to_all.21.lists_ref, bf16[1152,512]{1,0:T(8,128)(2,1)} %buffer_ref.1), custom_call_target="tpu_custom_call" | custom-call | flops 5400000000 | bytes 6000000 | tf_op jit(solution)/shard_map/serve/pallas_call | solution.py:200
  30.3 4.7 %all-to-all-start.1 = ((bf16[16,288,512]{2,1,0:T(8,128)(2,1)}), bf16[16,288,512]{2,1,0:T(8,128)(2,1)}, u32[]{:S(2)}, u32[]{:S(2)}) async-start(bf16[16,288,512]{2,1,0:T(8,128)(2,1)} %bitcast.14), calls=%async_computation.1 | async-start | bytes 9437184 | tf_op jit(solution)/shard_map/all_to_all | solution.py:672
  35.0 3.9 %reshape.51.grid_ref = bf16[2304,512]{1,0:T(8,128)(2,1)S(1)} reshape(bf16[12,48,4,512]{3,2,1,0:T(4,128)(2,1)} %param.22) | data formatting | bytes 4718592 | tf_op jit(solution)/shard_map/reshape | solution.py:690
  39.0 1.5 sort_pieces.1
  41.7 7.9 %collective-permute-start.5 = (bf16[80,512]{1,0:T(8,128)(2,1)}, bf16[80,512]{1,0:T(8,128)(2,1)}, u32[]{:S(2)}, u32[]{:S(2)}) collective-permute-start(bf16[80,512]{1,0:T(8,128)(2,1)} %get-tuple-element.57), channel_id=1, source_target_pairs={{0,127},{1,120},{2,121},{3,122},{4,123},{5,124},{6,125},{7,126},{8... | collective-permute-start | bytes 245768 | tf_op jit(solution)/shard_map/ppermute | solution.py:668
  50.8 12.7 %gather_fusion = s32[2336]{0:T(1024)S(1)} fusion(s32[2304]{0:T(1024)S(1)} %reduce, s32[3072]{0:T(1024)S(1)} %pad_clamp_fusion), kind=kCustom, calls=%fused_computation | custom fusion | bytes 28032 | tf_op jit(solution)/shard_map/gather | solution.py:694
  63.5 1.9 reshape.63.place_ref
  68.6 23.3 %all-to-all-done.1 = bf16[16,288,512]{2,1,0:T(8,128)(2,1)} async-done(((bf16[16,288,512]{2,1,0:T(8,128)(2,1)}), bf16[16,288,512]{2,1,0:T(8,128)(2,1)}, u32[]{:S(2)}, u32[]{:S(2)}) %all-to-all-start.1) | async-done | bytes 4718624 | tf_op jit(solution)/shard_map/all_to_all | solution.py:672
  91.9 9.6 %pick.1 = (bf16[512,512]{1,0:T(8,128)(2,1)}, bf16[224,512]{1,0:T(8,128)(2,1)}, bf16[80,512]{1,0:T(8,128)(2,1)}, bf16[864,512]{1,0:T(8,128)(2,1)}, bf16[656,512]{1,0:T(8,128)(2,1)}) custom-call(s32[16,8]{1,0:T(8,128)} %get-tuple-element.44.table_ref, s32[2336,1]{1,0:T(8,128)} %reshape.63.place_ref, bf16[4608,512]{1,0:T(8,128)(2,1)} %bitcast.5.replies_ref), custom_call_target="tpu_custom_call" | custom-call | flops 3600000000 | bytes 8000000 | tf_op jit(solution)/shard_map/pick/pallas_call | solution.py:249
  103.0 4.5 %prepare_edge.1 = (bf16[2304,512]{1,0:T(8,128)(2,1)S(1)}, bf16[1440,512]{1,0:T(8,128)(2,1)S(1)}) custom-call(bf16[656,512]{1,0:T(8,128)(2,1)S(1)} %get-tuple-element.54.edge, bf16[512,512]{1,0:T(8,128)(2,1)} %collective-permute-done.3.up, bf16[224,512]{1,0:T(8,128)(2,1)} %collective-permute-done.4.side, ...), custom_call_target="tpu_custom_call", output_to_operand_aliasing={{0}: (6, {})} | custom-call | flops 800000000 | bytes 5000000 | tf_op jit(solution)/shard_map/prepare_edge/pallas_call | solution.py:410
  107.5 3.5 %collective-permute-start.2 = (bf16[80,512]{1,0:T(8,128)(2,1)S(1)}, bf16[80,512]{1,0:T(8,128)(2,1)S(1)}, u32[]{:S(2)}, u32[]{:S(2)}) collective-permute-start(bf16[80,512]{1,0:T(8,128)(2,1)S(1)} %copy-done.22), channel_id=1, source_target_pairs={{0,127},{1,120},{2,121},{3,122},{4,123},{5,124},{6,125},{7,126},{8... | collective-permute-start | bytes 245768 | tf_op jit(solution)/shard_map/ppermute | solution.py:668
  111.9 10.3 %attend_inner.1 = (bf16[2304,512]{1,0:T(8,128)(2,1)S(1)}, bf16[2304,1024]{1,0:T(8,128)(2,1)S(1)}, bf16[2304,1536]{1,0:T(8,128)(2,1)S(1)}) custom-call(bf16[864,512]{1,0:T(8,128)(2,1)S(1)} %copy-done.17, bf16[864,512]{1,0:T(8,128)(2,1)S(1)} %copy-done.16, bf16[512,1536]{1,0:T(8,128)(2,1)S(1)} %copy-done, f32[1,512]{1,0:T(1,128)S(1)} %bitcast.10), custom_call_target="tpu_custom_call" | custom-call | flops 5184000000 | bytes 8640000 | tf_op jit(solution)/shard_map/attend_inner/pallas_call | solution.py:459
  122.3 17.6 %attend_edge.1 = (bf16[2304,512]{1,0:T(8,128)(2,1)S(1)}, bf16[2304,1024]{1,0:T(8,128)(2,1)S(1)}, bf16[2304,1536]{1,0:T(8,128)(2,1)S(1)}) custom-call(s32[1]{0:T(128)} %bitcast.1.flag_ref, bf16[656,512]{1,0:T(8,128)(2,1)S(1)} %copy-done.18, ...), custom_call_target="tpu_custom_call", output_to_operand_aliasing={{0}: (10, {}), {1}: (11, {}), {2}: (12, {})} | custom-call | flops 8640000000 | bytes 14400000 | tf_op jit(solution)/shard_map/attend_edge/pallas_call | solution.py:473
  139.8 8.5 %finish_edge.1 = (bf16[2,656,512]{2,1,0:T(8,128)(2,1)S(1)}, bf16[2,512,512]{2,1,0:T(8,128)(2,1)}, bf16[2,224,512]{2,1,0:T(8,128)(2,1)S(1)}, bf16[2,80,512]{2,1,0:T(8,128)(2,1)S(1)}) custom-call(bf16[2,384,288]{2,1,0:T(8,128)(2,1)S(1)} %copy-done.4, bf16[2304,512]{1,0:T(8,128)(2,1)S(1)} %get-tuple-element.67.refs_0_, ...), custom_call_target="tpu_custom_call" | custom-call | flops 3168000000 | bytes 12960000 | tf_op jit(solution)/shard_map/finish_edge/pallas_call | solution.py:590
  148.3 5.3 %weight_terms.1 = (f32[1024,512]{1,0:T(8,128)S(1)}, bf16[1024,512]{1,0:T(8,128)(2,1)S(1)}) custom-call(s32[1]{0:T(128)} %bitcast.core_ref, bf16[2304,1024]{1,0:T(8,128)(2,1)S(1)} %get-tuple-element.70.refs_1_.left_ref, bf16[2304,1536]{1,0:T(8,128)(2,1)S(1)} %get-tuple-element.71.refs_2_.dp_ref, bf16[2304,512]{1,0:T(8,128)(2,1)S(1)} %get-tuple-element.68.refs_3_.cot_ref), custom_call_target="tpu_custom_call" | custom-call | flops 1000 | bytes 1000 | tf_op jit(solution)/shard_map/weight_terms/pallas_call | solution.py:500
  154.0 2.6 %collective-permute-start.7 = (bf16[2,512,512]{2,1,0:T(8,128)(2,1)}, bf16[2,512,512]{2,1,0:T(8,128)(2,1)}, u32[]{:S(2)}, u32[]{:S(2)}) collective-permute-start(bf16[2,512,512]{2,1,0:T(8,128)(2,1)} %get-tuple-element.75), channel_id=1, source_target_pairs={{0,8},{1,9},{2,10},{3,11},{4,12},{5,13},{6,14},{7,15},{8,16},{9,17... | collective-permute-start | bytes 3145736 | tf_op jit(solution)/shard_map/ppermute | solution.py:668
  156.6 3.7 %finish_inner.1.inner = bf16[2,864,512]{2,1,0:T(8,128)(2,1)S(1)} custom-call(bf16[144,144]{1,0:T(8,128)(2,1)S(1)} %copy-done.6, bf16[2304,512]{1,0:T(8,128)(2,1)S(1)} %get-tuple-element.67.refs_0_, bf16[2304,1024]{1,0:T(8,128)(2,1)S(1)} %get-tuple-element.70.refs_1_.left_ref, bf16[2304,1536]{1,0:T(8,128)(2,1)S(1)} %get-tuple-element.71.refs_2_.dp_ref, ...), custom_call_target="tpu_custom_call" | custom-call | flops 1000 | bytes 1000 | tf_op jit(solution)/shard_map/finish_inner/pallas_call | solution.py:581
  160.4 1.6 add_halves.1
  162.0 8.2 %all-to-all-start.2 = ((bf16[64,16,512]{2,1,0:T(8,128)(2,1)}), bf16[64,16,512]{2,1,0:T(8,128)(2,1)S(1)}, u32[]{:S(2)}, u32[]{:S(2)}) async-start(bf16[64,16,512]{2,1,0:T(8,128)(2,1)} %bitcast.7), calls=%async_computation.2 | async-start | bytes 2097152 | tf_op jit(solution)/shard_map/all_to_all | solution.py:672
  170.2 3.2 %collective-permute-done.9.corner = bf16[2,80,512]{2,1,0:T(8,128)(2,1)} collective-permute-done((bf16[2,80,512]{2,1,0:T(8,128)(2,1)S(1)}, bf16[2,80,512]{2,1,0:T(8,128)(2,1)}, u32[]{:S(2)}, u32[]{:S(2)}) %collective-permute-start.9) | collective-permute-done | bytes 163872 | tf_op jit(solution)/shard_map/ppermute | solution.py:668
  173.4 12.9 %collective-permute-done.8.side = bf16[2,224,512]{2,1,0:T(8,128)(2,1)} collective-permute-done((bf16[2,224,512]{2,1,0:T(8,128)(2,1)S(1)}, bf16[2,224,512]{2,1,0:T(8,128)(2,1)}, u32[]{:S(2)}, u32[]{:S(2)}) %collective-permute-start.8) | collective-permute-done | bytes 458784 | tf_op jit(solution)/shard_map/ppermute | solution.py:668
  187.7 4.7 %join.1 = (bf16[12,48,4,512]{3,2,1,0:T(4,128)(2,1)}, bf16[12,48,4,512]{3,2,1,0:T(4,128)(2,1)}) custom-call(bf16[2,864,512]{2,1,0:T(8,128)(2,1)S(1)} %copy-done.3, bf16[2,656,512]{2,1,0:T(8,128)(2,1)S(1)} %copy-done.11, bf16[2,512,512]{2,1,0:T(8,128)(2,1)} %collective-permute-done.7.up, bf16[2,224,512]{2,1,0:T(8,128)(2,1)} %collective-permute-done.8.side, ...), custom_call_target="tpu_custom_call" | custom-call | flops 60000002048 | bytes 9000000 | tf_op jit(solution)/shard_map/join/pallas_call | solution.py:635
  (66 shorter events, 11.7 us)
Async XLA Ops:
  30.3 61.6 %all-to-all-start.1 = ((bf16[16,288,512]{2,1,0:T(8,128)(2,1)}), bf16[16,288,512]{2,1,0:T(8,128)(2,1)}, u32[]{:S(2)}, u32[]{:S(2)}) async-start(bf16[16,288,512]{2,1,0:T(8,128)(2,1)} %bitcast.14), calls=%async_computation.1 | async-start | bytes 9437184 | tf_op jit(solution)/shard_map/all_to_all | solution.py:672
  38.9 11.8 %copy-start.20 = (s32[1,2304]{1,0:T(1,128)S(1)}, s32[1,2304]{1,0:T(1,128)}, u32[]{:S(2)}) copy-start(s32[1,2304]{1,0:T(1,128)} %get-tuple-element.45) | copy-start | bytes 27652
  38.9 11.8 %copy-start.19 = (s32[2336]{0:T(1024)S(1)}, s32[2336]{0:T(1024)}, u32[]{:S(2)}) copy-start(s32[2336]{0:T(1024)} %constant.48) | copy-start | bytes 28036
  41.4 61.5 %collective-permute-start.3 = (bf16[512,512]{1,0:T(8,128)(2,1)}, bf16[512,512]{1,0:T(8,128)(2,1)}, u32[]{:S(2)}, u32[]{:S(2)}) collective-permute-start(bf16[512,512]{1,0:T(8,128)(2,1)} %get-tuple-element.55), channel_id=1, source_target_pairs={{0,120},{1,121},{2,122},{3,123},{4,124},{5,125},{6,126},{7,127},{8... | collective-permute-start | bytes 1572872 | tf_op jit(solution)/shard_map/ppermute | solution.py:668
  41.7 61.2 %collective-permute-start.5 = (bf16[80,512]{1,0:T(8,128)(2,1)}, bf16[80,512]{1,0:T(8,128)(2,1)}, u32[]{:S(2)}, u32[]{:S(2)}) collective-permute-start(bf16[80,512]{1,0:T(8,128)(2,1)} %get-tuple-element.57), channel_id=1, source_target_pairs={{0,127},{1,120},{2,121},{3,122},{4,123},{5,124},{6,125},{7,126},{8... | collective-permute-start | bytes 245768 | tf_op jit(solution)/shard_map/ppermute | solution.py:668
  49.5 53.4 %collective-permute-start.4 = (bf16[224,512]{1,0:T(8,128)(2,1)}, bf16[224,512]{1,0:T(8,128)(2,1)}, u32[]{:S(2)}, u32[]{:S(2)}) collective-permute-start(bf16[224,512]{1,0:T(8,128)(2,1)} %get-tuple-element.56), channel_id=1, source_target_pairs={{0,7},{1,0},{2,1},{3,2},{4,3},{5,4},{6,5},{7,6},{8,15},{9,8},{10,9... | collective-permute-start | bytes 688136 | tf_op jit(solution)/shard_map/ppermute | solution.py:668
  50.8 14.6 %copy-start.1 = (bf16[512,512]{1,0:T(8,128)(2,1)S(1)}, bf16[512,512]{1,0:T(8,128)(2,1)}, u32[]{:S(2)}) copy-start(bf16[512,512]{1,0:T(8,128)(2,1)} %refs_6_.3) | copy-start | bytes 1572868
  91.9 11.1 %copy-start.7 = (bf16[288,320]{1,0:T(8,128)(2,1)S(1)}, bf16[288,320]{1,0:T(8,128)(2,1)}, u32[]{:S(2)}) copy-start(bf16[288,320]{1,0:T(8,128)(2,1)} %constant.39.clone.join_ref) | copy-start | bytes 552964
  101.5 10.4 %copy-start = (bf16[512,1536]{1,0:T(8,128)(2,1)S(1)}, bf16[512,1536]{1,0:T(8,128)(2,1)}, u32[]{:S(2)}) copy-start(bf16[512,1536]{1,0:T(8,128)(2,1)} %refs_4_.3) | copy-start | bytes 4718596
  101.5 10.4 %copy-start.9 = (f32[512]{0:T(512)S(1)}, f32[512]{0:T(512)}, u32[]{:S(2)}) copy-start(f32[512]{0:T(512)} %param.19) | copy-start | bytes 6148
  101.5 10.4 %copy-start.16 = (bf16[864,512]{1,0:T(8,128)(2,1)S(1)}, bf16[864,512]{1,0:T(8,128)(2,1)}, u32[]{:S(2)}) copy-start(bf16[864,512]{1,0:T(8,128)(2,1)} %copy-done.15) | copy-start | bytes 2654212
  101.5 10.4 %copy-start.17 = (bf16[864,512]{1,0:T(8,128)(2,1)S(1)}, bf16[864,512]{1,0:T(8,128)(2,1)}, u32[]{:S(2)}) copy-start(bf16[864,512]{1,0:T(8,128)(2,1)} %get-tuple-element.60.x_ref) | copy-start | bytes 2654212
  101.5 20.7 %collective-permute-start = (bf16[512,512]{1,0:T(8,128)(2,1)}, bf16[512,512]{1,0:T(8,128)(2,1)S(1)}, u32[]{:S(2)}, u32[]{:S(2)}) collective-permute-start(bf16[512,512]{1,0:T(8,128)(2,1)} %get-tuple-element.51), channel_id=1, source_target_pairs={{0,120},{1,121},{2,122},{3,123},{4,124},{5,125},{6,126},{7,127},{8... | collective-permute-start | bytes 1572872 | tf_op jit(solution)/shard_map/ppermute | solution.py:668
  107.5 14.7 %collective-permute-start.2 = (bf16[80,512]{1,0:T(8,128)(2,1)S(1)}, bf16[80,512]{1,0:T(8,128)(2,1)S(1)}, u32[]{:S(2)}, u32[]{:S(2)}) collective-permute-start(bf16[80,512]{1,0:T(8,128)(2,1)S(1)} %copy-done.22), channel_id=1, source_target_pairs={{0,127},{1,120},{2,121},{3,122},{4,123},{5,124},{6,125},{7,126},{8... | collective-permute-start | bytes 245768 | tf_op jit(solution)/shard_map/ppermute | solution.py:668
  110.9 11.3 %collective-permute-start.1 = (bf16[224,512]{1,0:T(8,128)(2,1)S(1)}, bf16[224,512]{1,0:T(8,128)(2,1)S(1)}, u32[]{:S(2)}, u32[]{:S(2)}) collective-permute-start(bf16[224,512]{1,0:T(8,128)(2,1)S(1)} %copy-done.21), channel_id=1, source_target_pairs={{0,7},{1,0},{2,1},{3,2},{4,3},{5,4},{6,5},{7,6},{8,15},{9,8},{10,9... | collective-permute-start | bytes 688136 | tf_op jit(solution)/shard_map/ppermute | solution.py:668
  111.9 10.3 %copy-start.14 = (f32[144,576]{1,0:T(8,128)S(1)}, f32[144,576]{1,0:T(8,128)}, u32[]{:S(2)}) copy-start(f32[144,576]{1,0:T(8,128)} %constant.42.clone.apart_ref) | copy-start | bytes 995332
  111.9 10.3 %copy-start.18 = (bf16[656,512]{1,0:T(8,128)(2,1)S(1)}, bf16[656,512]{1,0:T(8,128)(2,1)}, u32[]{:S(2)}) copy-start(bf16[656,512]{1,0:T(8,128)(2,1)} %get-tuple-element.50.xe) | copy-start | bytes 2015236
  122.3 17.6 %copy-start.4 = (bf16[2,384,288]{2,1,0:T(8,128)(2,1)S(1)}, bf16[2,384,288]{2,1,0:T(8,128)(2,1)}, u32[]{:S(2)}) copy-start(bf16[2,384,288]{2,1,0:T(8,128)(2,1)} %constant.43.clone.back_ref) | copy-start | bytes 1327108
  153.7 6.6 %collective-permute-start.6 = (bf16[1024,512]{1,0:T(8,128)(2,1)S(1)}, bf16[1024,512]{1,0:T(8,128)(2,1)S(1)}, u32[]{:S(2)}, u32[]{:S(2)}) collective-permute-start(bf16[1024,512]{1,0:T(8,128)(2,1)S(1)} %get-tuple-element.72), channel_id=1, source_target_pairs={{0,8},{1,9},{2,10},{3,11},{4,12},{5,13},{6,14},{7,15},{8,0},{9,1},... | collective-permute-start | bytes 3145736 | tf_op jit(solution)/shard_map/ppermute | solution.py:709
  154.0 32.3 %collective-permute-start.7 = (bf16[2,512,512]{2,1,0:T(8,128)(2,1)}, bf16[2,512,512]{2,1,0:T(8,128)(2,1)}, u32[]{:S(2)}, u32[]{:S(2)}) collective-permute-start(bf16[2,512,512]{2,1,0:T(8,128)(2,1)} %get-tuple-element.75), channel_id=1, source_target_pairs={{0,8},{1,9},{2,10},{3,11},{4,12},{5,13},{6,14},{7,15},{8,16},{9,17... | collective-permute-start | bytes 3145736 | tf_op jit(solution)/shard_map/ppermute | solution.py:668
  156.6 29.7 %collective-permute-start.8 = (bf16[2,224,512]{2,1,0:T(8,128)(2,1)S(1)}, bf16[2,224,512]{2,1,0:T(8,128)(2,1)}, u32[]{:S(2)}, u32[]{:S(2)}) collective-permute-start(bf16[2,224,512]{2,1,0:T(8,128)(2,1)S(1)} %get-tuple-element.76), channel_id=1, source_target_pairs={{0,1},{1,2},{2,3},{3,4},{4,5},{5,6},{6,7},{7,0},{8,9},{9,10},{10,1... | collective-permute-start | bytes 1376264 | tf_op jit(solution)/shard_map/ppermute | solution.py:668
  156.6 16.8 %collective-permute-start.9 = (bf16[2,80,512]{2,1,0:T(8,128)(2,1)S(1)}, bf16[2,80,512]{2,1,0:T(8,128)(2,1)}, u32[]{:S(2)}, u32[]{:S(2)}) collective-permute-start(bf16[2,80,512]{2,1,0:T(8,128)(2,1)S(1)} %get-tuple-element.77), channel_id=1, source_target_pairs={{0,9},{1,10},{2,11},{3,12},{4,13},{5,14},{6,15},{7,8},{8,17},{9,18... | collective-permute-start | bytes 491528 | tf_op jit(solution)/shard_map/ppermute | solution.py:668
  160.3 25.9 %copy-start.11 = (bf16[2,656,512]{2,1,0:T(8,128)(2,1)S(1)}, bf16[2,656,512]{2,1,0:T(8,128)(2,1)}, u32[]{:S(2)}) copy-start(bf16[2,656,512]{2,1,0:T(8,128)(2,1)} %copy-done.10) | copy-start | bytes 4030468
  162.0 31.6 %all-to-all-start.2 = ((bf16[64,16,512]{2,1,0:T(8,128)(2,1)}), bf16[64,16,512]{2,1,0:T(8,128)(2,1)S(1)}, u32[]{:S(2)}, u32[]{:S(2)}) async-start(bf16[64,16,512]{2,1,0:T(8,128)(2,1)} %bitcast.7), calls=%async_computation.2 | async-start | bytes 2097152 | tf_op jit(solution)/shard_map/all_to_all | solution.py:672
  (11 other events, 43.1 us)

commit v10 on v9

--- a/solution.py
+++ b/solution.py
@@ -422,7 +422,7 @@
 
 
 def edge_kernel(flag_ref, xe, xu, xs, xc, join_ref, apart_ref, *refs):
-    sources, (*refs, x_all) = refs[:3], refs[6:]
+    sources, (*refs, x_all, mask) = refs[:3], refs[6:]
     step = pl.program_id(0)
 
     @pl.when(step == 0)
@@ -438,7 +438,8 @@
         x_all[...] = join_corner(join_ref, xe, xs, xu, xc)
 
     seam = jnp.where(step > 0, flag_ref[0], 0).astype(F32)
-    attend(x_all[...], lambda: apart_ref[...] * seam, *sources, *refs)
+    mask[...] = apart_ref[...] * seam
+    attend(x_all[...], lambda: mask[...], *sources, *refs)
 
 
 def attend_specs(rows, skip):
@@ -477,7 +478,7 @@
         + [whole(BLOCK, 4 * SMALL), whole(WIN, 4 * WIN)]
         + sources
         + [pl.BlockSpec(memory_space=pl.ANY)] * 3,
-        outs, out_shapes, scratch + [pltpu.VMEM((BLOCK, D), F32)], cost, 16,
+        outs, out_shapes, scratch + [pltpu.VMEM((BLOCK, D), F32), pltpu.VMEM((WIN, 4 * WIN), F32)], cost, 16,
         aliases={10 + n: n for n in range(3)},
     )(flag, *parts, jnp.asarray(CORNER_JOIN, BF16), jnp.asarray(apart_matrix()), ga, *weights[:2], *carried)
 

time: 195 us -> 195 us (level)
  no operation moved by 1% of the time
where the time goes in v10:
time: 195 us; the launch traced here: 194 us
  Pallas kernels  82.1 us (42%)
  waiting for transfers between devices  40.4 us (21%)
  starting transfers between devices  30.9 us (16%)
  local copies, waits for them, and re-layouts  23.1 us (12%)
  blocking collectives  16.7 us (9%)
    all_to_all x2, waiting for transfers between devices, swap_blocks(): lax.all_to_all(values, axis, split_axis=0, concat_axis=0, axis_index_grou...  24.3 us
    ppermute x9, starting transfers between devices, exchange(): lax.ppermute(part, BOTH, shift_pairs(*step))  17.7 us
    pallas_call x1, Pallas kernels, attend_edge(): call(edge_kernel, 'attend_edge', (5,), [pl.BlockSpec(memory_space=pltpu.S...  17.5 us
    all_to_all x1, blocking collectives, swap_blocks(): lax.all_to_all(values, axis, split_axis=0, concat_axis=0, axis_index_grou...  16.7 us
    ppermute x9, waiting for transfers between devices, exchange(): lax.ppermute(part, BOTH, shift_pairs(*step))  16.1 us
    all_to_all x2, starting transfers between devices, swap_blocks(): lax.all_to_all(values, axis, split_axis=0, concat_axis=0, axis_index_grou...  12.9 us
    gather x1, local copies, waits for them, and re-layouts, per_device(): place = place.reshape(TOKENS)[ORDER].reshape(-1, 1)  12.7 us
    pallas_call x1, Pallas kernels, serve(): call(serve_kernel, 'serve', (BANDS // ASKERS,), [pl.BlockSpec((ASKERS, 1,...  10.3 us
  transfers between devices with their start and end apart: 12, of which 4 were waited for; matrix products, arithmetic and copies ran while one was open for 10% of the time, Pallas kernels for 19%

profile of v10, /device:TPU:1, one launch (start us, length us, event | category | flops | bytes accessed | tf_op | source)
XLA Modules:
  0.0 194.3 jit_solution(11046547441313911860)
XLA Ops:
  0.6 2.7 %requests.1 = (s32[16,1,288]{2,1,0:T(1,128)}, s32[1,2304]{1,0:T(1,128)}, s32[16,8]{1,0:T(8,128)}) custom-call(s32[1,2304]{1,0:T(1,128)} %bitcast.15, s32[1,2304]{1,0:T(1,128)} %bitcast.16), custom_call_target="tpu_custom_call" | custom-call | flops 100000000 | bytes 100000 | tf_op jit(solution)/shard_map/requests/pallas_call | solution.py:175
  3.3 16.7 %all_to_all.21.lists_ref = s32[16,1,288]{2,1,0:T(1,128)} all-to-all(s32[16,1,288]{2,1,0:T(1,128)} %get-tuple-element.46), channel_id=1, replica_groups=mesh['lat'=16,'lon'=8] {'lat'}, dimensions={0} | all-to-all | bytes 36864 | tf_op jit(solution)/shard_map/all_to_all | solution.py:673
  20.0 10.3 %serve.1 = bf16[4608,512]{1,0:T(8,128)(2,1)} custom-call(s32[16,1,288]{2,1,0:T(1,128)} %all_to_all.21.lists_ref, bf16[1152,512]{1,0:T(8,128)(2,1)} %buffer_ref.1), custom_call_target="tpu_custom_call" | custom-call | flops 5400000000 | bytes 6000000 | tf_op jit(solution)/shard_map/serve/pallas_call | solution.py:200
  30.3 4.7 %all-to-all-start.1 = ((bf16[16,288,512]{2,1,0:T(8,128)(2,1)}), bf16[16,288,512]{2,1,0:T(8,128)(2,1)}, u32[]{:S(2)}, u32[]{:S(2)}) async-start(bf16[16,288,512]{2,1,0:T(8,128)(2,1)} %bitcast.14), calls=%async_computation.1 | async-start | bytes 9437184 | tf_op jit(solution)/shard_map/all_to_all | solution.py:673
  35.0 3.9 %reshape.51.grid_ref = bf16[2304,512]{1,0:T(8,128)(2,1)S(1)} reshape(bf16[12,48,4,512]{3,2,1,0:T(4,128)(2,1)} %param.22) | data formatting | bytes 4718592 | tf_op jit(solution)/shard_map/reshape | solution.py:691
  39.0 1.5 sort_pieces.1
  41.7 7.9 %collective-permute-start.5 = (bf16[80,512]{1,0:T(8,128)(2,1)}, bf16[80,512]{1,0:T(8,128)(2,1)}, u32[]{:S(2)}, u32[]{:S(2)}) collective-permute-start(bf16[80,512]{1,0:T(8,128)(2,1)} %get-tuple-element.57), channel_id=1, source_target_pairs={{0,127},{1,120},{2,121},{3,122},{4,123},{5,124},{6,125},{7,126},{8... | collective-permute-start | bytes 245768 | tf_op jit(solution)/shard_map/ppermute | solution.py:669
  50.8 12.7 %gather_fusion = s32[2336]{0:T(1024)S(1)} fusion(s32[2304]{0:T(1024)S(1)} %reduce, s32[3072]{0:T(1024)S(1)} %pad_clamp_fusion), kind=kCustom, calls=%fused_computation | custom fusion | bytes 28032 | tf_op jit(solution)/shard_map/gather | solution.py:695
  63.5 1.9 reshape.63.place_ref
  68.6 23.3 %all-to-all-done.1 = bf16[16,288,512]{2,1,0:T(8,128)(2,1)} async-done(((bf16[16,288,512]{2,1,0:T(8,128)(2,1)}), bf16[16,288,512]{2,1,0:T(8,128)(2,1)}, u32[]{:S(2)}, u32[]{:S(2)}) %all-to-all-start.1) | async-done | bytes 4718624 | tf_op jit(solution)/shard_map/all_to_all | solution.py:673
  91.9 9.6 %pick.1 = (bf16[512,512]{1,0:T(8,128)(2,1)}, bf16[224,512]{1,0:T(8,128)(2,1)}, bf16[80,512]{1,0:T(8,128)(2,1)}, bf16[864,512]{1,0:T(8,128)(2,1)}, bf16[656,512]{1,0:T(8,128)(2,1)}) custom-call(s32[16,8]{1,0:T(8,128)} %get-tuple-element.44.table_ref, s32[2336,1]{1,0:T(8,128)} %reshape.63.place_ref, bf16[4608,512]{1,0:T(8,128)(2,1)} %bitcast.5.replies_ref), custom_call_target="tpu_custom_call" | custom-call | flops 3600000000 | bytes 8000000 | tf_op jit(solution)/shard_map/pick/pallas_call | solution.py:249
  103.0 4.5 %prepare_edge.1 = (bf16[2304,512]{1,0:T(8,128)(2,1)S(1)}, bf16[1440,512]{1,0:T(8,128)(2,1)S(1)}) custom-call(bf16[656,512]{1,0:T(8,128)(2,1)S(1)} %get-tuple-element.54.edge, bf16[512,512]{1,0:T(8,128)(2,1)} %collective-permute-done.3.up, bf16[224,512]{1,0:T(8,128)(2,1)} %collective-permute-done.4.side, ...), custom_call_target="tpu_custom_call", output_to_operand_aliasing={{0}: (6, {})} | custom-call | flops 800000000 | bytes 5000000 | tf_op jit(solution)/shard_map/prepare_edge/pallas_call | solution.py:410
  107.5 3.5 %collective-permute-start.2 = (bf16[80,512]{1,0:T(8,128)(2,1)S(1)}, bf16[80,512]{1,0:T(8,128)(2,1)S(1)}, u32[]{:S(2)}, u32[]{:S(2)}) collective-permute-start(bf16[80,512]{1,0:T(8,128)(2,1)S(1)} %copy-done.22), channel_id=1, source_target_pairs={{0,127},{1,120},{2,121},{3,122},{4,123},{5,124},{6,125},{7,126},{8... | collective-permute-start | bytes 245768 | tf_op jit(solution)/shard_map/ppermute | solution.py:669
  111.9 10.3 %attend_inner.1 = (bf16[2304,512]{1,0:T(8,128)(2,1)S(1)}, bf16[2304,1024]{1,0:T(8,128)(2,1)S(1)}, bf16[2304,1536]{1,0:T(8,128)(2,1)S(1)}) custom-call(bf16[864,512]{1,0:T(8,128)(2,1)S(1)} %copy-done.17, bf16[864,512]{1,0:T(8,128)(2,1)S(1)} %copy-done.16, bf16[512,1536]{1,0:T(8,128)(2,1)S(1)} %copy-done, f32[1,512]{1,0:T(1,128)S(1)} %bitcast.10), custom_call_target="tpu_custom_call" | custom-call | flops 5184000000 | bytes 8640000 | tf_op jit(solution)/shard_map/attend_inner/pallas_call | solution.py:460
  122.2 17.5 %attend_edge.1 = (bf16[2304,512]{1,0:T(8,128)(2,1)S(1)}, bf16[2304,1024]{1,0:T(8,128)(2,1)S(1)}, bf16[2304,1536]{1,0:T(8,128)(2,1)S(1)}) custom-call(s32[1]{0:T(128)} %bitcast.1.flag_ref, bf16[656,512]{1,0:T(8,128)(2,1)S(1)} %copy-done.18, ...), custom_call_target="tpu_custom_call", output_to_operand_aliasing={{0}: (10, {}), {1}: (11, {}), {2}: (12, {})} | custom-call | flops 8640000000 | bytes 14400000 | tf_op jit(solution)/shard_map/attend_edge/pallas_call | solution.py:474
  139.8 8.5 %finish_edge.1 = (bf16[2,656,512]{2,1,0:T(8,128)(2,1)S(1)}, bf16[2,512,512]{2,1,0:T(8,128)(2,1)}, bf16[2,224,512]{2,1,0:T(8,128)(2,1)S(1)}, bf16[2,80,512]{2,1,0:T(8,128)(2,1)S(1)}) custom-call(bf16[2,384,288]{2,1,0:T(8,128)(2,1)S(1)} %copy-done.4, bf16[2304,512]{1,0:T(8,128)(2,1)S(1)} %get-tuple-element.67.refs_0_, ...), custom_call_target="tpu_custom_call" | custom-call | flops 3168000000 | bytes 12960000 | tf_op jit(solution)/shard_map/finish_edge/pallas_call | solution.py:591
  148.2 5.3 %weight_terms.1 = (f32[1024,512]{1,0:T(8,128)S(1)}, bf16[1024,512]{1,0:T(8,128)(2,1)S(1)}) custom-call(s32[1]{0:T(128)} %bitcast.core_ref, bf16[2304,1024]{1,0:T(8,128)(2,1)S(1)} %get-tuple-element.70.refs_1_.left_ref, bf16[2304,1536]{1,0:T(8,128)(2,1)S(1)} %get-tuple-element.71.refs_2_.dp_ref, bf16[2304,512]{1,0:T(8,128)(2,1)S(1)} %get-tuple-element.68.refs_3_.cot_ref), custom_call_target="tpu_custom_call" | custom-call | flops 1000 | bytes 1000 | tf_op jit(solution)/shard_map/weight_terms/pallas_call | solution.py:501
  153.9 2.6 %collective-permute-start.7 = (bf16[2,512,512]{2,1,0:T(8,128)(2,1)}, bf16[2,512,512]{2,1,0:T(8,128)(2,1)}, u32[]{:S(2)}, u32[]{:S(2)}) collective-permute-start(bf16[2,512,512]{2,1,0:T(8,128)(2,1)} %get-tuple-element.75), channel_id=1, source_target_pairs={{0,8},{1,9},{2,10},{3,11},{4,12},{5,13},{6,14},{7,15},{8,16},{9,17... | collective-permute-start | bytes 3145736 | tf_op jit(solution)/shard_map/ppermute | solution.py:669
  156.5 3.7 %finish_inner.1.inner = bf16[2,864,512]{2,1,0:T(8,128)(2,1)S(1)} custom-call(bf16[144,144]{1,0:T(8,128)(2,1)S(1)} %copy-done.6, bf16[2304,512]{1,0:T(8,128)(2,1)S(1)} %get-tuple-element.67.refs_0_, bf16[2304,1024]{1,0:T(8,128)(2,1)S(1)} %get-tuple-element.70.refs_1_.left_ref, bf16[2304,1536]{1,0:T(8,128)(2,1)S(1)} %get-tuple-element.71.refs_2_.dp_ref, ...), custom_call_target="tpu_custom_call" | custom-call | flops 1000 | bytes 1000 | tf_op jit(solution)/shard_map/finish_inner/pallas_call | solution.py:582
  160.3 1.6 add_halves.1
  161.9 8.2 %all-to-all-start.2 = ((bf16[64,16,512]{2,1,0:T(8,128)(2,1)}), bf16[64,16,512]{2,1,0:T(8,128)(2,1)S(1)}, u32[]{:S(2)}, u32[]{:S(2)}) async-start(bf16[64,16,512]{2,1,0:T(8,128)(2,1)} %bitcast.7), calls=%async_computation.2 | async-start | bytes 2097152 | tf_op jit(solution)/shard_map/all_to_all | solution.py:673
  170.1 3.2 %collective-permute-done.9.corner = bf16[2,80,512]{2,1,0:T(8,128)(2,1)} collective-permute-done((bf16[2,80,512]{2,1,0:T(8,128)(2,1)S(1)}, bf16[2,80,512]{2,1,0:T(8,128)(2,1)}, u32[]{:S(2)}, u32[]{:S(2)}) %collective-permute-start.9) | collective-permute-done | bytes 163872 | tf_op jit(solution)/shard_map/ppermute | solution.py:669
  173.3 12.9 %collective-permute-done.8.side = bf16[2,224,512]{2,1,0:T(8,128)(2,1)} collective-permute-done((bf16[2,224,512]{2,1,0:T(8,128)(2,1)S(1)}, bf16[2,224,512]{2,1,0:T(8,128)(2,1)}, u32[]{:S(2)}, u32[]{:S(2)}) %collective-permute-start.8) | collective-permute-done | bytes 458784 | tf_op jit(solution)/shard_map/ppermute | solution.py:669
  187.7 4.7 %join.1 = (bf16[12,48,4,512]{3,2,1,0:T(4,128)(2,1)}, bf16[12,48,4,512]{3,2,1,0:T(4,128)(2,1)}) custom-call(bf16[2,864,512]{2,1,0:T(8,128)(2,1)S(1)} %copy-done.3, bf16[2,656,512]{2,1,0:T(8,128)(2,1)S(1)} %copy-done.11, bf16[2,512,512]{2,1,0:T(8,128)(2,1)} %collective-permute-done.7.up, bf16[2,224,512]{2,1,0:T(8,128)(2,1)} %collective-permute-done.8.side, ...), custom_call_target="tpu_custom_call" | custom-call | flops 60000002048 | bytes 9000000 | tf_op jit(solution)/shard_map/join/pallas_call | solution.py:636
  (66 shorter events, 11.6 us)
Async XLA Ops:
  30.3 61.6 %all-to-all-start.1 = ((bf16[16,288,512]{2,1,0:T(8,128)(2,1)}), bf16[16,288,512]{2,1,0:T(8,128)(2,1)}, u32[]{:S(2)}, u32[]{:S(2)}) async-start(bf16[16,288,512]{2,1,0:T(8,128)(2,1)} %bitcast.14), calls=%async_computation.1 | async-start | bytes 9437184 | tf_op jit(solution)/shard_map/all_to_all | solution.py:673
  38.9 11.8 %copy-start.20 = (s32[1,2304]{1,0:T(1,128)S(1)}, s32[1,2304]{1,0:T(1,128)}, u32[]{:S(2)}) copy-start(s32[1,2304]{1,0:T(1,128)} %get-tuple-element.45) | copy-start | bytes 27652
  38.9 11.8 %copy-start.19 = (s32[2336]{0:T(1024)S(1)}, s32[2336]{0:T(1024)}, u32[]{:S(2)}) copy-start(s32[2336]{0:T(1024)} %constant.48) | copy-start | bytes 28036
  41.4 61.5 %collective-permute-start.3 = (bf16[512,512]{1,0:T(8,128)(2,1)}, bf16[512,512]{1,0:T(8,128)(2,1)}, u32[]{:S(2)}, u32[]{:S(2)}) collective-permute-start(bf16[512,512]{1,0:T(8,128)(2,1)} %get-tuple-element.55), channel_id=1, source_target_pairs={{0,120},{1,121},{2,122},{3,123},{4,124},{5,125},{6,126},{7,127},{8... | collective-permute-start | bytes 1572872 | tf_op jit(solution)/shard_map/ppermute | solution.py:669
  41.7 61.2 %collective-permute-start.5 = (bf16[80,512]{1,0:T(8,128)(2,1)}, bf16[80,512]{1,0:T(8,128)(2,1)}, u32[]{:S(2)}, u32[]{:S(2)}) collective-permute-start(bf16[80,512]{1,0:T(8,128)(2,1)} %get-tuple-element.57), channel_id=1, source_target_pairs={{0,127},{1,120},{2,121},{3,122},{4,123},{5,124},{6,125},{7,126},{8... | collective-permute-start | bytes 245768 | tf_op jit(solution)/shard_map/ppermute | solution.py:669
  49.5 53.4 %collective-permute-start.4 = (bf16[224,512]{1,0:T(8,128)(2,1)}, bf16[224,512]{1,0:T(8,128)(2,1)}, u32[]{:S(2)}, u32[]{:S(2)}) collective-permute-start(bf16[224,512]{1,0:T(8,128)(2,1)} %get-tuple-element.56), channel_id=1, source_target_pairs={{0,7},{1,0},{2,1},{3,2},{4,3},{5,4},{6,5},{7,6},{8,15},{9,8},{10,9... | collective-permute-start | bytes 688136 | tf_op jit(solution)/shard_map/ppermute | solution.py:669
  50.8 14.6 %copy-start.1 = (bf16[512,512]{1,0:T(8,128)(2,1)S(1)}, bf16[512,512]{1,0:T(8,128)(2,1)}, u32[]{:S(2)}) copy-start(bf16[512,512]{1,0:T(8,128)(2,1)} %refs_6_.3) | copy-start | bytes 1572868
  91.9 11.1 %copy-start.7 = (bf16[288,320]{1,0:T(8,128)(2,1)S(1)}, bf16[288,320]{1,0:T(8,128)(2,1)}, u32[]{:S(2)}) copy-start(bf16[288,320]{1,0:T(8,128)(2,1)} %constant.39.clone.join_ref) | copy-start | bytes 552964
  101.5 10.4 %copy-start = (bf16[512,1536]{1,0:T(8,128)(2,1)S(1)}, bf16[512,1536]{1,0:T(8,128)(2,1)}, u32[]{:S(2)}) copy-start(bf16[512,1536]{1,0:T(8,128)(2,1)} %refs_4_.3) | copy-start | bytes 4718596
  101.5 10.4 %copy-start.9 = (f32[512]{0:T(512)S(1)}, f32[512]{0:T(512)}, u32[]{:S(2)}) copy-start(f32[512]{0:T(512)} %param.19) | copy-start | bytes 6148
  101.5 10.4 %copy-start.16 = (bf16[864,512]{1,0:T(8,128)(2,1)S(1)}, bf16[864,512]{1,0:T(8,128)(2,1)}, u32[]{:S(2)}) copy-start(bf16[864,512]{1,0:T(8,128)(2,1)} %copy-done.15) | copy-start | bytes 2654212
  101.5 10.4 %copy-start.17 = (bf16[864,512]{1,0:T(8,128)(2,1)S(1)}, bf16[864,512]{1,0:T(8,128)(2,1)}, u32[]{:S(2)}) copy-start(bf16[864,512]{1,0:T(8,128)(2,1)} %get-tuple-element.60.x_ref) | copy-start | bytes 2654212
  101.5 20.7 %collective-permute-start = (bf16[512,512]{1,0:T(8,128)(2,1)}, bf16[512,512]{1,0:T(8,128)(2,1)S(1)}, u32[]{:S(2)}, u32[]{:S(2)}) collective-permute-start(bf16[512,512]{1,0:T(8,128)(2,1)} %get-tuple-element.51), channel_id=1, source_target_pairs={{0,120},{1,121},{2,122},{3,123},{4,124},{5,125},{6,126},{7,127},{8... | collective-permute-start | bytes 1572872 | tf_op jit(solution)/shard_map/ppermute | solution.py:669
  107.5 14.7 %collective-permute-start.2 = (bf16[80,512]{1,0:T(8,128)(2,1)S(1)}, bf16[80,512]{1,0:T(8,128)(2,1)S(1)}, u32[]{:S(2)}, u32[]{:S(2)}) collective-permute-start(bf16[80,512]{1,0:T(8,128)(2,1)S(1)} %copy-done.22), channel_id=1, source_target_pairs={{0,127},{1,120},{2,121},{3,122},{4,123},{5,124},{6,125},{7,126},{8... | collective-permute-start | bytes 245768 | tf_op jit(solution)/shard_map/ppermute | solution.py:669
  111.0 11.2 %collective-permute-start.1 = (bf16[224,512]{1,0:T(8,128)(2,1)S(1)}, bf16[224,512]{1,0:T(8,128)(2,1)S(1)}, u32[]{:S(2)}, u32[]{:S(2)}) collective-permute-start(bf16[224,512]{1,0:T(8,128)(2,1)S(1)} %copy-done.21), channel_id=1, source_target_pairs={{0,7},{1,0},{2,1},{3,2},{4,3},{5,4},{6,5},{7,6},{8,15},{9,8},{10,9... | collective-permute-start | bytes 688136 | tf_op jit(solution)/shard_map/ppermute | solution.py:669
  111.9 10.3 %copy-start.14 = (f32[144,576]{1,0:T(8,128)S(1)}, f32[144,576]{1,0:T(8,128)}, u32[]{:S(2)}) copy-start(f32[144,576]{1,0:T(8,128)} %constant.42.clone.apart_ref) | copy-start | bytes 995332
  111.9 10.3 %copy-start.18 = (bf16[656,512]{1,0:T(8,128)(2,1)S(1)}, bf16[656,512]{1,0:T(8,128)(2,1)}, u32[]{:S(2)}) copy-start(bf16[656,512]{1,0:T(8,128)(2,1)} %get-tuple-element.50.xe) | copy-start | bytes 2015236
  122.2 17.5 %copy-start.4 = (bf16[2,384,288]{2,1,0:T(8,128)(2,1)S(1)}, bf16[2,384,288]{2,1,0:T(8,128)(2,1)}, u32[]{:S(2)}) copy-start(bf16[2,384,288]{2,1,0:T(8,128)(2,1)} %constant.43.clone.back_ref) | copy-start | bytes 1327108
  153.6 6.7 %collective-permute-start.6 = (bf16[1024,512]{1,0:T(8,128)(2,1)S(1)}, bf16[1024,512]{1,0:T(8,128)(2,1)S(1)}, u32[]{:S(2)}, u32[]{:S(2)}) collective-permute-start(bf16[1024,512]{1,0:T(8,128)(2,1)S(1)} %get-tuple-element.72), channel_id=1, source_target_pairs={{0,8},{1,9},{2,10},{3,11},{4,12},{5,13},{6,14},{7,15},{8,0},{9,1},... | collective-permute-start | bytes 3145736 | tf_op jit(solution)/shard_map/ppermute | solution.py:710
  153.9 32.3 %collective-permute-start.7 = (bf16[2,512,512]{2,1,0:T(8,128)(2,1)}, bf16[2,512,512]{2,1,0:T(8,128)(2,1)}, u32[]{:S(2)}, u32[]{:S(2)}) collective-permute-start(bf16[2,512,512]{2,1,0:T(8,128)(2,1)} %get-tuple-element.75), channel_id=1, source_target_pairs={{0,8},{1,9},{2,10},{3,11},{4,12},{5,13},{6,14},{7,15},{8,16},{9,17... | collective-permute-start | bytes 3145736 | tf_op jit(solution)/shard_map/ppermute | solution.py:669
  156.5 29.7 %collective-permute-start.8 = (bf16[2,224,512]{2,1,0:T(8,128)(2,1)S(1)}, bf16[2,224,512]{2,1,0:T(8,128)(2,1)}, u32[]{:S(2)}, u32[]{:S(2)}) collective-permute-start(bf16[2,224,512]{2,1,0:T(8,128)(2,1)S(1)} %get-tuple-element.76), channel_id=1, source_target_pairs={{0,1},{1,2},{2,3},{3,4},{4,5},{5,6},{6,7},{7,0},{8,9},{9,10},{10,1... | collective-permute-start | bytes 1376264 | tf_op jit(solution)/shard_map/ppermute | solution.py:669
  156.5 16.7 %collective-permute-start.9 = (bf16[2,80,512]{2,1,0:T(8,128)(2,1)S(1)}, bf16[2,80,512]{2,1,0:T(8,128)(2,1)}, u32[]{:S(2)}, u32[]{:S(2)}) collective-permute-start(bf16[2,80,512]{2,1,0:T(8,128)(2,1)S(1)} %get-tuple-element.77), channel_id=1, source_target_pairs={{0,9},{1,10},{2,11},{3,12},{4,13},{5,14},{6,15},{7,8},{8,17},{9,18... | collective-permute-start | bytes 491528 | tf_op jit(solution)/shard_map/ppermute | solution.py:669
  160.3 25.9 %copy-start.11 = (bf16[2,656,512]{2,1,0:T(8,128)(2,1)S(1)}, bf16[2,656,512]{2,1,0:T(8,128)(2,1)}, u32[]{:S(2)}) copy-start(bf16[2,656,512]{2,1,0:T(8,128)(2,1)} %copy-done.10) | copy-start | bytes 4030468
  161.9 31.5 %all-to-all-start.2 = ((bf16[64,16,512]{2,1,0:T(8,128)(2,1)}), bf16[64,16,512]{2,1,0:T(8,128)(2,1)S(1)}, u32[]{:S(2)}, u32[]{:S(2)}) async-start(bf16[64,16,512]{2,1,0:T(8,128)(2,1)} %bitcast.7), calls=%async_computation.2 | async-start | bytes 2097152 | tf_op jit(solution)/shard_map/all_to_all | solution.py:673
  (11 other events, 43.2 us)
